TPU v7x, 256 devices: a whole 4x4x8 slice. The times are simulated.
256 devices in a mesh: seq: 32 (over y, x, core), head: 8 (over z).
Axes of the slice: x: 4, y: 4, z: 8, core: 2. Of those that a mesh axis runs over, the one named last changes fastest.
Arguments:
- tokens: bfloat16 [16384, 6144], P('seq', 'head'), may hold values from -6 to 6
- w_query: bfloat16 [6144, 4096], P('seq', 'head'), may hold values from -0.078125 to 0.078125
- w_key: bfloat16 [6144, 4096], P('seq', 'head'), may hold values from -0.078125 to 0.078125
- w_value: bfloat16 [6144, 4096], P('seq', 'head'), may hold values from -0.078125 to 0.078125
- gain: float32 [4096], P('head'), may hold values from 0.1 to 1.9
Outputs:
- output: bfloat16 [16384, 4096], P('seq', 'head')
All inputs are finite; a program needn't handle non-finite values.
Results may differ from a plain program's by a relative error of at most 0.007.
Values may be sent and summed in bfloat16 or wider, within the bound.
No kernel may reach another device: no remote copies, remote signals or barrier semaphores. Data moves between devices by JAX's collectives and lax.ppermute only.
A program may use at most 128 MiB of HBM per device.

v0:
```python
import jax
import jax.numpy as jnp
from jax import lax
from jax.sharding import PartitionSpec as P

HDIM = 128
SPAN = 256


def carried_in(array, axis, combine, identity):
    devices, position = (lax.axis_size(axis), lax.axis_index(axis))
    everything = lax.all_gather(array.astype(jnp.bfloat16), axis)
    start = jnp.broadcast_to(jnp.asarray(identity, array.dtype), array.shape)

    def lap(k, before):
        reached = k < position
        new = combine(before, everything[k].astype(array.dtype))
        return jnp.where(reached, new, before)

    return lax.fori_loop(0, devices, lap, start)


def add_rows(whole, piece):
    return jnp.dot(whole, piece, preferred_element_type=jnp.float32)


def local(tokens, w_query, w_key, w_value, gain):
    whole = lax.all_gather(tokens, "head", axis=1, tiled=True)
    tok_rows = whole.shape[0]
    columns_here = w_query.shape[1]

    def add_one(piece):
        return add_rows(whole, piece)

    query_sum = add_one(lax.all_gather(w_query, "seq", axis=0, tiled=True))
    key_sum = add_one(lax.all_gather(w_key, "seq", axis=0, tiled=True))
    value_sum = add_one(lax.all_gather(w_value, "seq", axis=0, tiled=True))
    heads_here = columns_here // HDIM
    blocks = tok_rows // SPAN

    def to_blocks(values):
        return jax.nn.silu(values).astype(jnp.bfloat16).reshape(blocks, SPAN, heads_here, HDIM)

    query_blocks = to_blocks(query_sum)
    key_blocks = to_blocks(key_sum)
    value_blocks = to_blocks(value_sum)
    pair_states = jnp.einsum(
        "cshd,cshe->chde", key_blocks, value_blocks, preferred_element_type=jnp.float32
    )
    slab_total = jnp.sum(pair_states, axis=0)
    within = jnp.cumsum(pair_states, axis=0) - pair_states
    earlier = carried_in(slab_total, "seq", jnp.add, jnp.zeros_like(slab_total))
    states = (earlier[None] + within).astype(jnp.bfloat16)
    scores = jnp.einsum(
        "cshd,cthd->chst", query_blocks, key_blocks, preferred_element_type=jnp.float32
    )
    causal = lax.broadcasted_iota(jnp.int32, (SPAN, SPAN), 0) >= lax.broadcasted_iota(
        jnp.int32, (SPAN, SPAN), 1
    )
    scores = jnp.where(causal[None, None], scores, 0.0).astype(jnp.bfloat16)
    local_part = jnp.einsum(
        "chst,cthe->cshe", scores, value_blocks, preferred_element_type=jnp.float32
    )
    carried = jnp.einsum(
        "cshd,chde->cshe", query_blocks, states, preferred_element_type=jnp.float32
    )
    attended = local_part + carried
    inverse_rms = lax.rsqrt(jnp.mean(attended * attended, axis=-1, keepdims=True) + 1e-06)
    return (
        (attended * inverse_rms * gain.reshape(heads_here, HDIM))
        .astype(jnp.bfloat16)
        .reshape(tok_rows, columns_here)
    )


def solution(mesh):
    in_specs = (P("seq", "head"), P("seq", "head"), P("seq", "head"), P("seq", "head"), P("head"))
    out_specs = P("seq", "head")
    return jax.shard_map(local, mesh=mesh, in_specs=in_specs, out_specs=out_specs, check_vma=False)
```

profile of v0, /device:TPU:1, one launch (start us, length us, event | category | flops | bytes accessed | tf_op | source)
XLA Modules:
  0.0 352.3 jit_solution(17569557021886751319)
XLA Ops:
  6.5 0.0 all-gather.7.cloned.1.call-start
  6.5 0.7 all-gather.7.cloned.1.call-update
  7.3 0.0 all-gather.13.cloned.1.call-start
  7.3 0.7 all-gather.13.cloned.1.call-update
  8.0 0.0 all-gather.9.cloned.1.call-start
  8.1 0.7 all-gather.9.cloned.1.call-update
  8.7 0.0 all-gather.11.cloned.1.call-start
  8.8 0.5 all-gather.11.cloned.1.call-update
  9.3 0.0 all-gather.15.cloned.1.call-start
  9.4 78.1 %all-gather.7.cloned.1.call-done = bf16[512,6144]{1,0:T(8,128)(2,1)} async-done(((bf16[512,768]{1,0:T(8,128)(2,1)}), bf16[512,6144]{1,0:T(8,128)(2,1)}) %all-gather.7.cloned.1.call-update) | async-done | bytes 6291472 | tf_op jit(solution)/shard_map/all_gather | solution.py:28
  87.4 55.8 %all-gather.13.cloned.1.call-done = bf16[6144,512]{1,0:T(8,128)(2,1)} async-done(((bf16[192,512]{1,0:T(8,128)(2,1)}), bf16[6144,512]{1,0:T(8,128)(2,1)}) %all-gather.13.cloned.1.call-update) | async-done | bytes 6291472 | tf_op jit(solution)/shard_map/all_gather | solution.py:36
  143.2 8.2 %multiply_convert_fusion.1 = bf16[512,512]{1,0:T(8,128)(2,1)S(1)} fusion(bf16[512,6144]{1,0:T(8,128)(2,1)} %all-gather.7.cloned.1.call-done, bf16[6144,512]{1,0:T(8,128)(2,1)} %all-gather.13.cloned.1.call-done), kind=kOutput, calls=%fused_computation.11 | convolution fusion | flops 3222536192 | bytes 13107200 | tf_op jit(solution)/shard_map/dot_general | solution.py:24
  151.4 0.1 reshape.41
  151.5 0.3 copy.20
  151.8 47.2 %all-gather.9.cloned.1.call-done = bf16[6144,512]{1,0:T(8,128)(2,1)} async-done(((bf16[192,512]{1,0:T(8,128)(2,1)}), bf16[6144,512]{1,0:T(8,128)(2,1)}) %all-gather.9.cloned.1.call-update) | async-done | bytes 6291472 | tf_op jit(solution)/shard_map/all_gather | solution.py:37
  199.0 8.2 %multiply_convert_fusion.3 = bf16[512,512]{1,0:T(8,128)(2,1)S(1)} fusion(bf16[512,6144]{1,0:T(8,128)(2,1)} %all-gather.7.cloned.1.call-done, bf16[6144,512]{1,0:T(8,128)(2,1)} %all-gather.9.cloned.1.call-done), kind=kOutput, calls=%fused_computation.13 | convolution fusion | flops 3222536192 | bytes 13107200 | tf_op jit(solution)/shard_map/dot_general | solution.py:24
  207.1 0.1 reshape.39
  207.3 0.9 fusion.15
  208.2 0.0 all-gather.15.cloned.1.call-update
  208.3 46.3 %all-gather.11.cloned.1.call-done = bf16[6144,512]{1,0:T(8,128)(2,1)} async-done(((bf16[192,512]{1,0:T(8,128)(2,1)}), bf16[6144,512]{1,0:T(8,128)(2,1)}) %all-gather.11.cloned.1.call-update) | async-done | bytes 6291472 | tf_op jit(solution)/shard_map/all_gather | solution.py:35
  254.6 8.2 %multiply_convert_fusion.2 = bf16[512,512]{1,0:T(8,128)(2,1)S(1)} fusion(bf16[512,6144]{1,0:T(8,128)(2,1)} %all-gather.7.cloned.1.call-done, bf16[6144,512]{1,0:T(8,128)(2,1)} %all-gather.11.cloned.1.call-done), kind=kOutput, calls=%fused_computation.12 | convolution fusion | flops 3222536192 | bytes 13107200 | tf_op jit(solution)/shard_map/dot_general | solution.py:24
  262.7 0.0 copy-start
  262.7 0.1 reshape.40
  262.9 44.3 %all-gather.15.cloned.1.call-done = bf16[128,128,128]{2,1,0:T(8,128)(2,1)} async-done(((bf16[4,128,128]{2,1,0:T(8,128)(2,1)}), bf16[128,128,128]{2,1,0:T(8,128)(2,1)}) %all-gather.15.cloned.1.call-update) | async-done | bytes 4194320 | tf_op jit(solution)/shard_map/all_gather | solution.py:12
  307.1 33.9 %while.14 = (s32[]{:T(128)}, f32[4,128,128]{2,1,0:T(8,128)S(1)}, s32[]{:T(128)}, bf16[32,4,128,128]{3,2,1,0:T(8,128)(2,1)}, s32[]{:T(128)}, /*index=5*/s32[]{:T(128)}) while((s32[]{:T(128)}, f32[4,128,128]{2,1,0:T(8,128)S(1)}, s32[]{:T(128)}, bf16[32,4,128,128]{3,2,1,0:T(8,128)(2,1)}, s32[]{:T(128)}, /*index=5*/s32[]{:T(128)}) %tuple.47), condition=%wide.region_2.3_spmd.clone, body=%wide.region_1.2_spmd.clone.sunk | while | flops 262148 | bytes 655461 | solution.py:20
  307.1 1.0 add_select_fusion.2
  308.2 1.0 add_select_fusion.2
  309.2 1.0 add_select_fusion.2
  310.3 1.0 add_select_fusion.2
  311.4 1.0 add_select_fusion.2
  312.4 1.0 add_select_fusion.2
  313.5 1.0 add_select_fusion.2
  314.6 1.0 add_select_fusion.2
  315.6 1.0 add_select_fusion.2
  316.7 1.0 add_select_fusion.2
  317.7 1.0 add_select_fusion.2
  318.8 1.0 add_select_fusion.2
  319.9 1.0 add_select_fusion.2
  320.9 1.0 add_select_fusion.2
  322.0 1.0 add_select_fusion.2
  323.0 1.0 add_select_fusion.2
  324.1 1.0 add_select_fusion.2
  325.2 1.0 add_select_fusion.2
  326.2 1.0 add_select_fusion.2
  327.3 1.0 add_select_fusion.2
  328.3 1.0 add_select_fusion.2
  329.4 1.0 add_select_fusion.2
  330.5 1.0 add_select_fusion.2
  331.5 1.0 add_select_fusion.2
  332.6 1.0 add_select_fusion.2
  333.6 1.0 add_select_fusion.2
  334.7 1.0 add_select_fusion.2
  335.8 1.0 add_select_fusion.2
  336.8 1.0 add_select_fusion.2
  337.9 1.0 add_select_fusion.2
  338.9 1.0 add_select_fusion.2
  340.0 1.0 add_select_fusion.2
  341.1 0.1 fusion.4
  341.1 0.3 fusion.10
  341.5 1.7 multiply_reduce_fusion
  343.2 0.0 copy-done
  343.2 1.4 multiply_convert_fusion
  344.6 0.3 copy.24
  344.9 0.9 copy.43
  (3 shorter events, 0.0 us)
Async XLA Ops:
  6.5 80.9 %all-gather.7.cloned.1.call-start = ((), (), s32[]{:S(2)}) async-start(), calls=%async_computation | async-start | bytes 7077888 | tf_op jit(solution)/shard_map/all_gather | solution.py:28
  7.3 135.9 %all-gather.13.cloned.1.call-start = ((), (), s32[]{:S(2)}) async-start(), calls=%async_computation.3 | async-start | bytes 6488064 | tf_op jit(solution)/shard_map/all_gather | solution.py:36
  8.0 191.0 %all-gather.9.cloned.1.call-start = ((), (), s32[]{:S(2)}) async-start(), calls=%async_computation.1 | async-start | bytes 6488064 | tf_op jit(solution)/shard_map/all_gather | solution.py:37
  8.7 245.8 %all-gather.11.cloned.1.call-start = ((), (), s32[]{:S(2)}) async-start(), calls=%async_computation.2 | async-start | bytes 6488064 | tf_op jit(solution)/shard_map/all_gather | solution.py:35
  9.3 297.8 %all-gather.15.cloned.1.call-start = ((), (), s32[]{:S(2)}) async-start(), calls=%async_computation.4 | async-start | bytes 4325376 | tf_op jit(solution)/shard_map/all_gather | solution.py:12
  262.7 80.5 %copy-start = (f32[512]{0:T(512)S(1)}, f32[512]{0:T(512)}, u32[]{:S(2)}) copy-start(f32[512]{0:T(512)} %param.11) | copy-start | bytes 6148
Sparse Core Ops, SparseCore 0:
  9.1 78.2 all-gather.6
  90.0 53.1 all-gather.12
  145.8 53.1 all-gather.8
  201.4 53.1 all-gather.10
  257.0 50.1 all-gather.14
where the time goes:
time: 353 us; the launch traced here: 352 us
  waiting for transfers between devices  274 us (78%)
  other arithmetic  34.7 us (10%)
  matrix products  27.5 us (8%)
  between operations  13.3 us (4%)
    all_gather x1, waiting for transfers between devices, local(): whole = lax.all_gather(tokens, 'head', axis=1, tiled=True)  78.1 us
    all_gather x1, waiting for transfers between devices, local(): key_sum = add_one(lax.all_gather(w_key, 'seq', axis=0, tiled=True))  55.8 us
    all_gather x1, waiting for transfers between devices, local(): value_sum = add_one(lax.all_gather(w_value, 'seq', axis=0, tiled=True))  47.2 us
    all_gather x1, waiting for transfers between devices, local(): query_sum = add_one(lax.all_gather(w_query, 'seq', axis=0, tiled=True))  46.3 us
    all_gather x1, waiting for transfers between devices, carried_in(): everything = lax.all_gather(array.astype(jnp.bfloat16), axis)  44.3 us
    select_n x32, other arithmetic, lap(): return jnp.where(reached, new, before)  33.2 us
    dot_general x3, matrix products, add_rows(): return jnp.dot(whole, piece, preferred_element_type=jnp.float32)  24.5 us
  transfers between devices with their start and end apart: 5, of which 5 were waited for; matrix products, arithmetic and copies ran while one was open for 7% of the time, Pallas kernels for 0%

commit v1 on v0

v1 whole, which is shorter than its diff:
```python
import jax
import jax.numpy as jnp
from jax import lax
from jax.sharding import PartitionSpec as P

HDIM = 128
SPAN = 256
X, Y, C = 4, 4, 2


def seq_of(y, x, c):
    return (y * X + x) * C + c


def shift_x(k):
    return [
        (seq_of(y, x, c), seq_of(y, x + k, c))
        for y in range(Y)
        for x in range(X)
        for c in range(C)
        if 0 <= x + k < X
    ]


def spin_x(k):
    return [
        (seq_of(y, x, c), seq_of(y, (x + k) % X, c))
        for y in range(Y)
        for x in range(X)
        for c in range(C)
    ]


def shift_y(k):
    return [
        (seq_of(y, x, c), seq_of(y + k, x, c))
        for y in range(Y)
        for x in range(X)
        for c in range(C)
        if 0 <= y + k < Y
    ]


def swap_core():
    return [(s, s ^ 1) for s in range(X * Y * C)]


def earlier_slabs(total):
    me = lax.axis_index("seq")
    core = me % C
    x = (me // C) % X
    other = lax.ppermute(total.astype(jnp.bfloat16), "seq", swap_core()).astype(jnp.float32)
    before = jnp.where(core == 1, other, 0.0)
    chip = (total + other).astype(jnp.bfloat16)
    row = chip.astype(jnp.float32)
    for k in range(1, X):
        got = lax.ppermute(chip, "seq", spin_x(k)).astype(jnp.float32)
        row = row + got
        before = before + jnp.where(x >= k, got, 0.0)
    row = row.astype(jnp.bfloat16)
    for k in range(1, Y):
        before = before + lax.ppermute(row, "seq", shift_y(k)).astype(jnp.float32)
    return before


def gather_tokens(tokens):
    n = lax.axis_size("head")
    z = lax.axis_index("head")
    rows, depth = tokens.shape
    up = [(i, (i + 1) % n) for i in range(n)]
    down = [(i, (i - 1) % n) for i in range(n)]
    whole = jnp.zeros((rows, n * depth), tokens.dtype)

    def put(whole, piece, at, row=0):
        return lax.dynamic_update_slice(whole, piece, (row, (at % n) * depth))

    whole = put(whole, tokens, z)
    a = b = tokens
    for step in range(1, n // 2):
        a = lax.ppermute(a, "head", up)
        b = lax.ppermute(b, "head", down)
        whole = put(whole, a, z - step + n)
        whole = put(whole, b, z + step)
    half = rows // 2
    a = lax.ppermute(a[:half], "head", up)
    b = lax.ppermute(b[half:], "head", down)
    whole = put(whole, a, z + n // 2)
    whole = put(whole, b, z + n // 2, half)
    return whole


def local(tokens, w_query, w_key, w_value, gain):
    weights = lax.all_gather(
        jnp.concatenate([w_key, w_value, w_query], axis=1), "seq", axis=0, tiled=True
    )
    whole = gather_tokens(tokens)
    tok_rows = whole.shape[0]
    columns_here = w_query.shape[1]
    heads_here = columns_here // HDIM
    blocks = tok_rows // SPAN

    def project(low, high):
        return jax.nn.silu(
            jnp.dot(whole, weights[:, low:high], preferred_element_type=jnp.float32)
        ).astype(jnp.bfloat16)

    def to_blocks(values):
        return values.reshape(blocks, SPAN, heads_here, HDIM)

    key_value = project(0, 2 * columns_here)
    key_blocks = to_blocks(key_value[:, :columns_here])
    value_blocks = to_blocks(key_value[:, columns_here:])
    query_blocks = to_blocks(project(2 * columns_here, 3 * columns_here))
    pair_states = jnp.einsum(
        "cshd,cshe->chde", key_blocks, value_blocks, preferred_element_type=jnp.float32
    )
    slab_total = jnp.sum(pair_states, axis=0)
    within = jnp.cumsum(pair_states, axis=0) - pair_states
    earlier = earlier_slabs(slab_total)
    states = (earlier[None] + within).astype(jnp.bfloat16)
    scores = jnp.einsum(
        "cshd,cthd->chst", query_blocks, key_blocks, preferred_element_type=jnp.float32
    )
    causal = lax.broadcasted_iota(jnp.int32, (SPAN, SPAN), 0) >= lax.broadcasted_iota(
        jnp.int32, (SPAN, SPAN), 1
    )
    scores = jnp.where(causal[None, None], scores, 0.0).astype(jnp.bfloat16)
    local_part = jnp.einsum(
        "chst,cthe->cshe", scores, value_blocks, preferred_element_type=jnp.float32
    )
    carried = jnp.einsum(
        "cshd,chde->cshe", query_blocks, states, preferred_element_type=jnp.float32
    )
    attended = local_part + carried
    inverse_rms = lax.rsqrt(jnp.mean(attended * attended, axis=-1, keepdims=True) + 1e-06)
    return (
        (attended * inverse_rms * gain.reshape(heads_here, HDIM))
        .astype(jnp.bfloat16)
        .reshape(tok_rows, columns_here)
    )


def solution(mesh):
    in_specs = (P("seq", "head"), P("seq", "head"), P("seq", "head"), P("seq", "head"), P("head"))
    out_specs = P("seq", "head")
    return jax.shard_map(local, mesh=mesh, in_specs=in_specs, out_specs=out_specs, check_vma=False)
```

time: 353 us -> 146 us (0.41)
  waiting for transfers between devices: 274 us -> 63.3 us
  other arithmetic: 34.7 us -> 2.77 us
  starting transfers between devices: 0.15 us -> 26.2 us
  local copies, waits for them, and re-layouts: 1.8 us -> 15.1 us
  matrix products: 27.5 us -> 23.5 us
    all_gather x5 -> x1, waiting for transfers between devices: 272 us -> 15.5 us  [local(): lax.all_gather(jnp.concatenate([w_key, w_value, w_query], axis=1), 'seq',...]
    ppermute x0 -> x15, waiting for transfers between devices: none -> 47.8 us  [the longest x3 41.3 us: gather_tokens(): a = lax.ppermute(a, 'head', up)]
    select_n x32 -> x0, other arithmetic: 33.2 us -> none  [lap(): return jnp.where(reached, new, before)]
    ppermute x0 -> x15, starting transfers between devices: none -> 26.2 us  [the longest x3 9.36 us: gather_tokens(): b = lax.ppermute(b, 'head', down)]
    dynamic_update_slice x0 -> x9, local copies, waits for them, and re-layouts: none -> 9.73 us  [put(): return lax.dynamic_update_slice(whole, piece, (row, at % n * depth))]
    dot_general x3 -> x2, matrix products: 24.5 us -> 19.9 us  [project(): jnp.dot(whole, weights[:, low:high], preferred_element_type=jnp.float32)]
  transfers between devices with their start and end apart: 5 -> 16, of which waited for: 5 -> 7; matrix products, arithmetic and copies ran while one was open for 7% -> 15% of each run, Pallas kernels for 0% -> 0%
where the time goes in v1:
time: 146 us; the launch traced here: 144 us
  waiting for transfers between devices  63.3 us (43%)
  starting transfers between devices  26.2 us (18%)
  matrix products  23.5 us (16%)
  local copies, waits for them, and re-layouts  15.1 us (10%)
  between operations  13.7 us (9%)
  other arithmetic  2.77 us (2%)
    ppermute x3, waiting for transfers between devices, gather_tokens(): a = lax.ppermute(a, 'head', up)  41.3 us
    dot_general x2, matrix products, project(): jnp.dot(whole, weights[:, low:high], preferred_element_type=jnp.float32)  19.9 us
    all_gather x1, waiting for transfers between devices, local(): lax.all_gather(jnp.concatenate([w_key, w_value, w_query], axis=1), 'seq',...  15.5 us
    dynamic_update_slice x9, local copies, waits for them, and re-layouts, put(): return lax.dynamic_update_slice(whole, piece, (row, at % n * depth))  9.73 us
    ppermute x3, starting transfers between devices, gather_tokens(): b = lax.ppermute(b, 'head', down)  9.36 us
    ppermute x3, starting transfers between devices, earlier_slabs(): before = before + lax.ppermute(row, 'seq', shift_y(k)).astype(jnp.float32)  6.25 us
    ppermute x3, starting transfers between devices, earlier_slabs(): got = lax.ppermute(chip, 'seq', spin_x(k)).astype(jnp.float32)  4.85 us
    broadcast_in_dim x1, local copies, waits for them, and re-layouts, gather_tokens(): whole = jnp.zeros((rows, n * depth), tokens.dtype)  3.37 us
  transfers between devices with their start and end apart: 16, of which 7 were waited for; matrix products, arithmetic and copies ran while one was open for 15% of the time, Pallas kernels for 0%

profile of v1, /device:TPU:1, one launch (start us, length us, event | category | flops | bytes accessed | tf_op | source)
XLA Modules:
  0.0 144.4 jit_solution(12282663070932004416)
XLA Ops:
  6.5 0.0 all-gather.2.cloned.1.call-start
  6.5 2.1 %pad_maximum_fusion = bf16[192,1536]{1,0:T(8,128)(2,1)} fusion(bf16[192,512]{1,0:T(8,128)(2,1)} %param.6, bf16[192,512]{1,0:T(8,128)(2,1)} %param.8, bf16[192,512]{1,0:T(8,128)(2,1)} %param.7), kind=kLoop, calls=%fused_computation.15 | loop fusion | flops 1769472 | bytes 1179648 | tf_op jit(solution)/shard_map/concatenate | solution.py:94
  8.6 0.0 all-gather.2.cloned.1.call-update
  8.6 2.5 %collective-permute-start = (bf16[512,768]{1,0:T(8,128)(2,1)}, bf16[512,768]{1,0:T(8,128)(2,1)S(1)}, u32[]{:S(2)}, u32[]{:S(2)}) collective-permute-start(bf16[512,768]{1,0:T(8,128)(2,1)} %param.5), channel_id=1, source_target_pairs={{0,1},{1,2},{2,3},{3,4},{4,5},{5,6},{6,7},{7,0},{8,9},{9,10},{10,1... | collective-permute-start | bytes 2359304 | tf_op jit(solution)/shard_map/ppermute | solution.py:80
  11.2 4.0 %collective-permute-start.1 = (bf16[512,768]{1,0:T(8,128)(2,1)}, bf16[512,768]{1,0:T(8,128)(2,1)S(1)}, u32[]{:S(2)}, u32[]{:S(2)}) collective-permute-start(bf16[512,768]{1,0:T(8,128)(2,1)} %param.5), channel_id=1, source_target_pairs={{0,7},{1,0},{2,1},{3,2},{4,3},{5,4},{6,5},{7,6},{8,15},{9,8},{10,9... | collective-permute-start | bytes 2359304 | tf_op jit(solution)/shard_map/ppermute | solution.py:81
  15.2 17.5 %collective-permute-done = bf16[512,768]{1,0:T(8,128)(2,1)S(1)} collective-permute-done((bf16[512,768]{1,0:T(8,128)(2,1)}, bf16[512,768]{1,0:T(8,128)(2,1)S(1)}, u32[]{:S(2)}, u32[]{:S(2)}) %collective-permute-start) | collective-permute-done | bytes 786464 | tf_op jit(solution)/shard_map/ppermute | solution.py:80
  32.7 0.0 collective-permute-start.2
  32.7 0.0 collective-permute-done.1
  32.7 0.0 copy-start.3
  32.7 2.7 %collective-permute-start.3 = (bf16[512,768]{1,0:T(8,128)(2,1)S(1)}, bf16[512,768]{1,0:T(8,128)(2,1)S(1)}, u32[]{:S(2)}, u32[]{:S(2)}) collective-permute-start(bf16[512,768]{1,0:T(8,128)(2,1)S(1)} %collective-permute-done.1), channel_id=1, source_target_pairs={{0,7},{1,0},{2,1},{3,2},{4,3},{5,4},{6,5},{7,6},{8,15},{9,8},{10,9... | collective-permute-start | bytes 2359304 | tf_op jit(solution)/shard_map/ppermute | solution.py:81
  35.4 0.0 copy-done.1
  35.4 16.5 %collective-permute-done.2 = bf16[512,768]{1,0:T(8,128)(2,1)} collective-permute-done((bf16[512,768]{1,0:T(8,128)(2,1)S(1)}, bf16[512,768]{1,0:T(8,128)(2,1)}, u32[]{:S(2)}, u32[]{:S(2)}) %collective-permute-start.2) | collective-permute-done | bytes 786464 | tf_op jit(solution)/shard_map/ppermute | solution.py:80
  51.9 0.0 collective-permute-start.4
  51.9 0.0 collective-permute-done.3
  51.9 2.7 %collective-permute-start.5 = (bf16[512,768]{1,0:T(8,128)(2,1)S(1)}, bf16[512,768]{1,0:T(8,128)(2,1)S(1)}, u32[]{:S(2)}, u32[]{:S(2)}) collective-permute-start(bf16[512,768]{1,0:T(8,128)(2,1)S(1)} %collective-permute-done.3), channel_id=1, source_target_pairs={{0,7},{1,0},{2,1},{3,2},{4,3},{5,4},{6,5},{7,6},{8,15},{9,8},{10,9... | collective-permute-start | bytes 2359304 | tf_op jit(solution)/shard_map/ppermute | solution.py:81
  54.6 3.4 %broadcast_in_dim.25 = bf16[512,6144]{1,0:T(8,128)(2,1)} broadcast(bf16[]{:T(256)} %constant.96.clone.1), dimensions={} | broadcast | bytes 6291458 | tf_op jit(solution)/shard_map/broadcast_in_dim | solution.py:72
  58.0 1.0 constant_dynamic-update-slice_fusion.7
  59.0 1.0 constant_dynamic-update-slice_fusion.6
  60.0 0.0 copy-done.4
  60.0 1.0 constant_dynamic-update-slice_fusion.5
  61.0 2.2 %constant_dynamic-update-slice_fusion.4 = bf16[512,6144]{1,0:T(8,128)(2,1)} fusion(bf16[512,6144]{1,0:T(8,128)(2,1)} %constant_dynamic-update-slice_fusion.5, bf16[512,768]{1,0:T(8,128)(2,1)} %collective-permute-done.2, s32[]{:T(128)S(6)} %select_n.111), kind=kLoop, calls=%fused_computation.47 | loop fusion | bytes 1572868 | tf_op jit(solution)/shard_map/dynamic_update_slice | solution.py:75
  63.1 7.3 %collective-permute-done.4 = bf16[512,768]{1,0:T(8,128)(2,1)S(1)} collective-permute-done((bf16[512,768]{1,0:T(8,128)(2,1)}, bf16[512,768]{1,0:T(8,128)(2,1)S(1)}, u32[]{:S(2)}, u32[]{:S(2)}) %collective-permute-start.4) | collective-permute-done | bytes 786464 | tf_op jit(solution)/shard_map/ppermute | solution.py:80
  70.5 0.1 collective-permute-start.6
  70.6 0.0 collective-permute-done.5
  70.6 2.7 %collective-permute-start.7 = (bf16[256,768]{1,0:T(8,128)(2,1)S(1)}, bf16[256,768]{1,0:T(8,128)(2,1)S(1)}, u32[]{:S(2)}, u32[]{:S(2)}) collective-permute-start(bf16[256,768]{1,0:T(8,128)(2,1)S(1)} %slice.25), channel_id=1, source_target_pairs={{0,7},{1,0},{2,1},{3,2},{4,3},{5,4},{6,5},{7,6},{8,15},{9,8},{10,9... | collective-permute-start | bytes 1179656 | tf_op jit(solution)/shard_map/ppermute | solution.py:86
  73.3 1.0 constant_dynamic-update-slice_fusion.3
  74.3 1.0 constant_dynamic-update-slice_fusion.2
  75.3 1.0 constant_dynamic-update-slice_fusion.1
  76.3 3.3 %collective-permute-done.6 = bf16[256,768]{1,0:T(8,128)(2,1)S(1)} collective-permute-done((bf16[256,768]{1,0:T(8,128)(2,1)S(1)}, bf16[256,768]{1,0:T(8,128)(2,1)S(1)}, u32[]{:S(2)}, u32[]{:S(2)}) %collective-permute-start.6) | collective-permute-done | bytes 393248 | tf_op jit(solution)/shard_map/ppermute | solution.py:85
  79.6 0.8 constant_dynamic-update-slice_fusion
  80.4 0.0 collective-permute-done.7
  80.4 0.8 constant_dynamic-update-slice_fusion.8
  81.2 15.5 %all-gather.2.cloned.1.call-done = bf16[6144,1536]{1,0:T(8,128)(2,1)} async-done(((bf16[192,1536]{1,0:T(8,128)(2,1)}), bf16[6144,1536]{1,0:T(8,128)(2,1)}) %all-gather.2.cloned.1.call-update) | async-done | bytes 18874384 | tf_op jit(solution)/shard_map/all_gather | solution.py:93
  96.7 11.8 %multiply_convert_fusion = bf16[512,1024]{1,0:T(8,128)(2,1)S(1)} fusion(bf16[512,6144]{1,0:T(8,128)(2,1)} %constant_dynamic-update-slice_fusion.8, bf16[6144,1536]{1,0:T(8,128)(2,1)} %all-gather.2.cloned.1.call-done), kind=kOutput, calls=%fused_computation.5 | convolution fusion | flops 6445072384 | bytes 19922944 | tf_op jit(solution)/shard_map/dot_general | solution.py:104
  108.5 0.1 fusion.30
  108.6 0.1 reshape.31
  108.7 0.3 copy.12
  109.0 0.1 reshape.29
  109.1 0.3 fusion.31
  109.4 0.3 collective-permute-start.8
  109.8 1.1 collective-permute-done.8
  110.9 1.3 collective-permute-start.9
  112.2 2.4 %collective-permute-start.10 = (bf16[4,128,128]{2,1,0:T(8,128)(2,1)S(1)}, bf16[4,128,128]{2,1,0:T(8,128)(2,1)S(1)}, u32[]{:S(2)}, u32[]{:S(2)}) collective-permute-start(bf16[4,128,128]{2,1,0:T(8,128)(2,1)S(1)} %fusion.26), channel_id=1, source_target_pairs={{0,32},{8,40},{16,48},{24,56},{32,0},{40,8},{48,16},{56,24},{64,96... | collective-permute-start | bytes 393224 | tf_op jit(solution)/shard_map/ppermute | solution.py:57
  114.6 1.2 collective-permute-start.11
  115.8 8.1 %multiply_convert_fusion.2 = bf16[512,512]{1,0:T(8,128)(2,1)S(1)} fusion(bf16[512,6144]{1,0:T(8,128)(2,1)} %constant_dynamic-update-slice_fusion.8, bf16[6144,1536]{1,0:T(8,128)(2,1)} %all-gather.2.cloned.1.call-done), kind=kOutput, calls=%fused_computation.13 | convolution fusion | flops 3222536192 | bytes 13107200 | tf_op jit(solution)/shard_map/dot_general | solution.py:104
  123.9 0.0 copy-start.5
  123.9 0.1 reshape.30
  124.1 0.0 collective-permute-done.9
  124.1 0.0 collective-permute-done.10
  124.1 0.0 collective-permute-done.11
  124.1 0.1 fusion.27
  124.2 2.5 %collective-permute-start.14 = (bf16[4,128,128]{2,1,0:T(8,128)(2,1)S(1)}, bf16[4,128,128]{2,1,0:T(8,128)(2,1)S(1)}, u32[]{:S(2)}, u32[]{:S(2)}) collective-permute-start(bf16[4,128,128]{2,1,0:T(8,128)(2,1)S(1)} %fusion.27), channel_id=1, source_target_pairs={{0,192},{8,200},{16,208},{24,216},{32,224},{40,232},{48,240},{56,2... | collective-permute-start | bytes 393224 | tf_op jit(solution)/shard_map/ppermute | solution.py:62
  126.6 1.3 collective-permute-start.13
  127.9 2.5 %collective-permute-start.12 = (bf16[4,128,128]{2,1,0:T(8,128)(2,1)S(1)}, bf16[4,128,128]{2,1,0:T(8,128)(2,1)S(1)}, u32[]{:S(2)}, u32[]{:S(2)}) collective-permute-start(bf16[4,128,128]{2,1,0:T(8,128)(2,1)S(1)} %fusion.27), channel_id=1, source_target_pairs={{0,64},{8,72},{16,80},{24,88},{32,96},{40,104},{48,112},{56,120},{... | collective-permute-start | bytes 393224 | tf_op jit(solution)/shard_map/ppermute | solution.py:62
  130.4 0.2 reduce-window_subtract_fusion
  130.7 0.0 collective-permute-done.14
  130.7 0.0 collective-permute-done.13
  130.7 2.1 %collective-permute-done.12 = bf16[4,128,128]{2,1,0:T(8,128)(2,1)S(1)} collective-permute-done((bf16[4,128,128]{2,1,0:T(8,128)(2,1)S(1)}, bf16[4,128,128]{2,1,0:T(8,128)(2,1)S(1)}, u32[]{:S(2)}, u32[]{:S(2)}) %collective-permute-start.12) | collective-permute-done | bytes 131104 | tf_op jit(solution)/shard_map/ppermute | solution.py:62
  132.8 0.2 fusion.25
  132.9 1.3 fusion.15
  134.3 1.9 %multiply_reduce_fusion = (f32[2,256,4]{1,2,0:T(4,128)S(1)}, f32[2,256,4,128]{1,3,2,0:T(8,128)S(1)}) fusion(f32[2,4,128,256]{3,2,1,0:T(8,128)} %fusion.15, bf16[2,256,4,128]{1,3,2,0:T(8,128)(2,1)S(1)} %copy.12, pred[256,256]{1,0:T(8,128)(4,1)S(1)} %iota_compare_fusion, bf16[2,256,4,128]{3,2,1,0:T(4,128)(2,1)S(1)} %reshape.30, ...), kind=kOutput, calls=%fused_computation.11 | convolution fusion | flops 270268416 | bytes 3743744 | tf_op jit(solution)/shard_map/chst,cthe->cshe/dot_general | solution.py:128
  136.2 0.2 multiply_convert_fusion.1
  136.4 0.3 copy.16
  136.7 0.9 copy.35
  (14 shorter events, 0.2 us)
Async XLA Ops:
  6.5 51.5 %copy-start = (bf16[512,768]{1,0:T(8,128)(2,1)S(1)}, bf16[512,768]{1,0:T(8,128)(2,1)}, u32[]{:S(2)}) copy-start(bf16[512,768]{1,0:T(8,128)(2,1)} %param.5) | copy-start | bytes 2359300
  6.5 90.2 %all-gather.2.cloned.1.call-start = ((), (), s32[]{:S(2)}) async-start(), calls=%async_computation | async-start | bytes 19464192 | tf_op jit(solution)/shard_map/all_gather | solution.py:93
  8.6 24.1 %collective-permute-start = (bf16[512,768]{1,0:T(8,128)(2,1)}, bf16[512,768]{1,0:T(8,128)(2,1)S(1)}, u32[]{:S(2)}, u32[]{:S(2)}) collective-permute-start(bf16[512,768]{1,0:T(8,128)(2,1)} %param.5), channel_id=1, source_target_pairs={{0,1},{1,2},{2,3},{3,4},{4,5},{5,6},{6,7},{7,0},{8,9},{9,10},{10,1... | collective-permute-start | bytes 2359304 | tf_op jit(solution)/shard_map/ppermute | solution.py:80
  11.2 21.5 %collective-permute-start.1 = (bf16[512,768]{1,0:T(8,128)(2,1)}, bf16[512,768]{1,0:T(8,128)(2,1)S(1)}, u32[]{:S(2)}, u32[]{:S(2)}) collective-permute-start(bf16[512,768]{1,0:T(8,128)(2,1)} %param.5), channel_id=1, source_target_pairs={{0,7},{1,0},{2,1},{3,2},{4,3},{5,4},{6,5},{7,6},{8,15},{9,8},{10,9... | collective-permute-start | bytes 2359304 | tf_op jit(solution)/shard_map/ppermute | solution.py:81
  32.7 2.7 %copy-start.1 = (bf16[512,768]{1,0:T(8,128)(2,1)}, bf16[512,768]{1,0:T(8,128)(2,1)S(1)}, u32[]{:S(2)}) copy-start(bf16[512,768]{1,0:T(8,128)(2,1)S(1)} %collective-permute-done) | copy-start | bytes 2359300
  32.7 19.2 %collective-permute-start.2 = (bf16[512,768]{1,0:T(8,128)(2,1)S(1)}, bf16[512,768]{1,0:T(8,128)(2,1)}, u32[]{:S(2)}, u32[]{:S(2)}) collective-permute-start(bf16[512,768]{1,0:T(8,128)(2,1)S(1)} %collective-permute-done), channel_id=1, source_target_pairs={{0,1},{1,2},{2,3},{3,4},{4,5},{5,6},{6,7},{7,0},{8,9},{9,10},{10,1... | collective-permute-start | bytes 2359304 | tf_op jit(solution)/shard_map/ppermute | solution.py:80
  32.7 19.2 %copy-start.3 = (bf16[512,768]{1,0:T(8,128)(2,1)}, bf16[512,768]{1,0:T(8,128)(2,1)S(1)}, u32[]{:S(2)}) copy-start(bf16[512,768]{1,0:T(8,128)(2,1)S(1)} %collective-permute-done.1) | copy-start | bytes 2359300
  32.7 19.2 %collective-permute-start.3 = (bf16[512,768]{1,0:T(8,128)(2,1)S(1)}, bf16[512,768]{1,0:T(8,128)(2,1)S(1)}, u32[]{:S(2)}, u32[]{:S(2)}) collective-permute-start(bf16[512,768]{1,0:T(8,128)(2,1)S(1)} %collective-permute-done.1), channel_id=1, source_target_pairs={{0,7},{1,0},{2,1},{3,2},{4,3},{5,4},{6,5},{7,6},{8,15},{9,8},{10,9... | collective-permute-start | bytes 2359304 | tf_op jit(solution)/shard_map/ppermute | solution.py:81
  51.9 18.5 %collective-permute-start.4 = (bf16[512,768]{1,0:T(8,128)(2,1)}, bf16[512,768]{1,0:T(8,128)(2,1)S(1)}, u32[]{:S(2)}, u32[]{:S(2)}) collective-permute-start(bf16[512,768]{1,0:T(8,128)(2,1)} %collective-permute-done.2), channel_id=1, source_target_pairs={{0,1},{1,2},{2,3},{3,4},{4,5},{5,6},{6,7},{7,0},{8,9},{9,10},{10,1... | collective-permute-start | bytes 2359304 | tf_op jit(solution)/shard_map/ppermute | solution.py:80
  51.9 18.6 %collective-permute-start.5 = (bf16[512,768]{1,0:T(8,128)(2,1)S(1)}, bf16[512,768]{1,0:T(8,128)(2,1)S(1)}, u32[]{:S(2)}, u32[]{:S(2)}) collective-permute-start(bf16[512,768]{1,0:T(8,128)(2,1)S(1)} %collective-permute-done.3), channel_id=1, source_target_pairs={{0,7},{1,0},{2,1},{3,2},{4,3},{5,4},{6,5},{7,6},{8,15},{9,8},{10,9... | collective-permute-start | bytes 2359304 | tf_op jit(solution)/shard_map/ppermute | solution.py:81
  54.6 4.4 %copy-start.2 = (bf16[512,768]{1,0:T(8,128)(2,1)S(1)}, bf16[512,768]{1,0:T(8,128)(2,1)}, u32[]{:S(2)}) copy-start(bf16[512,768]{1,0:T(8,128)(2,1)} %copy-done.1) | copy-start | bytes 2359300
  54.6 5.4 %copy-start.4 = (bf16[512,768]{1,0:T(8,128)(2,1)S(1)}, bf16[512,768]{1,0:T(8,128)(2,1)}, u32[]{:S(2)}) copy-start(bf16[512,768]{1,0:T(8,128)(2,1)} %copy-done.3) | copy-start | bytes 2359300
  70.5 9.1 %collective-permute-start.6 = (bf16[256,768]{1,0:T(8,128)(2,1)S(1)}, bf16[256,768]{1,0:T(8,128)(2,1)S(1)}, u32[]{:S(2)}, u32[]{:S(2)}) collective-permute-start(bf16[256,768]{1,0:T(8,128)(2,1)S(1)} %slice.24), channel_id=1, source_target_pairs={{0,1},{1,2},{2,3},{3,4},{4,5},{5,6},{6,7},{7,0},{8,9},{9,10},{10,1... | collective-permute-start | bytes 1179656 | tf_op jit(solution)/shard_map/ppermute | solution.py:85
  70.6 9.8 %collective-permute-start.7 = (bf16[256,768]{1,0:T(8,128)(2,1)S(1)}, bf16[256,768]{1,0:T(8,128)(2,1)S(1)}, u32[]{:S(2)}, u32[]{:S(2)}) collective-permute-start(bf16[256,768]{1,0:T(8,128)(2,1)S(1)} %slice.25), channel_id=1, source_target_pairs={{0,7},{1,0},{2,1},{3,2},{4,3},{5,4},{6,5},{7,6},{8,15},{9,8},{10,9... | collective-permute-start | bytes 1179656 | tf_op jit(solution)/shard_map/ppermute | solution.py:86
  109.4 1.4 collective-permute-start.8
  110.9 13.1 %collective-permute-start.9 = (bf16[4,128,128]{2,1,0:T(8,128)(2,1)S(1)}, bf16[4,128,128]{2,1,0:T(8,128)(2,1)S(1)}, u32[]{:S(2)}, u32[]{:S(2)}) collective-permute-start(bf16[4,128,128]{2,1,0:T(8,128)(2,1)S(1)} %fusion.26), channel_id=1, source_target_pairs={{0,16},{8,24},{16,32},{24,40},{32,48},{40,56},{48,0},{56,8},{64,80... | collective-permute-start | bytes 393224 | tf_op jit(solution)/shard_map/ppermute | solution.py:57
  112.2 11.9 %collective-permute-start.10 = (bf16[4,128,128]{2,1,0:T(8,128)(2,1)S(1)}, bf16[4,128,128]{2,1,0:T(8,128)(2,1)S(1)}, u32[]{:S(2)}, u32[]{:S(2)}) collective-permute-start(bf16[4,128,128]{2,1,0:T(8,128)(2,1)S(1)} %fusion.26), channel_id=1, source_target_pairs={{0,32},{8,40},{16,48},{24,56},{32,0},{40,8},{48,16},{56,24},{64,96... | collective-permute-start | bytes 393224 | tf_op jit(solution)/shard_map/ppermute | solution.py:57
  114.6 9.5 %collective-permute-start.11 = (bf16[4,128,128]{2,1,0:T(8,128)(2,1)S(1)}, bf16[4,128,128]{2,1,0:T(8,128)(2,1)S(1)}, u32[]{:S(2)}, u32[]{:S(2)}) collective-permute-start(bf16[4,128,128]{2,1,0:T(8,128)(2,1)S(1)} %fusion.26), channel_id=1, source_target_pairs={{0,48},{8,56},{16,0},{24,8},{32,16},{40,24},{48,32},{56,40},{64,11... | collective-permute-start | bytes 393224 | tf_op jit(solution)/shard_map/ppermute | solution.py:57
  123.9 12.3 %copy-start.5 = (f32[512]{0:T(512)S(1)}, f32[512]{0:T(512)}, u32[]{:S(2)}) copy-start(f32[512]{0:T(512)} %param.9) | copy-start | bytes 6148
  124.2 6.5 %collective-permute-start.14 = (bf16[4,128,128]{2,1,0:T(8,128)(2,1)S(1)}, bf16[4,128,128]{2,1,0:T(8,128)(2,1)S(1)}, u32[]{:S(2)}, u32[]{:S(2)}) collective-permute-start(bf16[4,128,128]{2,1,0:T(8,128)(2,1)S(1)} %fusion.27), channel_id=1, source_target_pairs={{0,192},{8,200},{16,208},{24,216},{32,224},{40,232},{48,240},{56,2... | collective-permute-start | bytes 393224 | tf_op jit(solution)/shard_map/ppermute | solution.py:62
  126.6 4.1 %collective-permute-start.13 = (bf16[4,128,128]{2,1,0:T(8,128)(2,1)S(1)}, bf16[4,128,128]{2,1,0:T(8,128)(2,1)S(1)}, u32[]{:S(2)}, u32[]{:S(2)}) collective-permute-start(bf16[4,128,128]{2,1,0:T(8,128)(2,1)S(1)} %fusion.27), channel_id=1, source_target_pairs={{0,128},{8,136},{16,144},{24,152},{32,160},{40,168},{48,176},{56,1... | collective-permute-start | bytes 393224 | tf_op jit(solution)/shard_map/ppermute | solution.py:62
  127.9 4.8 %collective-permute-start.12 = (bf16[4,128,128]{2,1,0:T(8,128)(2,1)S(1)}, bf16[4,128,128]{2,1,0:T(8,128)(2,1)S(1)}, u32[]{:S(2)}, u32[]{:S(2)}) collective-permute-start(bf16[4,128,128]{2,1,0:T(8,128)(2,1)S(1)} %fusion.27), channel_id=1, source_target_pairs={{0,64},{8,72},{16,80},{24,88},{32,96},{40,104},{48,112},{56,120},{... | collective-permute-start | bytes 393224 | tf_op jit(solution)/shard_map/ppermute | solution.py:62
Sparse Core Ops, SparseCore 0:
  9.9 86.7 all-gather.1

commit v2 on v0

v2 whole, which is shorter than its diff:
```python
import functools

import jax
import jax.numpy as jnp
import numpy as np
from jax import lax
from jax.experimental import pallas as pl
from jax.experimental.pallas import tpu as pltpu
from jax.sharding import PartitionSpec as P

HDIM = 128
SPAN = 256
Y, X, C, Z = 4, 4, 2, 8
ROWS = 192
PIECE = 2 * ROWS
SLAB = 512
CHIP = C * SLAB
HALF = 256
F32, BF16 = jnp.float32, jnp.bfloat16
DIMS = (
    lambda y, x: (y, x ^ 1),
    lambda y, x: (y ^ 1, x),
    lambda y, x: (y, x ^ 3),
    lambda y, x: (y ^ 3, x),
)
ANY = pl.BlockSpec(memory_space=pl.ANY)
VMEM = pl.BlockSpec(memory_space=pltpu.VMEM)
SMEM = pl.BlockSpec(memory_space=pltpu.SMEM)


def seq_of(y, x, c):
    return (y * X + x) * C + c


def chips():
    return [(y, x) for y in range(Y) for x in range(X)]


def dim_of(stream, core, step):
    return (2 * stream + core + step) % 4


def cube_pairs(stream, step):
    return [
        (seq_of(y, x, c), seq_of(*DIMS[dim_of(stream, c, step)](y, x), c))
        for y, x in chips()
        for c in range(C)
    ]


def ring_pairs():
    return [
        (s * Z + z, s * Z + (z + (1 if s % C == 0 else -1)) % Z)
        for s in range(Y * X * C)
        for z in range(Z)
    ]


SWAP = [(s, s ^ 1) for s in range(Y * X * C)]


def spin_x(k):
    return [(seq_of(y, x, c), seq_of(y, (x + k) % X, c)) for y, x in chips() for c in range(C)]


def shift_y(k):
    return [
        (seq_of(y, x, c), seq_of(y + k, x, c)) for y, x in chips() for c in range(C) if y + k < Y
    ]


def place_table():
    table = np.zeros((Y * X * C, Z, 2, Z, 2), np.int32)
    for y, x in chips():
        for c in range(C):
            for z in range(Z):
                for stream in range(2):
                    for k in range(Z):
                        for e in range(2):
                            source = 2 * ((z - k if c == 0 else z + k) % Z) + e
                            dx, dy = (source % X) ^ x, (source // X) ^ y
                            bits = (
                                (dx & 1) ^ (dx >> 1),
                                (dy & 1) ^ (dy >> 1),
                                dx >> 1,
                                dy >> 1,
                            )
                            table[seq_of(y, x, c), z, stream, k, e] = sum(
                                bits[dim_of(stream, c, step)] << step for step in range(4)
                            )
    return table.reshape(Y * X * C * Z, 4 * Z)


def silu(u):
    return u / (1.0 + jnp.exp(-u))


def product_kernel(parts, info, *refs):
    tokens, refs = refs[: 2 * Z], refs[2 * Z :]
    weights, refs = refs[:4], refs[4:]
    outs, refs = refs[: len(parts)], refs[len(parts) :]
    whole, piled, total, token_sem, weight_sem = refs
    core = info[0]
    groups = 2
    per = Z // groups
    depth = per * PIECE

    def weight_copy(source, part, at, columns, row):
        return pltpu.make_async_copy(
            source.at[pl.ds(pl.multiple_of(row * ROWS, ROWS), ROWS), columns],
            piled.at[part, pl.ds(at * ROWS, ROWS)],
            weight_sem.at[part, at],
        )

    for k in range(Z):
        for slab in range(2):
            first = pl.multiple_of(SLAB * (core if slab == 0 else 1 - core), SLAB)
            pltpu.make_async_copy(
                tokens[2 * k + slab],
                whole.at[pl.ds(first, SLAB), pl.ds(k * PIECE, PIECE)],
                token_sem.at[k, slab],
            ).start()
        for part, (mine, low, high) in enumerate(parts):
            half = core if mine else 1 - core
            for e in range(2):
                place = info[1 + half * 2 * Z + 2 * k + e]
                choice = half * 2 + place // 8
                for b in range(4):

                    @pl.when(choice == b)
                    def _():
                        weight_copy(
                            weights[b], part, 2 * k + e, pl.ds(low, high - low), place % 8
                        ).start()

    for g in range(groups):
        for k in range(g * per, (g + 1) * per):
            for slab in range(2):
                pltpu.make_async_copy(
                    tokens[2 * k + slab],
                    whole.at[pl.ds(0, SLAB), pl.ds(k * PIECE, PIECE)],
                    token_sem.at[k, slab],
                ).wait()
            for part, (mine, low, high) in enumerate(parts):
                for e in range(2):
                    weight_copy(weights[0], part, 2 * k + e, pl.ds(low, high - low), 0).wait()
        for part in range(len(parts)):
            for n in range(0, outs[part].shape[1], 256):

                @pl.loop(0, CHIP // 512)
                def _(m):
                    rows = pl.ds(pl.multiple_of(m * 512, 512), 512)
                    some = jnp.dot(
                        whole[rows, g * depth : (g + 1) * depth],
                        piled[part, g * depth : (g + 1) * depth, n : n + 256],
                        preferred_element_type=F32,
                    )
                    if g == 0:
                        total[part, rows, n : n + 256] = some
                    else:
                        outs[part][rows, n : n + 256] = (
                            total[part, rows, n : n + 256] + some
                        ).astype(outs[part].dtype)


def product(info, tokens, weights, parts):
    wide = max(high - low for _, low, high in parts)
    flops = sum(2 * CHIP * Z * PIECE * (high - low) for _, low, high in parts)
    return pl.pallas_call(
        functools.partial(product_kernel, parts),
        out_shape=[
            jax.ShapeDtypeStruct((CHIP, high - low), F32 if mine else BF16)
            for mine, low, high in parts
        ],
        in_specs=[SMEM] + [ANY] * (2 * Z + 4),
        out_specs=[VMEM] * len(parts),
        scratch_shapes=[
            pltpu.VMEM((CHIP, Z * PIECE), BF16),
            pltpu.VMEM((len(parts), Z * PIECE, wide), BF16),
            pltpu.VMEM((len(parts), CHIP, wide), F32),
            pltpu.SemaphoreType.DMA((Z, 2)),
            pltpu.SemaphoreType.DMA((len(parts), 2 * Z)),
        ],
        compiler_params=pltpu.CompilerParams(vmem_limit_bytes=40 * 2**20),
        cost_estimate=pl.CostEstimate(
            flops=flops, bytes_accessed=16 * 2**20, transcendentals=0
        ),
    )(info, *tokens, *weights)


def pairs_kernel(mine, other, key, value, within, total):
    for h in range(2):
        running = jnp.zeros((HDIM, HDIM), F32)
        for b in range(CHIP // SPAN):
            rows = slice(b * SPAN, (b + 1) * SPAN)
            got = []
            for at, out in ((0, key), (HALF, value)):
                cols = slice(at + h * HDIM, at + (h + 1) * HDIM)
                u = mine[rows, cols] + other[rows, cols].astype(F32)
                got.append(silu(u).astype(BF16))
                out[rows, h * HDIM : (h + 1) * HDIM] = got[-1]
            within[b, h] = running
            running = running + lax.dot_general(
                *got, (((0,), (0,)), ((), ())), preferred_element_type=F32
            )
        total[h] = running.astype(BF16)


def pair_states(mine, other):
    return pl.pallas_call(
        pairs_kernel,
        out_shape=[
            jax.ShapeDtypeStruct((CHIP, HALF), BF16),
            jax.ShapeDtypeStruct((CHIP, HALF), BF16),
            jax.ShapeDtypeStruct((CHIP // SPAN, 2, HDIM, HDIM), F32),
            jax.ShapeDtypeStruct((2, HDIM, HDIM), BF16),
        ],
        in_specs=[VMEM] * 2,
        out_specs=[VMEM] * 4,
        compiler_params=pltpu.CompilerParams(vmem_limit_bytes=32 * 2**20),
        cost_estimate=pl.CostEstimate(
            flops=2 * CHIP * 2 * HDIM * HDIM, bytes_accessed=5 * 2**20, transcendentals=CHIP * 512
        ),
    )(mine, other)


def local_kernel(mine, other, key, value, query, inside):
    causal = lax.broadcasted_iota(jnp.int32, (SPAN, SPAN), 0) >= lax.broadcasted_iota(
        jnp.int32, (SPAN, SPAN), 1
    )
    for b in range(CHIP // SPAN):
        for h in range(2):
            at = (slice(b * SPAN, (b + 1) * SPAN), slice(h * HDIM, (h + 1) * HDIM))
            q = silu(mine[at] + other[at].astype(F32)).astype(BF16)
            query[at] = q
            scores = lax.dot_general(
                q, key[at], (((1,), (1,)), ((), ())), preferred_element_type=F32
            )
            scores = jnp.where(causal, scores, 0.0).astype(BF16)
            inside[at] = jnp.dot(scores, value[at], preferred_element_type=F32)


def local_part(mine, other, key, value):
    return pl.pallas_call(
        local_kernel,
        out_shape=[
            jax.ShapeDtypeStruct((CHIP, HALF), BF16),
            jax.ShapeDtypeStruct((CHIP, HALF), F32),
        ],
        in_specs=[VMEM] * 4,
        out_specs=[VMEM] * 2,
        compiler_params=pltpu.CompilerParams(vmem_limit_bytes=32 * 2**20),
        cost_estimate=pl.CostEstimate(
            flops=8 * CHIP * SPAN * HDIM, bytes_accessed=5 * 2**20, transcendentals=CHIP * HALF
        ),
    )(mine, other, key, value)


def finish_kernel(mine, info, query, inside, within, before, rows_0, rows_1, rows_2, gain, out):
    core = info[0]
    first = core if mine else 1 - core
    for h in range(2):
        cols = slice(h * HDIM, (h + 1) * HDIM)
        earlier = before[h]
        for rows in (rows_0, rows_1, rows_2):
            earlier = earlier + rows[h].astype(F32)
        for b in range(SLAB // SPAN):
            at = pl.ds(pl.multiple_of(first * SLAB + b * SPAN, SPAN), SPAN)
            state = (earlier + within[first * (SLAB // SPAN) + b, h]).astype(BF16)
            attended = inside[at, cols] + jnp.dot(
                query[at, cols], state, preferred_element_type=F32
            )
            scale = lax.rsqrt(jnp.mean(attended * attended, axis=-1, keepdims=True) + 1e-06)
            out[b * SPAN : (b + 1) * SPAN, cols] = (attended * scale * gain[:, cols]).astype(BF16)


def finish(mine, *args):
    return pl.pallas_call(
        functools.partial(finish_kernel, mine),
        out_shape=jax.ShapeDtypeStruct((SLAB, HALF), BF16),
        in_specs=[SMEM] + [VMEM] * 8,
        out_specs=VMEM,
        compiler_params=pltpu.CompilerParams(vmem_limit_bytes=32 * 2**20),
        cost_estimate=pl.CostEstimate(
            flops=4 * SLAB * HDIM * HDIM, bytes_accessed=2 * 2**20, transcendentals=0
        ),
    )(*args)


def after(value, *others):
    return lax.optimization_barrier((value, others))[0]


def gather(tokens, weights, core):
    even = jnp.concatenate([tokens[:, :ROWS], tokens[:, 2 * ROWS : 3 * ROWS]], axis=1)
    odd = jnp.concatenate([tokens[:, ROWS : 2 * ROWS], tokens[:, 3 * ROWS :]], axis=1)
    own = jnp.where(core == 0, even, odd)
    theirs = lax.ppermute(jnp.where(core == 0, odd, even), "seq", SWAP)
    ring = ring_pairs()
    pieces = [[own, theirs]]
    for _ in range(1, Z):
        pieces.append([lax.ppermute(p, ("seq", "head"), ring) for p in pieces[-1]])
    gates = (None, (1, 0), (2, 1), (4, 0))
    streams = list(weights)
    blocks = []
    for step in range(4):
        for j in range(2):
            if gates[step] is not None:
                k, slab = gates[step]
                streams[j] = after(streams[j], pieces[k][slab])
            got = lax.ppermute(streams[j], "seq", cube_pairs(j, step))
            if step < 3:
                streams[j] = jnp.concatenate([streams[j], got], axis=0)
            else:
                blocks += [streams[j], got]
    return [p for pair in pieces for p in pair], blocks


def local(tokens, w_query, w_key, w_value, gain):
    seq = lax.axis_index("seq")
    core = seq % C
    x = (seq // C) % X
    info = jnp.concatenate(
        [
            core[None].astype(jnp.int32),
            jnp.asarray(place_table())[seq * Z + lax.axis_index("head")],
        ]
    )
    halves = [
        jnp.concatenate([w[:, j * HALF : (j + 1) * HALF] for w in (w_key, w_value, w_query)], axis=1)
        for j in range(2)
    ]
    pieces, blocks = gather(tokens, halves, core)

    (kv_theirs,) = product(info, pieces, blocks, ((False, 0, 2 * HALF),))
    kv_got = lax.ppermute(kv_theirs, "seq", SWAP)
    (kv_mine,) = product(info, pieces, blocks, ((True, 0, 2 * HALF),))
    key, value, within, total = pair_states(kv_mine, kv_got)

    row = total.astype(F32)
    before = jnp.zeros_like(row)
    for k in range(1, X):
        got = lax.ppermute(total, "seq", spin_x(k)).astype(F32)
        row = row + got
        before = before + jnp.where(x >= k, got, 0.0)
    row = row.astype(BF16)
    rows = [lax.ppermute(row, "seq", shift_y(k)) for k in range(1, Y)]

    q_theirs, q_mine = product(
        info, pieces, blocks, ((False, 2 * HALF, 3 * HALF), (True, 2 * HALF, 3 * HALF))
    )
    q_got = lax.ppermute(q_theirs, "seq", SWAP)
    query, inside = local_part(q_mine, q_got, key, value)

    gain_here = lax.dynamic_slice(gain, (core * HALF,), (HALF,)).reshape(1, HALF)
    last = (info, query, inside, within, before, *rows, gain_here)
    out_got = lax.ppermute(finish(False, *last), "seq", SWAP)
    out_mine = finish(True, *last)
    return jnp.concatenate(
        [jnp.where(core == 0, out_mine, out_got), jnp.where(core == 0, out_got, out_mine)], axis=1
    )


def solution(mesh):
    in_specs = (P("seq", "head"), P("seq", "head"), P("seq", "head"), P("seq", "head"), P("head"))
    out_specs = P("seq", "head")
    return jax.shard_map(local, mesh=mesh, in_specs=in_specs, out_specs=out_specs, check_vma=False)
```

time: 353 us -> 164 us (0.46)
  waiting for transfers between devices: 274 us -> 39.4 us
  starting transfers between devices: 0.15 us -> 78.3 us
  other arithmetic: 34.7 us -> 3.39 us
  matrix products: 27.5 us -> 0 us
  Pallas kernels: 0 us -> 27 us
  local copies, waits for them, and re-layouts: 1.8 us -> 15.1 us
  between operations: 13.3 us -> 0.32 us
    all_gather x5 -> x0, waiting for transfers between devices: 272 us -> none  [the longest x1 78.1 us: local(): whole = lax.all_gather(tokens, 'head', axis=1, tiled=True)]
    ppermute x0 -> x32, starting transfers between devices: none -> 78.3 us  [the longest x14 42.4 us: gather(): pieces.append([lax.ppermute(p, ('seq', 'head'), ring) for p in pieces[-1]])]
    ppermute x0 -> x32, waiting for transfers between devices: none -> 39.4 us  [the longest x14 31.2 us: gather(): pieces.append([lax.ppermute(p, ('seq', 'head'), ring) for p in pieces[-1]])]
    select_n x32 -> x2, other arithmetic: 33.2 us -> 0.38 us  [the longest x1 0.34 us: gather(): theirs = lax.ppermute(jnp.where(core == 0, odd, even), 'seq', SWAP)]
    dot_general x6 -> x0, matrix products: 27.5 us -> none  [the longest x3 24.5 us: add_rows(): return jnp.dot(whole, piece, preferred_element_type=jnp.float32)]
    pallas_call x0 -> x7, Pallas kernels: none -> 27 us  [the longest x3 22.4 us: product(): pl.pallas_call(functools.partial(product_kernel, parts), out_shape=[jax.S...]
    unnamed x3 -> x48, local copies, waits for them, and re-layouts: 0.88 us -> 12.8 us
  transfers between devices with their start and end apart: 5 -> 32, of which waited for: 5 -> 16; matrix products, arithmetic and copies ran while one was open for 7% -> 2% of each run, Pallas kernels for 0% -> 12%
where the time goes in v2:
time: 164 us
  starting transfers between devices  78.3 us (48%)
  waiting for transfers between devices  39.4 us (24%)
  Pallas kernels  27 us (16%)
  local copies, waits for them, and re-layouts  15.1 us (9%)
  other arithmetic  3.39 us (2%)
    ppermute x14, starting transfers between devices, gather(): pieces.append([lax.ppermute(p, ('seq', 'head'), ring) for p in pieces[-1]])  42.4 us
    ppermute x14, waiting for transfers between devices, gather(): pieces.append([lax.ppermute(p, ('seq', 'head'), ring) for p in pieces[-1]])  31.2 us
    pallas_call x3, Pallas kernels, product(): pl.pallas_call(functools.partial(product_kernel, parts), out_shape=[jax.S...  22.4 us
    unnamed x48, local copies, waits for them, and re-layouts  12.8 us
    ppermute x1, starting transfers between devices, local(): kv_got = lax.ppermute(kv_theirs, 'seq', SWAP)  10.8 us
    ppermute x8, starting transfers between devices, gather(): got = lax.ppermute(streams[j], 'seq', cube_pairs(j, step))  10.7 us
    ppermute x3, starting transfers between devices, local(): rows = [lax.ppermute(row, 'seq', shift_y(k)) for k in range(1, Y)]  7.29 us
    ppermute x3, waiting for transfers between devices, local(): got = lax.ppermute(total, 'seq', spin_x(k)).astype(F32)  5.06 us
  transfers between devices with their start and end apart: 32, of which 16 were waited for; matrix products, arithmetic and copies ran while one was open for 2% of the time, Pallas kernels for 12%

profile of v2, /device:TPU:1, one launch (start us, length us, event | category | flops | bytes accessed | tf_op | source)
XLA Modules:
  0.0 163.6 jit_solution(11052736389849164122)
XLA Ops:
  0.0 1.5 fusion.3
  1.9 3.3 %collective-permute-start = (bf16[512,384]{1,0:T(8,128)(2,1)S(1)}, bf16[512,384]{1,0:T(8,128)(2,1)S(1)}, u32[]{:S(2)}, u32[]{:S(2)}) collective-permute-start(bf16[512,384]{1,0:T(8,128)(2,1)S(1)} %get-tuple-element.33), channel_id=1, source_target_pairs={{0,8},{8,0},{16,24},{24,16},{32,40},{40,32},{48,56},{56,48},{64,72... | collective-permute-start | bytes 1179656 | tf_op jit(solution)/shard_map/ppermute | solution.py:298
  5.4 5.1 %collective-permute-start.1 = (bf16[512,384]{1,0:T(8,128)(2,1)S(1)}, bf16[512,384]{1,0:T(8,128)(2,1)S(1)}, u32[]{:S(2)}, u32[]{:S(2)}) collective-permute-start(bf16[512,384]{1,0:T(8,128)(2,1)S(1)} %get-tuple-element.34.refs_0_), channel_id=1, source_target_pairs={{0,1},{1,2},{2,3},{3,4},{4,5},{5,6},{6,7},{7,0},{8,15},{9,8},{10,9... | collective-permute-start | bytes 1179656 | tf_op jit(solution)/shard_map/ppermute | solution.py:302
  10.5 2.0 %collective-permute-start.19 = (bf16[192,768]{1,0:T(8,128)(2,1)S(1)}, bf16[192,768]{1,0:T(8,128)(2,1)S(1)}, u32[]{:S(2)}, u32[]{:S(2)}) collective-permute-start(bf16[192,768]{1,0:T(8,128)(2,1)S(1)} %pad_maximum_fusion.10), channel_id=1, source_target_pairs={{0,48},{8,200},{16,32},{24,216},{32,16},{40,232},{48,0},{56,248},{... | collective-permute-start | bytes 884744 | tf_op jit(solution)/shard_map/ppermute | solution.py:311
  12.5 0.7 collective-permute-start.2
  13.3 1.9 %collective-permute-done.1.refs_2_ = bf16[512,384]{1,0:T(8,128)(2,1)S(1)} collective-permute-done((bf16[512,384]{1,0:T(8,128)(2,1)S(1)}, bf16[512,384]{1,0:T(8,128)(2,1)S(1)}, u32[]{:S(2)}, u32[]{:S(2)}) %collective-permute-start.1) | collective-permute-done | bytes 393248 | tf_op jit(solution)/shard_map/ppermute | solution.py:302
  15.2 2.5 %collective-permute-start.16 = (bf16[384,768]{1,0:T(8,128)(2,1)S(1)}, bf16[384,768]{1,0:T(8,128)(2,1)S(1)}, u32[]{:S(2)}, u32[]{:S(2)}) collective-permute-start(bf16[384,768]{1,0:T(8,128)(2,1)S(1)} %pad_maximum_fusion.4), channel_id=1, source_target_pairs={{0,64},{8,56},{16,80},{24,40},{32,96},{40,24},{48,112},{56,8},{64,... | collective-permute-start | bytes 1769480 | tf_op jit(solution)/shard_map/ppermute | solution.py:311
  17.8 1.3 collective-permute-start.20
  19.5 3.1 %collective-permute-start.4 = (bf16[512,384]{1,0:T(8,128)(2,1)S(1)}, bf16[512,384]{1,0:T(8,128)(2,1)S(1)}, u32[]{:S(2)}, u32[]{:S(2)}) collective-permute-start(bf16[512,384]{1,0:T(8,128)(2,1)S(1)} %collective-permute-done.2.refs_3_), channel_id=1, source_target_pairs={{0,1},{1,2},{2,3},{3,4},{4,5},{5,6},{6,7},{7,0},{8,15},{9,8},{10,9... | collective-permute-start | bytes 1179656 | tf_op jit(solution)/shard_map/ppermute | solution.py:302
  22.6 2.9 %collective-permute-done.16 = bf16[384,768]{1,0:T(8,128)(2,1)S(1)} collective-permute-done((bf16[384,768]{1,0:T(8,128)(2,1)S(1)}, bf16[384,768]{1,0:T(8,128)(2,1)S(1)}, u32[]{:S(2)}, u32[]{:S(2)}) %collective-permute-start.16) | collective-permute-done | bytes 589856 | tf_op jit(solution)/shard_map/ppermute | solution.py:311
  25.6 1.7 %collective-permute-done.4.refs_5_ = bf16[512,384]{1,0:T(8,128)(2,1)S(1)} collective-permute-done((bf16[512,384]{1,0:T(8,128)(2,1)S(1)}, bf16[512,384]{1,0:T(8,128)(2,1)S(1)}, u32[]{:S(2)}, u32[]{:S(2)}) %collective-permute-start.4) | collective-permute-done | bytes 393248 | tf_op jit(solution)/shard_map/ppermute | solution.py:302
  27.3 1.9 %collective-permute-start.17 = (bf16[768,768]{1,0:T(8,128)(2,1)S(1)}, bf16[768,768]{1,0:T(8,128)(2,1)S(1)}, u32[]{:S(2)}, u32[]{:S(2)}) collective-permute-start(bf16[768,768]{1,0:T(8,128)(2,1)S(1)} %pad_maximum_fusion.2), channel_id=1, source_target_pairs={{0,48},{8,200},{16,32},{24,216},{32,16},{40,232},{48,0},{56,248},{... | collective-permute-start | bytes 3538952 | tf_op jit(solution)/shard_map/ppermute | solution.py:311
  29.2 3.4 %collective-permute-start.3 = (bf16[512,384]{1,0:T(8,128)(2,1)S(1)}, bf16[512,384]{1,0:T(8,128)(2,1)S(1)}, u32[]{:S(2)}, u32[]{:S(2)}) collective-permute-start(bf16[512,384]{1,0:T(8,128)(2,1)S(1)} %collective-permute-done.1.refs_2_), channel_id=1, source_target_pairs={{0,1},{1,2},{2,3},{3,4},{4,5},{5,6},{6,7},{7,0},{8,15},{9,8},{10,9... | collective-permute-start | bytes 1179656 | tf_op jit(solution)/shard_map/ppermute | solution.py:302
  32.9 4.4 %collective-permute-done.3.refs_4_ = bf16[512,384]{1,0:T(8,128)(2,1)S(1)} collective-permute-done((bf16[512,384]{1,0:T(8,128)(2,1)S(1)}, bf16[512,384]{1,0:T(8,128)(2,1)S(1)}, u32[]{:S(2)}, u32[]{:S(2)}) %collective-permute-start.3) | collective-permute-done | bytes 393248 | tf_op jit(solution)/shard_map/ppermute | solution.py:302
  37.3 3.4 %collective-permute-start.5 = (bf16[512,384]{1,0:T(8,128)(2,1)S(1)}, bf16[512,384]{1,0:T(8,128)(2,1)S(1)}, u32[]{:S(2)}, u32[]{:S(2)}) collective-permute-start(bf16[512,384]{1,0:T(8,128)(2,1)S(1)} %collective-permute-done.3.refs_4_), channel_id=1, source_target_pairs={{0,1},{1,2},{2,3},{3,4},{4,5},{5,6},{6,7},{7,0},{8,15},{9,8},{10,9... | collective-permute-start | bytes 1179656 | tf_op jit(solution)/shard_map/ppermute | solution.py:302
  40.7 0.8 copy-done.4
  41.5 3.9 %collective-permute-done.5.refs_6_ = bf16[512,384]{1,0:T(8,128)(2,1)S(1)} collective-permute-done((bf16[512,384]{1,0:T(8,128)(2,1)S(1)}, bf16[512,384]{1,0:T(8,128)(2,1)S(1)}, u32[]{:S(2)}, u32[]{:S(2)}) %collective-permute-start.5) | collective-permute-done | bytes 393248 | tf_op jit(solution)/shard_map/ppermute | solution.py:302
  45.5 3.1 %collective-permute-start.7 = (bf16[512,384]{1,0:T(8,128)(2,1)S(1)}, bf16[512,384]{1,0:T(8,128)(2,1)S(1)}, u32[]{:S(2)}, u32[]{:S(2)}) collective-permute-start(bf16[512,384]{1,0:T(8,128)(2,1)S(1)} %collective-permute-done.5.refs_6_), channel_id=1, source_target_pairs={{0,1},{1,2},{2,3},{3,4},{4,5},{5,6},{6,7},{7,0},{8,15},{9,8},{10,9... | collective-permute-start | bytes 1179656 | tf_op jit(solution)/shard_map/ppermute | solution.py:302
  48.8 4.6 %collective-permute-done.7.refs_8_ = bf16[512,384]{1,0:T(8,128)(2,1)S(1)} collective-permute-done((bf16[512,384]{1,0:T(8,128)(2,1)S(1)}, bf16[512,384]{1,0:T(8,128)(2,1)S(1)}, u32[]{:S(2)}, u32[]{:S(2)}) %collective-permute-start.7) | collective-permute-done | bytes 393248 | tf_op jit(solution)/shard_map/ppermute | solution.py:302
  53.3 0.8 collective-permute-start.18
  54.1 1.6 pad_maximum_fusion.1.refs_18_
  55.7 2.0 %collective-permute-start.22 = (bf16[1536,768]{1,0:T(8,128)(2,1)}, bf16[1536,768]{1,0:T(8,128)(2,1)}, u32[]{:S(2)}, u32[]{:S(2)}) collective-permute-start(bf16[1536,768]{1,0:T(8,128)(2,1)} %pad_maximum_fusion.1.refs_18_), channel_id=1, source_target_pairs={{0,64},{8,56},{16,80},{24,40},{32,96},{40,24},{48,112},{56,8},{64,... | collective-permute-start | bytes 7077896 | tf_op jit(solution)/shard_map/ppermute | solution.py:311
  57.7 3.1 %collective-permute-start.6 = (bf16[512,384]{1,0:T(8,128)(2,1)S(1)}, bf16[512,384]{1,0:T(8,128)(2,1)S(1)}, u32[]{:S(2)}, u32[]{:S(2)}) collective-permute-start(bf16[512,384]{1,0:T(8,128)(2,1)S(1)} %collective-permute-done.4.refs_5_), channel_id=1, source_target_pairs={{0,1},{1,2},{2,3},{3,4},{4,5},{5,6},{6,7},{7,0},{8,15},{9,8},{10,9... | collective-permute-start | bytes 1179656 | tf_op jit(solution)/shard_map/ppermute | solution.py:302
  60.8 4.7 %collective-permute-done.6.refs_7_ = bf16[512,384]{1,0:T(8,128)(2,1)S(1)} collective-permute-done((bf16[512,384]{1,0:T(8,128)(2,1)S(1)}, bf16[512,384]{1,0:T(8,128)(2,1)S(1)}, u32[]{:S(2)}, u32[]{:S(2)}) %collective-permute-start.6) | collective-permute-done | bytes 393248 | tf_op jit(solution)/shard_map/ppermute | solution.py:302
  65.5 3.5 %collective-permute-start.8 = (bf16[512,384]{1,0:T(8,128)(2,1)S(1)}, bf16[512,384]{1,0:T(8,128)(2,1)S(1)}, u32[]{:S(2)}, u32[]{:S(2)}) collective-permute-start(bf16[512,384]{1,0:T(8,128)(2,1)S(1)} %collective-permute-done.6.refs_7_), channel_id=1, source_target_pairs={{0,1},{1,2},{2,3},{3,4},{4,5},{5,6},{6,7},{7,0},{8,15},{9,8},{10,9... | collective-permute-start | bytes 1179656 | tf_op jit(solution)/shard_map/ppermute | solution.py:302
  69.0 0.8 copy-done.10
  69.8 4.0 %collective-permute-done.8.refs_9_ = bf16[512,384]{1,0:T(8,128)(2,1)S(1)} collective-permute-done((bf16[512,384]{1,0:T(8,128)(2,1)S(1)}, bf16[512,384]{1,0:T(8,128)(2,1)S(1)}, u32[]{:S(2)}, u32[]{:S(2)}) %collective-permute-start.8) | collective-permute-done | bytes 393248 | tf_op jit(solution)/shard_map/ppermute | solution.py:302
  73.7 3.5 %collective-permute-start.10 = (bf16[512,384]{1,0:T(8,128)(2,1)S(1)}, bf16[512,384]{1,0:T(8,128)(2,1)S(1)}, u32[]{:S(2)}, u32[]{:S(2)}) collective-permute-start(bf16[512,384]{1,0:T(8,128)(2,1)S(1)} %collective-permute-done.8.refs_9_), channel_id=1, source_target_pairs={{0,1},{1,2},{2,3},{3,4},{4,5},{5,6},{6,7},{7,0},{8,15},{9,8},{10,9... | collective-permute-start | bytes 1179656 | tf_op jit(solution)/shard_map/ppermute | solution.py:302
  77.3 0.7 copy-done.12
  78.0 3.5 %collective-permute-start.11 = (bf16[512,384]{1,0:T(8,128)(2,1)S(1)}, bf16[512,384]{1,0:T(8,128)(2,1)}, u32[]{:S(2)}, u32[]{:S(2)}) collective-permute-start(bf16[512,384]{1,0:T(8,128)(2,1)S(1)} %collective-permute-done.9.refs_10_), channel_id=1, source_target_pairs={{0,1},{1,2},{2,3},{3,4},{4,5},{5,6},{6,7},{7,0},{8,15},{9,8},{10,9... | collective-permute-start | bytes 1179656 | tf_op jit(solution)/shard_map/ppermute | solution.py:302
  81.5 0.7 copy-done.14
  82.2 3.5 %collective-permute-start.12 = (bf16[512,384]{1,0:T(8,128)(2,1)S(1)}, bf16[512,384]{1,0:T(8,128)(2,1)}, u32[]{:S(2)}, u32[]{:S(2)}) collective-permute-start(bf16[512,384]{1,0:T(8,128)(2,1)S(1)} %collective-permute-done.10.refs_11_), channel_id=1, source_target_pairs={{0,1},{1,2},{2,3},{3,4},{4,5},{5,6},{6,7},{7,0},{8,15},{9,8},{10,9... | collective-permute-start | bytes 1179656 | tf_op jit(solution)/shard_map/ppermute | solution.py:302
  85.7 0.7 copy-done.16
  86.4 3.2 %collective-permute-start.13 = (bf16[512,384]{1,0:T(8,128)(2,1)}, bf16[512,384]{1,0:T(8,128)(2,1)}, u32[]{:S(2)}, u32[]{:S(2)}) collective-permute-start(bf16[512,384]{1,0:T(8,128)(2,1)} %collective-permute-done.11.refs_12_), channel_id=1, source_target_pairs={{0,1},{1,2},{2,3},{3,4},{4,5},{5,6},{6,7},{7,0},{8,15},{9,8},{10,9... | collective-permute-start | bytes 1179656 | tf_op jit(solution)/shard_map/ppermute | solution.py:302
  89.6 1.0 collective-permute-done.12.refs_13_
  90.6 3.2 %collective-permute-start.14 = (bf16[512,384]{1,0:T(8,128)(2,1)}, bf16[512,384]{1,0:T(8,128)(2,1)}, u32[]{:S(2)}, u32[]{:S(2)}) collective-permute-start(bf16[512,384]{1,0:T(8,128)(2,1)} %collective-permute-done.12.refs_13_), channel_id=1, source_target_pairs={{0,1},{1,2},{2,3},{3,4},{4,5},{5,6},{6,7},{7,0},{8,15},{9,8},{10,9... | collective-permute-start | bytes 1179656 | tf_op jit(solution)/shard_map/ppermute | solution.py:302
  94.9 4.2 %collective-permute-done.14.refs_15_ = bf16[512,384]{1,0:T(8,128)(2,1)} collective-permute-done((bf16[512,384]{1,0:T(8,128)(2,1)}, bf16[512,384]{1,0:T(8,128)(2,1)}, u32[]{:S(2)}, u32[]{:S(2)}) %collective-permute-start.14) | collective-permute-done | bytes 393248 | tf_op jit(solution)/shard_map/ppermute | solution.py:302
  99.1 1.0 copy-done.1
  100.1 1.0 copy-done.3
  101.1 1.0 copy-done.5
  102.1 1.0 copy-done.7
  103.1 1.0 copy-done.9
  104.1 1.0 copy-done.11
  105.1 1.0 copy-done.13
  106.1 1.0 copy-done.15
  107.1 1.0 copy-done.17
  108.1 7.2 %shard_map.66 = bf16[1024,512]{1,0:T(8,128)(2,1)S(1)} custom-call(s32[33]{0:T(128)S(1)} %pad_add_fusion.info, bf16[512,384]{1,0:T(8,128)(2,1)S(1)} %get-tuple-element.34.refs_0_, bf16[512,384]{1,0:T(8,128)(2,1)S(1)} %collective-permute-done.refs_1_, bf16[512,384]{1,0:T(8,128)(2,1)S(1)} %collective-permute-done.1.refs_2_, bf16[512,384]{1,0:T(8,128)(2,1)S(1)} %copy-done.1, ...), custom_call_target="tpu_custom_call" | custom-call | flops 3221225472 | bytes 16777216 | tf_op jit(solution)/shard_map/pallas_call | solution.py:169
  115.3 10.8 %collective-permute-start.24 = (bf16[1024,512]{1,0:T(8,128)(2,1)S(1)}, bf16[1024,512]{1,0:T(8,128)(2,1)S(1)}, u32[]{:S(2)}, u32[]{:S(2)}) collective-permute-start(bf16[1024,512]{1,0:T(8,128)(2,1)S(1)} %shard_map.66), channel_id=1, source_target_pairs={{0,8},{8,0},{16,24},{24,16},{32,40},{40,32},{48,56},{56,48},{64,72... | collective-permute-start | bytes 3145736 | tf_op jit(solution)/shard_map/ppermute | solution.py:336
  126.1 7.7 %shard_map.64 = (bf16[1024,256]{1,0:T(8,128)(2,1)}, f32[1024,256]{1,0:T(8,128)S(1)}) custom-call(s32[33]{0:T(128)S(1)} %pad_add_fusion.info, bf16[512,384]{1,0:T(8,128)(2,1)S(1)} %get-tuple-element.34.refs_0_, bf16[512,384]{1,0:T(8,128)(2,1)S(1)} %collective-permute-done.refs_1_, bf16[512,384]{1,0:T(8,128)(2,1)S(1)} %collective-permute-done.1.refs_2_, ...), custom_call_target="tpu_custom_call" | custom-call | flops 3221225472 | bytes 16777216 | tf_op jit(solution)/shard_map/pallas_call | solution.py:169
  134.0 7.5 %shard_map.65.mine = f32[1024,512]{1,0:T(8,128)S(1)} custom-call(s32[33]{0:T(128)S(1)} %pad_add_fusion.info, bf16[512,384]{1,0:T(8,128)(2,1)S(1)} %get-tuple-element.34.refs_0_, bf16[512,384]{1,0:T(8,128)(2,1)S(1)} %collective-permute-done.refs_1_, bf16[512,384]{1,0:T(8,128)(2,1)S(1)} %collective-permute-done.1.refs_2_, bf16[512,384]{1,0:T(8,128)(2,1)S(1)} %copy-done.1, ...), custom_call_target="tpu_custom_call" | custom-call | flops 3221225472 | bytes 16777216 | tf_op jit(solution)/shard_map/pallas_call | solution.py:169
  141.5 0.8 shard_map.67
  142.3 0.9 collective-permute-start.27
  143.3 1.2 collective-permute-start.26
  144.5 1.0 collective-permute-done.27
  145.5 2.4 %collective-permute-done.26 = bf16[2,128,128]{2,1,0:T(8,128)(2,1)S(1)} collective-permute-done((bf16[2,128,128]{2,1,0:T(8,128)(2,1)S(1)}, bf16[2,128,128]{2,1,0:T(8,128)(2,1)S(1)}, u32[]{:S(2)}, u32[]{:S(2)}) %collective-permute-start.26) | collective-permute-done | bytes 65568 | tf_op jit(solution)/shard_map/ppermute | solution.py:343
  147.9 1.7 %collective-permute-done.25 = bf16[2,128,128]{2,1,0:T(8,128)(2,1)S(1)} collective-permute-done((bf16[2,128,128]{2,1,0:T(8,128)(2,1)S(1)}, bf16[2,128,128]{2,1,0:T(8,128)(2,1)S(1)}, u32[]{:S(2)}, u32[]{:S(2)}) %collective-permute-start.25) | collective-permute-done | bytes 65568 | tf_op jit(solution)/shard_map/ppermute | solution.py:343
  149.6 3.5 %collective-permute-start.28 = (bf16[2,128,128]{2,1,0:T(8,128)(2,1)S(1)}, bf16[2,128,128]{2,1,0:T(8,128)(2,1)S(1)}, u32[]{:S(2)}, u32[]{:S(2)}) collective-permute-start(bf16[2,128,128]{2,1,0:T(8,128)(2,1)S(1)} %get-tuple-element.41), channel_id=1, source_target_pairs={{0,64},{8,72},{16,80},{24,88},{32,96},{40,104},{48,112},{56,120},{... | collective-permute-start | bytes 196616 | tf_op jit(solution)/shard_map/ppermute | solution.py:347
  153.2 2.5 %collective-permute-start.29 = (bf16[2,128,128]{2,1,0:T(8,128)(2,1)S(1)}, bf16[2,128,128]{2,1,0:T(8,128)(2,1)S(1)}, u32[]{:S(2)}, u32[]{:S(2)}) collective-permute-start(bf16[2,128,128]{2,1,0:T(8,128)(2,1)S(1)} %get-tuple-element.41), channel_id=1, source_target_pairs={{0,128},{8,136},{16,144},{24,152},{32,160},{40,168},{48,176},{56,1... | collective-permute-start | bytes 196616 | tf_op jit(solution)/shard_map/ppermute | solution.py:347
  155.6 1.3 collective-permute-start.30
  157.0 2.0 %shard_map.68 = (bf16[1024,256]{1,0:T(8,128)(2,1)S(1)}, f32[1024,256]{1,0:T(8,128)S(1)}) custom-call(f32[1024,256]{1,0:T(8,128)S(1)} %copy-done.19, bf16[1024,256]{1,0:T(8,128)(2,1)} %collective-permute-done.23.other, bf16[1024,256]{1,0:T(8,128)(2,1)S(1)} %get-tuple-element.27.key, bf16[1024,256]{1,0:T(8,128)(2,1)S(1)} %get-tuple-element.28.value), custom_call_target="tpu_custom_call" | custom-call | flops 268435456 | bytes 5242880 | tf_op jit(solution)/shard_map/pallas_call | solution.py:244
  159.0 0.9 shard_map.70
  160.0 1.6 collective-permute-start.31
  161.5 0.9 shard_map.69
  162.7 0.8 pad_maximum_fusion.6
  (73 shorter events, 3.2 us)
Async XLA Ops:
  1.5 3.7 %copy-start.20 = (bf16[192,512]{1,0:T(8,128)(2,1)S(1)}, bf16[192,512]{1,0:T(8,128)(2,1)}, u32[]{:S(2)}) copy-start(bf16[192,512]{1,0:T(8,128)(2,1)} %param.7) | copy-start | bytes 589828
  1.5 3.7 %copy-start.21 = (bf16[192,512]{1,0:T(8,128)(2,1)S(1)}, bf16[192,512]{1,0:T(8,128)(2,1)}, u32[]{:S(2)}) copy-start(bf16[192,512]{1,0:T(8,128)(2,1)} %param.8) | copy-start | bytes 589828
  1.5 3.7 %copy-start.22 = (bf16[192,512]{1,0:T(8,128)(2,1)S(1)}, bf16[192,512]{1,0:T(8,128)(2,1)}, u32[]{:S(2)}) copy-start(bf16[192,512]{1,0:T(8,128)(2,1)} %param.9) | copy-start | bytes 589828
  1.9 10.7 %collective-permute-start = (bf16[512,384]{1,0:T(8,128)(2,1)S(1)}, bf16[512,384]{1,0:T(8,128)(2,1)S(1)}, u32[]{:S(2)}, u32[]{:S(2)}) collective-permute-start(bf16[512,384]{1,0:T(8,128)(2,1)S(1)} %get-tuple-element.33), channel_id=1, source_target_pairs={{0,8},{8,0},{16,24},{24,16},{32,40},{40,32},{48,56},{56,48},{64,72... | collective-permute-start | bytes 1179656 | tf_op jit(solution)/shard_map/ppermute | solution.py:298
  5.3 8.0 %collective-permute-start.15 = (bf16[192,768]{1,0:T(8,128)(2,1)S(1)}, bf16[192,768]{1,0:T(8,128)(2,1)S(1)}, u32[]{:S(2)}, u32[]{:S(2)}) collective-permute-start(bf16[192,768]{1,0:T(8,128)(2,1)S(1)} %pad_maximum_fusion.9), channel_id=1, source_target_pairs={{0,16},{8,72},{16,0},{24,88},{32,48},{40,104},{48,32},{56,120},{64... | collective-permute-start | bytes 884744 | tf_op jit(solution)/shard_map/ppermute | solution.py:311
  5.4 9.8 %collective-permute-start.1 = (bf16[512,384]{1,0:T(8,128)(2,1)S(1)}, bf16[512,384]{1,0:T(8,128)(2,1)S(1)}, u32[]{:S(2)}, u32[]{:S(2)}) collective-permute-start(bf16[512,384]{1,0:T(8,128)(2,1)S(1)} %get-tuple-element.34.refs_0_), channel_id=1, source_target_pairs={{0,1},{1,2},{2,3},{3,4},{4,5},{5,6},{6,7},{7,0},{8,15},{9,8},{10,9... | collective-permute-start | bytes 1179656 | tf_op jit(solution)/shard_map/ppermute | solution.py:302
  10.5 7.2 %collective-permute-start.19 = (bf16[192,768]{1,0:T(8,128)(2,1)S(1)}, bf16[192,768]{1,0:T(8,128)(2,1)S(1)}, u32[]{:S(2)}, u32[]{:S(2)}) collective-permute-start(bf16[192,768]{1,0:T(8,128)(2,1)S(1)} %pad_maximum_fusion.10), channel_id=1, source_target_pairs={{0,48},{8,200},{16,32},{24,216},{32,16},{40,232},{48,0},{56,248},{... | collective-permute-start | bytes 884744 | tf_op jit(solution)/shard_map/ppermute | solution.py:311
  12.5 6.9 %collective-permute-start.2 = (bf16[512,384]{1,0:T(8,128)(2,1)S(1)}, bf16[512,384]{1,0:T(8,128)(2,1)S(1)}, u32[]{:S(2)}, u32[]{:S(2)}) collective-permute-start(bf16[512,384]{1,0:T(8,128)(2,1)S(1)} %collective-permute-done.refs_1_), channel_id=1, source_target_pairs={{0,1},{1,2},{2,3},{3,4},{4,5},{5,6},{6,7},{7,0},{8,15},{9,8},{10,9... | collective-permute-start | bytes 1179656 | tf_op jit(solution)/shard_map/ppermute | solution.py:302
  15.2 10.2 %collective-permute-start.16 = (bf16[384,768]{1,0:T(8,128)(2,1)S(1)}, bf16[384,768]{1,0:T(8,128)(2,1)S(1)}, u32[]{:S(2)}, u32[]{:S(2)}) collective-permute-start(bf16[384,768]{1,0:T(8,128)(2,1)S(1)} %pad_maximum_fusion.4), channel_id=1, source_target_pairs={{0,64},{8,56},{16,80},{24,40},{32,96},{40,24},{48,112},{56,8},{64,... | collective-permute-start | bytes 1769480 | tf_op jit(solution)/shard_map/ppermute | solution.py:311
  17.8 14.8 %collective-permute-start.20 = (bf16[384,768]{1,0:T(8,128)(2,1)S(1)}, bf16[384,768]{1,0:T(8,128)(2,1)S(1)}, u32[]{:S(2)}, u32[]{:S(2)}) collective-permute-start(bf16[384,768]{1,0:T(8,128)(2,1)S(1)} %pad_maximum_fusion.5), channel_id=1, source_target_pairs={{0,192},{8,24},{16,208},{24,8},{32,224},{40,56},{48,240},{56,40},{... | collective-permute-start | bytes 1769480 | tf_op jit(solution)/shard_map/ppermute | solution.py:311
  19.5 13.2 %copy-start = (bf16[512,384]{1,0:T(8,128)(2,1)}, bf16[512,384]{1,0:T(8,128)(2,1)S(1)}, u32[]{:S(2)}) copy-start(bf16[512,384]{1,0:T(8,128)(2,1)S(1)} %collective-permute-done.2.refs_3_) | copy-start | bytes 1179652
  19.5 7.8 %collective-permute-start.4 = (bf16[512,384]{1,0:T(8,128)(2,1)S(1)}, bf16[512,384]{1,0:T(8,128)(2,1)S(1)}, u32[]{:S(2)}, u32[]{:S(2)}) collective-permute-start(bf16[512,384]{1,0:T(8,128)(2,1)S(1)} %collective-permute-done.2.refs_3_), channel_id=1, source_target_pairs={{0,1},{1,2},{2,3},{3,4},{4,5},{5,6},{6,7},{7,0},{8,15},{9,8},{10,9... | collective-permute-start | bytes 1179656 | tf_op jit(solution)/shard_map/ppermute | solution.py:302
  27.3 30.4 %copy-start.2 = (bf16[512,384]{1,0:T(8,128)(2,1)}, bf16[512,384]{1,0:T(8,128)(2,1)S(1)}, u32[]{:S(2)}) copy-start(bf16[512,384]{1,0:T(8,128)(2,1)S(1)} %collective-permute-done.4.refs_5_) | copy-start | bytes 1179652
  27.3 21.3 %collective-permute-start.17 = (bf16[768,768]{1,0:T(8,128)(2,1)S(1)}, bf16[768,768]{1,0:T(8,128)(2,1)S(1)}, u32[]{:S(2)}, u32[]{:S(2)}) collective-permute-start(bf16[768,768]{1,0:T(8,128)(2,1)S(1)} %pad_maximum_fusion.2), channel_id=1, source_target_pairs={{0,48},{8,200},{16,32},{24,216},{32,16},{40,232},{48,0},{56,248},{... | collective-permute-start | bytes 3538952 | tf_op jit(solution)/shard_map/ppermute | solution.py:311
  29.2 8.1 %collective-permute-start.3 = (bf16[512,384]{1,0:T(8,128)(2,1)S(1)}, bf16[512,384]{1,0:T(8,128)(2,1)S(1)}, u32[]{:S(2)}, u32[]{:S(2)}) collective-permute-start(bf16[512,384]{1,0:T(8,128)(2,1)S(1)} %collective-permute-done.1.refs_2_), channel_id=1, source_target_pairs={{0,1},{1,2},{2,3},{3,4},{4,5},{5,6},{6,7},{7,0},{8,15},{9,8},{10,9... | collective-permute-start | bytes 1179656 | tf_op jit(solution)/shard_map/ppermute | solution.py:302
  32.7 21.4 %collective-permute-start.21 = (bf16[768,768]{1,0:T(8,128)(2,1)S(1)}, bf16[768,768]{1,0:T(8,128)(2,1)S(1)}, u32[]{:S(2)}, u32[]{:S(2)}) collective-permute-start(bf16[768,768]{1,0:T(8,128)(2,1)S(1)} %pad_maximum_fusion.3), channel_id=1, source_target_pairs={{0,16},{8,72},{16,0},{24,88},{32,48},{40,104},{48,32},{56,120},{64... | collective-permute-start | bytes 3538952 | tf_op jit(solution)/shard_map/ppermute | solution.py:311
  37.3 8.1 %collective-permute-start.5 = (bf16[512,384]{1,0:T(8,128)(2,1)S(1)}, bf16[512,384]{1,0:T(8,128)(2,1)S(1)}, u32[]{:S(2)}, u32[]{:S(2)}) collective-permute-start(bf16[512,384]{1,0:T(8,128)(2,1)S(1)} %collective-permute-done.3.refs_4_), channel_id=1, source_target_pairs={{0,1},{1,2},{2,3},{3,4},{4,5},{5,6},{6,7},{7,0},{8,15},{9,8},{10,9... | collective-permute-start | bytes 1179656 | tf_op jit(solution)/shard_map/ppermute | solution.py:302
  40.7 0.8 copy-start.4
  45.5 3.3 %copy-start.6 = (bf16[512,384]{1,0:T(8,128)(2,1)}, bf16[512,384]{1,0:T(8,128)(2,1)S(1)}, u32[]{:S(2)}) copy-start(bf16[512,384]{1,0:T(8,128)(2,1)S(1)} %collective-permute-done.5.refs_6_) | copy-start | bytes 1179652
  45.5 7.8 %collective-permute-start.7 = (bf16[512,384]{1,0:T(8,128)(2,1)S(1)}, bf16[512,384]{1,0:T(8,128)(2,1)S(1)}, u32[]{:S(2)}, u32[]{:S(2)}) collective-permute-start(bf16[512,384]{1,0:T(8,128)(2,1)S(1)} %collective-permute-done.5.refs_6_), channel_id=1, source_target_pairs={{0,1},{1,2},{2,3},{3,4},{4,5},{5,6},{6,7},{7,0},{8,15},{9,8},{10,9... | collective-permute-start | bytes 1179656 | tf_op jit(solution)/shard_map/ppermute | solution.py:302
  53.3 15.7 %copy-start.8 = (bf16[512,384]{1,0:T(8,128)(2,1)}, bf16[512,384]{1,0:T(8,128)(2,1)S(1)}, u32[]{:S(2)}) copy-start(bf16[512,384]{1,0:T(8,128)(2,1)S(1)} %collective-permute-done.7.refs_8_) | copy-start | bytes 1179652
  53.3 45.8 %collective-permute-start.18 = (bf16[1536,768]{1,0:T(8,128)(2,1)S(1)}, bf16[1536,768]{1,0:T(8,128)(2,1)}, u32[]{:S(2)}, u32[]{:S(2)}) collective-permute-start(bf16[1536,768]{1,0:T(8,128)(2,1)S(1)} %pad_maximum_fusion.refs_16_), channel_id=1, source_target_pairs={{0,192},{8,24},{16,208},{24,8},{32,224},{40,56},{48,240},{56,40},{... | collective-permute-start | bytes 7077896 | tf_op jit(solution)/shard_map/ppermute | solution.py:311
  55.7 43.4 %collective-permute-start.22 = (bf16[1536,768]{1,0:T(8,128)(2,1)}, bf16[1536,768]{1,0:T(8,128)(2,1)}, u32[]{:S(2)}, u32[]{:S(2)}) collective-permute-start(bf16[1536,768]{1,0:T(8,128)(2,1)} %pad_maximum_fusion.1.refs_18_), channel_id=1, source_target_pairs={{0,64},{8,56},{16,80},{24,40},{32,96},{40,24},{48,112},{56,8},{64,... | collective-permute-start | bytes 7077896 | tf_op jit(solution)/shard_map/ppermute | solution.py:311
  57.7 7.8 %collective-permute-start.6 = (bf16[512,384]{1,0:T(8,128)(2,1)S(1)}, bf16[512,384]{1,0:T(8,128)(2,1)S(1)}, u32[]{:S(2)}, u32[]{:S(2)}) collective-permute-start(bf16[512,384]{1,0:T(8,128)(2,1)S(1)} %collective-permute-done.4.refs_5_), channel_id=1, source_target_pairs={{0,1},{1,2},{2,3},{3,4},{4,5},{5,6},{6,7},{7,0},{8,15},{9,8},{10,9... | collective-permute-start | bytes 1179656 | tf_op jit(solution)/shard_map/ppermute | solution.py:302
  65.5 8.2 %collective-permute-start.8 = (bf16[512,384]{1,0:T(8,128)(2,1)S(1)}, bf16[512,384]{1,0:T(8,128)(2,1)S(1)}, u32[]{:S(2)}, u32[]{:S(2)}) collective-permute-start(bf16[512,384]{1,0:T(8,128)(2,1)S(1)} %collective-permute-done.6.refs_7_), channel_id=1, source_target_pairs={{0,1},{1,2},{2,3},{3,4},{4,5},{5,6},{6,7},{7,0},{8,15},{9,8},{10,9... | collective-permute-start | bytes 1179656 | tf_op jit(solution)/shard_map/ppermute | solution.py:302
  69.0 0.8 copy-start.10
  69.8 8.2 %collective-permute-start.9 = (bf16[512,384]{1,0:T(8,128)(2,1)S(1)}, bf16[512,384]{1,0:T(8,128)(2,1)S(1)}, u32[]{:S(2)}, u32[]{:S(2)}) collective-permute-start(bf16[512,384]{1,0:T(8,128)(2,1)S(1)} %collective-permute-done.7.refs_8_), channel_id=1, source_target_pairs={{0,1},{1,2},{2,3},{3,4},{4,5},{5,6},{6,7},{7,0},{8,15},{9,8},{10,9... | collective-permute-start | bytes 1179656 | tf_op jit(solution)/shard_map/ppermute | solution.py:302
  73.7 8.5 %collective-permute-start.10 = (bf16[512,384]{1,0:T(8,128)(2,1)S(1)}, bf16[512,384]{1,0:T(8,128)(2,1)S(1)}, u32[]{:S(2)}, u32[]{:S(2)}) collective-permute-start(bf16[512,384]{1,0:T(8,128)(2,1)S(1)} %collective-permute-done.8.refs_9_), channel_id=1, source_target_pairs={{0,1},{1,2},{2,3},{3,4},{4,5},{5,6},{6,7},{7,0},{8,15},{9,8},{10,9... | collective-permute-start | bytes 1179656 | tf_op jit(solution)/shard_map/ppermute | solution.py:302
  77.3 0.7 copy-start.12
  78.0 8.4 %collective-permute-start.11 = (bf16[512,384]{1,0:T(8,128)(2,1)S(1)}, bf16[512,384]{1,0:T(8,128)(2,1)}, u32[]{:S(2)}, u32[]{:S(2)}) collective-permute-start(bf16[512,384]{1,0:T(8,128)(2,1)S(1)} %collective-permute-done.9.refs_10_), channel_id=1, source_target_pairs={{0,1},{1,2},{2,3},{3,4},{4,5},{5,6},{6,7},{7,0},{8,15},{9,8},{10,9... | collective-permute-start | bytes 1179656 | tf_op jit(solution)/shard_map/ppermute | solution.py:302
  81.5 0.7 copy-start.14
  82.2 8.4 %collective-permute-start.12 = (bf16[512,384]{1,0:T(8,128)(2,1)S(1)}, bf16[512,384]{1,0:T(8,128)(2,1)}, u32[]{:S(2)}, u32[]{:S(2)}) collective-permute-start(bf16[512,384]{1,0:T(8,128)(2,1)S(1)} %collective-permute-done.10.refs_11_), channel_id=1, source_target_pairs={{0,1},{1,2},{2,3},{3,4},{4,5},{5,6},{6,7},{7,0},{8,15},{9,8},{10,9... | collective-permute-start | bytes 1179656 | tf_op jit(solution)/shard_map/ppermute | solution.py:302
  85.7 0.7 copy-start.16
  86.4 8.5 %collective-permute-start.13 = (bf16[512,384]{1,0:T(8,128)(2,1)}, bf16[512,384]{1,0:T(8,128)(2,1)}, u32[]{:S(2)}, u32[]{:S(2)}) collective-permute-start(bf16[512,384]{1,0:T(8,128)(2,1)} %collective-permute-done.11.refs_12_), channel_id=1, source_target_pairs={{0,1},{1,2},{2,3},{3,4},{4,5},{5,6},{6,7},{7,0},{8,15},{9,8},{10,9... | collective-permute-start | bytes 1179656 | tf_op jit(solution)/shard_map/ppermute | solution.py:302
  90.6 8.5 %collective-permute-start.14 = (bf16[512,384]{1,0:T(8,128)(2,1)}, bf16[512,384]{1,0:T(8,128)(2,1)}, u32[]{:S(2)}, u32[]{:S(2)}) collective-permute-start(bf16[512,384]{1,0:T(8,128)(2,1)} %collective-permute-done.12.refs_13_), channel_id=1, source_target_pairs={{0,1},{1,2},{2,3},{3,4},{4,5},{5,6},{6,7},{7,0},{8,15},{9,8},{10,9... | collective-permute-start | bytes 1179656 | tf_op jit(solution)/shard_map/ppermute | solution.py:302
  99.1 1.0 copy-start.1
  100.1 1.0 copy-start.3
  101.1 1.0 copy-start.5
  102.1 1.0 copy-start.7
  103.1 1.0 copy-start.9
  104.1 1.0 copy-start.11
  105.1 1.0 copy-start.13
  106.1 1.0 copy-start.15
  107.1 1.0 copy-start.17
  115.3 26.2 %collective-permute-start.24 = (bf16[1024,512]{1,0:T(8,128)(2,1)S(1)}, bf16[1024,512]{1,0:T(8,128)(2,1)S(1)}, u32[]{:S(2)}, u32[]{:S(2)}) collective-permute-start(bf16[1024,512]{1,0:T(8,128)(2,1)S(1)} %shard_map.66), channel_id=1, source_target_pairs={{0,8},{8,0},{16,24},{24,16},{32,40},{40,32},{48,56},{56,48},{64,72... | collective-permute-start | bytes 3145736 | tf_op jit(solution)/shard_map/ppermute | solution.py:336
  133.8 7.6 %copy-start.18 = (f32[1024,256]{1,0:T(8,128)}, f32[1024,256]{1,0:T(8,128)S(1)}, u32[]{:S(2)}) copy-start(f32[1024,256]{1,0:T(8,128)S(1)} %get-tuple-element.25.mine) | copy-start | bytes 3145732
  133.8 23.2 %collective-permute-start.23 = (bf16[1024,256]{1,0:T(8,128)(2,1)}, bf16[1024,256]{1,0:T(8,128)(2,1)}, u32[]{:S(2)}, u32[]{:S(2)}) collective-permute-start(bf16[1024,256]{1,0:T(8,128)(2,1)} %get-tuple-element.26), channel_id=1, source_target_pairs={{0,8},{8,0},{16,24},{24,16},{32,40},{40,32},{48,56},{56,48},{64,72... | collective-permute-start | bytes 1572872 | tf_op jit(solution)/shard_map/ppermute | solution.py:352
  141.4 15.5 %copy-start.23 = (f32[512]{0:T(512)S(1)}, f32[512]{0:T(512)}, u32[]{:S(2)}) copy-start(f32[512]{0:T(512)} %param.10) | copy-start | bytes 6148
  141.5 15.6 %copy-start.19 = (f32[1024,256]{1,0:T(8,128)S(1)}, f32[1024,256]{1,0:T(8,128)}, u32[]{:S(2)}) copy-start(f32[1024,256]{1,0:T(8,128)} %copy-done.18) | copy-start | bytes 3145732
  142.3 3.2 %collective-permute-start.27 = (bf16[2,128,128]{2,1,0:T(8,128)(2,1)S(1)}, bf16[2,128,128]{2,1,0:T(8,128)(2,1)S(1)}, u32[]{:S(2)}, u32[]{:S(2)}) collective-permute-start(bf16[2,128,128]{2,1,0:T(8,128)(2,1)S(1)} %get-tuple-element.32), channel_id=1, source_target_pairs={{0,48},{8,56},{16,0},{24,8},{32,16},{40,24},{48,32},{56,40},{64,11... | collective-permute-start | bytes 196616 | tf_op jit(solution)/shard_map/ppermute | solution.py:343
  143.3 4.6 %collective-permute-start.26 = (bf16[2,128,128]{2,1,0:T(8,128)(2,1)S(1)}, bf16[2,128,128]{2,1,0:T(8,128)(2,1)S(1)}, u32[]{:S(2)}, u32[]{:S(2)}) collective-permute-start(bf16[2,128,128]{2,1,0:T(8,128)(2,1)S(1)} %get-tuple-element.32), channel_id=1, source_target_pairs={{0,32},{8,40},{16,48},{24,56},{32,0},{40,8},{48,16},{56,24},{64,96... | collective-permute-start | bytes 196616 | tf_op jit(solution)/shard_map/ppermute | solution.py:343
  144.5 5.1 %collective-permute-start.25 = (bf16[2,128,128]{2,1,0:T(8,128)(2,1)S(1)}, bf16[2,128,128]{2,1,0:T(8,128)(2,1)S(1)}, u32[]{:S(2)}, u32[]{:S(2)}) collective-permute-start(bf16[2,128,128]{2,1,0:T(8,128)(2,1)S(1)} %get-tuple-element.32), channel_id=1, source_target_pairs={{0,16},{8,24},{16,32},{24,40},{32,48},{40,56},{48,0},{56,8},{64,80... | collective-permute-start | bytes 196616 | tf_op jit(solution)/shard_map/ppermute | solution.py:343
  149.6 9.4 %collective-permute-start.28 = (bf16[2,128,128]{2,1,0:T(8,128)(2,1)S(1)}, bf16[2,128,128]{2,1,0:T(8,128)(2,1)S(1)}, u32[]{:S(2)}, u32[]{:S(2)}) collective-permute-start(bf16[2,128,128]{2,1,0:T(8,128)(2,1)S(1)} %get-tuple-element.41), channel_id=1, source_target_pairs={{0,64},{8,72},{16,80},{24,88},{32,96},{40,104},{48,112},{56,120},{... | collective-permute-start | bytes 196616 | tf_op jit(solution)/shard_map/ppermute | solution.py:347
  153.2 5.9 %collective-permute-start.29 = (bf16[2,128,128]{2,1,0:T(8,128)(2,1)S(1)}, bf16[2,128,128]{2,1,0:T(8,128)(2,1)S(1)}, u32[]{:S(2)}, u32[]{:S(2)}) collective-permute-start(bf16[2,128,128]{2,1,0:T(8,128)(2,1)S(1)} %get-tuple-element.41), channel_id=1, source_target_pairs={{0,128},{8,136},{16,144},{24,152},{32,160},{40,168},{48,176},{56,1... | collective-permute-start | bytes 196616 | tf_op jit(solution)/shard_map/ppermute | solution.py:347
  155.6 3.4 %collective-permute-start.30 = (bf16[2,128,128]{2,1,0:T(8,128)(2,1)S(1)}, bf16[2,128,128]{2,1,0:T(8,128)(2,1)S(1)}, u32[]{:S(2)}, u32[]{:S(2)}) collective-permute-start(bf16[2,128,128]{2,1,0:T(8,128)(2,1)S(1)} %get-tuple-element.41), channel_id=1, source_target_pairs={{0,192},{8,200},{16,208},{24,216},{32,224},{40,232},{48,240},{56,2... | collective-permute-start | bytes 196616 | tf_op jit(solution)/shard_map/ppermute | solution.py:347
  160.0 2.7 %collective-permute-start.31 = (bf16[512,256]{1,0:T(8,128)(2,1)S(1)}, bf16[512,256]{1,0:T(8,128)(2,1)S(1)}, u32[]{:S(2)}, u32[]{:S(2)}) collective-permute-start(bf16[512,256]{1,0:T(8,128)(2,1)S(1)} %shard_map.70), channel_id=1, source_target_pairs={{0,8},{8,0},{16,24},{24,16},{32,40},{40,32},{48,56},{56,48},{64,72... | collective-permute-start | bytes 786440 | tf_op jit(solution)/shard_map/ppermute | solution.py:357

commit v3 on v2

--- a/solution.py
+++ b/solution.py
@@ -98,69 +98,36 @@
 def product_kernel(parts, info, *refs):
     tokens, refs = refs[: 2 * Z], refs[2 * Z :]
     weights, refs = refs[:4], refs[4:]
-    outs, refs = refs[: len(parts)], refs[len(parts) :]
-    whole, piled, total, token_sem, weight_sem = refs
+    outs, (piled,) = refs[: len(parts)], refs[len(parts) :]
     core = info[0]
-    groups = 2
-    per = Z // groups
-    depth = per * PIECE
-
-    def weight_copy(source, part, at, columns, row):
-        return pltpu.make_async_copy(
-            source.at[pl.ds(pl.multiple_of(row * ROWS, ROWS), ROWS), columns],
-            piled.at[part, pl.ds(at * ROWS, ROWS)],
-            weight_sem.at[part, at],
-        )
-
-    for k in range(Z):
+    deep = 2 * PIECE
+    for part, (mine, low, high) in enumerate(parts):
+        half = core if mine else 1 - core
+        for at in range(2 * Z):
+            place = info[1 + half * 2 * Z + at]
+            row = pl.ds(pl.multiple_of((place % 8) * ROWS, ROWS), ROWS)
+            choice = half * 2 + place // 8
+            for b in range(4):
+
+                @pl.when(choice == b)
+                def _():
+                    piled[at * ROWS : (at + 1) * ROWS, 0 : high - low] = weights[b][row, low:high]
+
         for slab in range(2):
             first = pl.multiple_of(SLAB * (core if slab == 0 else 1 - core), SLAB)
-            pltpu.make_async_copy(
-                tokens[2 * k + slab],
-                whole.at[pl.ds(first, SLAB), pl.ds(k * PIECE, PIECE)],
-                token_sem.at[k, slab],
-            ).start()
-        for part, (mine, low, high) in enumerate(parts):
-            half = core if mine else 1 - core
-            for e in range(2):
-                place = info[1 + half * 2 * Z + 2 * k + e]
-                choice = half * 2 + place // 8
-                for b in range(4):
-
-                    @pl.when(choice == b)
-                    def _():
-                        weight_copy(
-                            weights[b], part, 2 * k + e, pl.ds(low, high - low), place % 8
-                        ).start()
-
-    for g in range(groups):
-        for k in range(g * per, (g + 1) * per):
-            for slab in range(2):
-                pltpu.make_async_copy(
-                    tokens[2 * k + slab],
-                    whole.at[pl.ds(0, SLAB), pl.ds(k * PIECE, PIECE)],
-                    token_sem.at[k, slab],
-                ).wait()
-            for part, (mine, low, high) in enumerate(parts):
-                for e in range(2):
-                    weight_copy(weights[0], part, 2 * k + e, pl.ds(low, high - low), 0).wait()
-        for part in range(len(parts)):
-            for n in range(0, outs[part].shape[1], 256):
-
-                @pl.loop(0, CHIP // 512)
-                def _(m):
-                    rows = pl.ds(pl.multiple_of(m * 512, 512), 512)
+            for n in range(0, high - low, 256):
+                total = None
+                for k in range(0, Z, 2):
+                    piece = jnp.concatenate(
+                        [tokens[2 * k + slab][...], tokens[2 * k + 2 + slab][...]], axis=1
+                    )
                     some = jnp.dot(
-                        whole[rows, g * depth : (g + 1) * depth],
-                        piled[part, g * depth : (g + 1) * depth, n : n + 256],
+                        piece,
+                        piled[k * PIECE : k * PIECE + deep, n : n + 256],
                         preferred_element_type=F32,
                     )
-                    if g == 0:
-                        total[part, rows, n : n + 256] = some
-                    else:
-                        outs[part][rows, n : n + 256] = (
-                            total[part, rows, n : n + 256] + some
-                        ).astype(outs[part].dtype)
+                    total = some if total is None else total + some
+                outs[part][pl.ds(first, SLAB), n : n + 256] = total.astype(outs[part].dtype)
 
 
 def product(info, tokens, weights, parts):
@@ -172,16 +139,10 @@
             jax.ShapeDtypeStruct((CHIP, high - low), F32 if mine else BF16)
             for mine, low, high in parts
         ],
-        in_specs=[SMEM] + [ANY] * (2 * Z + 4),
+        in_specs=[SMEM] + [VMEM] * (2 * Z + 4),
         out_specs=[VMEM] * len(parts),
-        scratch_shapes=[
-            pltpu.VMEM((CHIP, Z * PIECE), BF16),
-            pltpu.VMEM((len(parts), Z * PIECE, wide), BF16),
-            pltpu.VMEM((len(parts), CHIP, wide), F32),
-            pltpu.SemaphoreType.DMA((Z, 2)),
-            pltpu.SemaphoreType.DMA((len(parts), 2 * Z)),
-        ],
-        compiler_params=pltpu.CompilerParams(vmem_limit_bytes=40 * 2**20),
+        scratch_shapes=[pltpu.VMEM((Z * PIECE, wide), BF16)],
+        compiler_params=pltpu.CompilerParams(vmem_limit_bytes=20 * 2**20),
         cost_estimate=pl.CostEstimate(
             flops=flops, bytes_accessed=16 * 2**20, transcendentals=0
         ),
@@ -291,28 +252,49 @@
     return lax.optimization_barrier((value, others))[0]
 
 
+def pace_kernel(piece, out):
+    pass
+
+
+def pace(piece):
+    return pl.pallas_call(
+        pace_kernel,
+        out_shape=jax.ShapeDtypeStruct(piece.shape, piece.dtype),
+        in_specs=[ANY],
+        out_specs=ANY,
+        input_output_aliases={0: 0},
+        compiler_params=pltpu.CompilerParams(vmem_limit_bytes=2**20),
+        cost_estimate=pl.CostEstimate(flops=2500000000, bytes_accessed=0, transcendentals=0),
+    )(piece)
+
+
 def gather(tokens, weights, core):
     even = jnp.concatenate([tokens[:, :ROWS], tokens[:, 2 * ROWS : 3 * ROWS]], axis=1)
     odd = jnp.concatenate([tokens[:, ROWS : 2 * ROWS], tokens[:, 3 * ROWS :]], axis=1)
     own = jnp.where(core == 0, even, odd)
     theirs = lax.ppermute(jnp.where(core == 0, odd, even), "seq", SWAP)
     ring = ring_pairs()
-    pieces = [[own, theirs]]
-    for _ in range(1, Z):
-        pieces.append([lax.ppermute(p, ("seq", "head"), ring) for p in pieces[-1]])
-    gates = (None, (1, 0), (2, 1), (4, 0))
+
+    def pass_on(piece):
+        return lax.ppermute(piece, ("seq", "head"), ring)
+
+    first, second = [own], [theirs]
+    for k in range(1, Z):
+        for stream in (first, second):
+            piece = stream[-1]
+            stream.append(pace(pass_on(piece)))
     streams = list(weights)
+    got = [None, None]
     blocks = []
     for step in range(4):
-        for j in range(2):
-            if gates[step] is not None:
-                k, slab = gates[step]
-                streams[j] = after(streams[j], pieces[k][slab])
-            got = lax.ppermute(streams[j], "seq", cube_pairs(j, step))
-            if step < 3:
-                streams[j] = jnp.concatenate([streams[j], got], axis=0)
-            else:
-                blocks += [streams[j], got]
+        if step:
+            if (0, 0, 0, 0)[step]:
+                got = after(got, first[(0, 0, 0, 0)[step]])
+            streams = [jnp.concatenate(pair, axis=0) for pair in zip(streams, got)]
+        got = [lax.ppermute(streams[j], "seq", cube_pairs(j, step)) for j in range(2)]
+    for j in range(2):
+        blocks += [streams[j], got[j]]
+    pieces = zip(first, second)
     return [p for pair in pieces for p in pair], blocks
 
 
@@ -347,7 +329,7 @@
     rows = [lax.ppermute(row, "seq", shift_y(k)) for k in range(1, Y)]
 
     q_theirs, q_mine = product(
-        info, pieces, blocks, ((False, 2 * HALF, 3 * HALF), (True, 2 * HALF, 3 * HALF))
+        after(info, total), pieces, blocks, ((False, 2 * HALF, 3 * HALF), (True, 2 * HALF, 3 * HALF))
     )
     q_got = lax.ppermute(q_theirs, "seq", SWAP)
     query, inside = local_part(q_mine, q_got, key, value)

time: 164 us -> 142 us (0.87)
  starting transfers between devices: 78.3 us -> 60.4 us
  local copies, waits for them, and re-layouts: 15.1 us -> 9.25 us
  waiting for transfers between devices: 39.4 us -> 36.1 us
  other arithmetic: 3.39 us -> 6.34 us
  Pallas kernels: 27 us -> 28.8 us
    ppermute x22, starting transfers between devices: 53 us -> 37 us  [the longest x14 28.8 us: pass_on(): return lax.ppermute(piece, ('seq', 'head'), ring)]
    unnamed x48 -> x52, local copies, waits for them, and re-layouts: 12.8 us -> 6.89 us
    ppermute x22, waiting for transfers between devices: 34.1 us -> 30.4 us  [the longest x14 26.6 us: pass_on(): return lax.ppermute(piece, ('seq', 'head'), ring)]
    pallas_call x3, Pallas kernels: 22.4 us -> 24.5 us  [product(): pl.pallas_call(functools.partial(product_kernel, parts), out_shape=[jax.S...]
    concatenate x6, other arithmetic: 2.01 us -> 4.12 us  [gather(): streams = [jnp.concatenate(pair, axis=0) for pair in zip(streams, got)]]
    ppermute x3, starting transfers between devices: 7.29 us -> 5.47 us  [local(): rows = [lax.ppermute(row, 'seq', shift_y(k)) for k in range(1, Y)]]
  transfers between devices with their start and end apart: 32 -> 32, of which waited for: 16 -> 17; matrix products, arithmetic and copies ran while one was open for 2% -> 4% of each run, Pallas kernels for 12% -> 7%
where the time goes in v3:
time: 142 us; the launch traced here: 141 us
  starting transfers between devices  60.4 us (43%)
  waiting for transfers between devices  36.1 us (25%)
  Pallas kernels  28.8 us (20%)
  local copies, waits for them, and re-layouts  9.25 us (7%)
  other arithmetic  6.34 us (4%)
    ppermute x14, starting transfers between devices, pass_on(): return lax.ppermute(piece, ('seq', 'head'), ring)  28.8 us
    ppermute x14, waiting for transfers between devices, pass_on(): return lax.ppermute(piece, ('seq', 'head'), ring)  26.6 us
    pallas_call x3, Pallas kernels, product(): pl.pallas_call(functools.partial(product_kernel, parts), out_shape=[jax.S...  24.5 us
    ppermute x1, starting transfers between devices, local(): kv_got = lax.ppermute(kv_theirs, 'seq', SWAP)  11.5 us
    ppermute x8, starting transfers between devices, gather(): lax.ppermute(streams[j], 'seq', cube_pairs(j, step))  8.28 us
    unnamed x52, local copies, waits for them, and re-layouts  6.89 us
    ppermute x3, starting transfers between devices, local(): rows = [lax.ppermute(row, 'seq', shift_y(k)) for k in range(1, Y)]  5.47 us
    ppermute x3, waiting for transfers between devices, local(): got = lax.ppermute(total, 'seq', spin_x(k)).astype(F32)  5.44 us
  transfers between devices with their start and end apart: 32, of which 17 were waited for; matrix products, arithmetic and copies ran while one was open for 4% of the time, Pallas kernels for 7%

profile of v3, /device:TPU:1, one launch (start us, length us, event | category | flops | bytes accessed | tf_op | source)
XLA Modules:
  0.0 141.2 jit_solution(13202358135237634425)
XLA Ops:
  0.0 1.5 %fusion.3 = (bf16[512,192]{1,0:T(8,128)(2,1)S(1)}, bf16[512,192]{1,0:T(8,128)(2,1)S(1)}, bf16[512,192]{1,0:T(8,128)(2,1)S(1)}, bf16[512,192]{1,0:T(8,128)(2,1)S(1)}) fusion(bf16[512,768]{1,0:T(8,128)(2,1)} %param.6), kind=kLoop, calls=%fused_computation.26 | loop fusion | bytes 1572864 | tf_op jit(solution)/shard_map/slice | solution.py:272
  1.6 0.3 broadcast_select_fusion
  1.9 3.3 %collective-permute-start = (bf16[512,384]{1,0:T(8,128)(2,1)S(1)}, bf16[512,384]{1,0:T(8,128)(2,1)S(1)}, u32[]{:S(2)}, u32[]{:S(2)}) collective-permute-start(bf16[512,384]{1,0:T(8,128)(2,1)S(1)} %get-tuple-element.23), channel_id=1, source_target_pairs={{0,8},{8,0},{16,24},{24,16},{32,40},{40,32},{48,56},{56,48},{64,72... | collective-permute-start | bytes 1179656 | tf_op jit(solution)/shard_map/ppermute | solution.py:275
  5.3 1.1 collective-permute-start.19
  6.4 5.6 %collective-permute-start.1 = (bf16[512,384]{1,0:T(8,128)(2,1)S(1)}, bf16[512,384]{1,0:T(8,128)(2,1)S(1)}, u32[]{:S(2)}, u32[]{:S(2)}) collective-permute-start(bf16[512,384]{1,0:T(8,128)(2,1)S(1)} %get-tuple-element.24.refs_0_), channel_id=1, source_target_pairs={{0,1},{1,2},{2,3},{3,4},{4,5},{5,6},{6,7},{7,0},{8,15},{9,8},{10,9... | collective-permute-start | bytes 1179656 | tf_op jit(solution)/shard_map/ppermute | solution.py:279
  12.0 0.1 collective-permute-start.15
  12.1 0.8 collective-permute-start.2
  13.0 1.3 collective-permute-start.20
  14.3 2.4 %collective-permute-done.1.piece = bf16[512,384]{1,0:T(8,128)(2,1)S(1)} collective-permute-done((bf16[512,384]{1,0:T(8,128)(2,1)S(1)}, bf16[512,384]{1,0:T(8,128)(2,1)S(1)}, u32[]{:S(2)}, u32[]{:S(2)}) %collective-permute-start.1) | collective-permute-done | bytes 393248 | tf_op jit(solution)/shard_map/ppermute | solution.py:279
  16.7 3.1 %collective-permute-start.3 = (bf16[512,384]{1,0:T(8,128)(2,1)S(1)}, bf16[512,384]{1,0:T(8,128)(2,1)S(1)}, u32[]{:S(2)}, u32[]{:S(2)}) collective-permute-start(bf16[512,384]{1,0:T(8,128)(2,1)S(1)} %shard_map.64.refs_2_), channel_id=1, source_target_pairs={{0,1},{1,2},{2,3},{3,4},{4,5},{5,6},{6,7},{7,0},{8,15},{9,8},{10,9... | collective-permute-start | bytes 1179656 | tf_op jit(solution)/shard_map/ppermute | solution.py:279
  19.9 2.6 %collective-permute-start.16 = (bf16[384,768]{1,0:T(8,128)(2,1)S(1)}, bf16[384,768]{1,0:T(8,128)(2,1)S(1)}, u32[]{:S(2)}, u32[]{:S(2)}) collective-permute-start(bf16[384,768]{1,0:T(8,128)(2,1)S(1)} %pad_maximum_fusion.4), channel_id=1, source_target_pairs={{0,64},{8,56},{16,80},{24,40},{32,96},{40,24},{48,112},{56,8},{64,... | collective-permute-start | bytes 1769480 | tf_op jit(solution)/shard_map/ppermute | solution.py:294
  22.5 1.9 %collective-permute-start.4 = (bf16[512,384]{1,0:T(8,128)(2,1)S(1)}, bf16[512,384]{1,0:T(8,128)(2,1)S(1)}, u32[]{:S(2)}, u32[]{:S(2)}) collective-permute-start(bf16[512,384]{1,0:T(8,128)(2,1)S(1)} %shard_map.65.refs_3_), channel_id=1, source_target_pairs={{0,1},{1,2},{2,3},{3,4},{4,5},{5,6},{6,7},{7,0},{8,15},{9,8},{10,9... | collective-permute-start | bytes 1179656 | tf_op jit(solution)/shard_map/ppermute | solution.py:279
  24.5 0.6 collective-permute-done.3.piece
  25.2 3.1 %collective-permute-start.5 = (bf16[512,384]{1,0:T(8,128)(2,1)S(1)}, bf16[512,384]{1,0:T(8,128)(2,1)S(1)}, u32[]{:S(2)}, u32[]{:S(2)}) collective-permute-start(bf16[512,384]{1,0:T(8,128)(2,1)S(1)} %shard_map.66.refs_4_), channel_id=1, source_target_pairs={{0,1},{1,2},{2,3},{3,4},{4,5},{5,6},{6,7},{7,0},{8,15},{9,8},{10,9... | collective-permute-start | bytes 1179656 | tf_op jit(solution)/shard_map/ppermute | solution.py:279
  28.3 1.9 %collective-permute-done.16 = bf16[384,768]{1,0:T(8,128)(2,1)S(1)} collective-permute-done((bf16[384,768]{1,0:T(8,128)(2,1)S(1)}, bf16[384,768]{1,0:T(8,128)(2,1)S(1)}, u32[]{:S(2)}, u32[]{:S(2)}) %collective-permute-start.16) | collective-permute-done | bytes 589856 | tf_op jit(solution)/shard_map/ppermute | solution.py:294
  30.3 0.4 collective-permute-start.17
  30.7 1.8 %collective-permute-start.6 = (bf16[512,384]{1,0:T(8,128)(2,1)S(1)}, bf16[512,384]{1,0:T(8,128)(2,1)S(1)}, u32[]{:S(2)}, u32[]{:S(2)}) collective-permute-start(bf16[512,384]{1,0:T(8,128)(2,1)S(1)} %shard_map.67.refs_5_), channel_id=1, source_target_pairs={{0,1},{1,2},{2,3},{3,4},{4,5},{5,6},{6,7},{7,0},{8,15},{9,8},{10,9... | collective-permute-start | bytes 1179656 | tf_op jit(solution)/shard_map/ppermute | solution.py:279
  32.5 1.2 collective-permute-done.5.piece
  33.7 3.0 %collective-permute-start.7 = (bf16[512,384]{1,0:T(8,128)(2,1)S(1)}, bf16[512,384]{1,0:T(8,128)(2,1)S(1)}, u32[]{:S(2)}, u32[]{:S(2)}) collective-permute-start(bf16[512,384]{1,0:T(8,128)(2,1)S(1)} %shard_map.68.refs_6_), channel_id=1, source_target_pairs={{0,1},{1,2},{2,3},{3,4},{4,5},{5,6},{6,7},{7,0},{8,15},{9,8},{10,9... | collective-permute-start | bytes 1179656 | tf_op jit(solution)/shard_map/ppermute | solution.py:279
  36.7 1.2 collective-permute-done.6.piece
  37.9 3.3 %collective-permute-start.8 = (bf16[512,384]{1,0:T(8,128)(2,1)S(1)}, bf16[512,384]{1,0:T(8,128)(2,1)S(1)}, u32[]{:S(2)}, u32[]{:S(2)}) collective-permute-start(bf16[512,384]{1,0:T(8,128)(2,1)S(1)} %shard_map.69.refs_7_), channel_id=1, source_target_pairs={{0,1},{1,2},{2,3},{3,4},{4,5},{5,6},{6,7},{7,0},{8,15},{9,8},{10,9... | collective-permute-start | bytes 1179656 | tf_op jit(solution)/shard_map/ppermute | solution.py:279
  41.2 1.3 pad_maximum_fusion.1.refs_18_
  42.5 2.7 %collective-permute-start.22 = (bf16[1536,768]{1,0:T(8,128)(2,1)S(1)}, bf16[1536,768]{1,0:T(8,128)(2,1)}, u32[]{:S(2)}, u32[]{:S(2)}) collective-permute-start(bf16[1536,768]{1,0:T(8,128)(2,1)S(1)} %pad_maximum_fusion.1.refs_18_), channel_id=1, source_target_pairs={{0,64},{8,56},{16,80},{24,40},{32,96},{40,24},{48,112},{56,8},{64,... | collective-permute-start | bytes 7077896 | tf_op jit(solution)/shard_map/ppermute | solution.py:294
  45.3 1.7 %collective-permute-done.17 = bf16[768,768]{1,0:T(8,128)(2,1)S(1)} collective-permute-done((bf16[768,768]{1,0:T(8,128)(2,1)S(1)}, bf16[768,768]{1,0:T(8,128)(2,1)S(1)}, u32[]{:S(2)}, u32[]{:S(2)}) %collective-permute-start.17) | collective-permute-done | bytes 1179680 | tf_op jit(solution)/shard_map/ppermute | solution.py:294
  47.0 2.6 %pad_maximum_fusion.refs_16_ = bf16[1536,768]{1,0:T(8,128)(2,1)} fusion(bf16[768,768]{1,0:T(8,128)(2,1)S(1)} %collective-permute-done.17, bf16[384,768]{1,0:T(8,128)(2,1)S(1)} %collective-permute-done.16, bf16[192,768]{1,0:T(8,128)(2,1)S(1)} %collective-permute-done.15, bf16[192,256]{1,0:T(8,128)(2,1)S(1)} %get-tuple-element.38, ...), kind=kLoop, calls=%fused_computation | loop fusion | flops 14155776 | bytes 4718592 | tf_op jit(solution)/shard_map/concatenate | solution.py:293
  49.7 1.5 %collective-permute-start.10 = (bf16[512,384]{1,0:T(8,128)(2,1)S(1)}, bf16[512,384]{1,0:T(8,128)(2,1)}, u32[]{:S(2)}, u32[]{:S(2)}) collective-permute-start(bf16[512,384]{1,0:T(8,128)(2,1)S(1)} %shard_map.71.refs_9_), channel_id=1, source_target_pairs={{0,1},{1,2},{2,3},{3,4},{4,5},{5,6},{6,7},{7,0},{8,15},{9,8},{10,9... | collective-permute-start | bytes 1179656 | tf_op jit(solution)/shard_map/ppermute | solution.py:279
  51.1 5.5 %collective-permute-done.9.piece = bf16[512,384]{1,0:T(8,128)(2,1)} collective-permute-done((bf16[512,384]{1,0:T(8,128)(2,1)S(1)}, bf16[512,384]{1,0:T(8,128)(2,1)}, u32[]{:S(2)}, u32[]{:S(2)}) %collective-permute-start.9) | collective-permute-done | bytes 393248 | tf_op jit(solution)/shard_map/ppermute | solution.py:279
  56.7 0.9 collective-permute-start.11
  57.6 3.3 %collective-permute-done.10.piece = bf16[512,384]{1,0:T(8,128)(2,1)} collective-permute-done((bf16[512,384]{1,0:T(8,128)(2,1)S(1)}, bf16[512,384]{1,0:T(8,128)(2,1)}, u32[]{:S(2)}, u32[]{:S(2)}) %collective-permute-start.10) | collective-permute-done | bytes 393248 | tf_op jit(solution)/shard_map/ppermute | solution.py:279
  60.9 1.2 collective-permute-start.12
  62.1 3.0 %collective-permute-done.11.piece = bf16[512,384]{1,0:T(8,128)(2,1)} collective-permute-done((bf16[512,384]{1,0:T(8,128)(2,1)}, bf16[512,384]{1,0:T(8,128)(2,1)}, u32[]{:S(2)}, u32[]{:S(2)}) %collective-permute-start.11) | collective-permute-done | bytes 393248 | tf_op jit(solution)/shard_map/ppermute | solution.py:279
  65.1 1.2 collective-permute-start.13
  66.3 3.0 %collective-permute-done.12.piece = bf16[512,384]{1,0:T(8,128)(2,1)} collective-permute-done((bf16[512,384]{1,0:T(8,128)(2,1)}, bf16[512,384]{1,0:T(8,128)(2,1)}, u32[]{:S(2)}, u32[]{:S(2)}) %collective-permute-start.12) | collective-permute-done | bytes 393248 | tf_op jit(solution)/shard_map/ppermute | solution.py:279
  69.3 1.2 collective-permute-start.14
  70.5 0.7 dynamic-slice_bitcast_fusion
  71.3 2.2 %collective-permute-done.13.piece = bf16[512,384]{1,0:T(8,128)(2,1)S(1)} collective-permute-done((bf16[512,384]{1,0:T(8,128)(2,1)}, bf16[512,384]{1,0:T(8,128)(2,1)S(1)}, u32[]{:S(2)}, u32[]{:S(2)}) %collective-permute-start.13) | collective-permute-done | bytes 393248 | tf_op jit(solution)/shard_map/ppermute | solution.py:279
  73.6 4.2 %collective-permute-done.14.piece = bf16[512,384]{1,0:T(8,128)(2,1)S(1)} collective-permute-done((bf16[512,384]{1,0:T(8,128)(2,1)}, bf16[512,384]{1,0:T(8,128)(2,1)S(1)}, u32[]{:S(2)}, u32[]{:S(2)}) %collective-permute-start.14) | collective-permute-done | bytes 393248 | tf_op jit(solution)/shard_map/ppermute | solution.py:279
  77.7 0.1 collective-permute-done.18.refs_17_
  77.9 7.7 %shard_map.79 = bf16[1024,512]{1,0:T(8,128)(2,1)S(1)} custom-call(s32[33]{0:T(128)S(1)} %pad_add_fusion.info, bf16[512,384]{1,0:T(8,128)(2,1)S(1)} %get-tuple-element.24.refs_0_, bf16[512,384]{1,0:T(8,128)(2,1)S(1)} %collective-permute-done.refs_1_, bf16[512,384]{1,0:T(8,128)(2,1)S(1)} %copy-done.9, bf16[512,384]{1,0:T(8,128)(2,1)S(1)} %copy-done.3, ...), custom_call_target="tpu_custom_call" | custom-call | flops 3221225472 | bytes 16777216 | tf_op jit(solution)/shard_map/pallas_call | solution.py:136
  85.6 11.5 %collective-permute-start.23 = (bf16[1024,512]{1,0:T(8,128)(2,1)S(1)}, bf16[1024,512]{1,0:T(8,128)(2,1)S(1)}, u32[]{:S(2)}, u32[]{:S(2)}) collective-permute-start(bf16[1024,512]{1,0:T(8,128)(2,1)S(1)} %shard_map.79), channel_id=1, source_target_pairs={{0,8},{8,0},{16,24},{24,16},{32,40},{40,32},{48,56},{56,48},{64,72... | collective-permute-start | bytes 3145736 | tf_op jit(solution)/shard_map/ppermute | solution.py:318
  97.1 7.9 %shard_map.78.mine = f32[1024,512]{1,0:T(8,128)S(1)} custom-call(s32[33]{0:T(128)S(1)} %pad_add_fusion.info, bf16[512,384]{1,0:T(8,128)(2,1)S(1)} %get-tuple-element.24.refs_0_, bf16[512,384]{1,0:T(8,128)(2,1)S(1)} %collective-permute-done.refs_1_, bf16[512,384]{1,0:T(8,128)(2,1)S(1)} %copy-done.9, bf16[512,384]{1,0:T(8,128)(2,1)S(1)} %copy-done.3, ...), custom_call_target="tpu_custom_call" | custom-call | flops 3221225472 | bytes 16777216 | tf_op jit(solution)/shard_map/pallas_call | solution.py:136
  105.0 1.5 %shard_map.80 = (bf16[1024,256]{1,0:T(8,128)(2,1)S(1)}, bf16[1024,256]{1,0:T(8,128)(2,1)S(1)}, f32[4,2,128,128]{3,2,1,0:T(8,128)S(1)}, bf16[2,128,128]{2,1,0:T(8,128)(2,1)}) custom-call(f32[1024,512]{1,0:T(8,128)S(1)} %shard_map.78.mine, bf16[1024,512]{1,0:T(8,128)(2,1)S(1)} %collective-permute-done.23.other), custom_call_target="tpu_custom_call" | custom-call | flops 67108864 | bytes 5242880 | tf_op jit(solution)/shard_map/pallas_call | solution.py:171
  106.4 0.8 copy-done.14
  107.3 0.8 copy-done.18
  108.1 0.8 copy-done.20
  108.9 9.0 %shard_map.81 = (bf16[1024,256]{1,0:T(8,128)(2,1)}, f32[1024,256]{1,0:T(8,128)S(1)}) custom-call(s32[33]{0:T(128)S(1)} %pad_add_fusion.info, bf16[512,384]{1,0:T(8,128)(2,1)S(1)} %get-tuple-element.24.refs_0_, bf16[512,384]{1,0:T(8,128)(2,1)S(1)} %collective-permute-done.refs_1_, bf16[512,384]{1,0:T(8,128)(2,1)S(1)} %copy-done.9, ...), custom_call_target="tpu_custom_call" | custom-call | flops 3221225472 | bytes 16777216 | tf_op jit(solution)/shard_map/pallas_call | solution.py:136
  117.9 1.0 copy-done.16
  119.0 1.4 collective-permute-start.25
  120.4 1.9 %collective-permute-done.27 = bf16[2,128,128]{2,1,0:T(8,128)(2,1)S(1)} collective-permute-done((bf16[2,128,128]{2,1,0:T(8,128)(2,1)}, bf16[2,128,128]{2,1,0:T(8,128)(2,1)S(1)}, u32[]{:S(2)}, u32[]{:S(2)}) %collective-permute-start.27) | collective-permute-done | bytes 65568 | tf_op jit(solution)/shard_map/ppermute | solution.py:325
  122.3 1.6 %collective-permute-done.26 = bf16[2,128,128]{2,1,0:T(8,128)(2,1)S(1)} collective-permute-done((bf16[2,128,128]{2,1,0:T(8,128)(2,1)}, bf16[2,128,128]{2,1,0:T(8,128)(2,1)S(1)}, u32[]{:S(2)}, u32[]{:S(2)}) %collective-permute-start.26) | collective-permute-done | bytes 65568 | tf_op jit(solution)/shard_map/ppermute | solution.py:325
  123.9 2.0 %collective-permute-done.25 = bf16[2,128,128]{2,1,0:T(8,128)(2,1)S(1)} collective-permute-done((bf16[2,128,128]{2,1,0:T(8,128)(2,1)}, bf16[2,128,128]{2,1,0:T(8,128)(2,1)S(1)}, u32[]{:S(2)}, u32[]{:S(2)}) %collective-permute-start.25) | collective-permute-done | bytes 65568 | tf_op jit(solution)/shard_map/ppermute | solution.py:325
  125.9 0.9 fusion.2
  126.8 1.7 %collective-permute-start.30 = (bf16[2,128,128]{2,1,0:T(8,128)(2,1)S(1)}, bf16[2,128,128]{2,1,0:T(8,128)(2,1)S(1)}, u32[]{:S(2)}, u32[]{:S(2)}) collective-permute-start(bf16[2,128,128]{2,1,0:T(8,128)(2,1)S(1)} %get-tuple-element.31), channel_id=1, source_target_pairs={{0,192},{8,200},{16,208},{24,216},{32,224},{40,232},{48,240},{56,2... | collective-permute-start | bytes 196616 | tf_op jit(solution)/shard_map/ppermute | solution.py:329
  128.5 1.3 collective-permute-start.29
  129.8 2.5 %collective-permute-start.28 = (bf16[2,128,128]{2,1,0:T(8,128)(2,1)S(1)}, bf16[2,128,128]{2,1,0:T(8,128)(2,1)S(1)}, u32[]{:S(2)}, u32[]{:S(2)}) collective-permute-start(bf16[2,128,128]{2,1,0:T(8,128)(2,1)S(1)} %get-tuple-element.31), channel_id=1, source_target_pairs={{0,64},{8,72},{16,80},{24,88},{32,96},{40,104},{48,112},{56,120},{... | collective-permute-start | bytes 196616 | tf_op jit(solution)/shard_map/ppermute | solution.py:329
  132.4 1.2 copy-done.17
  133.6 1.0 copy-done.19
  134.6 1.0 copy-done.21
  135.7 0.9 shard_map.82
  136.7 0.9 shard_map.84
  137.6 1.6 %collective-permute-start.31 = (bf16[512,256]{1,0:T(8,128)(2,1)S(1)}, bf16[512,256]{1,0:T(8,128)(2,1)S(1)}, u32[]{:S(2)}, u32[]{:S(2)}) collective-permute-start(bf16[512,256]{1,0:T(8,128)(2,1)S(1)} %shard_map.84), channel_id=1, source_target_pairs={{0,8},{8,0},{16,24},{24,16},{32,40},{40,32},{48,56},{56,48},{64,72... | collective-permute-start | bytes 786440 | tf_op jit(solution)/shard_map/ppermute | solution.py:339
  139.2 0.9 shard_map.83
  140.1 0.2 collective-permute-done.31
  140.4 0.8 pad_maximum_fusion.6
  (91 shorter events, 0.9 us)
Async XLA Ops:
  0.0 5.2 %copy-start.22 = (bf16[192,512]{1,0:T(8,128)(2,1)S(1)}, bf16[192,512]{1,0:T(8,128)(2,1)}, u32[]{:S(2)}) copy-start(bf16[192,512]{1,0:T(8,128)(2,1)} %param.7) | copy-start | bytes 589828
  0.0 5.2 %copy-start.24 = (bf16[192,512]{1,0:T(8,128)(2,1)S(1)}, bf16[192,512]{1,0:T(8,128)(2,1)}, u32[]{:S(2)}) copy-start(bf16[192,512]{1,0:T(8,128)(2,1)} %param.9) | copy-start | bytes 589828
  0.0 5.2 %copy-start.23 = (bf16[192,512]{1,0:T(8,128)(2,1)S(1)}, bf16[192,512]{1,0:T(8,128)(2,1)}, u32[]{:S(2)}) copy-start(bf16[192,512]{1,0:T(8,128)(2,1)} %param.8) | copy-start | bytes 589828
  1.9 10.2 %collective-permute-start = (bf16[512,384]{1,0:T(8,128)(2,1)S(1)}, bf16[512,384]{1,0:T(8,128)(2,1)S(1)}, u32[]{:S(2)}, u32[]{:S(2)}) collective-permute-start(bf16[512,384]{1,0:T(8,128)(2,1)S(1)} %get-tuple-element.23), channel_id=1, source_target_pairs={{0,8},{8,0},{16,24},{24,16},{32,40},{40,32},{48,56},{56,48},{64,72... | collective-permute-start | bytes 1179656 | tf_op jit(solution)/shard_map/ppermute | solution.py:275
  5.3 7.6 %collective-permute-start.19 = (bf16[192,768]{1,0:T(8,128)(2,1)S(1)}, bf16[192,768]{1,0:T(8,128)(2,1)S(1)}, u32[]{:S(2)}, u32[]{:S(2)}) collective-permute-start(bf16[192,768]{1,0:T(8,128)(2,1)S(1)} %pad_maximum_fusion.10), channel_id=1, source_target_pairs={{0,48},{8,200},{16,32},{24,216},{32,16},{40,232},{48,0},{56,248},{... | collective-permute-start | bytes 884744 | tf_op jit(solution)/shard_map/ppermute | solution.py:294
  6.4 10.3 %collective-permute-start.1 = (bf16[512,384]{1,0:T(8,128)(2,1)S(1)}, bf16[512,384]{1,0:T(8,128)(2,1)S(1)}, u32[]{:S(2)}, u32[]{:S(2)}) collective-permute-start(bf16[512,384]{1,0:T(8,128)(2,1)S(1)} %get-tuple-element.24.refs_0_), channel_id=1, source_target_pairs={{0,1},{1,2},{2,3},{3,4},{4,5},{5,6},{6,7},{7,0},{8,15},{9,8},{10,9... | collective-permute-start | bytes 1179656 | tf_op jit(solution)/shard_map/ppermute | solution.py:279
  12.0 7.8 %collective-permute-start.15 = (bf16[192,768]{1,0:T(8,128)(2,1)S(1)}, bf16[192,768]{1,0:T(8,128)(2,1)S(1)}, u32[]{:S(2)}, u32[]{:S(2)}) collective-permute-start(bf16[192,768]{1,0:T(8,128)(2,1)S(1)} %pad_maximum_fusion.9), channel_id=1, source_target_pairs={{0,16},{8,72},{16,0},{24,88},{32,48},{40,104},{48,32},{56,120},{64... | collective-permute-start | bytes 884744 | tf_op jit(solution)/shard_map/ppermute | solution.py:294
  12.1 10.3 %collective-permute-start.2 = (bf16[512,384]{1,0:T(8,128)(2,1)S(1)}, bf16[512,384]{1,0:T(8,128)(2,1)S(1)}, u32[]{:S(2)}, u32[]{:S(2)}) collective-permute-start(bf16[512,384]{1,0:T(8,128)(2,1)S(1)} %collective-permute-done.refs_1_), channel_id=1, source_target_pairs={{0,1},{1,2},{2,3},{3,4},{4,5},{5,6},{6,7},{7,0},{8,15},{9,8},{10,9... | collective-permute-start | bytes 1179656 | tf_op jit(solution)/shard_map/ppermute | solution.py:279
  13.0 11.4 %collective-permute-start.20 = (bf16[384,768]{1,0:T(8,128)(2,1)S(1)}, bf16[384,768]{1,0:T(8,128)(2,1)S(1)}, u32[]{:S(2)}, u32[]{:S(2)}) collective-permute-start(bf16[384,768]{1,0:T(8,128)(2,1)S(1)} %pad_maximum_fusion.5), channel_id=1, source_target_pairs={{0,192},{8,24},{16,208},{24,8},{32,224},{40,56},{48,240},{56,40},{... | collective-permute-start | bytes 1769480 | tf_op jit(solution)/shard_map/ppermute | solution.py:294
  16.7 5.7 %copy-start.8 = (bf16[512,384]{1,0:T(8,128)(2,1)}, bf16[512,384]{1,0:T(8,128)(2,1)S(1)}, u32[]{:S(2)}) copy-start(bf16[512,384]{1,0:T(8,128)(2,1)S(1)} %shard_map.64.refs_2_) | copy-start | bytes 1179652
  16.7 8.4 %collective-permute-start.3 = (bf16[512,384]{1,0:T(8,128)(2,1)S(1)}, bf16[512,384]{1,0:T(8,128)(2,1)S(1)}, u32[]{:S(2)}, u32[]{:S(2)}) collective-permute-start(bf16[512,384]{1,0:T(8,128)(2,1)S(1)} %shard_map.64.refs_2_), channel_id=1, source_target_pairs={{0,1},{1,2},{2,3},{3,4},{4,5},{5,6},{6,7},{7,0},{8,15},{9,8},{10,9... | collective-permute-start | bytes 1179656 | tf_op jit(solution)/shard_map/ppermute | solution.py:279
  19.9 10.3 %collective-permute-start.16 = (bf16[384,768]{1,0:T(8,128)(2,1)S(1)}, bf16[384,768]{1,0:T(8,128)(2,1)S(1)}, u32[]{:S(2)}, u32[]{:S(2)}) collective-permute-start(bf16[384,768]{1,0:T(8,128)(2,1)S(1)} %pad_maximum_fusion.4), channel_id=1, source_target_pairs={{0,64},{8,56},{16,80},{24,40},{32,96},{40,24},{48,112},{56,8},{64,... | collective-permute-start | bytes 1769480 | tf_op jit(solution)/shard_map/ppermute | solution.py:294
  22.5 2.7 %copy-start.2 = (bf16[512,384]{1,0:T(8,128)(2,1)}, bf16[512,384]{1,0:T(8,128)(2,1)S(1)}, u32[]{:S(2)}) copy-start(bf16[512,384]{1,0:T(8,128)(2,1)S(1)} %shard_map.65.refs_3_) | copy-start | bytes 1179652
  22.5 8.2 %collective-permute-start.4 = (bf16[512,384]{1,0:T(8,128)(2,1)S(1)}, bf16[512,384]{1,0:T(8,128)(2,1)S(1)}, u32[]{:S(2)}, u32[]{:S(2)}) collective-permute-start(bf16[512,384]{1,0:T(8,128)(2,1)S(1)} %shard_map.65.refs_3_), channel_id=1, source_target_pairs={{0,1},{1,2},{2,3},{3,4},{4,5},{5,6},{6,7},{7,0},{8,15},{9,8},{10,9... | collective-permute-start | bytes 1179656 | tf_op jit(solution)/shard_map/ppermute | solution.py:279
  24.4 16.8 %collective-permute-start.21 = (bf16[768,768]{1,0:T(8,128)(2,1)S(1)}, bf16[768,768]{1,0:T(8,128)(2,1)S(1)}, u32[]{:S(2)}, u32[]{:S(2)}) collective-permute-start(bf16[768,768]{1,0:T(8,128)(2,1)S(1)} %pad_maximum_fusion.3), channel_id=1, source_target_pairs={{0,16},{8,72},{16,0},{24,88},{32,48},{40,104},{48,32},{56,120},{64... | collective-permute-start | bytes 3538952 | tf_op jit(solution)/shard_map/ppermute | solution.py:294
  25.2 5.5 %copy-start.4 = (bf16[512,384]{1,0:T(8,128)(2,1)}, bf16[512,384]{1,0:T(8,128)(2,1)S(1)}, u32[]{:S(2)}) copy-start(bf16[512,384]{1,0:T(8,128)(2,1)S(1)} %shard_map.66.refs_4_) | copy-start | bytes 1179652
  25.2 8.5 %collective-permute-start.5 = (bf16[512,384]{1,0:T(8,128)(2,1)S(1)}, bf16[512,384]{1,0:T(8,128)(2,1)S(1)}, u32[]{:S(2)}, u32[]{:S(2)}) collective-permute-start(bf16[512,384]{1,0:T(8,128)(2,1)S(1)} %shard_map.66.refs_4_), channel_id=1, source_target_pairs={{0,1},{1,2},{2,3},{3,4},{4,5},{5,6},{6,7},{7,0},{8,15},{9,8},{10,9... | collective-permute-start | bytes 1179656 | tf_op jit(solution)/shard_map/ppermute | solution.py:279
  30.3 16.6 %collective-permute-start.17 = (bf16[768,768]{1,0:T(8,128)(2,1)S(1)}, bf16[768,768]{1,0:T(8,128)(2,1)S(1)}, u32[]{:S(2)}, u32[]{:S(2)}) collective-permute-start(bf16[768,768]{1,0:T(8,128)(2,1)S(1)} %pad_maximum_fusion.2), channel_id=1, source_target_pairs={{0,48},{8,200},{16,32},{24,216},{32,16},{40,232},{48,0},{56,248},{... | collective-permute-start | bytes 3538952 | tf_op jit(solution)/shard_map/ppermute | solution.py:294
  30.7 3.0 %copy-start.6 = (bf16[512,384]{1,0:T(8,128)(2,1)}, bf16[512,384]{1,0:T(8,128)(2,1)S(1)}, u32[]{:S(2)}) copy-start(bf16[512,384]{1,0:T(8,128)(2,1)S(1)} %shard_map.67.refs_5_) | copy-start | bytes 1179652
  30.7 7.2 %collective-permute-start.6 = (bf16[512,384]{1,0:T(8,128)(2,1)S(1)}, bf16[512,384]{1,0:T(8,128)(2,1)S(1)}, u32[]{:S(2)}, u32[]{:S(2)}) collective-permute-start(bf16[512,384]{1,0:T(8,128)(2,1)S(1)} %shard_map.67.refs_5_), channel_id=1, source_target_pairs={{0,1},{1,2},{2,3},{3,4},{4,5},{5,6},{6,7},{7,0},{8,15},{9,8},{10,9... | collective-permute-start | bytes 1179656 | tf_op jit(solution)/shard_map/ppermute | solution.py:279
  33.7 4.2 %copy-start.10 = (bf16[512,384]{1,0:T(8,128)(2,1)}, bf16[512,384]{1,0:T(8,128)(2,1)S(1)}, u32[]{:S(2)}) copy-start(bf16[512,384]{1,0:T(8,128)(2,1)S(1)} %shard_map.68.refs_6_) | copy-start | bytes 1179652
  33.7 15.9 %collective-permute-start.7 = (bf16[512,384]{1,0:T(8,128)(2,1)S(1)}, bf16[512,384]{1,0:T(8,128)(2,1)S(1)}, u32[]{:S(2)}, u32[]{:S(2)}) collective-permute-start(bf16[512,384]{1,0:T(8,128)(2,1)S(1)} %shard_map.68.refs_6_), channel_id=1, source_target_pairs={{0,1},{1,2},{2,3},{3,4},{4,5},{5,6},{6,7},{7,0},{8,15},{9,8},{10,9... | collective-permute-start | bytes 1179656 | tf_op jit(solution)/shard_map/ppermute | solution.py:279
  37.9 4.6 %copy-start.12 = (bf16[512,384]{1,0:T(8,128)(2,1)}, bf16[512,384]{1,0:T(8,128)(2,1)S(1)}, u32[]{:S(2)}) copy-start(bf16[512,384]{1,0:T(8,128)(2,1)S(1)} %shard_map.69.refs_7_) | copy-start | bytes 1179652
  37.9 11.7 %collective-permute-start.8 = (bf16[512,384]{1,0:T(8,128)(2,1)S(1)}, bf16[512,384]{1,0:T(8,128)(2,1)S(1)}, u32[]{:S(2)}, u32[]{:S(2)}) collective-permute-start(bf16[512,384]{1,0:T(8,128)(2,1)S(1)} %shard_map.69.refs_7_), channel_id=1, source_target_pairs={{0,1},{1,2},{2,3},{3,4},{4,5},{5,6},{6,7},{7,0},{8,15},{9,8},{10,9... | collective-permute-start | bytes 1179656 | tf_op jit(solution)/shard_map/ppermute | solution.py:279
  42.5 35.2 %collective-permute-start.22 = (bf16[1536,768]{1,0:T(8,128)(2,1)S(1)}, bf16[1536,768]{1,0:T(8,128)(2,1)}, u32[]{:S(2)}, u32[]{:S(2)}) collective-permute-start(bf16[1536,768]{1,0:T(8,128)(2,1)S(1)} %pad_maximum_fusion.1.refs_18_), channel_id=1, source_target_pairs={{0,64},{8,56},{16,80},{24,40},{32,96},{40,24},{48,112},{56,8},{64,... | collective-permute-start | bytes 7077896 | tf_op jit(solution)/shard_map/ppermute | solution.py:294
  49.6 28.3 %collective-permute-start.18 = (bf16[1536,768]{1,0:T(8,128)(2,1)}, bf16[1536,768]{1,0:T(8,128)(2,1)}, u32[]{:S(2)}, u32[]{:S(2)}) collective-permute-start(bf16[1536,768]{1,0:T(8,128)(2,1)} %pad_maximum_fusion.refs_16_), channel_id=1, source_target_pairs={{0,192},{8,24},{16,208},{24,8},{32,224},{40,56},{48,240},{56,40},{... | collective-permute-start | bytes 7077896 | tf_op jit(solution)/shard_map/ppermute | solution.py:294
  49.6 7.1 %collective-permute-start.9 = (bf16[512,384]{1,0:T(8,128)(2,1)S(1)}, bf16[512,384]{1,0:T(8,128)(2,1)}, u32[]{:S(2)}, u32[]{:S(2)}) collective-permute-start(bf16[512,384]{1,0:T(8,128)(2,1)S(1)} %shard_map.70.refs_8_), channel_id=1, source_target_pairs={{0,1},{1,2},{2,3},{3,4},{4,5},{5,6},{6,7},{7,0},{8,15},{9,8},{10,9... | collective-permute-start | bytes 1179656 | tf_op jit(solution)/shard_map/ppermute | solution.py:279
  49.7 7.0 %copy-start = (bf16[512,384]{1,0:T(8,128)(2,1)}, bf16[512,384]{1,0:T(8,128)(2,1)S(1)}, u32[]{:S(2)}) copy-start(bf16[512,384]{1,0:T(8,128)(2,1)S(1)} %shard_map.71.refs_9_) | copy-start | bytes 1179652
  49.7 11.2 %collective-permute-start.10 = (bf16[512,384]{1,0:T(8,128)(2,1)S(1)}, bf16[512,384]{1,0:T(8,128)(2,1)}, u32[]{:S(2)}, u32[]{:S(2)}) collective-permute-start(bf16[512,384]{1,0:T(8,128)(2,1)S(1)} %shard_map.71.refs_9_), channel_id=1, source_target_pairs={{0,1},{1,2},{2,3},{3,4},{4,5},{5,6},{6,7},{7,0},{8,15},{9,8},{10,9... | collective-permute-start | bytes 1179656 | tf_op jit(solution)/shard_map/ppermute | solution.py:279
  56.7 8.4 %collective-permute-start.11 = (bf16[512,384]{1,0:T(8,128)(2,1)}, bf16[512,384]{1,0:T(8,128)(2,1)}, u32[]{:S(2)}, u32[]{:S(2)}) collective-permute-start(bf16[512,384]{1,0:T(8,128)(2,1)} %shard_map.72.refs_10_), channel_id=1, source_target_pairs={{0,1},{1,2},{2,3},{3,4},{4,5},{5,6},{6,7},{7,0},{8,15},{9,8},{10,9... | collective-permute-start | bytes 1179656 | tf_op jit(solution)/shard_map/ppermute | solution.py:279
  60.9 8.4 %collective-permute-start.12 = (bf16[512,384]{1,0:T(8,128)(2,1)}, bf16[512,384]{1,0:T(8,128)(2,1)}, u32[]{:S(2)}, u32[]{:S(2)}) collective-permute-start(bf16[512,384]{1,0:T(8,128)(2,1)} %shard_map.73.refs_11_), channel_id=1, source_target_pairs={{0,1},{1,2},{2,3},{3,4},{4,5},{5,6},{6,7},{7,0},{8,15},{9,8},{10,9... | collective-permute-start | bytes 1179656 | tf_op jit(solution)/shard_map/ppermute | solution.py:279
  65.1 8.4 %collective-permute-start.13 = (bf16[512,384]{1,0:T(8,128)(2,1)}, bf16[512,384]{1,0:T(8,128)(2,1)S(1)}, u32[]{:S(2)}, u32[]{:S(2)}) collective-permute-start(bf16[512,384]{1,0:T(8,128)(2,1)} %shard_map.74.refs_12_), channel_id=1, source_target_pairs={{0,1},{1,2},{2,3},{3,4},{4,5},{5,6},{6,7},{7,0},{8,15},{9,8},{10,9... | collective-permute-start | bytes 1179656 | tf_op jit(solution)/shard_map/ppermute | solution.py:279
  69.3 8.4 %collective-permute-start.14 = (bf16[512,384]{1,0:T(8,128)(2,1)}, bf16[512,384]{1,0:T(8,128)(2,1)S(1)}, u32[]{:S(2)}, u32[]{:S(2)}) collective-permute-start(bf16[512,384]{1,0:T(8,128)(2,1)} %shard_map.75.refs_13_), channel_id=1, source_target_pairs={{0,1},{1,2},{2,3},{3,4},{4,5},{5,6},{6,7},{7,0},{8,15},{9,8},{10,9... | collective-permute-start | bytes 1179656 | tf_op jit(solution)/shard_map/ppermute | solution.py:279
  73.5 4.3 %copy-start.1 = (bf16[512,384]{1,0:T(8,128)(2,1)S(1)}, bf16[512,384]{1,0:T(8,128)(2,1)}, u32[]{:S(2)}) copy-start(bf16[512,384]{1,0:T(8,128)(2,1)} %copy-done) | copy-start | bytes 1179652
  73.5 4.3 %copy-start.3 = (bf16[512,384]{1,0:T(8,128)(2,1)S(1)}, bf16[512,384]{1,0:T(8,128)(2,1)}, u32[]{:S(2)}) copy-start(bf16[512,384]{1,0:T(8,128)(2,1)} %copy-done.2) | copy-start | bytes 1179652
  73.5 4.3 %copy-start.5 = (bf16[512,384]{1,0:T(8,128)(2,1)S(1)}, bf16[512,384]{1,0:T(8,128)(2,1)}, u32[]{:S(2)}) copy-start(bf16[512,384]{1,0:T(8,128)(2,1)} %copy-done.4) | copy-start | bytes 1179652
  73.5 4.3 %copy-start.7 = (bf16[512,384]{1,0:T(8,128)(2,1)S(1)}, bf16[512,384]{1,0:T(8,128)(2,1)}, u32[]{:S(2)}) copy-start(bf16[512,384]{1,0:T(8,128)(2,1)} %copy-done.6) | copy-start | bytes 1179652
  73.5 4.4 %copy-start.9 = (bf16[512,384]{1,0:T(8,128)(2,1)S(1)}, bf16[512,384]{1,0:T(8,128)(2,1)}, u32[]{:S(2)}) copy-start(bf16[512,384]{1,0:T(8,128)(2,1)} %copy-done.8) | copy-start | bytes 1179652
  73.5 4.4 %copy-start.11 = (bf16[512,384]{1,0:T(8,128)(2,1)S(1)}, bf16[512,384]{1,0:T(8,128)(2,1)}, u32[]{:S(2)}) copy-start(bf16[512,384]{1,0:T(8,128)(2,1)} %copy-done.10) | copy-start | bytes 1179652
  73.5 4.4 %copy-start.13 = (bf16[512,384]{1,0:T(8,128)(2,1)S(1)}, bf16[512,384]{1,0:T(8,128)(2,1)}, u32[]{:S(2)}) copy-start(bf16[512,384]{1,0:T(8,128)(2,1)} %copy-done.12) | copy-start | bytes 1179652
  85.6 19.4 %collective-permute-start.23 = (bf16[1024,512]{1,0:T(8,128)(2,1)S(1)}, bf16[1024,512]{1,0:T(8,128)(2,1)S(1)}, u32[]{:S(2)}, u32[]{:S(2)}) collective-permute-start(bf16[1024,512]{1,0:T(8,128)(2,1)S(1)} %shard_map.79), channel_id=1, source_target_pairs={{0,8},{8,0},{16,24},{24,16},{32,40},{40,32},{48,56},{56,48},{64,72... | collective-permute-start | bytes 3145736 | tf_op jit(solution)/shard_map/ppermute | solution.py:318
  106.4 0.8 copy-start.14
  107.3 0.8 copy-start.18
  108.1 0.8 copy-start.20
  108.9 23.3 %copy-start.25 = (f32[512]{0:T(512)S(1)}, f32[512]{0:T(512)}, u32[]{:S(2)}) copy-start(f32[512]{0:T(512)} %param.10) | copy-start | bytes 6148
  117.9 1.0 copy-start.16
  118.9 17.7 %copy-start.15 = (f32[4,2,128,128]{3,2,1,0:T(8,128)S(1)}, f32[4,2,128,128]{3,2,1,0:T(8,128)}, u32[]{:S(2)}) copy-start(f32[4,2,128,128]{3,2,1,0:T(8,128)} %copy-done.14) | copy-start | bytes 1572868
  118.9 13.4 %collective-permute-start.24 = (bf16[1024,256]{1,0:T(8,128)(2,1)}, bf16[1024,256]{1,0:T(8,128)(2,1)S(1)}, u32[]{:S(2)}, u32[]{:S(2)}) collective-permute-start(bf16[1024,256]{1,0:T(8,128)(2,1)} %get-tuple-element.17), channel_id=1, source_target_pairs={{0,8},{8,0},{16,24},{24,16},{32,40},{40,32},{48,56},{56,48},{64,72... | collective-permute-start | bytes 1572872 | tf_op jit(solution)/shard_map/ppermute | solution.py:334
  119.0 3.3 %collective-permute-start.27 = (bf16[2,128,128]{2,1,0:T(8,128)(2,1)}, bf16[2,128,128]{2,1,0:T(8,128)(2,1)S(1)}, u32[]{:S(2)}, u32[]{:S(2)}) collective-permute-start(bf16[2,128,128]{2,1,0:T(8,128)(2,1)} %get-tuple-element.14), channel_id=1, source_target_pairs={{0,48},{8,56},{16,0},{24,8},{32,16},{40,24},{48,32},{56,40},{64,11... | collective-permute-start | bytes 196616 | tf_op jit(solution)/shard_map/ppermute | solution.py:325
  119.0 4.9 %collective-permute-start.26 = (bf16[2,128,128]{2,1,0:T(8,128)(2,1)}, bf16[2,128,128]{2,1,0:T(8,128)(2,1)S(1)}, u32[]{:S(2)}, u32[]{:S(2)}) collective-permute-start(bf16[2,128,128]{2,1,0:T(8,128)(2,1)} %get-tuple-element.14), channel_id=1, source_target_pairs={{0,32},{8,40},{16,48},{24,56},{32,0},{40,8},{48,16},{56,24},{64,96... | collective-permute-start | bytes 196616 | tf_op jit(solution)/shard_map/ppermute | solution.py:325
  119.0 6.8 %collective-permute-start.25 = (bf16[2,128,128]{2,1,0:T(8,128)(2,1)}, bf16[2,128,128]{2,1,0:T(8,128)(2,1)S(1)}, u32[]{:S(2)}, u32[]{:S(2)}) collective-permute-start(bf16[2,128,128]{2,1,0:T(8,128)(2,1)} %get-tuple-element.14), channel_id=1, source_target_pairs={{0,16},{8,24},{16,32},{24,40},{32,48},{40,56},{48,0},{56,8},{64,80... | collective-permute-start | bytes 196616 | tf_op jit(solution)/shard_map/ppermute | solution.py:325
  126.8 9.8 %collective-permute-start.30 = (bf16[2,128,128]{2,1,0:T(8,128)(2,1)S(1)}, bf16[2,128,128]{2,1,0:T(8,128)(2,1)S(1)}, u32[]{:S(2)}, u32[]{:S(2)}) collective-permute-start(bf16[2,128,128]{2,1,0:T(8,128)(2,1)S(1)} %get-tuple-element.31), channel_id=1, source_target_pairs={{0,192},{8,200},{16,208},{24,216},{32,224},{40,232},{48,240},{56,2... | collective-permute-start | bytes 196616 | tf_op jit(solution)/shard_map/ppermute | solution.py:329
  128.5 8.1 %collective-permute-start.29 = (bf16[2,128,128]{2,1,0:T(8,128)(2,1)S(1)}, bf16[2,128,128]{2,1,0:T(8,128)(2,1)S(1)}, u32[]{:S(2)}, u32[]{:S(2)}) collective-permute-start(bf16[2,128,128]{2,1,0:T(8,128)(2,1)S(1)} %get-tuple-element.31), channel_id=1, source_target_pairs={{0,128},{8,136},{16,144},{24,152},{32,160},{40,168},{48,176},{56,1... | collective-permute-start | bytes 196616 | tf_op jit(solution)/shard_map/ppermute | solution.py:329
  129.8 6.9 %collective-permute-start.28 = (bf16[2,128,128]{2,1,0:T(8,128)(2,1)S(1)}, bf16[2,128,128]{2,1,0:T(8,128)(2,1)S(1)}, u32[]{:S(2)}, u32[]{:S(2)}) collective-permute-start(bf16[2,128,128]{2,1,0:T(8,128)(2,1)S(1)} %get-tuple-element.31), channel_id=1, source_target_pairs={{0,64},{8,72},{16,80},{24,88},{32,96},{40,104},{48,112},{56,120},{... | collective-permute-start | bytes 196616 | tf_op jit(solution)/shard_map/ppermute | solution.py:329
  132.4 1.2 copy-start.17
  133.6 1.0 copy-start.19
  134.6 1.0 copy-start.21
  137.6 2.8 %collective-permute-start.31 = (bf16[512,256]{1,0:T(8,128)(2,1)S(1)}, bf16[512,256]{1,0:T(8,128)(2,1)S(1)}, u32[]{:S(2)}, u32[]{:S(2)}) collective-permute-start(bf16[512,256]{1,0:T(8,128)(2,1)S(1)} %shard_map.84), channel_id=1, source_target_pairs={{0,8},{8,0},{16,24},{24,16},{32,40},{40,32},{48,56},{56,48},{64,72... | collective-permute-start | bytes 786440 | tf_op jit(solution)/shard_map/ppermute | solution.py:339

commit v4 on v3

--- a/solution.py
+++ b/solution.py
@@ -16,6 +16,7 @@
 SLAB = 512
 CHIP = C * SLAB
 HALF = 256
+BLOCKS = 4
 F32, BF16 = jnp.float32, jnp.bfloat16
 DIMS = (
     lambda y, x: (y, x ^ 1),
@@ -70,10 +71,11 @@
 
 
 def place_table():
-    table = np.zeros((Y * X * C, Z, 2, Z, 2), np.int32)
+    table = np.zeros((Y * X * C, Z, 2 + 4 * Z), np.int32)
     for y, x in chips():
         for c in range(C):
             for z in range(Z):
+                places = []
                 for stream in range(2):
                     for k in range(Z):
                         for e in range(2):
@@ -85,10 +87,11 @@
                                 dx >> 1,
                                 dy >> 1,
                             )
-                            table[seq_of(y, x, c), z, stream, k, e] = sum(
-                                bits[dim_of(stream, c, step)] << step for step in range(4)
+                            places.append(
+                                sum(bits[dim_of(stream, c, step)] << step for step in range(4))
                             )
-    return table.reshape(Y * X * C * Z, 4 * Z)
+                table[seq_of(y, x, c), z] = [c, x] + places
+    return table.reshape(Y * X * C * Z, 2 + 4 * Z)
 
 
 def silu(u):
@@ -97,21 +100,24 @@
 
 def product_kernel(parts, info, *refs):
     tokens, refs = refs[: 2 * Z], refs[2 * Z :]
-    weights, refs = refs[:4], refs[4:]
+    weights, refs = refs[: 2 * BLOCKS], refs[2 * BLOCKS :]
     outs, (piled,) = refs[: len(parts)], refs[len(parts) :]
     core = info[0]
     deep = 2 * PIECE
     for part, (mine, low, high) in enumerate(parts):
         half = core if mine else 1 - core
-        for at in range(2 * Z):
-            place = info[1 + half * 2 * Z + at]
-            row = pl.ds(pl.multiple_of((place % 8) * ROWS, ROWS), ROWS)
-            choice = half * 2 + place // 8
-            for b in range(4):
+
+        @pl.loop(0, 2 * Z)
+        def _(at):
+            place = info[2 + half * 2 * Z + at]
+            source = pl.ds(pl.multiple_of((place % 4) * ROWS, ROWS), ROWS)
+            target = pl.ds(pl.multiple_of(at * ROWS, ROWS), ROWS)
+            choice = half * BLOCKS + place // 4
+            for b in range(2 * BLOCKS):
 
                 @pl.when(choice == b)
                 def _():
-                    piled[at * ROWS : (at + 1) * ROWS, 0 : high - low] = weights[b][row, low:high]
+                    piled[target, 0 : high - low] = weights[b][source, low:high]
 
         for slab in range(2):
             first = pl.multiple_of(SLAB * (core if slab == 0 else 1 - core), SLAB)
@@ -139,7 +145,7 @@
             jax.ShapeDtypeStruct((CHIP, high - low), F32 if mine else BF16)
             for mine, low, high in parts
         ],
-        in_specs=[SMEM] + [VMEM] * (2 * Z + 4),
+        in_specs=[SMEM] + [VMEM] * (2 * Z + 2 * BLOCKS),
         out_specs=[VMEM] * len(parts),
         scratch_shapes=[pltpu.VMEM((Z * PIECE, wide), BF16)],
         compiler_params=pltpu.CompilerParams(vmem_limit_bytes=20 * 2**20),
@@ -178,11 +184,37 @@
         ],
         in_specs=[VMEM] * 2,
         out_specs=[VMEM] * 4,
-        compiler_params=pltpu.CompilerParams(vmem_limit_bytes=32 * 2**20),
+        compiler_params=pltpu.CompilerParams(vmem_limit_bytes=12 * 2**20),
         cost_estimate=pl.CostEstimate(
             flops=2 * CHIP * 2 * HDIM * HDIM, bytes_accessed=5 * 2**20, transcendentals=CHIP * 512
         ),
     )(mine, other)
+
+
+def row_kernel(info, total, left_1, left_2, left_3, row, before):
+    x = info[1]
+    whole = total[...].astype(F32)
+    earlier = jnp.zeros_like(whole)
+    for k, left in enumerate((left_1, left_2, left_3), 1):
+        got = left[...].astype(F32)
+        whole = whole + got
+        earlier = earlier + jnp.where(x >= k, got, 0.0)
+    row[...] = whole.astype(BF16)
+    before[...] = earlier
+
+
+def row_sums(info, total, *from_left):
+    return pl.pallas_call(
+        row_kernel,
+        out_shape=[
+            jax.ShapeDtypeStruct(total.shape, BF16),
+            jax.ShapeDtypeStruct(total.shape, F32),
+        ],
+        in_specs=[SMEM] + [VMEM] * 4,
+        out_specs=[VMEM] * 2,
+        compiler_params=pltpu.CompilerParams(vmem_limit_bytes=4 * 2**20),
+        cost_estimate=pl.CostEstimate(flops=2**18, bytes_accessed=2**19, transcendentals=0),
+    )(info, total, *from_left)
 
 
 def local_kernel(mine, other, key, value, query, inside):
@@ -210,7 +242,7 @@
         ],
         in_specs=[VMEM] * 4,
         out_specs=[VMEM] * 2,
-        compiler_params=pltpu.CompilerParams(vmem_limit_bytes=32 * 2**20),
+        compiler_params=pltpu.CompilerParams(vmem_limit_bytes=12 * 2**20),
         cost_estimate=pl.CostEstimate(
             flops=8 * CHIP * SPAN * HDIM, bytes_accessed=5 * 2**20, transcendentals=CHIP * HALF
         ),
@@ -241,7 +273,7 @@
         out_shape=jax.ShapeDtypeStruct((SLAB, HALF), BF16),
         in_specs=[SMEM] + [VMEM] * 8,
         out_specs=VMEM,
-        compiler_params=pltpu.CompilerParams(vmem_limit_bytes=32 * 2**20),
+        compiler_params=pltpu.CompilerParams(vmem_limit_bytes=12 * 2**20),
         cost_estimate=pl.CostEstimate(
             flops=4 * SLAB * HDIM * HDIM, bytes_accessed=2 * 2**20, transcendentals=0
         ),
@@ -264,7 +296,7 @@
         out_specs=ANY,
         input_output_aliases={0: 0},
         compiler_params=pltpu.CompilerParams(vmem_limit_bytes=2**20),
-        cost_estimate=pl.CostEstimate(flops=2500000000, bytes_accessed=0, transcendentals=0),
+        cost_estimate=pl.CostEstimate(flops=2750000000, bytes_accessed=0, transcendentals=0),
     )(piece)
 
 
@@ -285,15 +317,14 @@
             stream.append(pace(pass_on(piece)))
     streams = list(weights)
     got = [None, None]
-    blocks = []
-    for step in range(4):
+    for step in range(3):
         if step:
-            if (0, 0, 0, 0)[step]:
-                got = after(got, first[(0, 0, 0, 0)[step]])
             streams = [jnp.concatenate(pair, axis=0) for pair in zip(streams, got)]
         got = [lax.ppermute(streams[j], "seq", cube_pairs(j, step)) for j in range(2)]
+    blocks = []
     for j in range(2):
         blocks += [streams[j], got[j]]
+        blocks += [lax.ppermute(part, "seq", cube_pairs(j, 3)) for part in (streams[j], got[j])]
     pieces = zip(first, second)
     return [p for pair in pieces for p in pair], blocks
 
@@ -301,13 +332,10 @@
 def local(tokens, w_query, w_key, w_value, gain):
     seq = lax.axis_index("seq")
     core = seq % C
-    x = (seq // C) % X
-    info = jnp.concatenate(
-        [
-            core[None].astype(jnp.int32),
-            jnp.asarray(place_table())[seq * Z + lax.axis_index("head")],
-        ]
-    )
+    table = jnp.asarray(place_table())
+    info = lax.dynamic_slice(table, (seq * Z + lax.axis_index("head"), 0), (1, table.shape[1]))[0]
+    gain_here = lax.dynamic_slice(gain, (core * HALF,), (HALF,)).reshape(1, HALF)
+    tokens, info, gain_here = lax.optimization_barrier((tokens, info, gain_here))
     halves = [
         jnp.concatenate([w[:, j * HALF : (j + 1) * HALF] for w in (w_key, w_value, w_query)], axis=1)
         for j in range(2)
@@ -319,22 +347,16 @@
     (kv_mine,) = product(info, pieces, blocks, ((True, 0, 2 * HALF),))
     key, value, within, total = pair_states(kv_mine, kv_got)
 
-    row = total.astype(F32)
-    before = jnp.zeros_like(row)
-    for k in range(1, X):
-        got = lax.ppermute(total, "seq", spin_x(k)).astype(F32)
-        row = row + got
-        before = before + jnp.where(x >= k, got, 0.0)
-    row = row.astype(BF16)
-    rows = [lax.ppermute(row, "seq", shift_y(k)) for k in range(1, Y)]
-
-    q_theirs, q_mine = product(
-        after(info, total), pieces, blocks, ((False, 2 * HALF, 3 * HALF), (True, 2 * HALF, 3 * HALF))
+    from_left = [lax.ppermute(total, "seq", spin_x(k)) for k in range(1, X)]
+    (q_theirs,) = product(
+        after(info, total), pieces, blocks, ((False, 2 * HALF, 3 * HALF),)
     )
     q_got = lax.ppermute(q_theirs, "seq", SWAP)
+    row, before = row_sums(info, after(total, q_theirs), *from_left)
+    rows = [lax.ppermute(row, "seq", shift_y(k)) for k in range(1, Y)]
+    (q_mine,) = product(after(info, row), pieces, blocks, ((True, 2 * HALF, 3 * HALF),))
     query, inside = local_part(q_mine, q_got, key, value)
 
-    gain_here = lax.dynamic_slice(gain, (core * HALF,), (HALF,)).reshape(1, HALF)
     last = (info, query, inside, within, before, *rows, gain_here)
     out_got = lax.ppermute(finish(False, *last), "seq", SWAP)
     out_mine = finish(True, *last)

time: 142 us -> 130 us (0.915)
  starting transfers between devices: 60.4 us -> 68.4 us
  Pallas kernels: 28.8 us -> 21.2 us
  local copies, waits for them, and re-layouts: 9.25 us -> 2.98 us
  other arithmetic: 6.34 us -> 1.49 us
    ppermute x1, starting transfers between devices: 11.5 us -> 1.5 us  [local(): kv_got = lax.ppermute(kv_theirs, 'seq', SWAP)]
    ppermute x3 -> x7, waiting for transfers between devices: 5.44 us -> 14.9 us  [the longest x4 9.48 us: gather(): lax.ppermute(part, 'seq', cube_pairs(j, 3))]
    pallas_call x3 -> x4, Pallas kernels: 24.5 us -> 17 us  [product(): pl.pallas_call(functools.partial(product_kernel, parts), out_shape=[jax.S...]
    ppermute x14, waiting for transfers between devices: 26.6 us -> 19.6 us  [pass_on(): return lax.ppermute(piece, ('seq', 'head'), ring)]
    unnamed x52 -> x6, local copies, waits for them, and re-layouts: 6.89 us -> 0.02 us
    ppermute x14, starting transfers between devices: 28.8 us -> 35.6 us  [pass_on(): return lax.ppermute(piece, ('seq', 'head'), ring)]
    ppermute x3 -> x7, starting transfers between devices: 1.46 us -> 7.92 us  [the longest x4 4.03 us: gather(): lax.ppermute(part, 'seq', cube_pairs(j, 3))]
    concatenate x6 -> x4, other arithmetic: 4.12 us -> 0.23 us  [gather(): streams = [jnp.concatenate(pair, axis=0) for pair in zip(streams, got)]]
  transfers between devices with their start and end apart: 32 -> 34, of which waited for: 17 -> 16; matrix products, arithmetic and copies ran while one was open for 4% -> 0% of each run, Pallas kernels for 7% -> 8%
where the time goes in v4:
time: 130 us; the launch traced here: 129 us
  starting transfers between devices  68.4 us (53%)
  waiting for transfers between devices  35.2 us (27%)
  Pallas kernels  21.2 us (16%)
  local copies, waits for them, and re-layouts  2.98 us (2%)
  other arithmetic  1.49 us (1%)
    ppermute x14, starting transfers between devices, pass_on(): return lax.ppermute(piece, ('seq', 'head'), ring)  35.6 us
    ppermute x14, waiting for transfers between devices, pass_on(): return lax.ppermute(piece, ('seq', 'head'), ring)  19.6 us
    pallas_call x4, Pallas kernels, product(): pl.pallas_call(functools.partial(product_kernel, parts), out_shape=[jax.S...  17 us
    ppermute x6, starting transfers between devices, gather(): lax.ppermute(streams[j], 'seq', cube_pairs(j, step))  10.8 us
    ppermute x4, waiting for transfers between devices, gather(): lax.ppermute(part, 'seq', cube_pairs(j, 3))  9.48 us
    ppermute x3, starting transfers between devices, local(): rows = [lax.ppermute(row, 'seq', shift_y(k)) for k in range(1, Y)]  7.59 us
    ppermute x3, waiting for transfers between devices, local(): from_left = [lax.ppermute(total, 'seq', spin_x(k)) for k in range(1, X)]  5.38 us
    ppermute x4, starting transfers between devices, gather(): lax.ppermute(part, 'seq', cube_pairs(j, 3))  4.03 us
  transfers between devices with their start and end apart: 34, of which 16 were waited for; matrix products, arithmetic and copies ran while one was open for 0% of the time, Pallas kernels for 8%

profile of v4, /device:TPU:1, one launch (start us, length us, event | category | flops | bytes accessed | tf_op | source)
XLA Modules:
  0.0 129.5 jit_solution(6045194365887546924)
XLA Ops:
  0.0 0.7 dynamic-slice_bitcast_fusion.info
  0.7 0.8 dynamic_slice.7
  1.4 1.5 %fusion = (bf16[512,192]{1,0:T(8,128)(2,1)S(1)}, bf16[512,192]{1,0:T(8,128)(2,1)S(1)}, bf16[512,192]{1,0:T(8,128)(2,1)S(1)}, bf16[512,192]{1,0:T(8,128)(2,1)S(1)}) fusion(bf16[512,768]{1,0:T(8,128)(2,1)} %param.6), kind=kLoop, calls=%fused_computation.14 | loop fusion | bytes 1572864 | tf_op jit(solution)/shard_map/slice | solution.py:304
  3.0 0.3 broadcast_select_fusion
  3.3 3.3 %collective-permute-start = (bf16[512,384]{1,0:T(8,128)(2,1)S(1)}, bf16[512,384]{1,0:T(8,128)(2,1)S(1)}, u32[]{:S(2)}, u32[]{:S(2)}) collective-permute-start(bf16[512,384]{1,0:T(8,128)(2,1)S(1)} %get-tuple-element.33), channel_id=1, source_target_pairs={{0,8},{8,0},{16,24},{24,16},{32,40},{40,32},{48,56},{56,48},{64,72... | collective-permute-start | bytes 1179656 | tf_op jit(solution)/shard_map/ppermute | solution.py:307
  6.6 3.8 %collective-permute-start.1 = (bf16[512,384]{1,0:T(8,128)(2,1)S(1)}, bf16[512,384]{1,0:T(8,128)(2,1)S(1)}, u32[]{:S(2)}, u32[]{:S(2)}) collective-permute-start(bf16[512,384]{1,0:T(8,128)(2,1)S(1)} %get-tuple-element.34.refs_0_), channel_id=1, source_target_pairs={{0,1},{1,2},{2,3},{3,4},{4,5},{5,6},{6,7},{7,0},{8,15},{9,8},{10,9... | collective-permute-start | bytes 1179656 | tf_op jit(solution)/shard_map/ppermute | solution.py:311
  10.5 1.3 collective-permute-start.2
  11.8 1.4 %collective-permute-start.15 = (bf16[192,768]{1,0:T(8,128)(2,1)S(1)}, bf16[192,768]{1,0:T(8,128)(2,1)S(1)}, u32[]{:S(2)}, u32[]{:S(2)}) collective-permute-start(bf16[192,768]{1,0:T(8,128)(2,1)S(1)} %pad_maximum_fusion.7), channel_id=1, source_target_pairs={{0,16},{8,72},{16,0},{24,88},{32,48},{40,104},{48,32},{56,120},{64... | collective-permute-start | bytes 884744 | tf_op jit(solution)/shard_map/ppermute | solution.py:323
  13.2 2.0 %collective-permute-start.20 = (bf16[192,768]{1,0:T(8,128)(2,1)S(1)}, bf16[192,768]{1,0:T(8,128)(2,1)S(1)}, u32[]{:S(2)}, u32[]{:S(2)}) collective-permute-start(bf16[192,768]{1,0:T(8,128)(2,1)S(1)} %pad_maximum_fusion.8), channel_id=1, source_target_pairs={{0,48},{8,200},{16,32},{24,216},{32,16},{40,232},{48,0},{56,248},{... | collective-permute-start | bytes 884744 | tf_op jit(solution)/shard_map/ppermute | solution.py:323
  15.2 3.4 %collective-permute-start.3 = (bf16[512,384]{1,0:T(8,128)(2,1)S(1)}, bf16[512,384]{1,0:T(8,128)(2,1)S(1)}, u32[]{:S(2)}, u32[]{:S(2)}) collective-permute-start(bf16[512,384]{1,0:T(8,128)(2,1)S(1)} %shard_map.64.refs_2_), channel_id=1, source_target_pairs={{0,1},{1,2},{2,3},{3,4},{4,5},{5,6},{6,7},{7,0},{8,15},{9,8},{10,9... | collective-permute-start | bytes 1179656 | tf_op jit(solution)/shard_map/ppermute | solution.py:311
  18.6 0.8 collective-permute-done.2.piece
  19.4 3.1 %collective-permute-start.4 = (bf16[512,384]{1,0:T(8,128)(2,1)S(1)}, bf16[512,384]{1,0:T(8,128)(2,1)S(1)}, u32[]{:S(2)}, u32[]{:S(2)}) collective-permute-start(bf16[512,384]{1,0:T(8,128)(2,1)S(1)} %shard_map.65.refs_3_), channel_id=1, source_target_pairs={{0,1},{1,2},{2,3},{3,4},{4,5},{5,6},{6,7},{7,0},{8,15},{9,8},{10,9... | collective-permute-start | bytes 1179656 | tf_op jit(solution)/shard_map/ppermute | solution.py:311
  22.6 1.3 %collective-permute-start.21 = (bf16[384,768]{1,0:T(8,128)(2,1)S(1)}, bf16[384,768]{1,0:T(8,128)(2,1)S(1)}, u32[]{:S(2)}, u32[]{:S(2)}) collective-permute-start(bf16[384,768]{1,0:T(8,128)(2,1)S(1)} %pad_maximum_fusion.3), channel_id=1, source_target_pairs={{0,192},{8,24},{16,208},{24,8},{32,224},{40,56},{48,240},{56,40},{... | collective-permute-start | bytes 1769480 | tf_op jit(solution)/shard_map/ppermute | solution.py:323
  23.9 1.9 %collective-permute-start.16 = (bf16[384,768]{1,0:T(8,128)(2,1)S(1)}, bf16[384,768]{1,0:T(8,128)(2,1)S(1)}, u32[]{:S(2)}, u32[]{:S(2)}) collective-permute-start(bf16[384,768]{1,0:T(8,128)(2,1)S(1)} %pad_maximum_fusion.2), channel_id=1, source_target_pairs={{0,64},{8,56},{16,80},{24,40},{32,96},{40,24},{48,112},{56,8},{64,... | collective-permute-start | bytes 1769480 | tf_op jit(solution)/shard_map/ppermute | solution.py:323
  25.8 0.9 collective-permute-start.5
  26.7 1.1 collective-permute-done.4.piece
  27.8 3.4 %collective-permute-start.6 = (bf16[512,384]{1,0:T(8,128)(2,1)S(1)}, bf16[512,384]{1,0:T(8,128)(2,1)S(1)}, u32[]{:S(2)}, u32[]{:S(2)}) collective-permute-start(bf16[512,384]{1,0:T(8,128)(2,1)S(1)} %shard_map.67.refs_5_), channel_id=1, source_target_pairs={{0,1},{1,2},{2,3},{3,4},{4,5},{5,6},{6,7},{7,0},{8,15},{9,8},{10,9... | collective-permute-start | bytes 1179656 | tf_op jit(solution)/shard_map/ppermute | solution.py:311
  31.2 0.4 collective-permute-done.21
  31.8 1.4 %collective-permute-start.22 = (bf16[768,768]{1,0:T(8,128)(2,1)S(1)}, bf16[768,768]{1,0:T(8,128)(2,1)S(1)}, u32[]{:S(2)}, u32[]{:S(2)}) collective-permute-start(bf16[768,768]{1,0:T(8,128)(2,1)S(1)} %pad_maximum_fusion.1.refs_20_), channel_id=1, source_target_pairs={{0,16},{8,72},{16,0},{24,88},{32,48},{40,104},{48,32},{56,120},{64... | collective-permute-start | bytes 3538952 | tf_op jit(solution)/shard_map/ppermute | solution.py:323
  33.2 2.0 %collective-permute-start.7 = (bf16[512,384]{1,0:T(8,128)(2,1)S(1)}, bf16[512,384]{1,0:T(8,128)(2,1)S(1)}, u32[]{:S(2)}, u32[]{:S(2)}) collective-permute-start(bf16[512,384]{1,0:T(8,128)(2,1)S(1)} %shard_map.68.refs_6_), channel_id=1, source_target_pairs={{0,1},{1,2},{2,3},{3,4},{4,5},{5,6},{6,7},{7,0},{8,15},{9,8},{10,9... | collective-permute-start | bytes 1179656 | tf_op jit(solution)/shard_map/ppermute | solution.py:311
  35.2 1.8 %collective-permute-done.6.piece = bf16[512,384]{1,0:T(8,128)(2,1)S(1)} collective-permute-done((bf16[512,384]{1,0:T(8,128)(2,1)S(1)}, bf16[512,384]{1,0:T(8,128)(2,1)S(1)}, u32[]{:S(2)}, u32[]{:S(2)}) %collective-permute-start.6) | collective-permute-done | bytes 393248 | tf_op jit(solution)/shard_map/ppermute | solution.py:311
  37.0 2.4 %collective-permute-start.8 = (bf16[512,384]{1,0:T(8,128)(2,1)S(1)}, bf16[512,384]{1,0:T(8,128)(2,1)S(1)}, u32[]{:S(2)}, u32[]{:S(2)}) collective-permute-start(bf16[512,384]{1,0:T(8,128)(2,1)S(1)} %shard_map.69.refs_7_), channel_id=1, source_target_pairs={{0,1},{1,2},{2,3},{3,4},{4,5},{5,6},{6,7},{7,0},{8,15},{9,8},{10,9... | collective-permute-start | bytes 1179656 | tf_op jit(solution)/shard_map/ppermute | solution.py:311
  39.4 0.1 pad_maximum_fusion.refs_16_
  39.5 2.8 %collective-permute-start.17 = (bf16[768,768]{1,0:T(8,128)(2,1)S(1)}, bf16[768,768]{1,0:T(8,128)(2,1)S(1)}, u32[]{:S(2)}, u32[]{:S(2)}) collective-permute-start(bf16[768,768]{1,0:T(8,128)(2,1)S(1)} %pad_maximum_fusion.refs_16_), channel_id=1, source_target_pairs={{0,48},{8,200},{16,32},{24,216},{32,16},{40,232},{48,0},{56,248},{... | collective-permute-start | bytes 3538952 | tf_op jit(solution)/shard_map/ppermute | solution.py:323
  42.3 1.3 %collective-permute-start.9 = (bf16[512,384]{1,0:T(8,128)(2,1)S(1)}, bf16[512,384]{1,0:T(8,128)(2,1)S(1)}, u32[]{:S(2)}, u32[]{:S(2)}) collective-permute-start(bf16[512,384]{1,0:T(8,128)(2,1)S(1)} %shard_map.70.refs_8_), channel_id=1, source_target_pairs={{0,1},{1,2},{2,3},{3,4},{4,5},{5,6},{6,7},{7,0},{8,15},{9,8},{10,9... | collective-permute-start | bytes 1179656 | tf_op jit(solution)/shard_map/ppermute | solution.py:311
  43.6 1.8 %collective-permute-done.8.piece = bf16[512,384]{1,0:T(8,128)(2,1)S(1)} collective-permute-done((bf16[512,384]{1,0:T(8,128)(2,1)S(1)}, bf16[512,384]{1,0:T(8,128)(2,1)S(1)}, u32[]{:S(2)}, u32[]{:S(2)}) %collective-permute-start.8) | collective-permute-done | bytes 393248 | tf_op jit(solution)/shard_map/ppermute | solution.py:311
  45.4 2.7 %collective-permute-start.10 = (bf16[512,384]{1,0:T(8,128)(2,1)S(1)}, bf16[512,384]{1,0:T(8,128)(2,1)S(1)}, u32[]{:S(2)}, u32[]{:S(2)}) collective-permute-start(bf16[512,384]{1,0:T(8,128)(2,1)S(1)} %shard_map.71.refs_9_), channel_id=1, source_target_pairs={{0,1},{1,2},{2,3},{3,4},{4,5},{5,6},{6,7},{7,0},{8,15},{9,8},{10,9... | collective-permute-start | bytes 1179656 | tf_op jit(solution)/shard_map/ppermute | solution.py:311
  48.1 1.5 %collective-permute-done.9.piece = bf16[512,384]{1,0:T(8,128)(2,1)S(1)} collective-permute-done((bf16[512,384]{1,0:T(8,128)(2,1)S(1)}, bf16[512,384]{1,0:T(8,128)(2,1)S(1)}, u32[]{:S(2)}, u32[]{:S(2)}) %collective-permute-start.9) | collective-permute-done | bytes 393248 | tf_op jit(solution)/shard_map/ppermute | solution.py:311
  49.6 2.7 %collective-permute-start.11 = (bf16[512,384]{1,0:T(8,128)(2,1)S(1)}, bf16[512,384]{1,0:T(8,128)(2,1)S(1)}, u32[]{:S(2)}, u32[]{:S(2)}) collective-permute-start(bf16[512,384]{1,0:T(8,128)(2,1)S(1)} %shard_map.72.refs_10_), channel_id=1, source_target_pairs={{0,1},{1,2},{2,3},{3,4},{4,5},{5,6},{6,7},{7,0},{8,15},{9,8},{10,9... | collective-permute-start | bytes 1179656 | tf_op jit(solution)/shard_map/ppermute | solution.py:311
  52.3 1.5 %collective-permute-done.10.piece = bf16[512,384]{1,0:T(8,128)(2,1)S(1)} collective-permute-done((bf16[512,384]{1,0:T(8,128)(2,1)S(1)}, bf16[512,384]{1,0:T(8,128)(2,1)S(1)}, u32[]{:S(2)}, u32[]{:S(2)}) %collective-permute-start.10) | collective-permute-done | bytes 393248 | tf_op jit(solution)/shard_map/ppermute | solution.py:311
  53.8 2.7 %collective-permute-start.12 = (bf16[512,384]{1,0:T(8,128)(2,1)S(1)}, bf16[512,384]{1,0:T(8,128)(2,1)S(1)}, u32[]{:S(2)}, u32[]{:S(2)}) collective-permute-start(bf16[512,384]{1,0:T(8,128)(2,1)S(1)} %shard_map.73.refs_11_), channel_id=1, source_target_pairs={{0,1},{1,2},{2,3},{3,4},{4,5},{5,6},{6,7},{7,0},{8,15},{9,8},{10,9... | collective-permute-start | bytes 1179656 | tf_op jit(solution)/shard_map/ppermute | solution.py:311
  56.5 2.5 %collective-permute-start.23 = (bf16[768,768]{1,0:T(8,128)(2,1)S(1)}, bf16[768,768]{1,0:T(8,128)(2,1)S(1)}, u32[]{:S(2)}, u32[]{:S(2)}) collective-permute-start(bf16[768,768]{1,0:T(8,128)(2,1)S(1)} %pad_maximum_fusion.1.refs_20_), channel_id=1, source_target_pairs={{0,64},{8,56},{16,80},{24,40},{32,96},{40,24},{48,112},{56,8},{64,... | collective-permute-start | bytes 3538952 | tf_op jit(solution)/shard_map/ppermute | solution.py:327
  59.0 0.5 collective-permute-start.24
  59.5 1.0 collective-permute-start.19
  60.6 1.7 %collective-permute-done.12.piece = bf16[512,384]{1,0:T(8,128)(2,1)S(1)} collective-permute-done((bf16[512,384]{1,0:T(8,128)(2,1)S(1)}, bf16[512,384]{1,0:T(8,128)(2,1)S(1)}, u32[]{:S(2)}, u32[]{:S(2)}) %collective-permute-start.12) | collective-permute-done | bytes 393248 | tf_op jit(solution)/shard_map/ppermute | solution.py:311
  62.2 2.4 %collective-permute-start.13 = (bf16[512,384]{1,0:T(8,128)(2,1)S(1)}, bf16[512,384]{1,0:T(8,128)(2,1)S(1)}, u32[]{:S(2)}, u32[]{:S(2)}) collective-permute-start(bf16[512,384]{1,0:T(8,128)(2,1)S(1)} %shard_map.74.refs_12_), channel_id=1, source_target_pairs={{0,1},{1,2},{2,3},{3,4},{4,5},{5,6},{6,7},{7,0},{8,15},{9,8},{10,9... | collective-permute-start | bytes 1179656 | tf_op jit(solution)/shard_map/ppermute | solution.py:311
  64.7 4.7 %collective-permute-done.13.piece = bf16[512,384]{1,0:T(8,128)(2,1)S(1)} collective-permute-done((bf16[512,384]{1,0:T(8,128)(2,1)S(1)}, bf16[512,384]{1,0:T(8,128)(2,1)S(1)}, u32[]{:S(2)}, u32[]{:S(2)}) %collective-permute-start.13) | collective-permute-done | bytes 393248 | tf_op jit(solution)/shard_map/ppermute | solution.py:311
  69.4 3.4 %collective-permute-start.14 = (bf16[512,384]{1,0:T(8,128)(2,1)S(1)}, bf16[512,384]{1,0:T(8,128)(2,1)S(1)}, u32[]{:S(2)}, u32[]{:S(2)}) collective-permute-start(bf16[512,384]{1,0:T(8,128)(2,1)S(1)} %shard_map.75.refs_13_), channel_id=1, source_target_pairs={{0,1},{1,2},{2,3},{3,4},{4,5},{5,6},{6,7},{7,0},{8,15},{9,8},{10,9... | collective-permute-start | bytes 1179656 | tf_op jit(solution)/shard_map/ppermute | solution.py:311
  72.8 4.7 %collective-permute-done.14.piece = bf16[512,384]{1,0:T(8,128)(2,1)S(1)} collective-permute-done((bf16[512,384]{1,0:T(8,128)(2,1)S(1)}, bf16[512,384]{1,0:T(8,128)(2,1)S(1)}, u32[]{:S(2)}, u32[]{:S(2)}) %collective-permute-start.14) | collective-permute-done | bytes 393248 | tf_op jit(solution)/shard_map/ppermute | solution.py:311
  77.5 8.2 %collective-permute-done.24.refs_23_ = bf16[768,768]{1,0:T(8,128)(2,1)S(1)} collective-permute-done((bf16[768,768]{1,0:T(8,128)(2,1)S(1)}, bf16[768,768]{1,0:T(8,128)(2,1)S(1)}, u32[]{:S(2)}, u32[]{:S(2)}) %collective-permute-start.24) | collective-permute-done | bytes 1179680 | tf_op jit(solution)/shard_map/ppermute | solution.py:327
  85.7 1.3 collective-permute-done.19.refs_19_
  87.0 5.1 %shard_map.79 = bf16[1024,512]{1,0:T(8,128)(2,1)S(1)} custom-call(s32[34]{0:T(128)S(1)} %dynamic-slice_bitcast_fusion.info, bf16[512,384]{1,0:T(8,128)(2,1)S(1)} %get-tuple-element.34.refs_0_, bf16[512,384]{1,0:T(8,128)(2,1)S(1)} %collective-permute-done.refs_1_, bf16[512,384]{1,0:T(8,128)(2,1)S(1)} %shard_map.64.refs_2_, ...), custom_call_target="tpu_custom_call" | custom-call | flops 3221225472 | bytes 16777216 | tf_op jit(solution)/shard_map/pallas_call | solution.py:142
  92.1 1.5 %collective-permute-start.25 = (bf16[1024,512]{1,0:T(8,128)(2,1)S(1)}, bf16[1024,512]{1,0:T(8,128)(2,1)S(1)}, u32[]{:S(2)}, u32[]{:S(2)}) collective-permute-start(bf16[1024,512]{1,0:T(8,128)(2,1)S(1)} %shard_map.79), channel_id=1, source_target_pairs={{0,8},{8,0},{16,24},{24,16},{32,40},{40,32},{48,56},{56,48},{64,72... | collective-permute-start | bytes 3145736 | tf_op jit(solution)/shard_map/ppermute | solution.py:346
  93.6 5.1 %shard_map.78.mine = f32[1024,512]{1,0:T(8,128)S(1)} custom-call(s32[34]{0:T(128)S(1)} %dynamic-slice_bitcast_fusion.info, bf16[512,384]{1,0:T(8,128)(2,1)S(1)} %get-tuple-element.34.refs_0_, bf16[512,384]{1,0:T(8,128)(2,1)S(1)} %collective-permute-done.refs_1_, bf16[512,384]{1,0:T(8,128)(2,1)S(1)} %shard_map.64.refs_2_, ...), custom_call_target="tpu_custom_call" | custom-call | flops 3221225472 | bytes 16777216 | tf_op jit(solution)/shard_map/pallas_call | solution.py:142
  98.7 0.8 shard_map.80
  99.5 3.4 %shard_map.81 = bf16[1024,256]{1,0:T(8,128)(2,1)S(1)} custom-call(s32[34]{0:T(128)S(1)} %dynamic-slice_bitcast_fusion.info, bf16[512,384]{1,0:T(8,128)(2,1)S(1)} %get-tuple-element.34.refs_0_, bf16[512,384]{1,0:T(8,128)(2,1)S(1)} %collective-permute-done.refs_1_, bf16[512,384]{1,0:T(8,128)(2,1)S(1)} %shard_map.64.refs_2_, ...), custom_call_target="tpu_custom_call" | custom-call | flops 1610612736 | bytes 16777216 | tf_op jit(solution)/shard_map/pallas_call | solution.py:142
  102.9 0.1 collective-permute-start.29
  103.0 2.8 %collective-permute-start.28 = (bf16[2,128,128]{2,1,0:T(8,128)(2,1)S(1)}, bf16[2,128,128]{2,1,0:T(8,128)(2,1)S(1)}, u32[]{:S(2)}, u32[]{:S(2)}) collective-permute-start(bf16[2,128,128]{2,1,0:T(8,128)(2,1)S(1)} %get-tuple-element.23.total), channel_id=1, source_target_pairs={{0,48},{8,56},{16,0},{24,8},{32,16},{40,24},{48,32},{56,40},{64,11... | collective-permute-start | bytes 196616 | tf_op jit(solution)/shard_map/ppermute | solution.py:350
  105.8 0.5 collective-permute-start.27
  106.3 0.6 collective-permute-start.26
  106.9 0.2 collective-permute-done.28.left_3
  107.1 3.3 %collective-permute-done.27.left_2 = bf16[2,128,128]{2,1,0:T(8,128)(2,1)S(1)} collective-permute-done((bf16[2,128,128]{2,1,0:T(8,128)(2,1)S(1)}, bf16[2,128,128]{2,1,0:T(8,128)(2,1)S(1)}, u32[]{:S(2)}, u32[]{:S(2)}) %collective-permute-start.27) | collective-permute-done | bytes 65568 | tf_op jit(solution)/shard_map/ppermute | solution.py:350
  110.5 1.8 %collective-permute-done.26.left_1 = bf16[2,128,128]{2,1,0:T(8,128)(2,1)S(1)} collective-permute-done((bf16[2,128,128]{2,1,0:T(8,128)(2,1)S(1)}, bf16[2,128,128]{2,1,0:T(8,128)(2,1)S(1)}, u32[]{:S(2)}, u32[]{:S(2)}) %collective-permute-start.26) | collective-permute-done | bytes 65568 | tf_op jit(solution)/shard_map/ppermute | solution.py:350
  112.3 0.6 shard_map.82
  112.9 3.8 %collective-permute-start.32 = (bf16[2,128,128]{2,1,0:T(8,128)(2,1)S(1)}, bf16[2,128,128]{2,1,0:T(8,128)(2,1)S(1)}, u32[]{:S(2)}, u32[]{:S(2)}) collective-permute-start(bf16[2,128,128]{2,1,0:T(8,128)(2,1)S(1)} %get-tuple-element.24), channel_id=1, source_target_pairs={{0,192},{8,200},{16,208},{24,216},{32,224},{40,232},{48,240},{56,2... | collective-permute-start | bytes 196616 | tf_op jit(solution)/shard_map/ppermute | solution.py:356
  116.7 1.3 collective-permute-start.31
  118.1 2.5 %collective-permute-start.30 = (bf16[2,128,128]{2,1,0:T(8,128)(2,1)S(1)}, bf16[2,128,128]{2,1,0:T(8,128)(2,1)S(1)}, u32[]{:S(2)}, u32[]{:S(2)}) collective-permute-start(bf16[2,128,128]{2,1,0:T(8,128)(2,1)S(1)} %get-tuple-element.24), channel_id=1, source_target_pairs={{0,64},{8,72},{16,80},{24,88},{32,96},{40,104},{48,112},{56,120},{... | collective-permute-start | bytes 196616 | tf_op jit(solution)/shard_map/ppermute | solution.py:356
  120.5 3.4 %shard_map.83.mine = f32[1024,256]{1,0:T(8,128)S(1)} custom-call(s32[34]{0:T(128)S(1)} %dynamic-slice_bitcast_fusion.info, bf16[512,384]{1,0:T(8,128)(2,1)S(1)} %get-tuple-element.34.refs_0_, bf16[512,384]{1,0:T(8,128)(2,1)S(1)} %collective-permute-done.refs_1_, bf16[512,384]{1,0:T(8,128)(2,1)S(1)} %shard_map.64.refs_2_, ...), custom_call_target="tpu_custom_call" | custom-call | flops 1610612736 | bytes 16777216 | tf_op jit(solution)/shard_map/pallas_call | solution.py:142
  124.0 0.9 shard_map.84
  124.9 0.9 shard_map.86
  125.9 1.6 %collective-permute-start.33 = (bf16[512,256]{1,0:T(8,128)(2,1)S(1)}, bf16[512,256]{1,0:T(8,128)(2,1)S(1)}, u32[]{:S(2)}, u32[]{:S(2)}) collective-permute-start(bf16[512,256]{1,0:T(8,128)(2,1)S(1)} %shard_map.86), channel_id=1, source_target_pairs={{0,8},{8,0},{16,24},{24,16},{32,40},{40,32},{48,56},{56,48},{64,72... | collective-permute-start | bytes 786440 | tf_op jit(solution)/shard_map/ppermute | solution.py:361
  127.4 0.9 shard_map.85
  128.4 0.2 collective-permute-done.33
  128.6 0.8 pad_maximum_fusion.4
  (47 shorter events, 0.4 us)
Async XLA Ops:
  2.9 7.5 %copy-start.1 = (bf16[192,512]{1,0:T(8,128)(2,1)S(1)}, bf16[192,512]{1,0:T(8,128)(2,1)}, u32[]{:S(2)}) copy-start(bf16[192,512]{1,0:T(8,128)(2,1)} %param.8) | copy-start | bytes 589828
  2.9 7.5 %copy-start.2 = (bf16[192,512]{1,0:T(8,128)(2,1)S(1)}, bf16[192,512]{1,0:T(8,128)(2,1)}, u32[]{:S(2)}) copy-start(bf16[192,512]{1,0:T(8,128)(2,1)} %param.9) | copy-start | bytes 589828
  3.0 7.6 %copy-start = (bf16[192,512]{1,0:T(8,128)(2,1)S(1)}, bf16[192,512]{1,0:T(8,128)(2,1)}, u32[]{:S(2)}) copy-start(bf16[192,512]{1,0:T(8,128)(2,1)} %param.7) | copy-start | bytes 589828
  3.3 7.2 %collective-permute-start = (bf16[512,384]{1,0:T(8,128)(2,1)S(1)}, bf16[512,384]{1,0:T(8,128)(2,1)S(1)}, u32[]{:S(2)}, u32[]{:S(2)}) collective-permute-start(bf16[512,384]{1,0:T(8,128)(2,1)S(1)} %get-tuple-element.33), channel_id=1, source_target_pairs={{0,8},{8,0},{16,24},{24,16},{32,40},{40,32},{48,56},{56,48},{64,72... | collective-permute-start | bytes 1179656 | tf_op jit(solution)/shard_map/ppermute | solution.py:307
  6.6 8.6 %collective-permute-start.1 = (bf16[512,384]{1,0:T(8,128)(2,1)S(1)}, bf16[512,384]{1,0:T(8,128)(2,1)S(1)}, u32[]{:S(2)}, u32[]{:S(2)}) collective-permute-start(bf16[512,384]{1,0:T(8,128)(2,1)S(1)} %get-tuple-element.34.refs_0_), channel_id=1, source_target_pairs={{0,1},{1,2},{2,3},{3,4},{4,5},{5,6},{6,7},{7,0},{8,15},{9,8},{10,9... | collective-permute-start | bytes 1179656 | tf_op jit(solution)/shard_map/ppermute | solution.py:311
  10.5 8.9 %collective-permute-start.2 = (bf16[512,384]{1,0:T(8,128)(2,1)S(1)}, bf16[512,384]{1,0:T(8,128)(2,1)S(1)}, u32[]{:S(2)}, u32[]{:S(2)}) collective-permute-start(bf16[512,384]{1,0:T(8,128)(2,1)S(1)} %collective-permute-done.refs_1_), channel_id=1, source_target_pairs={{0,1},{1,2},{2,3},{3,4},{4,5},{5,6},{6,7},{7,0},{8,15},{9,8},{10,9... | collective-permute-start | bytes 1179656 | tf_op jit(solution)/shard_map/ppermute | solution.py:311
  11.8 12.0 %collective-permute-start.15 = (bf16[192,768]{1,0:T(8,128)(2,1)S(1)}, bf16[192,768]{1,0:T(8,128)(2,1)S(1)}, u32[]{:S(2)}, u32[]{:S(2)}) collective-permute-start(bf16[192,768]{1,0:T(8,128)(2,1)S(1)} %pad_maximum_fusion.7), channel_id=1, source_target_pairs={{0,16},{8,72},{16,0},{24,88},{32,48},{40,104},{48,32},{56,120},{64... | collective-permute-start | bytes 884744 | tf_op jit(solution)/shard_map/ppermute | solution.py:323
  13.2 9.3 %collective-permute-start.20 = (bf16[192,768]{1,0:T(8,128)(2,1)S(1)}, bf16[192,768]{1,0:T(8,128)(2,1)S(1)}, u32[]{:S(2)}, u32[]{:S(2)}) collective-permute-start(bf16[192,768]{1,0:T(8,128)(2,1)S(1)} %pad_maximum_fusion.8), channel_id=1, source_target_pairs={{0,48},{8,200},{16,32},{24,216},{32,16},{40,232},{48,0},{56,248},{... | collective-permute-start | bytes 884744 | tf_op jit(solution)/shard_map/ppermute | solution.py:323
  15.2 10.6 %collective-permute-start.3 = (bf16[512,384]{1,0:T(8,128)(2,1)S(1)}, bf16[512,384]{1,0:T(8,128)(2,1)S(1)}, u32[]{:S(2)}, u32[]{:S(2)}) collective-permute-start(bf16[512,384]{1,0:T(8,128)(2,1)S(1)} %shard_map.64.refs_2_), channel_id=1, source_target_pairs={{0,1},{1,2},{2,3},{3,4},{4,5},{5,6},{6,7},{7,0},{8,15},{9,8},{10,9... | collective-permute-start | bytes 1179656 | tf_op jit(solution)/shard_map/ppermute | solution.py:311
  19.4 8.4 %collective-permute-start.4 = (bf16[512,384]{1,0:T(8,128)(2,1)S(1)}, bf16[512,384]{1,0:T(8,128)(2,1)S(1)}, u32[]{:S(2)}, u32[]{:S(2)}) collective-permute-start(bf16[512,384]{1,0:T(8,128)(2,1)S(1)} %shard_map.65.refs_3_), channel_id=1, source_target_pairs={{0,1},{1,2},{2,3},{3,4},{4,5},{5,6},{6,7},{7,0},{8,15},{9,8},{10,9... | collective-permute-start | bytes 1179656 | tf_op jit(solution)/shard_map/ppermute | solution.py:311
  22.6 9.1 %collective-permute-start.21 = (bf16[384,768]{1,0:T(8,128)(2,1)S(1)}, bf16[384,768]{1,0:T(8,128)(2,1)S(1)}, u32[]{:S(2)}, u32[]{:S(2)}) collective-permute-start(bf16[384,768]{1,0:T(8,128)(2,1)S(1)} %pad_maximum_fusion.3), channel_id=1, source_target_pairs={{0,192},{8,24},{16,208},{24,8},{32,224},{40,56},{48,240},{56,40},{... | collective-permute-start | bytes 1769480 | tf_op jit(solution)/shard_map/ppermute | solution.py:323
  23.9 15.5 %collective-permute-start.16 = (bf16[384,768]{1,0:T(8,128)(2,1)S(1)}, bf16[384,768]{1,0:T(8,128)(2,1)S(1)}, u32[]{:S(2)}, u32[]{:S(2)}) collective-permute-start(bf16[384,768]{1,0:T(8,128)(2,1)S(1)} %pad_maximum_fusion.2), channel_id=1, source_target_pairs={{0,64},{8,56},{16,80},{24,40},{32,96},{40,24},{48,112},{56,8},{64,... | collective-permute-start | bytes 1769480 | tf_op jit(solution)/shard_map/ppermute | solution.py:323
  25.8 7.3 %collective-permute-start.5 = (bf16[512,384]{1,0:T(8,128)(2,1)S(1)}, bf16[512,384]{1,0:T(8,128)(2,1)S(1)}, u32[]{:S(2)}, u32[]{:S(2)}) collective-permute-start(bf16[512,384]{1,0:T(8,128)(2,1)S(1)} %shard_map.66.refs_4_), channel_id=1, source_target_pairs={{0,1},{1,2},{2,3},{3,4},{4,5},{5,6},{6,7},{7,0},{8,15},{9,8},{10,9... | collective-permute-start | bytes 1179656 | tf_op jit(solution)/shard_map/ppermute | solution.py:311
  27.8 9.1 %collective-permute-start.6 = (bf16[512,384]{1,0:T(8,128)(2,1)S(1)}, bf16[512,384]{1,0:T(8,128)(2,1)S(1)}, u32[]{:S(2)}, u32[]{:S(2)}) collective-permute-start(bf16[512,384]{1,0:T(8,128)(2,1)S(1)} %shard_map.67.refs_5_), channel_id=1, source_target_pairs={{0,1},{1,2},{2,3},{3,4},{4,5},{5,6},{6,7},{7,0},{8,15},{9,8},{10,9... | collective-permute-start | bytes 1179656 | tf_op jit(solution)/shard_map/ppermute | solution.py:311
  31.8 27.2 %collective-permute-start.22 = (bf16[768,768]{1,0:T(8,128)(2,1)S(1)}, bf16[768,768]{1,0:T(8,128)(2,1)S(1)}, u32[]{:S(2)}, u32[]{:S(2)}) collective-permute-start(bf16[768,768]{1,0:T(8,128)(2,1)S(1)} %pad_maximum_fusion.1.refs_20_), channel_id=1, source_target_pairs={{0,16},{8,72},{16,0},{24,88},{32,48},{40,104},{48,32},{56,120},{64... | collective-permute-start | bytes 3538952 | tf_op jit(solution)/shard_map/ppermute | solution.py:323
  33.2 9.1 %collective-permute-start.7 = (bf16[512,384]{1,0:T(8,128)(2,1)S(1)}, bf16[512,384]{1,0:T(8,128)(2,1)S(1)}, u32[]{:S(2)}, u32[]{:S(2)}) collective-permute-start(bf16[512,384]{1,0:T(8,128)(2,1)S(1)} %shard_map.68.refs_6_), channel_id=1, source_target_pairs={{0,1},{1,2},{2,3},{3,4},{4,5},{5,6},{6,7},{7,0},{8,15},{9,8},{10,9... | collective-permute-start | bytes 1179656 | tf_op jit(solution)/shard_map/ppermute | solution.py:311
  37.0 8.4 %collective-permute-start.8 = (bf16[512,384]{1,0:T(8,128)(2,1)S(1)}, bf16[512,384]{1,0:T(8,128)(2,1)S(1)}, u32[]{:S(2)}, u32[]{:S(2)}) collective-permute-start(bf16[512,384]{1,0:T(8,128)(2,1)S(1)} %shard_map.69.refs_7_), channel_id=1, source_target_pairs={{0,1},{1,2},{2,3},{3,4},{4,5},{5,6},{6,7},{7,0},{8,15},{9,8},{10,9... | collective-permute-start | bytes 1179656 | tf_op jit(solution)/shard_map/ppermute | solution.py:311
  39.5 19.6 %collective-permute-start.17 = (bf16[768,768]{1,0:T(8,128)(2,1)S(1)}, bf16[768,768]{1,0:T(8,128)(2,1)S(1)}, u32[]{:S(2)}, u32[]{:S(2)}) collective-permute-start(bf16[768,768]{1,0:T(8,128)(2,1)S(1)} %pad_maximum_fusion.refs_16_), channel_id=1, source_target_pairs={{0,48},{8,200},{16,32},{24,216},{32,16},{40,232},{48,0},{56,248},{... | collective-permute-start | bytes 3538952 | tf_op jit(solution)/shard_map/ppermute | solution.py:323
  42.3 7.3 %collective-permute-start.9 = (bf16[512,384]{1,0:T(8,128)(2,1)S(1)}, bf16[512,384]{1,0:T(8,128)(2,1)S(1)}, u32[]{:S(2)}, u32[]{:S(2)}) collective-permute-start(bf16[512,384]{1,0:T(8,128)(2,1)S(1)} %shard_map.70.refs_8_), channel_id=1, source_target_pairs={{0,1},{1,2},{2,3},{3,4},{4,5},{5,6},{6,7},{7,0},{8,15},{9,8},{10,9... | collective-permute-start | bytes 1179656 | tf_op jit(solution)/shard_map/ppermute | solution.py:311
  45.4 8.4 %collective-permute-start.10 = (bf16[512,384]{1,0:T(8,128)(2,1)S(1)}, bf16[512,384]{1,0:T(8,128)(2,1)S(1)}, u32[]{:S(2)}, u32[]{:S(2)}) collective-permute-start(bf16[512,384]{1,0:T(8,128)(2,1)S(1)} %shard_map.71.refs_9_), channel_id=1, source_target_pairs={{0,1},{1,2},{2,3},{3,4},{4,5},{5,6},{6,7},{7,0},{8,15},{9,8},{10,9... | collective-permute-start | bytes 1179656 | tf_op jit(solution)/shard_map/ppermute | solution.py:311
  49.6 9.9 %collective-permute-start.11 = (bf16[512,384]{1,0:T(8,128)(2,1)S(1)}, bf16[512,384]{1,0:T(8,128)(2,1)S(1)}, u32[]{:S(2)}, u32[]{:S(2)}) collective-permute-start(bf16[512,384]{1,0:T(8,128)(2,1)S(1)} %shard_map.72.refs_10_), channel_id=1, source_target_pairs={{0,1},{1,2},{2,3},{3,4},{4,5},{5,6},{6,7},{7,0},{8,15},{9,8},{10,9... | collective-permute-start | bytes 1179656 | tf_op jit(solution)/shard_map/ppermute | solution.py:311
  53.8 8.4 %collective-permute-start.12 = (bf16[512,384]{1,0:T(8,128)(2,1)S(1)}, bf16[512,384]{1,0:T(8,128)(2,1)S(1)}, u32[]{:S(2)}, u32[]{:S(2)}) collective-permute-start(bf16[512,384]{1,0:T(8,128)(2,1)S(1)} %shard_map.73.refs_11_), channel_id=1, source_target_pairs={{0,1},{1,2},{2,3},{3,4},{4,5},{5,6},{6,7},{7,0},{8,15},{9,8},{10,9... | collective-permute-start | bytes 1179656 | tf_op jit(solution)/shard_map/ppermute | solution.py:311
  56.5 21.0 %collective-permute-start.23 = (bf16[768,768]{1,0:T(8,128)(2,1)S(1)}, bf16[768,768]{1,0:T(8,128)(2,1)S(1)}, u32[]{:S(2)}, u32[]{:S(2)}) collective-permute-start(bf16[768,768]{1,0:T(8,128)(2,1)S(1)} %pad_maximum_fusion.1.refs_20_), channel_id=1, source_target_pairs={{0,64},{8,56},{16,80},{24,40},{32,96},{40,24},{48,112},{56,8},{64,... | collective-permute-start | bytes 3538952 | tf_op jit(solution)/shard_map/ppermute | solution.py:327
  59.0 18.5 %collective-permute-start.18 = (bf16[768,768]{1,0:T(8,128)(2,1)S(1)}, bf16[768,768]{1,0:T(8,128)(2,1)S(1)}, u32[]{:S(2)}, u32[]{:S(2)}) collective-permute-start(bf16[768,768]{1,0:T(8,128)(2,1)S(1)} %pad_maximum_fusion.refs_16_), channel_id=1, source_target_pairs={{0,192},{8,24},{16,208},{24,8},{32,224},{40,56},{48,240},{56,40},{... | collective-permute-start | bytes 3538952 | tf_op jit(solution)/shard_map/ppermute | solution.py:327
  59.0 26.7 %collective-permute-start.24 = (bf16[768,768]{1,0:T(8,128)(2,1)S(1)}, bf16[768,768]{1,0:T(8,128)(2,1)S(1)}, u32[]{:S(2)}, u32[]{:S(2)}) collective-permute-start(bf16[768,768]{1,0:T(8,128)(2,1)S(1)} %collective-permute-done.22.refs_21_), channel_id=1, source_target_pairs={{0,64},{8,56},{16,80},{24,40},{32,96},{40,24},{48,112},{56,8},{64,... | collective-permute-start | bytes 3538952 | tf_op jit(solution)/shard_map/ppermute | solution.py:327
  59.5 27.5 %collective-permute-start.19 = (bf16[768,768]{1,0:T(8,128)(2,1)S(1)}, bf16[768,768]{1,0:T(8,128)(2,1)S(1)}, u32[]{:S(2)}, u32[]{:S(2)}) collective-permute-start(bf16[768,768]{1,0:T(8,128)(2,1)S(1)} %collective-permute-done.17.refs_17_), channel_id=1, source_target_pairs={{0,192},{8,24},{16,208},{24,8},{32,224},{40,56},{48,240},{56,40},{... | collective-permute-start | bytes 3538952 | tf_op jit(solution)/shard_map/ppermute | solution.py:327
  62.2 7.1 %collective-permute-start.13 = (bf16[512,384]{1,0:T(8,128)(2,1)S(1)}, bf16[512,384]{1,0:T(8,128)(2,1)S(1)}, u32[]{:S(2)}, u32[]{:S(2)}) collective-permute-start(bf16[512,384]{1,0:T(8,128)(2,1)S(1)} %shard_map.74.refs_12_), channel_id=1, source_target_pairs={{0,1},{1,2},{2,3},{3,4},{4,5},{5,6},{6,7},{7,0},{8,15},{9,8},{10,9... | collective-permute-start | bytes 1179656 | tf_op jit(solution)/shard_map/ppermute | solution.py:311
  69.4 8.1 %collective-permute-start.14 = (bf16[512,384]{1,0:T(8,128)(2,1)S(1)}, bf16[512,384]{1,0:T(8,128)(2,1)S(1)}, u32[]{:S(2)}, u32[]{:S(2)}) collective-permute-start(bf16[512,384]{1,0:T(8,128)(2,1)S(1)} %shard_map.75.refs_13_), channel_id=1, source_target_pairs={{0,1},{1,2},{2,3},{3,4},{4,5},{5,6},{6,7},{7,0},{8,15},{9,8},{10,9... | collective-permute-start | bytes 1179656 | tf_op jit(solution)/shard_map/ppermute | solution.py:311
  92.1 6.6 %collective-permute-start.25 = (bf16[1024,512]{1,0:T(8,128)(2,1)S(1)}, bf16[1024,512]{1,0:T(8,128)(2,1)S(1)}, u32[]{:S(2)}, u32[]{:S(2)}) collective-permute-start(bf16[1024,512]{1,0:T(8,128)(2,1)S(1)} %shard_map.79), channel_id=1, source_target_pairs={{0,8},{8,0},{16,24},{24,16},{32,40},{40,32},{48,56},{56,48},{64,72... | collective-permute-start | bytes 3145736 | tf_op jit(solution)/shard_map/ppermute | solution.py:346
  102.9 21.0 %collective-permute-start.29 = (bf16[1024,256]{1,0:T(8,128)(2,1)S(1)}, bf16[1024,256]{1,0:T(8,128)(2,1)S(1)}, u32[]{:S(2)}, u32[]{:S(2)}) collective-permute-start(bf16[1024,256]{1,0:T(8,128)(2,1)S(1)} %shard_map.81), channel_id=1, source_target_pairs={{0,8},{8,0},{16,24},{24,16},{32,40},{40,32},{48,56},{56,48},{64,72... | collective-permute-start | bytes 1572872 | tf_op jit(solution)/shard_map/ppermute | solution.py:354
  103.0 4.1 %collective-permute-start.28 = (bf16[2,128,128]{2,1,0:T(8,128)(2,1)S(1)}, bf16[2,128,128]{2,1,0:T(8,128)(2,1)S(1)}, u32[]{:S(2)}, u32[]{:S(2)}) collective-permute-start(bf16[2,128,128]{2,1,0:T(8,128)(2,1)S(1)} %get-tuple-element.23.total), channel_id=1, source_target_pairs={{0,48},{8,56},{16,0},{24,8},{32,16},{40,24},{48,32},{56,40},{64,11... | collective-permute-start | bytes 196616 | tf_op jit(solution)/shard_map/ppermute | solution.py:350
  105.8 4.7 %collective-permute-start.27 = (bf16[2,128,128]{2,1,0:T(8,128)(2,1)S(1)}, bf16[2,128,128]{2,1,0:T(8,128)(2,1)S(1)}, u32[]{:S(2)}, u32[]{:S(2)}) collective-permute-start(bf16[2,128,128]{2,1,0:T(8,128)(2,1)S(1)} %get-tuple-element.23.total), channel_id=1, source_target_pairs={{0,32},{8,40},{16,48},{24,56},{32,0},{40,8},{48,16},{56,24},{64,96... | collective-permute-start | bytes 196616 | tf_op jit(solution)/shard_map/ppermute | solution.py:350
  106.3 6.0 %collective-permute-start.26 = (bf16[2,128,128]{2,1,0:T(8,128)(2,1)S(1)}, bf16[2,128,128]{2,1,0:T(8,128)(2,1)S(1)}, u32[]{:S(2)}, u32[]{:S(2)}) collective-permute-start(bf16[2,128,128]{2,1,0:T(8,128)(2,1)S(1)} %get-tuple-element.23.total), channel_id=1, source_target_pairs={{0,16},{8,24},{16,32},{24,40},{32,48},{40,56},{48,0},{56,8},{64,80... | collective-permute-start | bytes 196616 | tf_op jit(solution)/shard_map/ppermute | solution.py:350
  112.9 12.0 %collective-permute-start.32 = (bf16[2,128,128]{2,1,0:T(8,128)(2,1)S(1)}, bf16[2,128,128]{2,1,0:T(8,128)(2,1)S(1)}, u32[]{:S(2)}, u32[]{:S(2)}) collective-permute-start(bf16[2,128,128]{2,1,0:T(8,128)(2,1)S(1)} %get-tuple-element.24), channel_id=1, source_target_pairs={{0,192},{8,200},{16,208},{24,216},{32,224},{40,232},{48,240},{56,2... | collective-permute-start | bytes 196616 | tf_op jit(solution)/shard_map/ppermute | solution.py:356
  116.7 8.2 %collective-permute-start.31 = (bf16[2,128,128]{2,1,0:T(8,128)(2,1)S(1)}, bf16[2,128,128]{2,1,0:T(8,128)(2,1)S(1)}, u32[]{:S(2)}, u32[]{:S(2)}) collective-permute-start(bf16[2,128,128]{2,1,0:T(8,128)(2,1)S(1)} %get-tuple-element.24), channel_id=1, source_target_pairs={{0,128},{8,136},{16,144},{24,152},{32,160},{40,168},{48,176},{56,1... | collective-permute-start | bytes 196616 | tf_op jit(solution)/shard_map/ppermute | solution.py:356
  118.1 6.9 %collective-permute-start.30 = (bf16[2,128,128]{2,1,0:T(8,128)(2,1)S(1)}, bf16[2,128,128]{2,1,0:T(8,128)(2,1)S(1)}, u32[]{:S(2)}, u32[]{:S(2)}) collective-permute-start(bf16[2,128,128]{2,1,0:T(8,128)(2,1)S(1)} %get-tuple-element.24), channel_id=1, source_target_pairs={{0,64},{8,72},{16,80},{24,88},{32,96},{40,104},{48,112},{56,120},{... | collective-permute-start | bytes 196616 | tf_op jit(solution)/shard_map/ppermute | solution.py:356
  125.9 2.7 %collective-permute-start.33 = (bf16[512,256]{1,0:T(8,128)(2,1)S(1)}, bf16[512,256]{1,0:T(8,128)(2,1)S(1)}, u32[]{:S(2)}, u32[]{:S(2)}) collective-permute-start(bf16[512,256]{1,0:T(8,128)(2,1)S(1)} %shard_map.86), channel_id=1, source_target_pairs={{0,8},{8,0},{16,24},{24,16},{32,40},{40,32},{48,56},{56,48},{64,72... | collective-permute-start | bytes 786440 | tf_op jit(solution)/shard_map/ppermute | solution.py:361

commit v5 on v4

--- a/solution.py
+++ b/solution.py
@@ -16,7 +16,7 @@
 SLAB = 512
 CHIP = C * SLAB
 HALF = 256
-BLOCKS = 4
+BLOCKS = 2
 F32, BF16 = jnp.float32, jnp.bfloat16
 DIMS = (
     lambda y, x: (y, x ^ 1),
@@ -98,61 +98,40 @@
     return u / (1.0 + jnp.exp(-u))
 
 
-def product_kernel(parts, info, *refs):
-    tokens, refs = refs[: 2 * Z], refs[2 * Z :]
-    weights, refs = refs[: 2 * BLOCKS], refs[2 * BLOCKS :]
-    outs, (piled,) = refs[: len(parts)], refs[len(parts) :]
+def product_kernel(mine, low, high, info, *refs):
+    tokens, weights, (out, piled) = refs[: 2 * Z], refs[2 * Z : 2 * Z + BLOCKS], refs[-2:]
     core = info[0]
-    deep = 2 * PIECE
-    for part, (mine, low, high) in enumerate(parts):
-        half = core if mine else 1 - core
-
-        @pl.loop(0, 2 * Z)
-        def _(at):
-            place = info[2 + half * 2 * Z + at]
-            source = pl.ds(pl.multiple_of((place % 4) * ROWS, ROWS), ROWS)
-            target = pl.ds(pl.multiple_of(at * ROWS, ROWS), ROWS)
-            choice = half * BLOCKS + place // 4
-            for b in range(2 * BLOCKS):
-
-                @pl.when(choice == b)
-                def _():
-                    piled[target, 0 : high - low] = weights[b][source, low:high]
-
-        for slab in range(2):
-            first = pl.multiple_of(SLAB * (core if slab == 0 else 1 - core), SLAB)
-            for n in range(0, high - low, 256):
-                total = None
-                for k in range(0, Z, 2):
-                    piece = jnp.concatenate(
-                        [tokens[2 * k + slab][...], tokens[2 * k + 2 + slab][...]], axis=1
-                    )
-                    some = jnp.dot(
-                        piece,
-                        piled[k * PIECE : k * PIECE + deep, n : n + 256],
-                        preferred_element_type=F32,
-                    )
-                    total = some if total is None else total + some
-                outs[part][pl.ds(first, SLAB), n : n + 256] = total.astype(outs[part].dtype)
-
-
-def product(info, tokens, weights, parts):
-    wide = max(high - low for _, low, high in parts)
-    flops = sum(2 * CHIP * Z * PIECE * (high - low) for _, low, high in parts)
-    return pl.pallas_call(
-        functools.partial(product_kernel, parts),
-        out_shape=[
-            jax.ShapeDtypeStruct((CHIP, high - low), F32 if mine else BF16)
-            for mine, low, high in parts
-        ],
-        in_specs=[SMEM] + [VMEM] * (2 * Z + 2 * BLOCKS),
-        out_specs=[VMEM] * len(parts),
-        scratch_shapes=[pltpu.VMEM((Z * PIECE, wide), BF16)],
+    for slab in range(2):
+        first = pl.multiple_of(SLAB * (core if slab == 0 else 1 - core), SLAB)
+        total = None
+        for k in range(0, Z, 2):
+            deep = slice(k * PIECE, (k + 2) * PIECE)
+            if slab == 0:
+                for at in range(2 * k, 2 * k + 4):
+                    place = info[2 + mine * 2 * Z + at]
+                    row = pl.ds(pl.multiple_of((place % 8) * ROWS, ROWS), ROWS)
+                    one, two = (w[row, low:high] for w in weights)
+                    piled[at * ROWS : (at + 1) * ROWS] = jnp.where(place < 8, one, two)
+            piece = jnp.concatenate(
+                [tokens[2 * k + slab][...], tokens[2 * k + 2 + slab][...]], axis=1
+            )
+            some = jnp.dot(piece, piled[deep], preferred_element_type=F32)
+            total = some if total is None else total + some
+        out[pl.ds(first, SLAB), :] = total.astype(out.dtype)
+
+
+def product(info, tokens, blocks, mine, low, high):
+    return pl.pallas_call(
+        functools.partial(product_kernel, mine, low, high),
+        out_shape=jax.ShapeDtypeStruct((CHIP, high - low), F32 if mine else BF16),
+        in_specs=[SMEM] + [VMEM] * (2 * Z + BLOCKS),
+        out_specs=VMEM,
+        scratch_shapes=[pltpu.VMEM((Z * PIECE, high - low), BF16)],
         compiler_params=pltpu.CompilerParams(vmem_limit_bytes=20 * 2**20),
         cost_estimate=pl.CostEstimate(
-            flops=flops, bytes_accessed=16 * 2**20, transcendentals=0
+            flops=2 * CHIP * Z * PIECE * (high - low), bytes_accessed=2**20, transcendentals=0
         ),
-    )(info, *tokens, *weights)
+    )(info, *tokens, *blocks[mine])
 
 
 def pairs_kernel(mine, other, key, value, within, total):
@@ -254,6 +233,7 @@
     first = core if mine else 1 - core
     for h in range(2):
         cols = slice(h * HDIM, (h + 1) * HDIM)
+        gain_here = gain[:, pl.ds(pl.multiple_of(core * HALF + h * HDIM, HDIM), HDIM)]
         earlier = before[h]
         for rows in (rows_0, rows_1, rows_2):
             earlier = earlier + rows[h].astype(F32)
@@ -264,7 +244,7 @@
                 query[at, cols], state, preferred_element_type=F32
             )
             scale = lax.rsqrt(jnp.mean(attended * attended, axis=-1, keepdims=True) + 1e-06)
-            out[b * SPAN : (b + 1) * SPAN, cols] = (attended * scale * gain[:, cols]).astype(BF16)
+            out[b * SPAN : (b + 1) * SPAN, cols] = (attended * scale * gain_here).astype(BF16)
 
 
 def finish(mine, *args):
@@ -296,7 +276,7 @@
         out_specs=ANY,
         input_output_aliases={0: 0},
         compiler_params=pltpu.CompilerParams(vmem_limit_bytes=2**20),
-        cost_estimate=pl.CostEstimate(flops=2750000000, bytes_accessed=0, transcendentals=0),
+        cost_estimate=pl.CostEstimate(flops=2500000000, bytes_accessed=0, transcendentals=0),
     )(piece)
 
 
@@ -317,47 +297,42 @@
             stream.append(pace(pass_on(piece)))
     streams = list(weights)
     got = [None, None]
-    for step in range(3):
+    for step in range(4):
         if step:
             streams = [jnp.concatenate(pair, axis=0) for pair in zip(streams, got)]
         got = [lax.ppermute(streams[j], "seq", cube_pairs(j, step)) for j in range(2)]
-    blocks = []
-    for j in range(2):
-        blocks += [streams[j], got[j]]
-        blocks += [lax.ppermute(part, "seq", cube_pairs(j, 3)) for part in (streams[j], got[j])]
+    blocks = [[streams[j], got[j]] for j in range(2)]
     pieces = zip(first, second)
     return [p for pair in pieces for p in pair], blocks
 
 
 def local(tokens, w_query, w_key, w_value, gain):
-    seq = lax.axis_index("seq")
-    core = seq % C
+    index = (lax.axis_index("seq") * Z + lax.axis_index("head")).astype(jnp.uint32)
+    core = (lax.axis_index("seq").astype(jnp.uint32)) % C
+    tokens, index, core = lax.optimization_barrier((tokens, index, core))
     table = jnp.asarray(place_table())
-    info = lax.dynamic_slice(table, (seq * Z + lax.axis_index("head"), 0), (1, table.shape[1]))[0]
-    gain_here = lax.dynamic_slice(gain, (core * HALF,), (HALF,)).reshape(1, HALF)
-    tokens, info, gain_here = lax.optimization_barrier((tokens, info, gain_here))
-    halves = [
+    info = lax.dynamic_slice(table, (index, jnp.uint32(0)), (1, table.shape[1]))[0]
+    low, high = (
         jnp.concatenate([w[:, j * HALF : (j + 1) * HALF] for w in (w_key, w_value, w_query)], axis=1)
         for j in range(2)
-    ]
+    )
+    halves = [jnp.where(core == 0, high, low), jnp.where(core == 0, low, high)]
     pieces, blocks = gather(tokens, halves, core)
 
-    (kv_theirs,) = product(info, pieces, blocks, ((False, 0, 2 * HALF),))
+    kv_theirs = product(info, pieces, blocks, 0, 0, 2 * HALF)
     kv_got = lax.ppermute(kv_theirs, "seq", SWAP)
-    (kv_mine,) = product(info, pieces, blocks, ((True, 0, 2 * HALF),))
+    kv_mine = product(info, pieces, blocks, 1, 0, 2 * HALF)
     key, value, within, total = pair_states(kv_mine, kv_got)
 
     from_left = [lax.ppermute(total, "seq", spin_x(k)) for k in range(1, X)]
-    (q_theirs,) = product(
-        after(info, total), pieces, blocks, ((False, 2 * HALF, 3 * HALF),)
-    )
+    q_theirs = product(after(info, total), pieces, blocks, 0, 2 * HALF, 3 * HALF)
     q_got = lax.ppermute(q_theirs, "seq", SWAP)
     row, before = row_sums(info, after(total, q_theirs), *from_left)
     rows = [lax.ppermute(row, "seq", shift_y(k)) for k in range(1, Y)]
-    (q_mine,) = product(after(info, row), pieces, blocks, ((True, 2 * HALF, 3 * HALF),))
+    q_mine = product(after(info, row), pieces, blocks, 1, 2 * HALF, 3 * HALF)
     query, inside = local_part(q_mine, q_got, key, value)
 
-    last = (info, query, inside, within, before, *rows, gain_here)
+    last = (info, query, inside, within, before, *rows, gain.reshape(1, 2 * HALF))
     out_got = lax.ppermute(finish(False, *last), "seq", SWAP)
     out_mine = finish(True, *last)
     return jnp.concatenate(

time: 130 us -> 118 us (0.908)
  the two profiles are of different devices: /device:TPU:1 before, /device:TPU:97 now
where the time goes in v5:
time: 118 us
  waiting for transfers between devices  62.7 us (53%)
  starting transfers between devices  34 us (29%)
  Pallas kernels  17 us (14%)
  local copies, waits for them, and re-layouts  2.29 us (2%)
  other arithmetic  1.85 us (2%)
    ppermute x14, waiting for transfers between devices, pass_on(): return lax.ppermute(piece, ('seq', 'head'), ring)  43.3 us
    ppermute x8, waiting for transfers between devices, gather(): lax.ppermute(streams[j], 'seq', cube_pairs(j, step))  13.5 us
    ppermute x8, starting transfers between devices, gather(): lax.ppermute(streams[j], 'seq', cube_pairs(j, step))  13.2 us
    pallas_call x4, Pallas kernels, product(): pl.pallas_call(functools.partial(product_kernel, mine, low, high), out_sh...  12.8 us
    ppermute x3, starting transfers between devices, local(): rows = [lax.ppermute(row, 'seq', shift_y(k)) for k in range(1, Y)]  7.6 us
    ppermute x1, starting transfers between devices, local(): q_got = lax.ppermute(q_theirs, 'seq', SWAP)  6.39 us
    ppermute x3, waiting for transfers between devices, local(): from_left = [lax.ppermute(total, 'seq', spin_x(k)) for k in range(1, X)]  5.53 us
    ppermute x3, starting transfers between devices, local(): from_left = [lax.ppermute(total, 'seq', spin_x(k)) for k in range(1, X)]  3.52 us
  transfers between devices with their start and end apart: 32, of which 19 were waited for; matrix products, arithmetic and copies ran while one was open for 1% of the time, Pallas kernels for 11%

profile of v5, /device:TPU:97, one launch (start us, length us, event | category | flops | bytes accessed | tf_op | source)
XLA Modules:
  0.0 118.0 jit_solution(5767530827815534811)
XLA Ops:
  0.0 1.5 %fusion = (bf16[512,192]{1,0:T(8,128)(2,1)S(1)}, bf16[512,192]{1,0:T(8,128)(2,1)S(1)}, bf16[512,192]{1,0:T(8,128)(2,1)S(1)}, bf16[512,192]{1,0:T(8,128)(2,1)S(1)}) fusion(bf16[512,768]{1,0:T(8,128)(2,1)} %param.6), kind=kLoop, calls=%fused_computation.18 | loop fusion | bytes 1572864 | tf_op jit(solution)/shard_map/slice | solution.py:284
  1.6 0.3 broadcast_select_fusion
  1.9 0.8 collective-permute-start
  2.7 0.0 collective-permute-start.1
  2.7 0.1 broadcast_select_fusion.2
  2.8 1.4 %collective-permute-start.19 = (bf16[192,768]{1,0:T(8,128)(2,1)S(1)}, bf16[192,768]{1,0:T(8,128)(2,1)S(1)}, u32[]{:S(2)}, u32[]{:S(2)}) collective-permute-start(bf16[192,768]{1,0:T(8,128)(2,1)S(1)} %get-tuple-element.39), channel_id=1, source_target_pairs={{0,16},{8,72},{16,0},{24,88},{32,48},{40,104},{48,32},{56,120},{64... | collective-permute-start | bytes 884744 | tf_op jit(solution)/shard_map/ppermute | solution.py:303
  4.2 1.9 %collective-permute-start.15 = (bf16[192,768]{1,0:T(8,128)(2,1)S(1)}, bf16[192,768]{1,0:T(8,128)(2,1)S(1)}, u32[]{:S(2)}, u32[]{:S(2)}) collective-permute-start(bf16[192,768]{1,0:T(8,128)(2,1)S(1)} %get-tuple-element.40), channel_id=1, source_target_pairs={{0,48},{8,200},{16,32},{24,216},{32,16},{40,232},{48,0},{56,248},{... | collective-permute-start | bytes 884744 | tf_op jit(solution)/shard_map/ppermute | solution.py:303
  6.1 0.0 collective-permute-done.refs_1_
  6.1 0.0 collective-permute-start.2
  6.1 4.5 %collective-permute-done.1.piece = bf16[512,384]{1,0:T(8,128)(2,1)S(1)} collective-permute-done((bf16[512,384]{1,0:T(8,128)(2,1)S(1)}, bf16[512,384]{1,0:T(8,128)(2,1)S(1)}, u32[]{:S(2)}, u32[]{:S(2)}) %collective-permute-start.1) | collective-permute-done | bytes 393248 | tf_op jit(solution)/shard_map/ppermute | solution.py:291
  10.7 0.0 collective-permute-start.3
  10.7 0.0 collective-permute-done.19
  10.7 2.6 %collective-permute-start.20 = (bf16[384,768]{1,0:T(8,128)(2,1)S(1)}, bf16[384,768]{1,0:T(8,128)(2,1)S(1)}, u32[]{:S(2)}, u32[]{:S(2)}) collective-permute-start(bf16[384,768]{1,0:T(8,128)(2,1)S(1)} %pad_maximum_fusion.5), channel_id=1, source_target_pairs={{0,64},{8,56},{16,80},{24,40},{32,96},{40,24},{48,112},{56,8},{64,... | collective-permute-start | bytes 1769480 | tf_op jit(solution)/shard_map/ppermute | solution.py:303
  13.3 0.1 collective-permute-start.16
  13.4 1.7 %collective-permute-done.2.piece = bf16[512,384]{1,0:T(8,128)(2,1)S(1)} collective-permute-done((bf16[512,384]{1,0:T(8,128)(2,1)S(1)}, bf16[512,384]{1,0:T(8,128)(2,1)S(1)}, u32[]{:S(2)}, u32[]{:S(2)}) %collective-permute-start.2) | collective-permute-done | bytes 393248 | tf_op jit(solution)/shard_map/ppermute | solution.py:291
  15.2 0.0 collective-permute-start.4
  15.2 3.9 %collective-permute-done.3.piece = bf16[512,384]{1,0:T(8,128)(2,1)S(1)} collective-permute-done((bf16[512,384]{1,0:T(8,128)(2,1)S(1)}, bf16[512,384]{1,0:T(8,128)(2,1)S(1)}, u32[]{:S(2)}, u32[]{:S(2)}) %collective-permute-start.3) | collective-permute-done | bytes 393248 | tf_op jit(solution)/shard_map/ppermute | solution.py:291
  19.1 0.0 collective-permute-start.5
  19.1 2.4 %collective-permute-done.20 = bf16[384,768]{1,0:T(8,128)(2,1)S(1)} collective-permute-done((bf16[384,768]{1,0:T(8,128)(2,1)S(1)}, bf16[384,768]{1,0:T(8,128)(2,1)S(1)}, u32[]{:S(2)}, u32[]{:S(2)}) %collective-permute-start.20) | collective-permute-done | bytes 589856 | tf_op jit(solution)/shard_map/ppermute | solution.py:303
  21.5 0.1 pad_maximum_fusion.3
  21.6 2.8 %collective-permute-start.21 = (bf16[768,768]{1,0:T(8,128)(2,1)S(1)}, bf16[768,768]{1,0:T(8,128)(2,1)S(1)}, u32[]{:S(2)}, u32[]{:S(2)}) collective-permute-start(bf16[768,768]{1,0:T(8,128)(2,1)S(1)} %pad_maximum_fusion.3), channel_id=1, source_target_pairs={{0,48},{8,200},{16,32},{24,216},{32,16},{40,232},{48,0},{56,248},{... | collective-permute-start | bytes 3538952 | tf_op jit(solution)/shard_map/ppermute | solution.py:303
  24.4 0.0 collective-permute-start.6
  24.4 3.4 %collective-permute-done.5.piece = bf16[512,384]{1,0:T(8,128)(2,1)S(1)} collective-permute-done((bf16[512,384]{1,0:T(8,128)(2,1)S(1)}, bf16[512,384]{1,0:T(8,128)(2,1)S(1)}, u32[]{:S(2)}, u32[]{:S(2)}) %collective-permute-start.5) | collective-permute-done | bytes 393248 | tf_op jit(solution)/shard_map/ppermute | solution.py:291
  27.8 0.1 pad_maximum_fusion.2
  27.9 1.1 collective-permute-start.17
  29.0 3.5 %collective-permute-done.6.piece = bf16[512,384]{1,0:T(8,128)(2,1)S(1)} collective-permute-done((bf16[512,384]{1,0:T(8,128)(2,1)S(1)}, bf16[512,384]{1,0:T(8,128)(2,1)S(1)}, u32[]{:S(2)}, u32[]{:S(2)}) %collective-permute-start.6) | collective-permute-done | bytes 393248 | tf_op jit(solution)/shard_map/ppermute | solution.py:291
  32.5 4.2 %collective-permute-done.7.piece = bf16[512,384]{1,0:T(8,128)(2,1)S(1)} collective-permute-done((bf16[512,384]{1,0:T(8,128)(2,1)S(1)}, bf16[512,384]{1,0:T(8,128)(2,1)S(1)}, u32[]{:S(2)}, u32[]{:S(2)}) %collective-permute-start.7) | collective-permute-done | bytes 393248 | tf_op jit(solution)/shard_map/ppermute | solution.py:291
  36.7 3.3 %collective-permute-done.21 = bf16[768,768]{1,0:T(8,128)(2,1)S(1)} collective-permute-done((bf16[768,768]{1,0:T(8,128)(2,1)S(1)}, bf16[768,768]{1,0:T(8,128)(2,1)S(1)}, u32[]{:S(2)}, u32[]{:S(2)}) %collective-permute-start.21) | collective-permute-done | bytes 1179680 | tf_op jit(solution)/shard_map/ppermute | solution.py:303
  40.0 0.2 pad_maximum_fusion.1.refs_16_
  40.2 1.2 %collective-permute-start.22 = (bf16[1536,768]{1,0:T(8,128)(2,1)S(1)}, bf16[1536,768]{1,0:T(8,128)(2,1)S(1)}, u32[]{:S(2)}, u32[]{:S(2)}) collective-permute-start(bf16[1536,768]{1,0:T(8,128)(2,1)S(1)} %pad_maximum_fusion.1.refs_16_), channel_id=1, source_target_pairs={{0,192},{8,24},{16,208},{24,8},{32,224},{40,56},{48,240},{56,40},{... | collective-permute-start | bytes 7077896 | tf_op jit(solution)/shard_map/ppermute | solution.py:303
  41.4 3.5 %collective-permute-done.9.piece = bf16[512,384]{1,0:T(8,128)(2,1)S(1)} collective-permute-done((bf16[512,384]{1,0:T(8,128)(2,1)S(1)}, bf16[512,384]{1,0:T(8,128)(2,1)S(1)}, u32[]{:S(2)}, u32[]{:S(2)}) %collective-permute-start.9) | collective-permute-done | bytes 393248 | tf_op jit(solution)/shard_map/ppermute | solution.py:291
  44.9 0.2 pad_maximum_fusion.refs_16_
  45.0 2.1 %collective-permute-start.18 = (bf16[1536,768]{1,0:T(8,128)(2,1)S(1)}, bf16[1536,768]{1,0:T(8,128)(2,1)S(1)}, u32[]{:S(2)}, u32[]{:S(2)}) collective-permute-start(bf16[1536,768]{1,0:T(8,128)(2,1)S(1)} %pad_maximum_fusion.refs_16_), channel_id=1, source_target_pairs={{0,64},{8,56},{16,80},{24,40},{32,96},{40,24},{48,112},{56,8},{64,... | collective-permute-start | bytes 7077896 | tf_op jit(solution)/shard_map/ppermute | solution.py:303
  47.2 2.4 %collective-permute-done.10.piece = bf16[512,384]{1,0:T(8,128)(2,1)S(1)} collective-permute-done((bf16[512,384]{1,0:T(8,128)(2,1)S(1)}, bf16[512,384]{1,0:T(8,128)(2,1)S(1)}, u32[]{:S(2)}, u32[]{:S(2)}) %collective-permute-start.10) | collective-permute-done | bytes 393248 | tf_op jit(solution)/shard_map/ppermute | solution.py:291
  49.5 4.2 %collective-permute-done.11.piece = bf16[512,384]{1,0:T(8,128)(2,1)S(1)} collective-permute-done((bf16[512,384]{1,0:T(8,128)(2,1)S(1)}, bf16[512,384]{1,0:T(8,128)(2,1)S(1)}, u32[]{:S(2)}, u32[]{:S(2)}) %collective-permute-start.11) | collective-permute-done | bytes 393248 | tf_op jit(solution)/shard_map/ppermute | solution.py:291
  53.7 4.2 %collective-permute-done.12.piece = bf16[512,384]{1,0:T(8,128)(2,1)S(1)} collective-permute-done((bf16[512,384]{1,0:T(8,128)(2,1)S(1)}, bf16[512,384]{1,0:T(8,128)(2,1)S(1)}, u32[]{:S(2)}, u32[]{:S(2)}) %collective-permute-start.12) | collective-permute-done | bytes 393248 | tf_op jit(solution)/shard_map/ppermute | solution.py:291
  58.0 0.7 dynamic-slice_bitcast_fusion.info
  58.6 3.5 %collective-permute-done.13.piece = bf16[512,384]{1,0:T(8,128)(2,1)S(1)} collective-permute-done((bf16[512,384]{1,0:T(8,128)(2,1)S(1)}, bf16[512,384]{1,0:T(8,128)(2,1)S(1)}, u32[]{:S(2)}, u32[]{:S(2)}) %collective-permute-start.13) | collective-permute-done | bytes 393248 | tf_op jit(solution)/shard_map/ppermute | solution.py:291
  62.2 4.2 %collective-permute-done.14.piece = bf16[512,384]{1,0:T(8,128)(2,1)S(1)} collective-permute-done((bf16[512,384]{1,0:T(8,128)(2,1)S(1)}, bf16[512,384]{1,0:T(8,128)(2,1)S(1)}, u32[]{:S(2)}, u32[]{:S(2)}) %collective-permute-start.14) | collective-permute-done | bytes 393248 | tf_op jit(solution)/shard_map/ppermute | solution.py:291
  66.4 7.8 %collective-permute-done.22.refs_17_ = bf16[1536,768]{1,0:T(8,128)(2,1)S(1)} collective-permute-done((bf16[1536,768]{1,0:T(8,128)(2,1)S(1)}, bf16[1536,768]{1,0:T(8,128)(2,1)S(1)}, u32[]{:S(2)}, u32[]{:S(2)}) %collective-permute-start.22) | collective-permute-done | bytes 2359328 | tf_op jit(solution)/shard_map/ppermute | solution.py:303
  74.2 4.0 %shard_map.79 = bf16[1024,512]{1,0:T(8,128)(2,1)S(1)} custom-call(s32[34]{0:T(128)S(1)} %dynamic-slice_bitcast_fusion.info, bf16[512,384]{1,0:T(8,128)(2,1)S(1)} %get-tuple-element.34.refs_0_, bf16[512,384]{1,0:T(8,128)(2,1)S(1)} %collective-permute-done.refs_1_, bf16[512,384]{1,0:T(8,128)(2,1)S(1)} %shard_map.64.refs_2_, ...), custom_call_target="tpu_custom_call" | custom-call | flops 3221225472 | bytes 1048576 | tf_op jit(solution)/shard_map/pallas_call | solution.py:124
  78.2 1.0 collective-permute-start.23
  79.2 4.0 %shard_map.78.mine = f32[1024,512]{1,0:T(8,128)S(1)} custom-call(s32[34]{0:T(128)S(1)} %dynamic-slice_bitcast_fusion.info, bf16[512,384]{1,0:T(8,128)(2,1)S(1)} %get-tuple-element.34.refs_0_, bf16[512,384]{1,0:T(8,128)(2,1)S(1)} %collective-permute-done.refs_1_, bf16[512,384]{1,0:T(8,128)(2,1)S(1)} %shard_map.64.refs_2_, ...), custom_call_target="tpu_custom_call" | custom-call | flops 3221225472 | bytes 1048576 | tf_op jit(solution)/shard_map/pallas_call | solution.py:124
  83.2 0.8 shard_map.80
  84.0 2.4 %shard_map.81 = bf16[1024,256]{1,0:T(8,128)(2,1)S(1)} custom-call(s32[34]{0:T(128)S(1)} %dynamic-slice_bitcast_fusion.info, bf16[512,384]{1,0:T(8,128)(2,1)S(1)} %get-tuple-element.34.refs_0_, bf16[512,384]{1,0:T(8,128)(2,1)S(1)} %collective-permute-done.refs_1_, bf16[512,384]{1,0:T(8,128)(2,1)S(1)} %shard_map.64.refs_2_, ...), custom_call_target="tpu_custom_call" | custom-call | flops 1610612736 | bytes 1048576 | tf_op jit(solution)/shard_map/pallas_call | solution.py:124
  86.4 6.4 %collective-permute-start.27 = (bf16[1024,256]{1,0:T(8,128)(2,1)S(1)}, bf16[1024,256]{1,0:T(8,128)(2,1)S(1)}, u32[]{:S(2)}, u32[]{:S(2)}) collective-permute-start(bf16[1024,256]{1,0:T(8,128)(2,1)S(1)} %shard_map.81), channel_id=1, source_target_pairs={{0,8},{8,0},{16,24},{24,16},{32,40},{40,32},{48,56},{56,48},{64,72... | collective-permute-start | bytes 1572872 | tf_op jit(solution)/shard_map/ppermute | solution.py:329
  92.8 2.4 %collective-permute-start.26 = (bf16[2,128,128]{2,1,0:T(8,128)(2,1)S(1)}, bf16[2,128,128]{2,1,0:T(8,128)(2,1)S(1)}, u32[]{:S(2)}, u32[]{:S(2)}) collective-permute-start(bf16[2,128,128]{2,1,0:T(8,128)(2,1)S(1)} %get-tuple-element.24.total), channel_id=1, source_target_pairs={{0,48},{8,56},{16,0},{24,8},{32,16},{40,24},{48,32},{56,40},{64,11... | collective-permute-start | bytes 196616 | tf_op jit(solution)/shard_map/ppermute | solution.py:327
  95.2 0.5 collective-permute-start.25
  95.7 0.6 collective-permute-start.24
  96.3 0.2 collective-permute-done.26.left_3
  96.5 3.3 %collective-permute-done.25.left_2 = bf16[2,128,128]{2,1,0:T(8,128)(2,1)S(1)} collective-permute-done((bf16[2,128,128]{2,1,0:T(8,128)(2,1)S(1)}, bf16[2,128,128]{2,1,0:T(8,128)(2,1)S(1)}, u32[]{:S(2)}, u32[]{:S(2)}) %collective-permute-start.25) | collective-permute-done | bytes 65568 | tf_op jit(solution)/shard_map/ppermute | solution.py:327
  99.9 2.0 %collective-permute-done.24.left_1 = bf16[2,128,128]{2,1,0:T(8,128)(2,1)S(1)} collective-permute-done((bf16[2,128,128]{2,1,0:T(8,128)(2,1)S(1)}, bf16[2,128,128]{2,1,0:T(8,128)(2,1)S(1)}, u32[]{:S(2)}, u32[]{:S(2)}) %collective-permute-start.24) | collective-permute-done | bytes 65568 | tf_op jit(solution)/shard_map/ppermute | solution.py:327
  101.9 0.6 shard_map.82
  102.5 3.8 %collective-permute-start.30 = (bf16[2,128,128]{2,1,0:T(8,128)(2,1)S(1)}, bf16[2,128,128]{2,1,0:T(8,128)(2,1)S(1)}, u32[]{:S(2)}, u32[]{:S(2)}) collective-permute-start(bf16[2,128,128]{2,1,0:T(8,128)(2,1)S(1)} %get-tuple-element.25), channel_id=1, source_target_pairs={{0,192},{8,200},{16,208},{24,216},{32,224},{40,232},{48,240},{56,2... | collective-permute-start | bytes 196616 | tf_op jit(solution)/shard_map/ppermute | solution.py:331
  106.3 1.7 %collective-permute-start.29 = (bf16[2,128,128]{2,1,0:T(8,128)(2,1)S(1)}, bf16[2,128,128]{2,1,0:T(8,128)(2,1)S(1)}, u32[]{:S(2)}, u32[]{:S(2)}) collective-permute-start(bf16[2,128,128]{2,1,0:T(8,128)(2,1)S(1)} %get-tuple-element.25), channel_id=1, source_target_pairs={{0,128},{8,136},{16,144},{24,152},{32,160},{40,168},{48,176},{56,1... | collective-permute-start | bytes 196616 | tf_op jit(solution)/shard_map/ppermute | solution.py:331
  108.0 2.1 %collective-permute-start.28 = (bf16[2,128,128]{2,1,0:T(8,128)(2,1)S(1)}, bf16[2,128,128]{2,1,0:T(8,128)(2,1)S(1)}, u32[]{:S(2)}, u32[]{:S(2)}) collective-permute-start(bf16[2,128,128]{2,1,0:T(8,128)(2,1)S(1)} %get-tuple-element.25), channel_id=1, source_target_pairs={{0,64},{8,72},{16,80},{24,88},{32,96},{40,104},{48,112},{56,120},{... | collective-permute-start | bytes 196616 | tf_op jit(solution)/shard_map/ppermute | solution.py:331
  110.1 2.4 %shard_map.83.mine = f32[1024,256]{1,0:T(8,128)S(1)} custom-call(s32[34]{0:T(128)S(1)} %dynamic-slice_bitcast_fusion.info, bf16[512,384]{1,0:T(8,128)(2,1)S(1)} %get-tuple-element.34.refs_0_, bf16[512,384]{1,0:T(8,128)(2,1)S(1)} %collective-permute-done.refs_1_, bf16[512,384]{1,0:T(8,128)(2,1)S(1)} %shard_map.64.refs_2_, ...), custom_call_target="tpu_custom_call" | custom-call | flops 1610612736 | bytes 1048576 | tf_op jit(solution)/shard_map/pallas_call | solution.py:124
  112.5 0.0 copy-start
  112.5 0.9 shard_map.84
  113.5 0.9 shard_map.86
  114.4 1.6 %collective-permute-start.31 = (bf16[512,256]{1,0:T(8,128)(2,1)S(1)}, bf16[512,256]{1,0:T(8,128)(2,1)S(1)}, u32[]{:S(2)}, u32[]{:S(2)}) collective-permute-start(bf16[512,256]{1,0:T(8,128)(2,1)S(1)} %shard_map.86), channel_id=1, source_target_pairs={{0,8},{8,0},{16,24},{24,16},{32,40},{40,32},{48,56},{56,48},{64,72... | collective-permute-start | bytes 786440 | tf_op jit(solution)/shard_map/ppermute | solution.py:336
  116.0 0.9 shard_map.85
  116.9 0.2 collective-permute-done.31
  117.2 0.8 pad_maximum_fusion.6
  (45 shorter events, 0.2 us)
Async XLA Ops:
  0.0 2.7 %copy-start.3 = (bf16[192,512]{1,0:T(8,128)(2,1)S(1)}, bf16[192,512]{1,0:T(8,128)(2,1)}, u32[]{:S(2)}) copy-start(bf16[192,512]{1,0:T(8,128)(2,1)} %param.9) | copy-start | bytes 589828
  0.0 2.7 %copy-start.2 = (bf16[192,512]{1,0:T(8,128)(2,1)S(1)}, bf16[192,512]{1,0:T(8,128)(2,1)}, u32[]{:S(2)}) copy-start(bf16[192,512]{1,0:T(8,128)(2,1)} %param.8) | copy-start | bytes 589828
  0.0 2.7 %copy-start.1 = (bf16[192,512]{1,0:T(8,128)(2,1)S(1)}, bf16[192,512]{1,0:T(8,128)(2,1)}, u32[]{:S(2)}) copy-start(bf16[192,512]{1,0:T(8,128)(2,1)} %param.7) | copy-start | bytes 589828
  1.9 4.2 %collective-permute-start = (bf16[512,384]{1,0:T(8,128)(2,1)S(1)}, bf16[512,384]{1,0:T(8,128)(2,1)S(1)}, u32[]{:S(2)}, u32[]{:S(2)}) collective-permute-start(bf16[512,384]{1,0:T(8,128)(2,1)S(1)} %get-tuple-element.33), channel_id=1, source_target_pairs={{0,8},{8,0},{16,24},{24,16},{32,40},{40,32},{48,56},{56,48},{64,72... | collective-permute-start | bytes 1179656 | tf_op jit(solution)/shard_map/ppermute | solution.py:287
  2.7 8.0 %collective-permute-start.1 = (bf16[512,384]{1,0:T(8,128)(2,1)S(1)}, bf16[512,384]{1,0:T(8,128)(2,1)S(1)}, u32[]{:S(2)}, u32[]{:S(2)}) collective-permute-start(bf16[512,384]{1,0:T(8,128)(2,1)S(1)} %get-tuple-element.34.refs_0_), channel_id=1, source_target_pairs={{0,1},{1,2},{2,3},{3,4},{4,5},{5,6},{6,7},{7,0},{8,15},{9,8},{10,9... | collective-permute-start | bytes 1179656 | tf_op jit(solution)/shard_map/ppermute | solution.py:291
  2.8 7.8 %collective-permute-start.19 = (bf16[192,768]{1,0:T(8,128)(2,1)S(1)}, bf16[192,768]{1,0:T(8,128)(2,1)S(1)}, u32[]{:S(2)}, u32[]{:S(2)}) collective-permute-start(bf16[192,768]{1,0:T(8,128)(2,1)S(1)} %get-tuple-element.39), channel_id=1, source_target_pairs={{0,16},{8,72},{16,0},{24,88},{32,48},{40,104},{48,32},{56,120},{64... | collective-permute-start | bytes 884744 | tf_op jit(solution)/shard_map/ppermute | solution.py:303
  4.2 9.1 %collective-permute-start.15 = (bf16[192,768]{1,0:T(8,128)(2,1)S(1)}, bf16[192,768]{1,0:T(8,128)(2,1)S(1)}, u32[]{:S(2)}, u32[]{:S(2)}) collective-permute-start(bf16[192,768]{1,0:T(8,128)(2,1)S(1)} %get-tuple-element.40), channel_id=1, source_target_pairs={{0,48},{8,200},{16,32},{24,216},{32,16},{40,232},{48,0},{56,248},{... | collective-permute-start | bytes 884744 | tf_op jit(solution)/shard_map/ppermute | solution.py:303
  6.1 9.0 %collective-permute-start.2 = (bf16[512,384]{1,0:T(8,128)(2,1)S(1)}, bf16[512,384]{1,0:T(8,128)(2,1)S(1)}, u32[]{:S(2)}, u32[]{:S(2)}) collective-permute-start(bf16[512,384]{1,0:T(8,128)(2,1)S(1)} %collective-permute-done.refs_1_), channel_id=1, source_target_pairs={{0,1},{1,2},{2,3},{3,4},{4,5},{5,6},{6,7},{7,0},{8,15},{9,8},{10,9... | collective-permute-start | bytes 1179656 | tf_op jit(solution)/shard_map/ppermute | solution.py:291
  10.7 8.4 %collective-permute-start.3 = (bf16[512,384]{1,0:T(8,128)(2,1)S(1)}, bf16[512,384]{1,0:T(8,128)(2,1)S(1)}, u32[]{:S(2)}, u32[]{:S(2)}) collective-permute-start(bf16[512,384]{1,0:T(8,128)(2,1)S(1)} %shard_map.64.refs_2_), channel_id=1, source_target_pairs={{0,1},{1,2},{2,3},{3,4},{4,5},{5,6},{6,7},{7,0},{8,15},{9,8},{10,9... | collective-permute-start | bytes 1179656 | tf_op jit(solution)/shard_map/ppermute | solution.py:291
  10.7 10.8 %collective-permute-start.20 = (bf16[384,768]{1,0:T(8,128)(2,1)S(1)}, bf16[384,768]{1,0:T(8,128)(2,1)S(1)}, u32[]{:S(2)}, u32[]{:S(2)}) collective-permute-start(bf16[384,768]{1,0:T(8,128)(2,1)S(1)} %pad_maximum_fusion.5), channel_id=1, source_target_pairs={{0,64},{8,56},{16,80},{24,40},{32,96},{40,24},{48,112},{56,8},{64,... | collective-permute-start | bytes 1769480 | tf_op jit(solution)/shard_map/ppermute | solution.py:303
  13.3 14.5 %collective-permute-start.16 = (bf16[384,768]{1,0:T(8,128)(2,1)S(1)}, bf16[384,768]{1,0:T(8,128)(2,1)S(1)}, u32[]{:S(2)}, u32[]{:S(2)}) collective-permute-start(bf16[384,768]{1,0:T(8,128)(2,1)S(1)} %pad_maximum_fusion.4), channel_id=1, source_target_pairs={{0,192},{8,24},{16,208},{24,8},{32,224},{40,56},{48,240},{56,40},{... | collective-permute-start | bytes 1769480 | tf_op jit(solution)/shard_map/ppermute | solution.py:303
  15.2 9.2 %collective-permute-start.4 = (bf16[512,384]{1,0:T(8,128)(2,1)S(1)}, bf16[512,384]{1,0:T(8,128)(2,1)S(1)}, u32[]{:S(2)}, u32[]{:S(2)}) collective-permute-start(bf16[512,384]{1,0:T(8,128)(2,1)S(1)} %shard_map.65.refs_3_), channel_id=1, source_target_pairs={{0,1},{1,2},{2,3},{3,4},{4,5},{5,6},{6,7},{7,0},{8,15},{9,8},{10,9... | collective-permute-start | bytes 1179656 | tf_op jit(solution)/shard_map/ppermute | solution.py:291
  19.1 8.7 %collective-permute-start.5 = (bf16[512,384]{1,0:T(8,128)(2,1)S(1)}, bf16[512,384]{1,0:T(8,128)(2,1)S(1)}, u32[]{:S(2)}, u32[]{:S(2)}) collective-permute-start(bf16[512,384]{1,0:T(8,128)(2,1)S(1)} %shard_map.66.refs_4_), channel_id=1, source_target_pairs={{0,1},{1,2},{2,3},{3,4},{4,5},{5,6},{6,7},{7,0},{8,15},{9,8},{10,9... | collective-permute-start | bytes 1179656 | tf_op jit(solution)/shard_map/ppermute | solution.py:291
  21.6 18.5 %collective-permute-start.21 = (bf16[768,768]{1,0:T(8,128)(2,1)S(1)}, bf16[768,768]{1,0:T(8,128)(2,1)S(1)}, u32[]{:S(2)}, u32[]{:S(2)}) collective-permute-start(bf16[768,768]{1,0:T(8,128)(2,1)S(1)} %pad_maximum_fusion.3), channel_id=1, source_target_pairs={{0,48},{8,200},{16,32},{24,216},{32,16},{40,232},{48,0},{56,248},{... | collective-permute-start | bytes 3538952 | tf_op jit(solution)/shard_map/ppermute | solution.py:303
  24.4 8.1 %collective-permute-start.6 = (bf16[512,384]{1,0:T(8,128)(2,1)S(1)}, bf16[512,384]{1,0:T(8,128)(2,1)S(1)}, u32[]{:S(2)}, u32[]{:S(2)}) collective-permute-start(bf16[512,384]{1,0:T(8,128)(2,1)S(1)} %shard_map.67.refs_5_), channel_id=1, source_target_pairs={{0,1},{1,2},{2,3},{3,4},{4,5},{5,6},{6,7},{7,0},{8,15},{9,8},{10,9... | collective-permute-start | bytes 1179656 | tf_op jit(solution)/shard_map/ppermute | solution.py:291
  27.8 8.9 %collective-permute-start.7 = (bf16[512,384]{1,0:T(8,128)(2,1)S(1)}, bf16[512,384]{1,0:T(8,128)(2,1)S(1)}, u32[]{:S(2)}, u32[]{:S(2)}) collective-permute-start(bf16[512,384]{1,0:T(8,128)(2,1)S(1)} %shard_map.68.refs_6_), channel_id=1, source_target_pairs={{0,1},{1,2},{2,3},{3,4},{4,5},{5,6},{6,7},{7,0},{8,15},{9,8},{10,9... | collective-permute-start | bytes 1179656 | tf_op jit(solution)/shard_map/ppermute | solution.py:291
  27.9 17.0 %collective-permute-start.17 = (bf16[768,768]{1,0:T(8,128)(2,1)S(1)}, bf16[768,768]{1,0:T(8,128)(2,1)S(1)}, u32[]{:S(2)}, u32[]{:S(2)}) collective-permute-start(bf16[768,768]{1,0:T(8,128)(2,1)S(1)} %pad_maximum_fusion.2), channel_id=1, source_target_pairs={{0,16},{8,72},{16,0},{24,88},{32,48},{40,104},{48,32},{56,120},{64... | collective-permute-start | bytes 3538952 | tf_op jit(solution)/shard_map/ppermute | solution.py:303
  32.5 8.9 %collective-permute-start.8 = (bf16[512,384]{1,0:T(8,128)(2,1)S(1)}, bf16[512,384]{1,0:T(8,128)(2,1)S(1)}, u32[]{:S(2)}, u32[]{:S(2)}) collective-permute-start(bf16[512,384]{1,0:T(8,128)(2,1)S(1)} %shard_map.69.refs_7_), channel_id=1, source_target_pairs={{0,1},{1,2},{2,3},{3,4},{4,5},{5,6},{6,7},{7,0},{8,15},{9,8},{10,9... | collective-permute-start | bytes 1179656 | tf_op jit(solution)/shard_map/ppermute | solution.py:291
  36.7 8.1 %collective-permute-start.9 = (bf16[512,384]{1,0:T(8,128)(2,1)S(1)}, bf16[512,384]{1,0:T(8,128)(2,1)S(1)}, u32[]{:S(2)}, u32[]{:S(2)}) collective-permute-start(bf16[512,384]{1,0:T(8,128)(2,1)S(1)} %shard_map.70.refs_8_), channel_id=1, source_target_pairs={{0,1},{1,2},{2,3},{3,4},{4,5},{5,6},{6,7},{7,0},{8,15},{9,8},{10,9... | collective-permute-start | bytes 1179656 | tf_op jit(solution)/shard_map/ppermute | solution.py:291
  40.2 34.0 %collective-permute-start.22 = (bf16[1536,768]{1,0:T(8,128)(2,1)S(1)}, bf16[1536,768]{1,0:T(8,128)(2,1)S(1)}, u32[]{:S(2)}, u32[]{:S(2)}) collective-permute-start(bf16[1536,768]{1,0:T(8,128)(2,1)S(1)} %pad_maximum_fusion.1.refs_16_), channel_id=1, source_target_pairs={{0,192},{8,24},{16,208},{24,8},{32,224},{40,56},{48,240},{56,40},{... | collective-permute-start | bytes 7077896 | tf_op jit(solution)/shard_map/ppermute | solution.py:303
  41.4 8.1 %collective-permute-start.10 = (bf16[512,384]{1,0:T(8,128)(2,1)S(1)}, bf16[512,384]{1,0:T(8,128)(2,1)S(1)}, u32[]{:S(2)}, u32[]{:S(2)}) collective-permute-start(bf16[512,384]{1,0:T(8,128)(2,1)S(1)} %shard_map.71.refs_9_), channel_id=1, source_target_pairs={{0,1},{1,2},{2,3},{3,4},{4,5},{5,6},{6,7},{7,0},{8,15},{9,8},{10,9... | collective-permute-start | bytes 1179656 | tf_op jit(solution)/shard_map/ppermute | solution.py:291
  44.9 8.9 %collective-permute-start.11 = (bf16[512,384]{1,0:T(8,128)(2,1)S(1)}, bf16[512,384]{1,0:T(8,128)(2,1)S(1)}, u32[]{:S(2)}, u32[]{:S(2)}) collective-permute-start(bf16[512,384]{1,0:T(8,128)(2,1)S(1)} %shard_map.72.refs_10_), channel_id=1, source_target_pairs={{0,1},{1,2},{2,3},{3,4},{4,5},{5,6},{6,7},{7,0},{8,15},{9,8},{10,9... | collective-permute-start | bytes 1179656 | tf_op jit(solution)/shard_map/ppermute | solution.py:291
  45.0 34.1 %collective-permute-start.18 = (bf16[1536,768]{1,0:T(8,128)(2,1)S(1)}, bf16[1536,768]{1,0:T(8,128)(2,1)S(1)}, u32[]{:S(2)}, u32[]{:S(2)}) collective-permute-start(bf16[1536,768]{1,0:T(8,128)(2,1)S(1)} %pad_maximum_fusion.refs_16_), channel_id=1, source_target_pairs={{0,64},{8,56},{16,80},{24,40},{32,96},{40,24},{48,112},{56,8},{64,... | collective-permute-start | bytes 7077896 | tf_op jit(solution)/shard_map/ppermute | solution.py:303
  49.5 8.4 %collective-permute-start.12 = (bf16[512,384]{1,0:T(8,128)(2,1)S(1)}, bf16[512,384]{1,0:T(8,128)(2,1)S(1)}, u32[]{:S(2)}, u32[]{:S(2)}) collective-permute-start(bf16[512,384]{1,0:T(8,128)(2,1)S(1)} %shard_map.73.refs_11_), channel_id=1, source_target_pairs={{0,1},{1,2},{2,3},{3,4},{4,5},{5,6},{6,7},{7,0},{8,15},{9,8},{10,9... | collective-permute-start | bytes 1179656 | tf_op jit(solution)/shard_map/ppermute | solution.py:291
  53.7 8.4 %collective-permute-start.13 = (bf16[512,384]{1,0:T(8,128)(2,1)S(1)}, bf16[512,384]{1,0:T(8,128)(2,1)S(1)}, u32[]{:S(2)}, u32[]{:S(2)}) collective-permute-start(bf16[512,384]{1,0:T(8,128)(2,1)S(1)} %shard_map.74.refs_12_), channel_id=1, source_target_pairs={{0,1},{1,2},{2,3},{3,4},{4,5},{5,6},{6,7},{7,0},{8,15},{9,8},{10,9... | collective-permute-start | bytes 1179656 | tf_op jit(solution)/shard_map/ppermute | solution.py:291
  58.0 8.4 %collective-permute-start.14 = (bf16[512,384]{1,0:T(8,128)(2,1)S(1)}, bf16[512,384]{1,0:T(8,128)(2,1)S(1)}, u32[]{:S(2)}, u32[]{:S(2)}) collective-permute-start(bf16[512,384]{1,0:T(8,128)(2,1)S(1)} %shard_map.75.refs_13_), channel_id=1, source_target_pairs={{0,1},{1,2},{2,3},{3,4},{4,5},{5,6},{6,7},{7,0},{8,15},{9,8},{10,9... | collective-permute-start | bytes 1179656 | tf_op jit(solution)/shard_map/ppermute | solution.py:291
  78.2 5.0 %collective-permute-start.23 = (bf16[1024,512]{1,0:T(8,128)(2,1)S(1)}, bf16[1024,512]{1,0:T(8,128)(2,1)S(1)}, u32[]{:S(2)}, u32[]{:S(2)}) collective-permute-start(bf16[1024,512]{1,0:T(8,128)(2,1)S(1)} %shard_map.79), channel_id=1, source_target_pairs={{0,8},{8,0},{16,24},{24,16},{32,40},{40,32},{48,56},{56,48},{64,72... | collective-permute-start | bytes 3145736 | tf_op jit(solution)/shard_map/ppermute | solution.py:323
  86.4 26.1 %collective-permute-start.27 = (bf16[1024,256]{1,0:T(8,128)(2,1)S(1)}, bf16[1024,256]{1,0:T(8,128)(2,1)S(1)}, u32[]{:S(2)}, u32[]{:S(2)}) collective-permute-start(bf16[1024,256]{1,0:T(8,128)(2,1)S(1)} %shard_map.81), channel_id=1, source_target_pairs={{0,8},{8,0},{16,24},{24,16},{32,40},{40,32},{48,56},{56,48},{64,72... | collective-permute-start | bytes 1572872 | tf_op jit(solution)/shard_map/ppermute | solution.py:329
  92.8 3.7 %collective-permute-start.26 = (bf16[2,128,128]{2,1,0:T(8,128)(2,1)S(1)}, bf16[2,128,128]{2,1,0:T(8,128)(2,1)S(1)}, u32[]{:S(2)}, u32[]{:S(2)}) collective-permute-start(bf16[2,128,128]{2,1,0:T(8,128)(2,1)S(1)} %get-tuple-element.24.total), channel_id=1, source_target_pairs={{0,48},{8,56},{16,0},{24,8},{32,16},{40,24},{48,32},{56,40},{64,11... | collective-permute-start | bytes 196616 | tf_op jit(solution)/shard_map/ppermute | solution.py:327
  95.2 4.7 %collective-permute-start.25 = (bf16[2,128,128]{2,1,0:T(8,128)(2,1)S(1)}, bf16[2,128,128]{2,1,0:T(8,128)(2,1)S(1)}, u32[]{:S(2)}, u32[]{:S(2)}) collective-permute-start(bf16[2,128,128]{2,1,0:T(8,128)(2,1)S(1)} %get-tuple-element.24.total), channel_id=1, source_target_pairs={{0,32},{8,40},{16,48},{24,56},{32,0},{40,8},{48,16},{56,24},{64,96... | collective-permute-start | bytes 196616 | tf_op jit(solution)/shard_map/ppermute | solution.py:327
  95.7 6.1 %collective-permute-start.24 = (bf16[2,128,128]{2,1,0:T(8,128)(2,1)S(1)}, bf16[2,128,128]{2,1,0:T(8,128)(2,1)S(1)}, u32[]{:S(2)}, u32[]{:S(2)}) collective-permute-start(bf16[2,128,128]{2,1,0:T(8,128)(2,1)S(1)} %get-tuple-element.24.total), channel_id=1, source_target_pairs={{0,16},{8,24},{16,32},{24,40},{32,48},{40,56},{48,0},{56,8},{64,80... | collective-permute-start | bytes 196616 | tf_op jit(solution)/shard_map/ppermute | solution.py:327
  102.5 11.0 %collective-permute-start.30 = (bf16[2,128,128]{2,1,0:T(8,128)(2,1)S(1)}, bf16[2,128,128]{2,1,0:T(8,128)(2,1)S(1)}, u32[]{:S(2)}, u32[]{:S(2)}) collective-permute-start(bf16[2,128,128]{2,1,0:T(8,128)(2,1)S(1)} %get-tuple-element.25), channel_id=1, source_target_pairs={{0,192},{8,200},{16,208},{24,216},{32,224},{40,232},{48,240},{56,2... | collective-permute-start | bytes 196616 | tf_op jit(solution)/shard_map/ppermute | solution.py:331
  106.3 7.2 %collective-permute-start.29 = (bf16[2,128,128]{2,1,0:T(8,128)(2,1)S(1)}, bf16[2,128,128]{2,1,0:T(8,128)(2,1)S(1)}, u32[]{:S(2)}, u32[]{:S(2)}) collective-permute-start(bf16[2,128,128]{2,1,0:T(8,128)(2,1)S(1)} %get-tuple-element.25), channel_id=1, source_target_pairs={{0,128},{8,136},{16,144},{24,152},{32,160},{40,168},{48,176},{56,1... | collective-permute-start | bytes 196616 | tf_op jit(solution)/shard_map/ppermute | solution.py:331
  108.0 5.5 %collective-permute-start.28 = (bf16[2,128,128]{2,1,0:T(8,128)(2,1)S(1)}, bf16[2,128,128]{2,1,0:T(8,128)(2,1)S(1)}, u32[]{:S(2)}, u32[]{:S(2)}) collective-permute-start(bf16[2,128,128]{2,1,0:T(8,128)(2,1)S(1)} %get-tuple-element.25), channel_id=1, source_target_pairs={{0,64},{8,72},{16,80},{24,88},{32,96},{40,104},{48,112},{56,120},{... | collective-permute-start | bytes 196616 | tf_op jit(solution)/shard_map/ppermute | solution.py:331
  112.5 1.0 copy-start
  114.4 2.7 %collective-permute-start.31 = (bf16[512,256]{1,0:T(8,128)(2,1)S(1)}, bf16[512,256]{1,0:T(8,128)(2,1)S(1)}, u32[]{:S(2)}, u32[]{:S(2)}) collective-permute-start(bf16[512,256]{1,0:T(8,128)(2,1)S(1)} %shard_map.86), channel_id=1, source_target_pairs={{0,8},{8,0},{16,24},{24,16},{32,40},{40,32},{48,56},{56,48},{64,72... | collective-permute-start | bytes 786440 | tf_op jit(solution)/shard_map/ppermute | solution.py:336

commit v6 on v5

--- a/solution.py
+++ b/solution.py
@@ -16,6 +16,7 @@
 SLAB = 512
 CHIP = C * SLAB
 HALF = 256
+PLACES = 5
 BLOCKS = 2
 F32, BF16 = jnp.float32, jnp.bfloat16
 DIMS = (
@@ -60,18 +61,12 @@
 SWAP = [(s, s ^ 1) for s in range(Y * X * C)]
 
 
-def spin_x(k):
-    return [(seq_of(y, x, c), seq_of(y, (x + k) % X, c)) for y, x in chips() for c in range(C)]
-
-
-def shift_y(k):
-    return [
-        (seq_of(y, x, c), seq_of(y + k, x, c)) for y, x in chips() for c in range(C) if y + k < Y
-    ]
+def exchange_pairs(dim):
+    return [(seq_of(y, x, c), seq_of(*DIMS[dim](y, x), c)) for y, x in chips() for c in range(C)]
 
 
 def place_table():
-    table = np.zeros((Y * X * C, Z, 2 + 4 * Z), np.int32)
+    table = np.zeros((Y * X * C, Z, PLACES + 4 * Z), np.int32)
     for y, x in chips():
         for c in range(C):
             for z in range(Z):
@@ -90,8 +85,9 @@
                             places.append(
                                 sum(bits[dim_of(stream, c, step)] << step for step in range(4))
                             )
-                table[seq_of(y, x, c), z] = [c, x] + places
-    return table.reshape(Y * X * C * Z, 2 + 4 * Z)
+                after_partner = [x & 1, x >> 1, y & 1, y >> 1]
+                table[seq_of(y, x, c), z] = [c] + after_partner + places
+    return table.reshape(Y * X * C * Z, PLACES + 4 * Z)
 
 
 def silu(u):
@@ -108,7 +104,7 @@
             deep = slice(k * PIECE, (k + 2) * PIECE)
             if slab == 0:
                 for at in range(2 * k, 2 * k + 4):
-                    place = info[2 + mine * 2 * Z + at]
+                    place = info[PLACES + mine * 2 * Z + at]
                     row = pl.ds(pl.multiple_of((place % 8) * ROWS, ROWS), ROWS)
                     one, two = (w[row, low:high] for w in weights)
                     piled[at * ROWS : (at + 1) * ROWS] = jnp.where(place < 8, one, two)
@@ -170,32 +166,6 @@
     )(mine, other)
 
 
-def row_kernel(info, total, left_1, left_2, left_3, row, before):
-    x = info[1]
-    whole = total[...].astype(F32)
-    earlier = jnp.zeros_like(whole)
-    for k, left in enumerate((left_1, left_2, left_3), 1):
-        got = left[...].astype(F32)
-        whole = whole + got
-        earlier = earlier + jnp.where(x >= k, got, 0.0)
-    row[...] = whole.astype(BF16)
-    before[...] = earlier
-
-
-def row_sums(info, total, *from_left):
-    return pl.pallas_call(
-        row_kernel,
-        out_shape=[
-            jax.ShapeDtypeStruct(total.shape, BF16),
-            jax.ShapeDtypeStruct(total.shape, F32),
-        ],
-        in_specs=[SMEM] + [VMEM] * 4,
-        out_specs=[VMEM] * 2,
-        compiler_params=pltpu.CompilerParams(vmem_limit_bytes=4 * 2**20),
-        cost_estimate=pl.CostEstimate(flops=2**18, bytes_accessed=2**19, transcendentals=0),
-    )(info, total, *from_left)
-
-
 def local_kernel(mine, other, key, value, query, inside):
     causal = lax.broadcasted_iota(jnp.int32, (SPAN, SPAN), 0) >= lax.broadcasted_iota(
         jnp.int32, (SPAN, SPAN), 1
@@ -228,15 +198,15 @@
     )(mine, other, key, value)
 
 
-def finish_kernel(mine, info, query, inside, within, before, rows_0, rows_1, rows_2, gain, out):
+def finish_kernel(mine, info, query, inside, within, got_0, got_1, got_2, got_3, gain, out):
     core = info[0]
     first = core if mine else 1 - core
     for h in range(2):
         cols = slice(h * HDIM, (h + 1) * HDIM)
         gain_here = gain[:, pl.ds(pl.multiple_of(core * HALF + h * HDIM, HDIM), HDIM)]
-        earlier = before[h]
-        for rows in (rows_0, rows_1, rows_2):
-            earlier = earlier + rows[h].astype(F32)
+        earlier = jnp.zeros((HDIM, HDIM), F32)
+        for step, got in enumerate((got_0, got_1, got_2, got_3)):
+            earlier = earlier + jnp.where(info[1 + step] > 0, got[h].astype(F32), 0.0)
         for b in range(SLAB // SPAN):
             at = pl.ds(pl.multiple_of(first * SLAB + b * SPAN, SPAN), SPAN)
             state = (earlier + within[first * (SLAB // SPAN) + b, h]).astype(BF16)
@@ -276,7 +246,7 @@
         out_specs=ANY,
         input_output_aliases={0: 0},
         compiler_params=pltpu.CompilerParams(vmem_limit_bytes=2**20),
-        cost_estimate=pl.CostEstimate(flops=2500000000, bytes_accessed=0, transcendentals=0),
+        cost_estimate=pl.CostEstimate(flops=2250000000, bytes_accessed=0, transcendentals=0),
     )(piece)
 
 
@@ -299,6 +269,7 @@
     got = [None, None]
     for step in range(4):
         if step:
+            got = lax.optimization_barrier(tuple(got))
             streams = [jnp.concatenate(pair, axis=0) for pair in zip(streams, got)]
         got = [lax.ppermute(streams[j], "seq", cube_pairs(j, step)) for j in range(2)]
     blocks = [[streams[j], got[j]] for j in range(2)]
@@ -324,15 +295,21 @@
     kv_mine = product(info, pieces, blocks, 1, 0, 2 * HALF)
     key, value, within, total = pair_states(kv_mine, kv_got)
 
-    from_left = [lax.ppermute(total, "seq", spin_x(k)) for k in range(1, X)]
     q_theirs = product(after(info, total), pieces, blocks, 0, 2 * HALF, 3 * HALF)
     q_got = lax.ppermute(q_theirs, "seq", SWAP)
-    row, before = row_sums(info, after(total, q_theirs), *from_left)
-    rows = [lax.ppermute(row, "seq", shift_y(k)) for k in range(1, Y)]
-    q_mine = product(after(info, row), pieces, blocks, 1, 2 * HALF, 3 * HALF)
+    q_mine = product(after(info, total), pieces, blocks, 1, 2 * HALF, 3 * HALF)
+    got, group = [], total
+    for step, dim in enumerate((0, 2, 1, 3)):
+        if got:
+            group = (group.astype(F32) + got[-1].astype(F32)).astype(BF16)
+        if step == 1:
+            group = after(group, q_theirs)
+        if step == 3:
+            group = after(group, q_mine)
+        got.append(lax.ppermute(group, "seq", exchange_pairs(dim)))
     query, inside = local_part(q_mine, q_got, key, value)
 
-    last = (info, query, inside, within, before, *rows, gain.reshape(1, 2 * HALF))
+    last = (info, query, inside, within, *got, gain.reshape(1, 2 * HALF))
     out_got = lax.ppermute(finish(False, *last), "seq", SWAP)
     out_mine = finish(True, *last)
     return jnp.concatenate(

time: 118 us -> 122 us (1.034)
  the two profiles are of different devices: /device:TPU:97 before, /device:TPU:71 now
where the time goes in v6:
time: 122 us
  starting transfers between devices  58.9 us (48%)
  waiting for transfers between devices  41.6 us (34%)
  Pallas kernels  16.4 us (13%)
  local copies, waits for them, and re-layouts  3.04 us (2%)
  other arithmetic  1.92 us (2%)
    ppermute x14, waiting for transfers between devices, pass_on(): return lax.ppermute(piece, ('seq', 'head'), ring)  27.9 us
    ppermute x14, starting transfers between devices, pass_on(): return lax.ppermute(piece, ('seq', 'head'), ring)  20.4 us
    ppermute x1, starting transfers between devices, local(): kv_got = lax.ppermute(kv_theirs, 'seq', SWAP)  14.2 us
    pallas_call x4, Pallas kernels, product(): pl.pallas_call(functools.partial(product_kernel, mine, low, high), out_sh...  12.8 us
    ppermute x8, waiting for transfers between devices, gather(): lax.ppermute(streams[j], 'seq', cube_pairs(j, step))  10 us
    ppermute x1, starting transfers between devices, local(): q_got = lax.ppermute(q_theirs, 'seq', SWAP)  7.95 us
    ppermute x8, starting transfers between devices, gather(): lax.ppermute(streams[j], 'seq', cube_pairs(j, step))  6.66 us
    ppermute x1, starting transfers between devices, local(): out_got = lax.ppermute(finish(False, *last), 'seq', SWAP)  6.54 us
  transfers between devices with their start and end apart: 30, of which 21 were waited for; matrix products, arithmetic and copies ran while one was open for 2% of the time, Pallas kernels for 12%

profile of v6, /device:TPU:71, one launch (start us, length us, event | category | flops | bytes accessed | tf_op | source)
XLA Modules:
  0.0 122.1 jit_solution(15730113336000864332)
XLA Ops:
  0.0 1.0 fusion.3
  1.0 1.1 fusion.1
  2.1 0.1 broadcast_select_fusion.3
  2.2 2.8 %collective-permute-start.16 = (bf16[192,768]{1,0:T(8,128)(2,1)S(1)}, bf16[192,768]{1,0:T(8,128)(2,1)S(1)}, u32[]{:S(2)}, u32[]{:S(2)}) collective-permute-start(bf16[192,768]{1,0:T(8,128)(2,1)S(1)} %get-tuple-element.47), channel_id=1, source_target_pairs={{0,48},{8,200},{16,32},{24,216},{32,16},{40,232},{48,0},{56,248},{... | collective-permute-start | bytes 884744 | tf_op jit(solution)/shard_map/ppermute | solution.py:274
  5.0 0.2 fusion
  5.3 0.3 broadcast_select_fusion
  5.6 0.1 collective-permute-start
  5.7 0.1 collective-permute-start.1
  5.8 3.6 %collective-permute-done.16 = bf16[192,768]{1,0:T(8,128)(2,1)S(1)} collective-permute-done((bf16[192,768]{1,0:T(8,128)(2,1)S(1)}, bf16[192,768]{1,0:T(8,128)(2,1)S(1)}, u32[]{:S(2)}, u32[]{:S(2)}) %collective-permute-start.16) | collective-permute-done | bytes 294944 | tf_op jit(solution)/shard_map/ppermute | solution.py:274
  9.4 1.5 %collective-permute-done.15 = bf16[192,768]{1,0:T(8,128)(2,1)S(1)} collective-permute-done((bf16[192,768]{1,0:T(8,128)(2,1)S(1)}, bf16[192,768]{1,0:T(8,128)(2,1)S(1)}, u32[]{:S(2)}, u32[]{:S(2)}) %collective-permute-start.15) | collective-permute-done | bytes 294944 | tf_op jit(solution)/shard_map/ppermute | solution.py:274
  11.1 0.3 collective-permute-start.17
  11.4 0.6 collective-permute-start.18
  12.0 0.9 collective-permute-done.1.piece
  12.9 0.4 collective-permute-start.3
  13.3 4.9 %collective-permute-done.2.piece = bf16[512,384]{1,0:T(8,128)(2,1)S(1)} collective-permute-done((bf16[512,384]{1,0:T(8,128)(2,1)S(1)}, bf16[512,384]{1,0:T(8,128)(2,1)S(1)}, u32[]{:S(2)}, u32[]{:S(2)}) %collective-permute-start.2) | collective-permute-done | bytes 393248 | tf_op jit(solution)/shard_map/ppermute | solution.py:261
  18.1 3.3 %collective-permute-done.17 = bf16[384,768]{1,0:T(8,128)(2,1)S(1)} collective-permute-done((bf16[384,768]{1,0:T(8,128)(2,1)S(1)}, bf16[384,768]{1,0:T(8,128)(2,1)S(1)}, u32[]{:S(2)}, u32[]{:S(2)}) %collective-permute-start.17) | collective-permute-done | bytes 589856 | tf_op jit(solution)/shard_map/ppermute | solution.py:274
  21.6 1.3 %collective-permute-start.19 = (bf16[768,768]{1,0:T(8,128)(2,1)S(1)}, bf16[768,768]{1,0:T(8,128)(2,1)S(1)}, u32[]{:S(2)}, u32[]{:S(2)}) collective-permute-start(bf16[768,768]{1,0:T(8,128)(2,1)S(1)} %pad_maximum_fusion.2), channel_id=1, source_target_pairs={{0,48},{8,200},{16,32},{24,216},{32,16},{40,232},{48,0},{56,248},{... | collective-permute-start | bytes 3538952 | tf_op jit(solution)/shard_map/ppermute | solution.py:274
  22.9 1.5 %collective-permute-start.5 = (bf16[512,384]{1,0:T(8,128)(2,1)S(1)}, bf16[512,384]{1,0:T(8,128)(2,1)S(1)}, u32[]{:S(2)}, u32[]{:S(2)}) collective-permute-start(bf16[512,384]{1,0:T(8,128)(2,1)S(1)} %shard_map.66.refs_4_), channel_id=1, source_target_pairs={{0,1},{1,2},{2,3},{3,4},{4,5},{5,6},{6,7},{7,0},{8,15},{9,8},{10,9... | collective-permute-start | bytes 1179656 | tf_op jit(solution)/shard_map/ppermute | solution.py:261
  24.4 2.2 %collective-permute-done.4.piece = bf16[512,384]{1,0:T(8,128)(2,1)S(1)} collective-permute-done((bf16[512,384]{1,0:T(8,128)(2,1)S(1)}, bf16[512,384]{1,0:T(8,128)(2,1)S(1)}, u32[]{:S(2)}, u32[]{:S(2)}) %collective-permute-start.4) | collective-permute-done | bytes 393248 | tf_op jit(solution)/shard_map/ppermute | solution.py:261
  26.6 1.6 %collective-permute-start.6 = (bf16[512,384]{1,0:T(8,128)(2,1)S(1)}, bf16[512,384]{1,0:T(8,128)(2,1)S(1)}, u32[]{:S(2)}, u32[]{:S(2)}) collective-permute-start(bf16[512,384]{1,0:T(8,128)(2,1)S(1)} %shard_map.67.refs_5_), channel_id=1, source_target_pairs={{0,1},{1,2},{2,3},{3,4},{4,5},{5,6},{6,7},{7,0},{8,15},{9,8},{10,9... | collective-permute-start | bytes 1179656 | tf_op jit(solution)/shard_map/ppermute | solution.py:261
  28.1 2.7 %collective-permute-done.5.piece = bf16[512,384]{1,0:T(8,128)(2,1)S(1)} collective-permute-done((bf16[512,384]{1,0:T(8,128)(2,1)S(1)}, bf16[512,384]{1,0:T(8,128)(2,1)S(1)}, u32[]{:S(2)}, u32[]{:S(2)}) %collective-permute-start.5) | collective-permute-done | bytes 393248 | tf_op jit(solution)/shard_map/ppermute | solution.py:261
  30.8 2.1 %collective-permute-start.7 = (bf16[512,384]{1,0:T(8,128)(2,1)S(1)}, bf16[512,384]{1,0:T(8,128)(2,1)S(1)}, u32[]{:S(2)}, u32[]{:S(2)}) collective-permute-start(bf16[512,384]{1,0:T(8,128)(2,1)S(1)} %shard_map.68.refs_6_), channel_id=1, source_target_pairs={{0,1},{1,2},{2,3},{3,4},{4,5},{5,6},{6,7},{7,0},{8,15},{9,8},{10,9... | collective-permute-start | bytes 1179656 | tf_op jit(solution)/shard_map/ppermute | solution.py:261
  32.8 2.1 %collective-permute-done.6.piece = bf16[512,384]{1,0:T(8,128)(2,1)S(1)} collective-permute-done((bf16[512,384]{1,0:T(8,128)(2,1)S(1)}, bf16[512,384]{1,0:T(8,128)(2,1)S(1)}, u32[]{:S(2)}, u32[]{:S(2)}) %collective-permute-start.6) | collective-permute-done | bytes 393248 | tf_op jit(solution)/shard_map/ppermute | solution.py:261
  35.0 2.1 %collective-permute-start.8 = (bf16[512,384]{1,0:T(8,128)(2,1)S(1)}, bf16[512,384]{1,0:T(8,128)(2,1)S(1)}, u32[]{:S(2)}, u32[]{:S(2)}) collective-permute-start(bf16[512,384]{1,0:T(8,128)(2,1)S(1)} %shard_map.69.refs_7_), channel_id=1, source_target_pairs={{0,1},{1,2},{2,3},{3,4},{4,5},{5,6},{6,7},{7,0},{8,15},{9,8},{10,9... | collective-permute-start | bytes 1179656 | tf_op jit(solution)/shard_map/ppermute | solution.py:261
  37.1 1.2 collective-permute-done.19
  38.2 0.2 pad_maximum_fusion.1.refs_16_
  38.4 0.1 collective-permute-start.22
  38.5 0.7 collective-permute-done.7.piece
  39.2 2.1 %collective-permute-start.9 = (bf16[512,384]{1,0:T(8,128)(2,1)S(1)}, bf16[512,384]{1,0:T(8,128)(2,1)S(1)}, u32[]{:S(2)}, u32[]{:S(2)}) collective-permute-start(bf16[512,384]{1,0:T(8,128)(2,1)S(1)} %shard_map.70.refs_8_), channel_id=1, source_target_pairs={{0,1},{1,2},{2,3},{3,4},{4,5},{5,6},{6,7},{7,0},{8,15},{9,8},{10,9... | collective-permute-start | bytes 1179656 | tf_op jit(solution)/shard_map/ppermute | solution.py:261
  41.3 2.1 %collective-permute-done.8.piece = bf16[512,384]{1,0:T(8,128)(2,1)S(1)} collective-permute-done((bf16[512,384]{1,0:T(8,128)(2,1)S(1)}, bf16[512,384]{1,0:T(8,128)(2,1)S(1)}, u32[]{:S(2)}, u32[]{:S(2)}) %collective-permute-start.8) | collective-permute-done | bytes 393248 | tf_op jit(solution)/shard_map/ppermute | solution.py:261
  43.4 2.1 %collective-permute-start.10 = (bf16[512,384]{1,0:T(8,128)(2,1)S(1)}, bf16[512,384]{1,0:T(8,128)(2,1)S(1)}, u32[]{:S(2)}, u32[]{:S(2)}) collective-permute-start(bf16[512,384]{1,0:T(8,128)(2,1)S(1)} %shard_map.71.refs_9_), channel_id=1, source_target_pairs={{0,1},{1,2},{2,3},{3,4},{4,5},{5,6},{6,7},{7,0},{8,15},{9,8},{10,9... | collective-permute-start | bytes 1179656 | tf_op jit(solution)/shard_map/ppermute | solution.py:261
  45.5 2.1 %collective-permute-done.9.piece = bf16[512,384]{1,0:T(8,128)(2,1)S(1)} collective-permute-done((bf16[512,384]{1,0:T(8,128)(2,1)S(1)}, bf16[512,384]{1,0:T(8,128)(2,1)S(1)}, u32[]{:S(2)}, u32[]{:S(2)}) %collective-permute-start.9) | collective-permute-done | bytes 393248 | tf_op jit(solution)/shard_map/ppermute | solution.py:261
  47.6 2.1 %collective-permute-start.11 = (bf16[512,384]{1,0:T(8,128)(2,1)S(1)}, bf16[512,384]{1,0:T(8,128)(2,1)S(1)}, u32[]{:S(2)}, u32[]{:S(2)}) collective-permute-start(bf16[512,384]{1,0:T(8,128)(2,1)S(1)} %shard_map.72.refs_10_), channel_id=1, source_target_pairs={{0,1},{1,2},{2,3},{3,4},{4,5},{5,6},{6,7},{7,0},{8,15},{9,8},{10,9... | collective-permute-start | bytes 1179656 | tf_op jit(solution)/shard_map/ppermute | solution.py:261
  49.7 0.2 pad_maximum_fusion.refs_16_
  49.9 1.5 %collective-permute-start.21 = (bf16[1536,768]{1,0:T(8,128)(2,1)S(1)}, bf16[1536,768]{1,0:T(8,128)(2,1)S(1)}, u32[]{:S(2)}, u32[]{:S(2)}) collective-permute-start(bf16[1536,768]{1,0:T(8,128)(2,1)S(1)} %pad_maximum_fusion.refs_16_), channel_id=1, source_target_pairs={{0,64},{8,56},{16,80},{24,40},{32,96},{40,24},{48,112},{56,8},{64,... | collective-permute-start | bytes 7077896 | tf_op jit(solution)/shard_map/ppermute | solution.py:274
  51.4 0.1 collective-permute-done.10.piece
  51.5 2.4 %collective-permute-start.12 = (bf16[512,384]{1,0:T(8,128)(2,1)S(1)}, bf16[512,384]{1,0:T(8,128)(2,1)S(1)}, u32[]{:S(2)}, u32[]{:S(2)}) collective-permute-start(bf16[512,384]{1,0:T(8,128)(2,1)S(1)} %shard_map.73.refs_11_), channel_id=1, source_target_pairs={{0,1},{1,2},{2,3},{3,4},{4,5},{5,6},{6,7},{7,0},{8,15},{9,8},{10,9... | collective-permute-start | bytes 1179656 | tf_op jit(solution)/shard_map/ppermute | solution.py:261
  53.9 2.1 %collective-permute-done.11.piece = bf16[512,384]{1,0:T(8,128)(2,1)S(1)} collective-permute-done((bf16[512,384]{1,0:T(8,128)(2,1)S(1)}, bf16[512,384]{1,0:T(8,128)(2,1)S(1)}, u32[]{:S(2)}, u32[]{:S(2)}) %collective-permute-start.11) | collective-permute-done | bytes 393248 | tf_op jit(solution)/shard_map/ppermute | solution.py:261
  56.1 2.1 %collective-permute-start.13 = (bf16[512,384]{1,0:T(8,128)(2,1)S(1)}, bf16[512,384]{1,0:T(8,128)(2,1)S(1)}, u32[]{:S(2)}, u32[]{:S(2)}) collective-permute-start(bf16[512,384]{1,0:T(8,128)(2,1)S(1)} %shard_map.74.refs_12_), channel_id=1, source_target_pairs={{0,1},{1,2},{2,3},{3,4},{4,5},{5,6},{6,7},{7,0},{8,15},{9,8},{10,9... | collective-permute-start | bytes 1179656 | tf_op jit(solution)/shard_map/ppermute | solution.py:261
  58.1 2.1 %collective-permute-done.12.piece = bf16[512,384]{1,0:T(8,128)(2,1)S(1)} collective-permute-done((bf16[512,384]{1,0:T(8,128)(2,1)S(1)}, bf16[512,384]{1,0:T(8,128)(2,1)S(1)}, u32[]{:S(2)}, u32[]{:S(2)}) %collective-permute-start.12) | collective-permute-done | bytes 393248 | tf_op jit(solution)/shard_map/ppermute | solution.py:261
  60.3 2.1 %collective-permute-start.14 = (bf16[512,384]{1,0:T(8,128)(2,1)S(1)}, bf16[512,384]{1,0:T(8,128)(2,1)S(1)}, u32[]{:S(2)}, u32[]{:S(2)}) collective-permute-start(bf16[512,384]{1,0:T(8,128)(2,1)S(1)} %shard_map.75.refs_13_), channel_id=1, source_target_pairs={{0,1},{1,2},{2,3},{3,4},{4,5},{5,6},{6,7},{7,0},{8,15},{9,8},{10,9... | collective-permute-start | bytes 1179656 | tf_op jit(solution)/shard_map/ppermute | solution.py:261
  62.3 0.7 dynamic-slice_bitcast_fusion.info
  63.0 1.5 %collective-permute-done.13.piece = bf16[512,384]{1,0:T(8,128)(2,1)S(1)} collective-permute-done((bf16[512,384]{1,0:T(8,128)(2,1)S(1)}, bf16[512,384]{1,0:T(8,128)(2,1)S(1)}, u32[]{:S(2)}, u32[]{:S(2)}) %collective-permute-start.13) | collective-permute-done | bytes 393248 | tf_op jit(solution)/shard_map/ppermute | solution.py:261
  64.5 4.2 %collective-permute-done.14.piece = bf16[512,384]{1,0:T(8,128)(2,1)S(1)} collective-permute-done((bf16[512,384]{1,0:T(8,128)(2,1)S(1)}, bf16[512,384]{1,0:T(8,128)(2,1)S(1)}, u32[]{:S(2)}, u32[]{:S(2)}) %collective-permute-start.14) | collective-permute-done | bytes 393248 | tf_op jit(solution)/shard_map/ppermute | solution.py:261
  68.7 0.4 collective-permute-done.22.refs_17_
  69.1 4.0 %shard_map.79 = bf16[1024,512]{1,0:T(8,128)(2,1)S(1)} custom-call(s32[37]{0:T(128)S(1)} %dynamic-slice_bitcast_fusion.info, bf16[512,384]{1,0:T(8,128)(2,1)S(1)} %get-tuple-element.42.refs_0_, bf16[512,384]{1,0:T(8,128)(2,1)S(1)} %collective-permute-done.refs_1_, bf16[512,384]{1,0:T(8,128)(2,1)S(1)} %shard_map.64.refs_2_, ...), custom_call_target="tpu_custom_call" | custom-call | flops 3221225472 | bytes 1048576 | tf_op jit(solution)/shard_map/pallas_call | solution.py:120
  73.1 14.2 %collective-permute-start.23 = (bf16[1024,512]{1,0:T(8,128)(2,1)S(1)}, bf16[1024,512]{1,0:T(8,128)(2,1)S(1)}, u32[]{:S(2)}, u32[]{:S(2)}) collective-permute-start(bf16[1024,512]{1,0:T(8,128)(2,1)S(1)} %shard_map.79), channel_id=1, source_target_pairs={{0,8},{8,0},{16,24},{24,16},{32,40},{40,32},{48,56},{56,48},{64,72... | collective-permute-start | bytes 3145736 | tf_op jit(solution)/shard_map/ppermute | solution.py:294
  87.3 4.0 %shard_map.78.mine = f32[1024,512]{1,0:T(8,128)S(1)} custom-call(s32[37]{0:T(128)S(1)} %dynamic-slice_bitcast_fusion.info, bf16[512,384]{1,0:T(8,128)(2,1)S(1)} %get-tuple-element.42.refs_0_, bf16[512,384]{1,0:T(8,128)(2,1)S(1)} %collective-permute-done.refs_1_, bf16[512,384]{1,0:T(8,128)(2,1)S(1)} %shard_map.64.refs_2_, ...), custom_call_target="tpu_custom_call" | custom-call | flops 3221225472 | bytes 1048576 | tf_op jit(solution)/shard_map/pallas_call | solution.py:120
  91.3 0.8 shard_map.80
  92.2 0.3 collective-permute-start.25
  92.5 2.4 %shard_map.82 = bf16[1024,256]{1,0:T(8,128)(2,1)S(1)} custom-call(s32[37]{0:T(128)S(1)} %dynamic-slice_bitcast_fusion.info, bf16[512,384]{1,0:T(8,128)(2,1)S(1)} %get-tuple-element.42.refs_0_, bf16[512,384]{1,0:T(8,128)(2,1)S(1)} %collective-permute-done.refs_1_, bf16[512,384]{1,0:T(8,128)(2,1)S(1)} %shard_map.64.refs_2_, ...), custom_call_target="tpu_custom_call" | custom-call | flops 1610612736 | bytes 1048576 | tf_op jit(solution)/shard_map/pallas_call | solution.py:120
  94.9 0.7 collective-permute-done.25.got_0
  95.6 0.2 collective-permute-start.26
  95.9 8.0 %collective-permute-start.24 = (bf16[1024,256]{1,0:T(8,128)(2,1)S(1)}, bf16[1024,256]{1,0:T(8,128)(2,1)S(1)}, u32[]{:S(2)}, u32[]{:S(2)}) collective-permute-start(bf16[1024,256]{1,0:T(8,128)(2,1)S(1)} %shard_map.82), channel_id=1, source_target_pairs={{0,8},{8,0},{16,24},{24,16},{32,40},{40,32},{48,56},{56,48},{64,72... | collective-permute-start | bytes 1572872 | tf_op jit(solution)/shard_map/ppermute | solution.py:299
  103.9 1.8 %collective-permute-start.27 = (bf16[2,128,128]{2,1,0:T(8,128)(2,1)S(1)}, bf16[2,128,128]{2,1,0:T(8,128)(2,1)S(1)}, u32[]{:S(2)}, u32[]{:S(2)}) collective-permute-start(bf16[2,128,128]{2,1,0:T(8,128)(2,1)S(1)} %add_convert_fusion.1), channel_id=1, source_target_pairs={{0,64},{8,72},{16,80},{24,88},{32,96},{40,104},{48,112},{56,120},{... | collective-permute-start | bytes 196616 | tf_op jit(solution)/shard_map/ppermute | solution.py:309
  105.7 2.4 %shard_map.81.mine = f32[1024,256]{1,0:T(8,128)S(1)} custom-call(s32[37]{0:T(128)S(1)} %dynamic-slice_bitcast_fusion.info, bf16[512,384]{1,0:T(8,128)(2,1)S(1)} %get-tuple-element.42.refs_0_, bf16[512,384]{1,0:T(8,128)(2,1)S(1)} %collective-permute-done.refs_1_, bf16[512,384]{1,0:T(8,128)(2,1)S(1)} %shard_map.64.refs_2_, ...), custom_call_target="tpu_custom_call" | custom-call | flops 1610612736 | bytes 1048576 | tf_op jit(solution)/shard_map/pallas_call | solution.py:120
  108.1 0.7 collective-permute-start.28
  108.8 0.9 shard_map.83
  109.8 2.8 %collective-permute-done.28.got_3 = bf16[2,128,128]{2,1,0:T(8,128)(2,1)S(1)} collective-permute-done((bf16[2,128,128]{2,1,0:T(8,128)(2,1)S(1)}, bf16[2,128,128]{2,1,0:T(8,128)(2,1)S(1)}, u32[]{:S(2)}, u32[]{:S(2)}) %collective-permute-start.28) | collective-permute-done | bytes 65568 | tf_op jit(solution)/shard_map/ppermute | solution.py:309
  112.6 0.9 shard_map.85
  113.5 6.5 %collective-permute-start.29 = (bf16[512,256]{1,0:T(8,128)(2,1)S(1)}, bf16[512,256]{1,0:T(8,128)(2,1)S(1)}, u32[]{:S(2)}, u32[]{:S(2)}) collective-permute-start(bf16[512,256]{1,0:T(8,128)(2,1)S(1)} %shard_map.85), channel_id=1, source_target_pairs={{0,8},{8,0},{16,24},{24,16},{32,40},{40,32},{48,56},{56,48},{64,72... | collective-permute-start | bytes 786440 | tf_op jit(solution)/shard_map/ppermute | solution.py:313
  120.0 0.9 shard_map.84
  121.0 0.2 collective-permute-done.29
  121.2 0.8 pad_maximum_fusion.6
  (39 shorter events, 0.5 us)
Async XLA Ops:
  0.0 5.0 %copy-start.1 = (bf16[512,768]{1,0:T(8,128)(2,1)S(1)}, bf16[512,768]{1,0:T(8,128)(2,1)}, u32[]{:S(2)}) copy-start(bf16[512,768]{1,0:T(8,128)(2,1)} %param.6) | copy-start | bytes 2359300
  2.2 7.2 %collective-permute-start.16 = (bf16[192,768]{1,0:T(8,128)(2,1)S(1)}, bf16[192,768]{1,0:T(8,128)(2,1)S(1)}, u32[]{:S(2)}, u32[]{:S(2)}) collective-permute-start(bf16[192,768]{1,0:T(8,128)(2,1)S(1)} %get-tuple-element.47), channel_id=1, source_target_pairs={{0,48},{8,200},{16,32},{24,216},{32,16},{40,232},{48,0},{56,248},{... | collective-permute-start | bytes 884744 | tf_op jit(solution)/shard_map/ppermute | solution.py:274
  5.0 5.9 %collective-permute-start.15 = (bf16[192,768]{1,0:T(8,128)(2,1)S(1)}, bf16[192,768]{1,0:T(8,128)(2,1)S(1)}, u32[]{:S(2)}, u32[]{:S(2)}) collective-permute-start(bf16[192,768]{1,0:T(8,128)(2,1)S(1)} %get-tuple-element.48), channel_id=1, source_target_pairs={{0,16},{8,72},{16,0},{24,88},{32,48},{40,104},{48,32},{56,120},{64... | collective-permute-start | bytes 884744 | tf_op jit(solution)/shard_map/ppermute | solution.py:274
  5.6 5.3 %collective-permute-start = (bf16[512,384]{1,0:T(8,128)(2,1)S(1)}, bf16[512,384]{1,0:T(8,128)(2,1)S(1)}, u32[]{:S(2)}, u32[]{:S(2)}) collective-permute-start(bf16[512,384]{1,0:T(8,128)(2,1)S(1)} %get-tuple-element.41), channel_id=1, source_target_pairs={{0,8},{8,0},{16,24},{24,16},{32,40},{40,32},{48,56},{56,48},{64,72... | collective-permute-start | bytes 1179656 | tf_op jit(solution)/shard_map/ppermute | solution.py:257
  5.7 7.2 %collective-permute-start.1 = (bf16[512,384]{1,0:T(8,128)(2,1)S(1)}, bf16[512,384]{1,0:T(8,128)(2,1)S(1)}, u32[]{:S(2)}, u32[]{:S(2)}) collective-permute-start(bf16[512,384]{1,0:T(8,128)(2,1)S(1)} %get-tuple-element.42.refs_0_), channel_id=1, source_target_pairs={{0,1},{1,2},{2,3},{3,4},{4,5},{5,6},{6,7},{7,0},{8,15},{9,8},{10,9... | collective-permute-start | bytes 1179656 | tf_op jit(solution)/shard_map/ppermute | solution.py:261
  11.0 7.2 %collective-permute-start.2 = (bf16[512,384]{1,0:T(8,128)(2,1)S(1)}, bf16[512,384]{1,0:T(8,128)(2,1)S(1)}, u32[]{:S(2)}, u32[]{:S(2)}) collective-permute-start(bf16[512,384]{1,0:T(8,128)(2,1)S(1)} %collective-permute-done.refs_1_), channel_id=1, source_target_pairs={{0,1},{1,2},{2,3},{3,4},{4,5},{5,6},{6,7},{7,0},{8,15},{9,8},{10,9... | collective-permute-start | bytes 1179656 | tf_op jit(solution)/shard_map/ppermute | solution.py:261
  11.1 10.3 %collective-permute-start.17 = (bf16[384,768]{1,0:T(8,128)(2,1)S(1)}, bf16[384,768]{1,0:T(8,128)(2,1)S(1)}, u32[]{:S(2)}, u32[]{:S(2)}) collective-permute-start(bf16[384,768]{1,0:T(8,128)(2,1)S(1)} %pad_maximum_fusion.4), channel_id=1, source_target_pairs={{0,64},{8,56},{16,80},{24,40},{32,96},{40,24},{48,112},{56,8},{64,... | collective-permute-start | bytes 1769480 | tf_op jit(solution)/shard_map/ppermute | solution.py:274
  11.4 10.0 %collective-permute-start.18 = (bf16[384,768]{1,0:T(8,128)(2,1)S(1)}, bf16[384,768]{1,0:T(8,128)(2,1)S(1)}, u32[]{:S(2)}, u32[]{:S(2)}) collective-permute-start(bf16[384,768]{1,0:T(8,128)(2,1)S(1)} %pad_maximum_fusion.5), channel_id=1, source_target_pairs={{0,192},{8,24},{16,208},{24,8},{32,224},{40,56},{48,240},{56,40},{... | collective-permute-start | bytes 1769480 | tf_op jit(solution)/shard_map/ppermute | solution.py:274
  12.9 10.0 %collective-permute-start.3 = (bf16[512,384]{1,0:T(8,128)(2,1)S(1)}, bf16[512,384]{1,0:T(8,128)(2,1)S(1)}, u32[]{:S(2)}, u32[]{:S(2)}) collective-permute-start(bf16[512,384]{1,0:T(8,128)(2,1)S(1)} %shard_map.64.refs_2_), channel_id=1, source_target_pairs={{0,1},{1,2},{2,3},{3,4},{4,5},{5,6},{6,7},{7,0},{8,15},{9,8},{10,9... | collective-permute-start | bytes 1179656 | tf_op jit(solution)/shard_map/ppermute | solution.py:261
  18.1 8.4 %collective-permute-start.4 = (bf16[512,384]{1,0:T(8,128)(2,1)S(1)}, bf16[512,384]{1,0:T(8,128)(2,1)S(1)}, u32[]{:S(2)}, u32[]{:S(2)}) collective-permute-start(bf16[512,384]{1,0:T(8,128)(2,1)S(1)} %shard_map.65.refs_3_), channel_id=1, source_target_pairs={{0,1},{1,2},{2,3},{3,4},{4,5},{5,6},{6,7},{7,0},{8,15},{9,8},{10,9... | collective-permute-start | bytes 1179656 | tf_op jit(solution)/shard_map/ppermute | solution.py:261
  21.6 16.6 %collective-permute-start.19 = (bf16[768,768]{1,0:T(8,128)(2,1)S(1)}, bf16[768,768]{1,0:T(8,128)(2,1)S(1)}, u32[]{:S(2)}, u32[]{:S(2)}) collective-permute-start(bf16[768,768]{1,0:T(8,128)(2,1)S(1)} %pad_maximum_fusion.2), channel_id=1, source_target_pairs={{0,48},{8,200},{16,32},{24,216},{32,16},{40,232},{48,0},{56,248},{... | collective-permute-start | bytes 3538952 | tf_op jit(solution)/shard_map/ppermute | solution.py:274
  22.9 15.3 %collective-permute-start.20 = (bf16[768,768]{1,0:T(8,128)(2,1)S(1)}, bf16[768,768]{1,0:T(8,128)(2,1)S(1)}, u32[]{:S(2)}, u32[]{:S(2)}) collective-permute-start(bf16[768,768]{1,0:T(8,128)(2,1)S(1)} %pad_maximum_fusion.3), channel_id=1, source_target_pairs={{0,16},{8,72},{16,0},{24,88},{32,48},{40,104},{48,32},{56,120},{64... | collective-permute-start | bytes 3538952 | tf_op jit(solution)/shard_map/ppermute | solution.py:274
  22.9 7.9 %collective-permute-start.5 = (bf16[512,384]{1,0:T(8,128)(2,1)S(1)}, bf16[512,384]{1,0:T(8,128)(2,1)S(1)}, u32[]{:S(2)}, u32[]{:S(2)}) collective-permute-start(bf16[512,384]{1,0:T(8,128)(2,1)S(1)} %shard_map.66.refs_4_), channel_id=1, source_target_pairs={{0,1},{1,2},{2,3},{3,4},{4,5},{5,6},{6,7},{7,0},{8,15},{9,8},{10,9... | collective-permute-start | bytes 1179656 | tf_op jit(solution)/shard_map/ppermute | solution.py:261
  26.6 8.4 %collective-permute-start.6 = (bf16[512,384]{1,0:T(8,128)(2,1)S(1)}, bf16[512,384]{1,0:T(8,128)(2,1)S(1)}, u32[]{:S(2)}, u32[]{:S(2)}) collective-permute-start(bf16[512,384]{1,0:T(8,128)(2,1)S(1)} %shard_map.67.refs_5_), channel_id=1, source_target_pairs={{0,1},{1,2},{2,3},{3,4},{4,5},{5,6},{6,7},{7,0},{8,15},{9,8},{10,9... | collective-permute-start | bytes 1179656 | tf_op jit(solution)/shard_map/ppermute | solution.py:261
  30.8 8.4 %collective-permute-start.7 = (bf16[512,384]{1,0:T(8,128)(2,1)S(1)}, bf16[512,384]{1,0:T(8,128)(2,1)S(1)}, u32[]{:S(2)}, u32[]{:S(2)}) collective-permute-start(bf16[512,384]{1,0:T(8,128)(2,1)S(1)} %shard_map.68.refs_6_), channel_id=1, source_target_pairs={{0,1},{1,2},{2,3},{3,4},{4,5},{5,6},{6,7},{7,0},{8,15},{9,8},{10,9... | collective-permute-start | bytes 1179656 | tf_op jit(solution)/shard_map/ppermute | solution.py:261
  35.0 8.4 %collective-permute-start.8 = (bf16[512,384]{1,0:T(8,128)(2,1)S(1)}, bf16[512,384]{1,0:T(8,128)(2,1)S(1)}, u32[]{:S(2)}, u32[]{:S(2)}) collective-permute-start(bf16[512,384]{1,0:T(8,128)(2,1)S(1)} %shard_map.69.refs_7_), channel_id=1, source_target_pairs={{0,1},{1,2},{2,3},{3,4},{4,5},{5,6},{6,7},{7,0},{8,15},{9,8},{10,9... | collective-permute-start | bytes 1179656 | tf_op jit(solution)/shard_map/ppermute | solution.py:261
  38.4 30.7 %collective-permute-start.22 = (bf16[1536,768]{1,0:T(8,128)(2,1)S(1)}, bf16[1536,768]{1,0:T(8,128)(2,1)S(1)}, u32[]{:S(2)}, u32[]{:S(2)}) collective-permute-start(bf16[1536,768]{1,0:T(8,128)(2,1)S(1)} %pad_maximum_fusion.1.refs_16_), channel_id=1, source_target_pairs={{0,192},{8,24},{16,208},{24,8},{32,224},{40,56},{48,240},{56,40},{... | collective-permute-start | bytes 7077896 | tf_op jit(solution)/shard_map/ppermute | solution.py:274
  39.2 8.4 %collective-permute-start.9 = (bf16[512,384]{1,0:T(8,128)(2,1)S(1)}, bf16[512,384]{1,0:T(8,128)(2,1)S(1)}, u32[]{:S(2)}, u32[]{:S(2)}) collective-permute-start(bf16[512,384]{1,0:T(8,128)(2,1)S(1)} %shard_map.70.refs_8_), channel_id=1, source_target_pairs={{0,1},{1,2},{2,3},{3,4},{4,5},{5,6},{6,7},{7,0},{8,15},{9,8},{10,9... | collective-permute-start | bytes 1179656 | tf_op jit(solution)/shard_map/ppermute | solution.py:261
  43.4 8.1 %collective-permute-start.10 = (bf16[512,384]{1,0:T(8,128)(2,1)S(1)}, bf16[512,384]{1,0:T(8,128)(2,1)S(1)}, u32[]{:S(2)}, u32[]{:S(2)}) collective-permute-start(bf16[512,384]{1,0:T(8,128)(2,1)S(1)} %shard_map.71.refs_9_), channel_id=1, source_target_pairs={{0,1},{1,2},{2,3},{3,4},{4,5},{5,6},{6,7},{7,0},{8,15},{9,8},{10,9... | collective-permute-start | bytes 1179656 | tf_op jit(solution)/shard_map/ppermute | solution.py:261
  47.6 8.4 %collective-permute-start.11 = (bf16[512,384]{1,0:T(8,128)(2,1)S(1)}, bf16[512,384]{1,0:T(8,128)(2,1)S(1)}, u32[]{:S(2)}, u32[]{:S(2)}) collective-permute-start(bf16[512,384]{1,0:T(8,128)(2,1)S(1)} %shard_map.72.refs_10_), channel_id=1, source_target_pairs={{0,1},{1,2},{2,3},{3,4},{4,5},{5,6},{6,7},{7,0},{8,15},{9,8},{10,9... | collective-permute-start | bytes 1179656 | tf_op jit(solution)/shard_map/ppermute | solution.py:261
  49.9 37.5 %collective-permute-start.21 = (bf16[1536,768]{1,0:T(8,128)(2,1)S(1)}, bf16[1536,768]{1,0:T(8,128)(2,1)S(1)}, u32[]{:S(2)}, u32[]{:S(2)}) collective-permute-start(bf16[1536,768]{1,0:T(8,128)(2,1)S(1)} %pad_maximum_fusion.refs_16_), channel_id=1, source_target_pairs={{0,64},{8,56},{16,80},{24,40},{32,96},{40,24},{48,112},{56,8},{64,... | collective-permute-start | bytes 7077896 | tf_op jit(solution)/shard_map/ppermute | solution.py:274
  51.5 8.7 %collective-permute-start.12 = (bf16[512,384]{1,0:T(8,128)(2,1)S(1)}, bf16[512,384]{1,0:T(8,128)(2,1)S(1)}, u32[]{:S(2)}, u32[]{:S(2)}) collective-permute-start(bf16[512,384]{1,0:T(8,128)(2,1)S(1)} %shard_map.73.refs_11_), channel_id=1, source_target_pairs={{0,1},{1,2},{2,3},{3,4},{4,5},{5,6},{6,7},{7,0},{8,15},{9,8},{10,9... | collective-permute-start | bytes 1179656 | tf_op jit(solution)/shard_map/ppermute | solution.py:261
  56.1 8.4 %collective-permute-start.13 = (bf16[512,384]{1,0:T(8,128)(2,1)S(1)}, bf16[512,384]{1,0:T(8,128)(2,1)S(1)}, u32[]{:S(2)}, u32[]{:S(2)}) collective-permute-start(bf16[512,384]{1,0:T(8,128)(2,1)S(1)} %shard_map.74.refs_12_), channel_id=1, source_target_pairs={{0,1},{1,2},{2,3},{3,4},{4,5},{5,6},{6,7},{7,0},{8,15},{9,8},{10,9... | collective-permute-start | bytes 1179656 | tf_op jit(solution)/shard_map/ppermute | solution.py:261
  60.3 8.4 %collective-permute-start.14 = (bf16[512,384]{1,0:T(8,128)(2,1)S(1)}, bf16[512,384]{1,0:T(8,128)(2,1)S(1)}, u32[]{:S(2)}, u32[]{:S(2)}) collective-permute-start(bf16[512,384]{1,0:T(8,128)(2,1)S(1)} %shard_map.75.refs_13_), channel_id=1, source_target_pairs={{0,1},{1,2},{2,3},{3,4},{4,5},{5,6},{6,7},{7,0},{8,15},{9,8},{10,9... | collective-permute-start | bytes 1179656 | tf_op jit(solution)/shard_map/ppermute | solution.py:261
  73.1 18.2 %collective-permute-start.23 = (bf16[1024,512]{1,0:T(8,128)(2,1)S(1)}, bf16[1024,512]{1,0:T(8,128)(2,1)S(1)}, u32[]{:S(2)}, u32[]{:S(2)}) collective-permute-start(bf16[1024,512]{1,0:T(8,128)(2,1)S(1)} %shard_map.79), channel_id=1, source_target_pairs={{0,8},{8,0},{16,24},{24,16},{32,40},{40,32},{48,56},{56,48},{64,72... | collective-permute-start | bytes 3145736 | tf_op jit(solution)/shard_map/ppermute | solution.py:294
  92.2 3.4 %collective-permute-start.25 = (bf16[2,128,128]{2,1,0:T(8,128)(2,1)S(1)}, bf16[2,128,128]{2,1,0:T(8,128)(2,1)S(1)}, u32[]{:S(2)}, u32[]{:S(2)}) collective-permute-start(bf16[2,128,128]{2,1,0:T(8,128)(2,1)S(1)} %get-tuple-element.32), channel_id=1, source_target_pairs={{0,16},{8,24},{16,0},{24,8},{32,48},{40,56},{48,32},{56,40},{64,80... | collective-permute-start | bytes 196616 | tf_op jit(solution)/shard_map/ppermute | solution.py:309
  95.6 8.2 %collective-permute-start.26 = (bf16[2,128,128]{2,1,0:T(8,128)(2,1)S(1)}, bf16[2,128,128]{2,1,0:T(8,128)(2,1)S(1)}, u32[]{:S(2)}, u32[]{:S(2)}) collective-permute-start(bf16[2,128,128]{2,1,0:T(8,128)(2,1)S(1)} %add_convert_fusion.2), channel_id=1, source_target_pairs={{0,48},{8,56},{16,32},{24,40},{32,16},{40,24},{48,0},{56,8},{64,11... | collective-permute-start | bytes 196616 | tf_op jit(solution)/shard_map/ppermute | solution.py:309
  95.9 13.0 %collective-permute-start.24 = (bf16[1024,256]{1,0:T(8,128)(2,1)S(1)}, bf16[1024,256]{1,0:T(8,128)(2,1)S(1)}, u32[]{:S(2)}, u32[]{:S(2)}) collective-permute-start(bf16[1024,256]{1,0:T(8,128)(2,1)S(1)} %shard_map.82), channel_id=1, source_target_pairs={{0,8},{8,0},{16,24},{24,16},{32,40},{40,32},{48,56},{56,48},{64,72... | collective-permute-start | bytes 1572872 | tf_op jit(solution)/shard_map/ppermute | solution.py:299
  103.9 4.2 %collective-permute-start.27 = (bf16[2,128,128]{2,1,0:T(8,128)(2,1)S(1)}, bf16[2,128,128]{2,1,0:T(8,128)(2,1)S(1)}, u32[]{:S(2)}, u32[]{:S(2)}) collective-permute-start(bf16[2,128,128]{2,1,0:T(8,128)(2,1)S(1)} %add_convert_fusion.1), channel_id=1, source_target_pairs={{0,64},{8,72},{16,80},{24,88},{32,96},{40,104},{48,112},{56,120},{... | collective-permute-start | bytes 196616 | tf_op jit(solution)/shard_map/ppermute | solution.py:309
  108.1 4.5 %copy-start = (f32[512]{0:T(512)S(1)}, f32[512]{0:T(512)}, u32[]{:S(2)}) copy-start(f32[512]{0:T(512)} %param.10) | copy-start | bytes 6148
  108.1 4.4 %collective-permute-start.28 = (bf16[2,128,128]{2,1,0:T(8,128)(2,1)S(1)}, bf16[2,128,128]{2,1,0:T(8,128)(2,1)S(1)}, u32[]{:S(2)}, u32[]{:S(2)}) collective-permute-start(bf16[2,128,128]{2,1,0:T(8,128)(2,1)S(1)} %add_convert_fusion), channel_id=1, source_target_pairs={{0,192},{8,200},{16,208},{24,216},{32,224},{40,232},{48,240},{56,2... | collective-permute-start | bytes 196616 | tf_op jit(solution)/shard_map/ppermute | solution.py:309
  113.5 7.7 %collective-permute-start.29 = (bf16[512,256]{1,0:T(8,128)(2,1)S(1)}, bf16[512,256]{1,0:T(8,128)(2,1)S(1)}, u32[]{:S(2)}, u32[]{:S(2)}) collective-permute-start(bf16[512,256]{1,0:T(8,128)(2,1)S(1)} %shard_map.85), channel_id=1, source_target_pairs={{0,8},{8,0},{16,24},{24,16},{32,40},{40,32},{48,56},{56,48},{64,72... | collective-permute-start | bytes 786440 | tf_op jit(solution)/shard_map/ppermute | solution.py:313

commit v7 on v6

--- a/solution.py
+++ b/solution.py
@@ -246,7 +246,7 @@
         out_specs=ANY,
         input_output_aliases={0: 0},
         compiler_params=pltpu.CompilerParams(vmem_limit_bytes=2**20),
-        cost_estimate=pl.CostEstimate(flops=2250000000, bytes_accessed=0, transcendentals=0),
+        cost_estimate=pl.CostEstimate(flops=2500000000, bytes_accessed=0, transcendentals=0),
     )(piece)
 
 
@@ -269,7 +269,6 @@
     got = [None, None]
     for step in range(4):
         if step:
-            got = lax.optimization_barrier(tuple(got))
             streams = [jnp.concatenate(pair, axis=0) for pair in zip(streams, got)]
         got = [lax.ppermute(streams[j], "seq", cube_pairs(j, step)) for j in range(2)]
     blocks = [[streams[j], got[j]] for j in range(2)]
@@ -290,7 +289,7 @@
     halves = [jnp.where(core == 0, high, low), jnp.where(core == 0, low, high)]
     pieces, blocks = gather(tokens, halves, core)
 
-    kv_theirs = product(info, pieces, blocks, 0, 0, 2 * HALF)
+    kv_theirs = product(after(info, blocks[1][1]), pieces, blocks, 0, 0, 2 * HALF)
     kv_got = lax.ppermute(kv_theirs, "seq", SWAP)
     kv_mine = product(info, pieces, blocks, 1, 0, 2 * HALF)
     key, value, within, total = pair_states(kv_mine, kv_got)

time: 122 us -> 114 us (0.934)
  the two profiles are of different devices: /device:TPU:71 before, /device:TPU:1 now
where the time goes in v7:
time: 114 us; the launch traced here: 113 us
  starting transfers between devices  72.4 us (64%)
  waiting for transfers between devices  20.1 us (18%)
  Pallas kernels  16.4 us (14%)
  local copies, waits for them, and re-layouts  2.29 us (2%)
  other arithmetic  1.91 us (2%)
    ppermute x14, starting transfers between devices, pass_on(): return lax.ppermute(piece, ('seq', 'head'), ring)  43.8 us
    ppermute x14, waiting for transfers between devices, pass_on(): return lax.ppermute(piece, ('seq', 'head'), ring)  15.2 us
    pallas_call x4, Pallas kernels, product(): pl.pallas_call(functools.partial(product_kernel, mine, low, high), out_sh...  12.8 us
    ppermute x8, starting transfers between devices, gather(): lax.ppermute(streams[j], 'seq', cube_pairs(j, step))  7.92 us
    ppermute x1, starting transfers between devices, local(): kv_got = lax.ppermute(kv_theirs, 'seq', SWAP)  7.48 us
    ppermute x4, waiting for transfers between devices, local(): got.append(lax.ppermute(group, 'seq', exchange_pairs(dim)))  4.64 us
    ppermute x4, starting transfers between devices, local(): got.append(lax.ppermute(group, 'seq', exchange_pairs(dim)))  4.51 us
    ppermute x1, starting transfers between devices, local(): out_got = lax.ppermute(finish(False, *last), 'seq', SWAP)  4.34 us
  transfers between devices with their start and end apart: 30, of which 16 were waited for; matrix products, arithmetic and copies ran while one was open for 1% of the time, Pallas kernels for 9%

profile of v7, /device:TPU:1, one launch (start us, length us, event | category | flops | bytes accessed | tf_op | source)
XLA Modules:
  0.0 113.5 jit_solution(16017155748336372539)
XLA Ops:
  0.0 1.5 %fusion = (bf16[512,192]{1,0:T(8,128)(2,1)S(1)}, bf16[512,192]{1,0:T(8,128)(2,1)S(1)}, bf16[512,192]{1,0:T(8,128)(2,1)S(1)}, bf16[512,192]{1,0:T(8,128)(2,1)S(1)}) fusion(bf16[512,768]{1,0:T(8,128)(2,1)} %param.6), kind=kLoop, calls=%fused_computation.21 | loop fusion | bytes 1572864 | tf_op jit(solution)/shard_map/slice | solution.py:254
  1.6 0.3 broadcast_select_fusion
  1.9 3.3 %collective-permute-start = (bf16[512,384]{1,0:T(8,128)(2,1)S(1)}, bf16[512,384]{1,0:T(8,128)(2,1)S(1)}, u32[]{:S(2)}, u32[]{:S(2)}) collective-permute-start(bf16[512,384]{1,0:T(8,128)(2,1)S(1)} %get-tuple-element.31), channel_id=1, source_target_pairs={{0,8},{8,0},{16,24},{24,16},{32,40},{40,32},{48,56},{56,48},{64,72... | collective-permute-start | bytes 1179656 | tf_op jit(solution)/shard_map/ppermute | solution.py:257
  5.3 0.1 broadcast_select_fusion.2
  5.4 1.1 collective-permute-start.15
  6.5 5.6 %collective-permute-start.1 = (bf16[512,384]{1,0:T(8,128)(2,1)S(1)}, bf16[512,384]{1,0:T(8,128)(2,1)S(1)}, u32[]{:S(2)}, u32[]{:S(2)}) collective-permute-start(bf16[512,384]{1,0:T(8,128)(2,1)S(1)} %get-tuple-element.32.refs_0_), channel_id=1, source_target_pairs={{0,1},{1,2},{2,3},{3,4},{4,5},{5,6},{6,7},{7,0},{8,15},{9,8},{10,9... | collective-permute-start | bytes 1179656 | tf_op jit(solution)/shard_map/ppermute | solution.py:261
  12.1 0.0 collective-permute-done.refs_1_
  12.1 0.7 collective-permute-start.2
  12.9 1.3 %collective-permute-start.16 = (bf16[384,768]{1,0:T(8,128)(2,1)S(1)}, bf16[384,768]{1,0:T(8,128)(2,1)S(1)}, u32[]{:S(2)}, u32[]{:S(2)}) collective-permute-start(bf16[384,768]{1,0:T(8,128)(2,1)S(1)} %pad_maximum_fusion.4), channel_id=1, source_target_pairs={{0,192},{8,24},{16,208},{24,8},{32,224},{40,56},{48,240},{56,40},{... | collective-permute-start | bytes 1769480 | tf_op jit(solution)/shard_map/ppermute | solution.py:273
  14.2 1.9 %collective-permute-start.20 = (bf16[384,768]{1,0:T(8,128)(2,1)S(1)}, bf16[384,768]{1,0:T(8,128)(2,1)S(1)}, u32[]{:S(2)}, u32[]{:S(2)}) collective-permute-start(bf16[384,768]{1,0:T(8,128)(2,1)S(1)} %pad_maximum_fusion.5), channel_id=1, source_target_pairs={{0,64},{8,56},{16,80},{24,40},{32,96},{40,24},{48,112},{56,8},{64,... | collective-permute-start | bytes 1769480 | tf_op jit(solution)/shard_map/ppermute | solution.py:273
  16.1 0.7 collective-permute-done.1.piece
  16.8 3.8 %collective-permute-start.3 = (bf16[512,384]{1,0:T(8,128)(2,1)S(1)}, bf16[512,384]{1,0:T(8,128)(2,1)S(1)}, u32[]{:S(2)}, u32[]{:S(2)}) collective-permute-start(bf16[512,384]{1,0:T(8,128)(2,1)S(1)} %shard_map.64.refs_2_), channel_id=1, source_target_pairs={{0,1},{1,2},{2,3},{3,4},{4,5},{5,6},{6,7},{7,0},{8,15},{9,8},{10,9... | collective-permute-start | bytes 1179656 | tf_op jit(solution)/shard_map/ppermute | solution.py:261
  20.6 0.5 collective-permute-done.2.piece
  21.0 3.4 %collective-permute-start.4 = (bf16[512,384]{1,0:T(8,128)(2,1)S(1)}, bf16[512,384]{1,0:T(8,128)(2,1)S(1)}, u32[]{:S(2)}, u32[]{:S(2)}) collective-permute-start(bf16[512,384]{1,0:T(8,128)(2,1)S(1)} %shard_map.65.refs_3_), channel_id=1, source_target_pairs={{0,1},{1,2},{2,3},{3,4},{4,5},{5,6},{6,7},{7,0},{8,15},{9,8},{10,9... | collective-permute-start | bytes 1179656 | tf_op jit(solution)/shard_map/ppermute | solution.py:261
  24.4 0.1 pad_maximum_fusion.2
  24.5 1.3 %collective-permute-start.17 = (bf16[768,768]{1,0:T(8,128)(2,1)S(1)}, bf16[768,768]{1,0:T(8,128)(2,1)S(1)}, u32[]{:S(2)}, u32[]{:S(2)}) collective-permute-start(bf16[768,768]{1,0:T(8,128)(2,1)S(1)} %pad_maximum_fusion.2), channel_id=1, source_target_pairs={{0,16},{8,72},{16,0},{24,88},{32,48},{40,104},{48,32},{56,120},{64... | collective-permute-start | bytes 3538952 | tf_op jit(solution)/shard_map/ppermute | solution.py:273
  25.8 0.1 pad_maximum_fusion.3
  25.9 0.2 collective-permute-start.21
  26.0 4.7 %collective-permute-start.5 = (bf16[512,384]{1,0:T(8,128)(2,1)S(1)}, bf16[512,384]{1,0:T(8,128)(2,1)S(1)}, u32[]{:S(2)}, u32[]{:S(2)}) collective-permute-start(bf16[512,384]{1,0:T(8,128)(2,1)S(1)} %shard_map.66.refs_4_), channel_id=1, source_target_pairs={{0,1},{1,2},{2,3},{3,4},{4,5},{5,6},{6,7},{7,0},{8,15},{9,8},{10,9... | collective-permute-start | bytes 1179656 | tf_op jit(solution)/shard_map/ppermute | solution.py:261
  30.7 1.9 %collective-permute-start.6 = (bf16[512,384]{1,0:T(8,128)(2,1)S(1)}, bf16[512,384]{1,0:T(8,128)(2,1)S(1)}, u32[]{:S(2)}, u32[]{:S(2)}) collective-permute-start(bf16[512,384]{1,0:T(8,128)(2,1)S(1)} %shard_map.67.refs_5_), channel_id=1, source_target_pairs={{0,1},{1,2},{2,3},{3,4},{4,5},{5,6},{6,7},{7,0},{8,15},{9,8},{10,9... | collective-permute-start | bytes 1179656 | tf_op jit(solution)/shard_map/ppermute | solution.py:261
  32.6 2.9 %collective-permute-done.5.piece = bf16[512,384]{1,0:T(8,128)(2,1)S(1)} collective-permute-done((bf16[512,384]{1,0:T(8,128)(2,1)S(1)}, bf16[512,384]{1,0:T(8,128)(2,1)S(1)}, u32[]{:S(2)}, u32[]{:S(2)}) %collective-permute-start.5) | collective-permute-done | bytes 393248 | tf_op jit(solution)/shard_map/ppermute | solution.py:261
  35.5 3.4 %collective-permute-start.7 = (bf16[512,384]{1,0:T(8,128)(2,1)S(1)}, bf16[512,384]{1,0:T(8,128)(2,1)S(1)}, u32[]{:S(2)}, u32[]{:S(2)}) collective-permute-start(bf16[512,384]{1,0:T(8,128)(2,1)S(1)} %shard_map.68.refs_6_), channel_id=1, source_target_pairs={{0,1},{1,2},{2,3},{3,4},{4,5},{5,6},{6,7},{7,0},{8,15},{9,8},{10,9... | collective-permute-start | bytes 1179656 | tf_op jit(solution)/shard_map/ppermute | solution.py:261
  38.9 0.8 collective-permute-done.6.piece
  39.7 3.4 %collective-permute-start.8 = (bf16[512,384]{1,0:T(8,128)(2,1)S(1)}, bf16[512,384]{1,0:T(8,128)(2,1)S(1)}, u32[]{:S(2)}, u32[]{:S(2)}) collective-permute-start(bf16[512,384]{1,0:T(8,128)(2,1)S(1)} %shard_map.69.refs_7_), channel_id=1, source_target_pairs={{0,1},{1,2},{2,3},{3,4},{4,5},{5,6},{6,7},{7,0},{8,15},{9,8},{10,9... | collective-permute-start | bytes 1179656 | tf_op jit(solution)/shard_map/ppermute | solution.py:261
  43.1 0.2 pad_maximum_fusion.refs_16_
  43.3 1.9 %collective-permute-start.18 = (bf16[1536,768]{1,0:T(8,128)(2,1)S(1)}, bf16[1536,768]{1,0:T(8,128)(2,1)S(1)}, u32[]{:S(2)}, u32[]{:S(2)}) collective-permute-start(bf16[1536,768]{1,0:T(8,128)(2,1)S(1)} %pad_maximum_fusion.refs_16_), channel_id=1, source_target_pairs={{0,64},{8,56},{16,80},{24,40},{32,96},{40,24},{48,112},{56,8},{64,... | collective-permute-start | bytes 7077896 | tf_op jit(solution)/shard_map/ppermute | solution.py:273
  45.2 0.2 pad_maximum_fusion.1.refs_16_
  45.3 0.3 collective-permute-start.22
  45.6 1.7 %collective-permute-start.9 = (bf16[512,384]{1,0:T(8,128)(2,1)S(1)}, bf16[512,384]{1,0:T(8,128)(2,1)S(1)}, u32[]{:S(2)}, u32[]{:S(2)}) collective-permute-start(bf16[512,384]{1,0:T(8,128)(2,1)S(1)} %shard_map.70.refs_8_), channel_id=1, source_target_pairs={{0,1},{1,2},{2,3},{3,4},{4,5},{5,6},{6,7},{7,0},{8,15},{9,8},{10,9... | collective-permute-start | bytes 1179656 | tf_op jit(solution)/shard_map/ppermute | solution.py:261
  47.3 0.8 collective-permute-done.8.piece
  48.1 3.1 %collective-permute-start.10 = (bf16[512,384]{1,0:T(8,128)(2,1)S(1)}, bf16[512,384]{1,0:T(8,128)(2,1)S(1)}, u32[]{:S(2)}, u32[]{:S(2)}) collective-permute-start(bf16[512,384]{1,0:T(8,128)(2,1)S(1)} %shard_map.71.refs_9_), channel_id=1, source_target_pairs={{0,1},{1,2},{2,3},{3,4},{4,5},{5,6},{6,7},{7,0},{8,15},{9,8},{10,9... | collective-permute-start | bytes 1179656 | tf_op jit(solution)/shard_map/ppermute | solution.py:261
  51.2 1.4 %collective-permute-done.9.piece = bf16[512,384]{1,0:T(8,128)(2,1)S(1)} collective-permute-done((bf16[512,384]{1,0:T(8,128)(2,1)S(1)}, bf16[512,384]{1,0:T(8,128)(2,1)S(1)}, u32[]{:S(2)}, u32[]{:S(2)}) %collective-permute-start.9) | collective-permute-done | bytes 393248 | tf_op jit(solution)/shard_map/ppermute | solution.py:261
  52.6 2.8 %collective-permute-start.11 = (bf16[512,384]{1,0:T(8,128)(2,1)S(1)}, bf16[512,384]{1,0:T(8,128)(2,1)S(1)}, u32[]{:S(2)}, u32[]{:S(2)}) collective-permute-start(bf16[512,384]{1,0:T(8,128)(2,1)S(1)} %shard_map.72.refs_10_), channel_id=1, source_target_pairs={{0,1},{1,2},{2,3},{3,4},{4,5},{5,6},{6,7},{7,0},{8,15},{9,8},{10,9... | collective-permute-start | bytes 1179656 | tf_op jit(solution)/shard_map/ppermute | solution.py:261
  55.4 1.4 %collective-permute-done.10.piece = bf16[512,384]{1,0:T(8,128)(2,1)S(1)} collective-permute-done((bf16[512,384]{1,0:T(8,128)(2,1)S(1)}, bf16[512,384]{1,0:T(8,128)(2,1)S(1)}, u32[]{:S(2)}, u32[]{:S(2)}) %collective-permute-start.10) | collective-permute-done | bytes 393248 | tf_op jit(solution)/shard_map/ppermute | solution.py:261
  56.8 3.1 %collective-permute-start.12 = (bf16[512,384]{1,0:T(8,128)(2,1)S(1)}, bf16[512,384]{1,0:T(8,128)(2,1)S(1)}, u32[]{:S(2)}, u32[]{:S(2)}) collective-permute-start(bf16[512,384]{1,0:T(8,128)(2,1)S(1)} %shard_map.73.refs_11_), channel_id=1, source_target_pairs={{0,1},{1,2},{2,3},{3,4},{4,5},{5,6},{6,7},{7,0},{8,15},{9,8},{10,9... | collective-permute-start | bytes 1179656 | tf_op jit(solution)/shard_map/ppermute | solution.py:261
  59.9 1.1 collective-permute-done.11.piece
  61.0 3.1 %collective-permute-start.13 = (bf16[512,384]{1,0:T(8,128)(2,1)S(1)}, bf16[512,384]{1,0:T(8,128)(2,1)S(1)}, u32[]{:S(2)}, u32[]{:S(2)}) collective-permute-start(bf16[512,384]{1,0:T(8,128)(2,1)S(1)} %shard_map.74.refs_12_), channel_id=1, source_target_pairs={{0,1},{1,2},{2,3},{3,4},{4,5},{5,6},{6,7},{7,0},{8,15},{9,8},{10,9... | collective-permute-start | bytes 1179656 | tf_op jit(solution)/shard_map/ppermute | solution.py:261
  64.2 1.1 collective-permute-done.12.piece
  65.3 3.1 %collective-permute-start.14 = (bf16[512,384]{1,0:T(8,128)(2,1)S(1)}, bf16[512,384]{1,0:T(8,128)(2,1)S(1)}, u32[]{:S(2)}, u32[]{:S(2)}) collective-permute-start(bf16[512,384]{1,0:T(8,128)(2,1)S(1)} %shard_map.75.refs_13_), channel_id=1, source_target_pairs={{0,1},{1,2},{2,3},{3,4},{4,5},{5,6},{6,7},{7,0},{8,15},{9,8},{10,9... | collective-permute-start | bytes 1179656 | tf_op jit(solution)/shard_map/ppermute | solution.py:261
  68.4 0.7 dynamic-slice_bitcast_fusion.info
  69.1 0.4 collective-permute-done.13.piece
  69.5 4.2 %collective-permute-done.14.piece = bf16[512,384]{1,0:T(8,128)(2,1)S(1)} collective-permute-done((bf16[512,384]{1,0:T(8,128)(2,1)S(1)}, bf16[512,384]{1,0:T(8,128)(2,1)S(1)}, u32[]{:S(2)}, u32[]{:S(2)}) %collective-permute-start.14) | collective-permute-done | bytes 393248 | tf_op jit(solution)/shard_map/ppermute | solution.py:261
  73.7 4.0 %shard_map.79 = bf16[1024,512]{1,0:T(8,128)(2,1)S(1)} custom-call(s32[37]{0:T(128)S(1)} %dynamic-slice_bitcast_fusion.info, bf16[512,384]{1,0:T(8,128)(2,1)S(1)} %get-tuple-element.32.refs_0_, bf16[512,384]{1,0:T(8,128)(2,1)S(1)} %collective-permute-done.refs_1_, bf16[512,384]{1,0:T(8,128)(2,1)S(1)} %shard_map.64.refs_2_, ...), custom_call_target="tpu_custom_call" | custom-call | flops 3221225472 | bytes 1048576 | tf_op jit(solution)/shard_map/pallas_call | solution.py:120
  77.7 7.5 %collective-permute-start.23 = (bf16[1024,512]{1,0:T(8,128)(2,1)S(1)}, bf16[1024,512]{1,0:T(8,128)(2,1)S(1)}, u32[]{:S(2)}, u32[]{:S(2)}) collective-permute-start(bf16[1024,512]{1,0:T(8,128)(2,1)S(1)} %shard_map.79), channel_id=1, source_target_pairs={{0,8},{8,0},{16,24},{24,16},{32,40},{40,32},{48,56},{56,48},{64,72... | collective-permute-start | bytes 3145736 | tf_op jit(solution)/shard_map/ppermute | solution.py:293
  85.2 4.0 %shard_map.78.mine = f32[1024,512]{1,0:T(8,128)S(1)} custom-call(s32[37]{0:T(128)S(1)} %dynamic-slice_bitcast_fusion.info, bf16[512,384]{1,0:T(8,128)(2,1)S(1)} %get-tuple-element.32.refs_0_, bf16[512,384]{1,0:T(8,128)(2,1)S(1)} %collective-permute-done.refs_1_, bf16[512,384]{1,0:T(8,128)(2,1)S(1)} %shard_map.64.refs_2_, ...), custom_call_target="tpu_custom_call" | custom-call | flops 3221225472 | bytes 1048576 | tf_op jit(solution)/shard_map/pallas_call | solution.py:120
  89.2 0.8 shard_map.80
  90.0 0.3 collective-permute-start.25
  90.4 2.4 %shard_map.82 = bf16[1024,256]{1,0:T(8,128)(2,1)S(1)} custom-call(s32[37]{0:T(128)S(1)} %dynamic-slice_bitcast_fusion.info, bf16[512,384]{1,0:T(8,128)(2,1)S(1)} %get-tuple-element.32.refs_0_, bf16[512,384]{1,0:T(8,128)(2,1)S(1)} %collective-permute-done.refs_1_, bf16[512,384]{1,0:T(8,128)(2,1)S(1)} %shard_map.64.refs_2_, ...), custom_call_target="tpu_custom_call" | custom-call | flops 1610612736 | bytes 1048576 | tf_op jit(solution)/shard_map/pallas_call | solution.py:120
  92.8 1.3 %collective-permute-done.25.got_0 = bf16[2,128,128]{2,1,0:T(8,128)(2,1)S(1)} collective-permute-done((bf16[2,128,128]{2,1,0:T(8,128)(2,1)S(1)}, bf16[2,128,128]{2,1,0:T(8,128)(2,1)S(1)}, u32[]{:S(2)}, u32[]{:S(2)}) %collective-permute-start.25) | collective-permute-done | bytes 65568 | tf_op jit(solution)/shard_map/ppermute | solution.py:308
  94.1 2.0 %collective-permute-start.26 = (bf16[2,128,128]{2,1,0:T(8,128)(2,1)S(1)}, bf16[2,128,128]{2,1,0:T(8,128)(2,1)S(1)}, u32[]{:S(2)}, u32[]{:S(2)}) collective-permute-start(bf16[2,128,128]{2,1,0:T(8,128)(2,1)S(1)} %add_convert_fusion.2), channel_id=1, source_target_pairs={{0,48},{8,56},{16,32},{24,40},{32,16},{40,24},{48,0},{56,8},{64,11... | collective-permute-start | bytes 196616 | tf_op jit(solution)/shard_map/ppermute | solution.py:308
  96.0 1.1 collective-permute-start.24
  97.1 1.4 %collective-permute-done.26.got_1 = bf16[2,128,128]{2,1,0:T(8,128)(2,1)S(1)} collective-permute-done((bf16[2,128,128]{2,1,0:T(8,128)(2,1)S(1)}, bf16[2,128,128]{2,1,0:T(8,128)(2,1)S(1)}, u32[]{:S(2)}, u32[]{:S(2)}) %collective-permute-start.26) | collective-permute-done | bytes 65568 | tf_op jit(solution)/shard_map/ppermute | solution.py:308
  98.5 0.1 collective-permute-start.27
  98.6 2.4 %shard_map.81.mine = f32[1024,256]{1,0:T(8,128)S(1)} custom-call(s32[37]{0:T(128)S(1)} %dynamic-slice_bitcast_fusion.info, bf16[512,384]{1,0:T(8,128)(2,1)S(1)} %get-tuple-element.32.refs_0_, bf16[512,384]{1,0:T(8,128)(2,1)S(1)} %collective-permute-done.refs_1_, bf16[512,384]{1,0:T(8,128)(2,1)S(1)} %shard_map.64.refs_2_, ...), custom_call_target="tpu_custom_call" | custom-call | flops 1610612736 | bytes 1048576 | tf_op jit(solution)/shard_map/pallas_call | solution.py:120
  101.0 0.0 copy-start
  101.0 0.7 collective-permute-done.27.got_2
  101.7 2.1 %collective-permute-start.28 = (bf16[2,128,128]{2,1,0:T(8,128)(2,1)S(1)}, bf16[2,128,128]{2,1,0:T(8,128)(2,1)S(1)}, u32[]{:S(2)}, u32[]{:S(2)}) collective-permute-start(bf16[2,128,128]{2,1,0:T(8,128)(2,1)S(1)} %add_convert_fusion), channel_id=1, source_target_pairs={{0,192},{8,200},{16,208},{24,216},{32,224},{40,232},{48,240},{56,2... | collective-permute-start | bytes 196616 | tf_op jit(solution)/shard_map/ppermute | solution.py:308
  103.9 0.9 shard_map.83
  104.8 1.3 %collective-permute-done.28.got_3 = bf16[2,128,128]{2,1,0:T(8,128)(2,1)S(1)} collective-permute-done((bf16[2,128,128]{2,1,0:T(8,128)(2,1)S(1)}, bf16[2,128,128]{2,1,0:T(8,128)(2,1)S(1)}, u32[]{:S(2)}, u32[]{:S(2)}) %collective-permute-start.28) | collective-permute-done | bytes 65568 | tf_op jit(solution)/shard_map/ppermute | solution.py:308
  106.2 0.9 shard_map.85
  107.1 4.3 %collective-permute-start.29 = (bf16[512,256]{1,0:T(8,128)(2,1)S(1)}, bf16[512,256]{1,0:T(8,128)(2,1)S(1)}, u32[]{:S(2)}, u32[]{:S(2)}) collective-permute-start(bf16[512,256]{1,0:T(8,128)(2,1)S(1)} %shard_map.85), channel_id=1, source_target_pairs={{0,8},{8,0},{16,24},{24,16},{32,40},{40,32},{48,56},{56,48},{64,72... | collective-permute-start | bytes 786440 | tf_op jit(solution)/shard_map/ppermute | solution.py:312
  111.4 0.9 shard_map.84
  112.4 0.2 collective-permute-done.29
  112.6 0.8 pad_maximum_fusion.6
  (43 shorter events, 0.3 us)
Async XLA Ops:
  0.0 5.2 %copy-start.1 = (bf16[192,512]{1,0:T(8,128)(2,1)S(1)}, bf16[192,512]{1,0:T(8,128)(2,1)}, u32[]{:S(2)}) copy-start(bf16[192,512]{1,0:T(8,128)(2,1)} %param.7) | copy-start | bytes 589828
  0.0 5.2 %copy-start.3 = (bf16[192,512]{1,0:T(8,128)(2,1)S(1)}, bf16[192,512]{1,0:T(8,128)(2,1)}, u32[]{:S(2)}) copy-start(bf16[192,512]{1,0:T(8,128)(2,1)} %param.9) | copy-start | bytes 589828
  0.0 5.2 %copy-start.2 = (bf16[192,512]{1,0:T(8,128)(2,1)S(1)}, bf16[192,512]{1,0:T(8,128)(2,1)}, u32[]{:S(2)}) copy-start(bf16[192,512]{1,0:T(8,128)(2,1)} %param.8) | copy-start | bytes 589828
  1.9 10.2 %collective-permute-start = (bf16[512,384]{1,0:T(8,128)(2,1)S(1)}, bf16[512,384]{1,0:T(8,128)(2,1)S(1)}, u32[]{:S(2)}, u32[]{:S(2)}) collective-permute-start(bf16[512,384]{1,0:T(8,128)(2,1)S(1)} %get-tuple-element.31), channel_id=1, source_target_pairs={{0,8},{8,0},{16,24},{24,16},{32,40},{40,32},{48,56},{56,48},{64,72... | collective-permute-start | bytes 1179656 | tf_op jit(solution)/shard_map/ppermute | solution.py:257
  5.4 7.4 %collective-permute-start.15 = (bf16[192,768]{1,0:T(8,128)(2,1)S(1)}, bf16[192,768]{1,0:T(8,128)(2,1)S(1)}, u32[]{:S(2)}, u32[]{:S(2)}) collective-permute-start(bf16[192,768]{1,0:T(8,128)(2,1)S(1)} %get-tuple-element.38), channel_id=1, source_target_pairs={{0,48},{8,200},{16,32},{24,216},{32,16},{40,232},{48,0},{56,248},{... | collective-permute-start | bytes 884744 | tf_op jit(solution)/shard_map/ppermute | solution.py:273
  6.5 7.7 %collective-permute-start.19 = (bf16[192,768]{1,0:T(8,128)(2,1)S(1)}, bf16[192,768]{1,0:T(8,128)(2,1)S(1)}, u32[]{:S(2)}, u32[]{:S(2)}) collective-permute-start(bf16[192,768]{1,0:T(8,128)(2,1)S(1)} %get-tuple-element.37), channel_id=1, source_target_pairs={{0,16},{8,72},{16,0},{24,88},{32,48},{40,104},{48,32},{56,120},{64... | collective-permute-start | bytes 884744 | tf_op jit(solution)/shard_map/ppermute | solution.py:273
  6.5 10.3 %collective-permute-start.1 = (bf16[512,384]{1,0:T(8,128)(2,1)S(1)}, bf16[512,384]{1,0:T(8,128)(2,1)S(1)}, u32[]{:S(2)}, u32[]{:S(2)}) collective-permute-start(bf16[512,384]{1,0:T(8,128)(2,1)S(1)} %get-tuple-element.32.refs_0_), channel_id=1, source_target_pairs={{0,1},{1,2},{2,3},{3,4},{4,5},{5,6},{6,7},{7,0},{8,15},{9,8},{10,9... | collective-permute-start | bytes 1179656 | tf_op jit(solution)/shard_map/ppermute | solution.py:261
  12.1 8.9 %collective-permute-start.2 = (bf16[512,384]{1,0:T(8,128)(2,1)S(1)}, bf16[512,384]{1,0:T(8,128)(2,1)S(1)}, u32[]{:S(2)}, u32[]{:S(2)}) collective-permute-start(bf16[512,384]{1,0:T(8,128)(2,1)S(1)} %collective-permute-done.refs_1_), channel_id=1, source_target_pairs={{0,1},{1,2},{2,3},{3,4},{4,5},{5,6},{6,7},{7,0},{8,15},{9,8},{10,9... | collective-permute-start | bytes 1179656 | tf_op jit(solution)/shard_map/ppermute | solution.py:261
  12.9 11.6 %collective-permute-start.16 = (bf16[384,768]{1,0:T(8,128)(2,1)S(1)}, bf16[384,768]{1,0:T(8,128)(2,1)S(1)}, u32[]{:S(2)}, u32[]{:S(2)}) collective-permute-start(bf16[384,768]{1,0:T(8,128)(2,1)S(1)} %pad_maximum_fusion.4), channel_id=1, source_target_pairs={{0,192},{8,24},{16,208},{24,8},{32,224},{40,56},{48,240},{56,40},{... | collective-permute-start | bytes 1769480 | tf_op jit(solution)/shard_map/ppermute | solution.py:273
  14.2 11.6 %collective-permute-start.20 = (bf16[384,768]{1,0:T(8,128)(2,1)S(1)}, bf16[384,768]{1,0:T(8,128)(2,1)S(1)}, u32[]{:S(2)}, u32[]{:S(2)}) collective-permute-start(bf16[384,768]{1,0:T(8,128)(2,1)S(1)} %pad_maximum_fusion.5), channel_id=1, source_target_pairs={{0,64},{8,56},{16,80},{24,40},{32,96},{40,24},{48,112},{56,8},{64,... | collective-permute-start | bytes 1769480 | tf_op jit(solution)/shard_map/ppermute | solution.py:273
  16.8 9.2 %collective-permute-start.3 = (bf16[512,384]{1,0:T(8,128)(2,1)S(1)}, bf16[512,384]{1,0:T(8,128)(2,1)S(1)}, u32[]{:S(2)}, u32[]{:S(2)}) collective-permute-start(bf16[512,384]{1,0:T(8,128)(2,1)S(1)} %shard_map.64.refs_2_), channel_id=1, source_target_pairs={{0,1},{1,2},{2,3},{3,4},{4,5},{5,6},{6,7},{7,0},{8,15},{9,8},{10,9... | collective-permute-start | bytes 1179656 | tf_op jit(solution)/shard_map/ppermute | solution.py:261
  21.0 9.7 %collective-permute-start.4 = (bf16[512,384]{1,0:T(8,128)(2,1)S(1)}, bf16[512,384]{1,0:T(8,128)(2,1)S(1)}, u32[]{:S(2)}, u32[]{:S(2)}) collective-permute-start(bf16[512,384]{1,0:T(8,128)(2,1)S(1)} %shard_map.65.refs_3_), channel_id=1, source_target_pairs={{0,1},{1,2},{2,3},{3,4},{4,5},{5,6},{6,7},{7,0},{8,15},{9,8},{10,9... | collective-permute-start | bytes 1179656 | tf_op jit(solution)/shard_map/ppermute | solution.py:261
  24.5 18.6 %collective-permute-start.17 = (bf16[768,768]{1,0:T(8,128)(2,1)S(1)}, bf16[768,768]{1,0:T(8,128)(2,1)S(1)}, u32[]{:S(2)}, u32[]{:S(2)}) collective-permute-start(bf16[768,768]{1,0:T(8,128)(2,1)S(1)} %pad_maximum_fusion.2), channel_id=1, source_target_pairs={{0,16},{8,72},{16,0},{24,88},{32,48},{40,104},{48,32},{56,120},{64... | collective-permute-start | bytes 3538952 | tf_op jit(solution)/shard_map/ppermute | solution.py:273
  25.9 19.3 %collective-permute-start.21 = (bf16[768,768]{1,0:T(8,128)(2,1)S(1)}, bf16[768,768]{1,0:T(8,128)(2,1)S(1)}, u32[]{:S(2)}, u32[]{:S(2)}) collective-permute-start(bf16[768,768]{1,0:T(8,128)(2,1)S(1)} %pad_maximum_fusion.3), channel_id=1, source_target_pairs={{0,48},{8,200},{16,32},{24,216},{32,16},{40,232},{48,0},{56,248},{... | collective-permute-start | bytes 3538952 | tf_op jit(solution)/shard_map/ppermute | solution.py:273
  26.0 9.4 %collective-permute-start.5 = (bf16[512,384]{1,0:T(8,128)(2,1)S(1)}, bf16[512,384]{1,0:T(8,128)(2,1)S(1)}, u32[]{:S(2)}, u32[]{:S(2)}) collective-permute-start(bf16[512,384]{1,0:T(8,128)(2,1)S(1)} %shard_map.66.refs_4_), channel_id=1, source_target_pairs={{0,1},{1,2},{2,3},{3,4},{4,5},{5,6},{6,7},{7,0},{8,15},{9,8},{10,9... | collective-permute-start | bytes 1179656 | tf_op jit(solution)/shard_map/ppermute | solution.py:261
  30.7 8.9 %collective-permute-start.6 = (bf16[512,384]{1,0:T(8,128)(2,1)S(1)}, bf16[512,384]{1,0:T(8,128)(2,1)S(1)}, u32[]{:S(2)}, u32[]{:S(2)}) collective-permute-start(bf16[512,384]{1,0:T(8,128)(2,1)S(1)} %shard_map.67.refs_5_), channel_id=1, source_target_pairs={{0,1},{1,2},{2,3},{3,4},{4,5},{5,6},{6,7},{7,0},{8,15},{9,8},{10,9... | collective-permute-start | bytes 1179656 | tf_op jit(solution)/shard_map/ppermute | solution.py:261
  35.5 10.1 %collective-permute-start.7 = (bf16[512,384]{1,0:T(8,128)(2,1)S(1)}, bf16[512,384]{1,0:T(8,128)(2,1)S(1)}, u32[]{:S(2)}, u32[]{:S(2)}) collective-permute-start(bf16[512,384]{1,0:T(8,128)(2,1)S(1)} %shard_map.68.refs_6_), channel_id=1, source_target_pairs={{0,1},{1,2},{2,3},{3,4},{4,5},{5,6},{6,7},{7,0},{8,15},{9,8},{10,9... | collective-permute-start | bytes 1179656 | tf_op jit(solution)/shard_map/ppermute | solution.py:261
  39.7 8.4 %collective-permute-start.8 = (bf16[512,384]{1,0:T(8,128)(2,1)S(1)}, bf16[512,384]{1,0:T(8,128)(2,1)S(1)}, u32[]{:S(2)}, u32[]{:S(2)}) collective-permute-start(bf16[512,384]{1,0:T(8,128)(2,1)S(1)} %shard_map.69.refs_7_), channel_id=1, source_target_pairs={{0,1},{1,2},{2,3},{3,4},{4,5},{5,6},{6,7},{7,0},{8,15},{9,8},{10,9... | collective-permute-start | bytes 1179656 | tf_op jit(solution)/shard_map/ppermute | solution.py:261
  43.3 30.4 %collective-permute-start.18 = (bf16[1536,768]{1,0:T(8,128)(2,1)S(1)}, bf16[1536,768]{1,0:T(8,128)(2,1)S(1)}, u32[]{:S(2)}, u32[]{:S(2)}) collective-permute-start(bf16[1536,768]{1,0:T(8,128)(2,1)S(1)} %pad_maximum_fusion.refs_16_), channel_id=1, source_target_pairs={{0,64},{8,56},{16,80},{24,40},{32,96},{40,24},{48,112},{56,8},{64,... | collective-permute-start | bytes 7077896 | tf_op jit(solution)/shard_map/ppermute | solution.py:273
  45.3 28.4 %collective-permute-start.22 = (bf16[1536,768]{1,0:T(8,128)(2,1)S(1)}, bf16[1536,768]{1,0:T(8,128)(2,1)S(1)}, u32[]{:S(2)}, u32[]{:S(2)}) collective-permute-start(bf16[1536,768]{1,0:T(8,128)(2,1)S(1)} %pad_maximum_fusion.1.refs_16_), channel_id=1, source_target_pairs={{0,192},{8,24},{16,208},{24,8},{32,224},{40,56},{48,240},{56,40},{... | collective-permute-start | bytes 7077896 | tf_op jit(solution)/shard_map/ppermute | solution.py:273
  45.6 7.0 %collective-permute-start.9 = (bf16[512,384]{1,0:T(8,128)(2,1)S(1)}, bf16[512,384]{1,0:T(8,128)(2,1)S(1)}, u32[]{:S(2)}, u32[]{:S(2)}) collective-permute-start(bf16[512,384]{1,0:T(8,128)(2,1)S(1)} %shard_map.70.refs_8_), channel_id=1, source_target_pairs={{0,1},{1,2},{2,3},{3,4},{4,5},{5,6},{6,7},{7,0},{8,15},{9,8},{10,9... | collective-permute-start | bytes 1179656 | tf_op jit(solution)/shard_map/ppermute | solution.py:261
  48.1 8.7 %collective-permute-start.10 = (bf16[512,384]{1,0:T(8,128)(2,1)S(1)}, bf16[512,384]{1,0:T(8,128)(2,1)S(1)}, u32[]{:S(2)}, u32[]{:S(2)}) collective-permute-start(bf16[512,384]{1,0:T(8,128)(2,1)S(1)} %shard_map.71.refs_9_), channel_id=1, source_target_pairs={{0,1},{1,2},{2,3},{3,4},{4,5},{5,6},{6,7},{7,0},{8,15},{9,8},{10,9... | collective-permute-start | bytes 1179656 | tf_op jit(solution)/shard_map/ppermute | solution.py:261
  52.6 8.4 %collective-permute-start.11 = (bf16[512,384]{1,0:T(8,128)(2,1)S(1)}, bf16[512,384]{1,0:T(8,128)(2,1)S(1)}, u32[]{:S(2)}, u32[]{:S(2)}) collective-permute-start(bf16[512,384]{1,0:T(8,128)(2,1)S(1)} %shard_map.72.refs_10_), channel_id=1, source_target_pairs={{0,1},{1,2},{2,3},{3,4},{4,5},{5,6},{6,7},{7,0},{8,15},{9,8},{10,9... | collective-permute-start | bytes 1179656 | tf_op jit(solution)/shard_map/ppermute | solution.py:261
  56.8 8.4 %collective-permute-start.12 = (bf16[512,384]{1,0:T(8,128)(2,1)S(1)}, bf16[512,384]{1,0:T(8,128)(2,1)S(1)}, u32[]{:S(2)}, u32[]{:S(2)}) collective-permute-start(bf16[512,384]{1,0:T(8,128)(2,1)S(1)} %shard_map.73.refs_11_), channel_id=1, source_target_pairs={{0,1},{1,2},{2,3},{3,4},{4,5},{5,6},{6,7},{7,0},{8,15},{9,8},{10,9... | collective-permute-start | bytes 1179656 | tf_op jit(solution)/shard_map/ppermute | solution.py:261
  61.0 8.4 %collective-permute-start.13 = (bf16[512,384]{1,0:T(8,128)(2,1)S(1)}, bf16[512,384]{1,0:T(8,128)(2,1)S(1)}, u32[]{:S(2)}, u32[]{:S(2)}) collective-permute-start(bf16[512,384]{1,0:T(8,128)(2,1)S(1)} %shard_map.74.refs_12_), channel_id=1, source_target_pairs={{0,1},{1,2},{2,3},{3,4},{4,5},{5,6},{6,7},{7,0},{8,15},{9,8},{10,9... | collective-permute-start | bytes 1179656 | tf_op jit(solution)/shard_map/ppermute | solution.py:261
  65.3 8.4 %collective-permute-start.14 = (bf16[512,384]{1,0:T(8,128)(2,1)S(1)}, bf16[512,384]{1,0:T(8,128)(2,1)S(1)}, u32[]{:S(2)}, u32[]{:S(2)}) collective-permute-start(bf16[512,384]{1,0:T(8,128)(2,1)S(1)} %shard_map.75.refs_13_), channel_id=1, source_target_pairs={{0,1},{1,2},{2,3},{3,4},{4,5},{5,6},{6,7},{7,0},{8,15},{9,8},{10,9... | collective-permute-start | bytes 1179656 | tf_op jit(solution)/shard_map/ppermute | solution.py:261
  77.7 11.5 %collective-permute-start.23 = (bf16[1024,512]{1,0:T(8,128)(2,1)S(1)}, bf16[1024,512]{1,0:T(8,128)(2,1)S(1)}, u32[]{:S(2)}, u32[]{:S(2)}) collective-permute-start(bf16[1024,512]{1,0:T(8,128)(2,1)S(1)} %shard_map.79), channel_id=1, source_target_pairs={{0,8},{8,0},{16,24},{24,16},{32,40},{40,32},{48,56},{56,48},{64,72... | collective-permute-start | bytes 3145736 | tf_op jit(solution)/shard_map/ppermute | solution.py:293
  90.0 4.0 %collective-permute-start.25 = (bf16[2,128,128]{2,1,0:T(8,128)(2,1)S(1)}, bf16[2,128,128]{2,1,0:T(8,128)(2,1)S(1)}, u32[]{:S(2)}, u32[]{:S(2)}) collective-permute-start(bf16[2,128,128]{2,1,0:T(8,128)(2,1)S(1)} %get-tuple-element.22), channel_id=1, source_target_pairs={{0,16},{8,24},{16,0},{24,8},{32,48},{40,56},{48,32},{56,40},{64,80... | collective-permute-start | bytes 196616 | tf_op jit(solution)/shard_map/ppermute | solution.py:308
  94.1 4.4 %collective-permute-start.26 = (bf16[2,128,128]{2,1,0:T(8,128)(2,1)S(1)}, bf16[2,128,128]{2,1,0:T(8,128)(2,1)S(1)}, u32[]{:S(2)}, u32[]{:S(2)}) collective-permute-start(bf16[2,128,128]{2,1,0:T(8,128)(2,1)S(1)} %add_convert_fusion.2), channel_id=1, source_target_pairs={{0,48},{8,56},{16,32},{24,40},{32,16},{40,24},{48,0},{56,8},{64,11... | collective-permute-start | bytes 196616 | tf_op jit(solution)/shard_map/ppermute | solution.py:308
  96.0 7.9 %collective-permute-start.24 = (bf16[1024,256]{1,0:T(8,128)(2,1)S(1)}, bf16[1024,256]{1,0:T(8,128)(2,1)S(1)}, u32[]{:S(2)}, u32[]{:S(2)}) collective-permute-start(bf16[1024,256]{1,0:T(8,128)(2,1)S(1)} %shard_map.82), channel_id=1, source_target_pairs={{0,8},{8,0},{16,24},{24,16},{32,40},{40,32},{48,56},{56,48},{64,72... | collective-permute-start | bytes 1572872 | tf_op jit(solution)/shard_map/ppermute | solution.py:298
  98.5 3.2 %collective-permute-start.27 = (bf16[2,128,128]{2,1,0:T(8,128)(2,1)S(1)}, bf16[2,128,128]{2,1,0:T(8,128)(2,1)S(1)}, u32[]{:S(2)}, u32[]{:S(2)}) collective-permute-start(bf16[2,128,128]{2,1,0:T(8,128)(2,1)S(1)} %add_convert_fusion.1), channel_id=1, source_target_pairs={{0,64},{8,72},{16,80},{24,88},{32,96},{40,104},{48,112},{56,120},{... | collective-permute-start | bytes 196616 | tf_op jit(solution)/shard_map/ppermute | solution.py:308
  101.0 5.1 %copy-start = (f32[512]{0:T(512)S(1)}, f32[512]{0:T(512)}, u32[]{:S(2)}) copy-start(f32[512]{0:T(512)} %param.10) | copy-start | bytes 6148
  101.7 4.4 %collective-permute-start.28 = (bf16[2,128,128]{2,1,0:T(8,128)(2,1)S(1)}, bf16[2,128,128]{2,1,0:T(8,128)(2,1)S(1)}, u32[]{:S(2)}, u32[]{:S(2)}) collective-permute-start(bf16[2,128,128]{2,1,0:T(8,128)(2,1)S(1)} %add_convert_fusion), channel_id=1, source_target_pairs={{0,192},{8,200},{16,208},{24,216},{32,224},{40,232},{48,240},{56,2... | collective-permute-start | bytes 196616 | tf_op jit(solution)/shard_map/ppermute | solution.py:308
  107.1 5.5 %collective-permute-start.29 = (bf16[512,256]{1,0:T(8,128)(2,1)S(1)}, bf16[512,256]{1,0:T(8,128)(2,1)S(1)}, u32[]{:S(2)}, u32[]{:S(2)}) collective-permute-start(bf16[512,256]{1,0:T(8,128)(2,1)S(1)} %shard_map.85), channel_id=1, source_target_pairs={{0,8},{8,0},{16,24},{24,16},{32,40},{40,32},{48,56},{56,48},{64,72... | collective-permute-start | bytes 786440 | tf_op jit(solution)/shard_map/ppermute | solution.py:312

commit v8 on v7

--- a/solution.py
+++ b/solution.py
@@ -94,7 +94,7 @@
     return u / (1.0 + jnp.exp(-u))
 
 
-def product_kernel(mine, low, high, info, *refs):
+def product_kernel(mine, info, *refs):
     tokens, weights, (out, piled) = refs[: 2 * Z], refs[2 * Z : 2 * Z + BLOCKS], refs[-2:]
     core = info[0]
     for slab in range(2):
@@ -106,7 +106,7 @@
                 for at in range(2 * k, 2 * k + 4):
                     place = info[PLACES + mine * 2 * Z + at]
                     row = pl.ds(pl.multiple_of((place % 8) * ROWS, ROWS), ROWS)
-                    one, two = (w[row, low:high] for w in weights)
+                    one, two = (w[row, :] for w in weights)
                     piled[at * ROWS : (at + 1) * ROWS] = jnp.where(place < 8, one, two)
             piece = jnp.concatenate(
                 [tokens[2 * k + slab][...], tokens[2 * k + 2 + slab][...]], axis=1
@@ -116,16 +116,17 @@
         out[pl.ds(first, SLAB), :] = total.astype(out.dtype)
 
 
-def product(info, tokens, blocks, mine, low, high):
-    return pl.pallas_call(
-        functools.partial(product_kernel, mine, low, high),
-        out_shape=jax.ShapeDtypeStruct((CHIP, high - low), F32 if mine else BF16),
+def product(info, tokens, blocks, mine):
+    width = blocks[mine][0].shape[1]
+    return pl.pallas_call(
+        functools.partial(product_kernel, mine),
+        out_shape=jax.ShapeDtypeStruct((CHIP, width), F32 if mine else BF16),
         in_specs=[SMEM] + [VMEM] * (2 * Z + BLOCKS),
         out_specs=VMEM,
-        scratch_shapes=[pltpu.VMEM((Z * PIECE, high - low), BF16)],
+        scratch_shapes=[pltpu.VMEM((Z * PIECE, width), BF16)],
         compiler_params=pltpu.CompilerParams(vmem_limit_bytes=20 * 2**20),
         cost_estimate=pl.CostEstimate(
-            flops=2 * CHIP * Z * PIECE * (high - low), bytes_accessed=2**20, transcendentals=0
+            flops=2 * CHIP * Z * PIECE * width, bytes_accessed=2**20, transcendentals=0
         ),
     )(info, *tokens, *blocks[mine])
 
@@ -266,12 +267,17 @@
             piece = stream[-1]
             stream.append(pace(pass_on(piece)))
     streams = list(weights)
-    got = [None, None]
-    for step in range(4):
-        if step:
-            streams = [jnp.concatenate(pair, axis=0) for pair in zip(streams, got)]
+    for step in range(3):
         got = [lax.ppermute(streams[j], "seq", cube_pairs(j, step)) for j in range(2)]
-    blocks = [[streams[j], got[j]] for j in range(2)]
+        pairs = list(zip(streams, got))
+        if step < 2:
+            streams = [jnp.concatenate(pair, axis=0) for pair in pairs]
+    blocks = []
+    for low, high in ((0, 2 * HALF), (2 * HALF, 3 * HALF)):
+        near = [jnp.concatenate([part[:, low:high] for part in pair], axis=0) for pair in pairs]
+        if low:
+            near = [after(part, second[-1]) for part in near]
+        blocks.append([[near[j], lax.ppermute(near[j], "seq", cube_pairs(j, 3))] for j in range(2)])
     pieces = zip(first, second)
     return [p for pair in pieces for p in pair], blocks
 
@@ -287,16 +293,16 @@
         for j in range(2)
     )
     halves = [jnp.where(core == 0, high, low), jnp.where(core == 0, low, high)]
-    pieces, blocks = gather(tokens, halves, core)
-
-    kv_theirs = product(after(info, blocks[1][1]), pieces, blocks, 0, 0, 2 * HALF)
+    pieces, (kv_blocks, q_blocks) = gather(tokens, halves, core)
+
+    kv_theirs = product(after(info, kv_blocks[1][1]), pieces, kv_blocks, 0)
     kv_got = lax.ppermute(kv_theirs, "seq", SWAP)
-    kv_mine = product(info, pieces, blocks, 1, 0, 2 * HALF)
+    kv_mine = product(info, pieces, kv_blocks, 1)
     key, value, within, total = pair_states(kv_mine, kv_got)
 
-    q_theirs = product(after(info, total), pieces, blocks, 0, 2 * HALF, 3 * HALF)
+    q_theirs = product(after(info, total), pieces, q_blocks, 0)
     q_got = lax.ppermute(q_theirs, "seq", SWAP)
-    q_mine = product(after(info, total), pieces, blocks, 1, 2 * HALF, 3 * HALF)
+    q_mine = product(after(info, total), pieces, q_blocks, 1)
     got, group = [], total
     for step, dim in enumerate((0, 2, 1, 3)):
         if got:

time: 114 us -> 115 us (level); the launches traced: 113 us -> 113 us
  starting transfers between devices: 72.4 us -> 58.2 us
  waiting for transfers between devices: 20.1 us -> 33.6 us
    ppermute x14, starting transfers between devices: 43.8 us -> 25.8 us  [pass_on(): return lax.ppermute(piece, ('seq', 'head'), ring)]
    ppermute x14, waiting for transfers between devices: 15.2 us -> 23.7 us  [pass_on(): return lax.ppermute(piece, ('seq', 'head'), ring)]
    ppermute x0 -> x4, starting transfers between devices: none -> 5.17 us  [gather(): lax.ppermute(near[j], 'seq', cube_pairs(j, 3))]
    ppermute x1, starting transfers between devices: 7.48 us -> 2.44 us  [local(): kv_got = lax.ppermute(kv_theirs, 'seq', SWAP)]
    ppermute x8 -> x6, waiting for transfers between devices: 0.02 us -> 4.27 us  [gather(): lax.ppermute(streams[j], 'seq', cube_pairs(j, step))]
    ppermute x0 -> x4, waiting for transfers between devices: none -> 3.38 us  [gather(): lax.ppermute(near[j], 'seq', cube_pairs(j, 3))]
    ppermute x4, waiting for transfers between devices: 4.64 us -> 2.01 us  [local(): got.append(lax.ppermute(group, 'seq', exchange_pairs(dim)))]
    ppermute x1, starting transfers between devices: 1.09 us -> 2.36 us  [local(): q_got = lax.ppermute(q_theirs, 'seq', SWAP)]
  transfers between devices with their start and end apart: 30 -> 32, of which waited for: 16 -> 18; matrix products, arithmetic and copies ran while one was open for 1% -> 2% of each run, Pallas kernels for 9% -> 10%
where the time goes in v8:
time: 115 us; the launch traced here: 113 us
  starting transfers between devices  58.2 us (51%)
  waiting for transfers between devices  33.6 us (29%)
  Pallas kernels  16.4 us (14%)
  local copies, waits for them, and re-layouts  2.6 us (2%)
  other arithmetic  1.92 us (2%)
    ppermute x14, starting transfers between devices, pass_on(): return lax.ppermute(piece, ('seq', 'head'), ring)  25.8 us
    ppermute x14, waiting for transfers between devices, pass_on(): return lax.ppermute(piece, ('seq', 'head'), ring)  23.7 us
    pallas_call x4, Pallas kernels, product(): pl.pallas_call(functools.partial(product_kernel, mine), out_shape=jax.Sha...  12.7 us
    ppermute x6, starting transfers between devices, gather(): lax.ppermute(streams[j], 'seq', cube_pairs(j, step))  8.86 us
    ppermute x1, starting transfers between devices, local(): out_got = lax.ppermute(finish(False, *last), 'seq', SWAP)  5.35 us
    ppermute x4, starting transfers between devices, gather(): lax.ppermute(near[j], 'seq', cube_pairs(j, 3))  5.17 us
    ppermute x4, starting transfers between devices, local(): got.append(lax.ppermute(group, 'seq', exchange_pairs(dim)))  4.95 us
    ppermute x6, waiting for transfers between devices, gather(): lax.ppermute(streams[j], 'seq', cube_pairs(j, step))  4.27 us
  transfers between devices with their start and end apart: 32, of which 18 were waited for; matrix products, arithmetic and copies ran while one was open for 2% of the time, Pallas kernels for 10%

profile of v8, /device:TPU:1, one launch (start us, length us, event | category | flops | bytes accessed | tf_op | source)
XLA Modules:
  0.0 113.1 jit_solution(3318827149929209523)
XLA Ops:
  0.0 1.5 %fusion = (bf16[512,192]{1,0:T(8,128)(2,1)S(1)}, bf16[512,192]{1,0:T(8,128)(2,1)S(1)}, bf16[512,192]{1,0:T(8,128)(2,1)S(1)}, bf16[512,192]{1,0:T(8,128)(2,1)S(1)}) fusion(bf16[512,768]{1,0:T(8,128)(2,1)} %param.6), kind=kLoop, calls=%fused_computation.23 | loop fusion | bytes 1572864 | tf_op jit(solution)/shard_map/slice | solution.py:255
  1.6 0.3 broadcast_select_fusion
  1.9 3.3 %collective-permute-start = (bf16[512,384]{1,0:T(8,128)(2,1)S(1)}, bf16[512,384]{1,0:T(8,128)(2,1)S(1)}, u32[]{:S(2)}, u32[]{:S(2)}) collective-permute-start(bf16[512,384]{1,0:T(8,128)(2,1)S(1)} %get-tuple-element.35), channel_id=1, source_target_pairs={{0,8},{8,0},{16,24},{24,16},{32,40},{40,32},{48,56},{56,48},{64,72... | collective-permute-start | bytes 1179656 | tf_op jit(solution)/shard_map/ppermute | solution.py:258
  5.2 3.8 %collective-permute-start.1 = (bf16[512,384]{1,0:T(8,128)(2,1)S(1)}, bf16[512,384]{1,0:T(8,128)(2,1)S(1)}, u32[]{:S(2)}, u32[]{:S(2)}) collective-permute-start(bf16[512,384]{1,0:T(8,128)(2,1)S(1)} %get-tuple-element.36.refs_0_), channel_id=1, source_target_pairs={{0,1},{1,2},{2,3},{3,4},{4,5},{5,6},{6,7},{7,0},{8,15},{9,8},{10,9... | collective-permute-start | bytes 1179656 | tf_op jit(solution)/shard_map/ppermute | solution.py:262
  9.1 1.3 %collective-permute-start.2 = (bf16[512,384]{1,0:T(8,128)(2,1)S(1)}, bf16[512,384]{1,0:T(8,128)(2,1)S(1)}, u32[]{:S(2)}, u32[]{:S(2)}) collective-permute-start(bf16[512,384]{1,0:T(8,128)(2,1)S(1)} %collective-permute-done.refs_1_), channel_id=1, source_target_pairs={{0,1},{1,2},{2,3},{3,4},{4,5},{5,6},{6,7},{7,0},{8,15},{9,8},{10,9... | collective-permute-start | bytes 1179656 | tf_op jit(solution)/shard_map/ppermute | solution.py:262
  10.4 0.1 broadcast_select_fusion.2
  10.5 1.4 %collective-permute-start.19 = (bf16[192,768]{1,0:T(8,128)(2,1)S(1)}, bf16[192,768]{1,0:T(8,128)(2,1)S(1)}, u32[]{:S(2)}, u32[]{:S(2)}) collective-permute-start(bf16[192,768]{1,0:T(8,128)(2,1)S(1)} %get-tuple-element.41), channel_id=1, source_target_pairs={{0,16},{8,72},{16,0},{24,88},{32,48},{40,104},{48,32},{56,120},{64... | collective-permute-start | bytes 884744 | tf_op jit(solution)/shard_map/ppermute | solution.py:271
  11.9 1.9 %collective-permute-start.15 = (bf16[192,768]{1,0:T(8,128)(2,1)S(1)}, bf16[192,768]{1,0:T(8,128)(2,1)S(1)}, u32[]{:S(2)}, u32[]{:S(2)}) collective-permute-start(bf16[192,768]{1,0:T(8,128)(2,1)S(1)} %get-tuple-element.42), channel_id=1, source_target_pairs={{0,48},{8,200},{16,32},{24,216},{32,16},{40,232},{48,0},{56,248},{... | collective-permute-start | bytes 884744 | tf_op jit(solution)/shard_map/ppermute | solution.py:271
  13.8 3.4 %collective-permute-start.3 = (bf16[512,384]{1,0:T(8,128)(2,1)S(1)}, bf16[512,384]{1,0:T(8,128)(2,1)S(1)}, u32[]{:S(2)}, u32[]{:S(2)}) collective-permute-start(bf16[512,384]{1,0:T(8,128)(2,1)S(1)} %shard_map.64.refs_2_), channel_id=1, source_target_pairs={{0,1},{1,2},{2,3},{3,4},{4,5},{5,6},{6,7},{7,0},{8,15},{9,8},{10,9... | collective-permute-start | bytes 1179656 | tf_op jit(solution)/shard_map/ppermute | solution.py:262
  17.2 0.8 collective-permute-done.2.piece
  18.0 3.1 %collective-permute-start.4 = (bf16[512,384]{1,0:T(8,128)(2,1)S(1)}, bf16[512,384]{1,0:T(8,128)(2,1)S(1)}, u32[]{:S(2)}, u32[]{:S(2)}) collective-permute-start(bf16[512,384]{1,0:T(8,128)(2,1)S(1)} %shard_map.65.refs_3_), channel_id=1, source_target_pairs={{0,1},{1,2},{2,3},{3,4},{4,5},{5,6},{6,7},{7,0},{8,15},{9,8},{10,9... | collective-permute-start | bytes 1179656 | tf_op jit(solution)/shard_map/ppermute | solution.py:262
  21.2 2.6 %collective-permute-start.20 = (bf16[384,768]{1,0:T(8,128)(2,1)S(1)}, bf16[384,768]{1,0:T(8,128)(2,1)S(1)}, u32[]{:S(2)}, u32[]{:S(2)}) collective-permute-start(bf16[384,768]{1,0:T(8,128)(2,1)S(1)} %pad_maximum_fusion.7), channel_id=1, source_target_pairs={{0,64},{8,56},{16,80},{24,40},{32,96},{40,24},{48,112},{56,8},{64,... | collective-permute-start | bytes 1769480 | tf_op jit(solution)/shard_map/ppermute | solution.py:271
  23.8 0.1 collective-permute-start.16
  23.9 1.4 %collective-permute-start.5 = (bf16[512,384]{1,0:T(8,128)(2,1)S(1)}, bf16[512,384]{1,0:T(8,128)(2,1)S(1)}, u32[]{:S(2)}, u32[]{:S(2)}) collective-permute-start(bf16[512,384]{1,0:T(8,128)(2,1)S(1)} %shard_map.66.refs_4_), channel_id=1, source_target_pairs={{0,1},{1,2},{2,3},{3,4},{4,5},{5,6},{6,7},{7,0},{8,15},{9,8},{10,9... | collective-permute-start | bytes 1179656 | tf_op jit(solution)/shard_map/ppermute | solution.py:262
  25.3 1.1 collective-permute-done.4.piece
  26.4 3.4 %collective-permute-start.6 = (bf16[512,384]{1,0:T(8,128)(2,1)S(1)}, bf16[512,384]{1,0:T(8,128)(2,1)S(1)}, u32[]{:S(2)}, u32[]{:S(2)}) collective-permute-start(bf16[512,384]{1,0:T(8,128)(2,1)S(1)} %shard_map.67.refs_5_), channel_id=1, source_target_pairs={{0,1},{1,2},{2,3},{3,4},{4,5},{5,6},{6,7},{7,0},{8,15},{9,8},{10,9... | collective-permute-start | bytes 1179656 | tf_op jit(solution)/shard_map/ppermute | solution.py:262
  29.8 1.7 %collective-permute-done.20 = bf16[384,768]{1,0:T(8,128)(2,1)S(1)} collective-permute-done((bf16[384,768]{1,0:T(8,128)(2,1)S(1)}, bf16[384,768]{1,0:T(8,128)(2,1)S(1)}, u32[]{:S(2)}, u32[]{:S(2)}) %collective-permute-start.20) | collective-permute-done | bytes 589856 | tf_op jit(solution)/shard_map/ppermute | solution.py:271
  31.6 2.8 %collective-permute-start.21 = (bf16[768,768]{1,0:T(8,128)(2,1)S(1)}, bf16[768,768]{1,0:T(8,128)(2,1)S(1)}, u32[]{:S(2)}, u32[]{:S(2)}) collective-permute-start(bf16[768,768]{1,0:T(8,128)(2,1)S(1)} %pad_maximum_fusion.3), channel_id=1, source_target_pairs={{0,48},{8,200},{16,32},{24,216},{32,16},{40,232},{48,0},{56,248},{... | collective-permute-start | bytes 3538952 | tf_op jit(solution)/shard_map/ppermute | solution.py:271
  34.5 0.1 collective-permute-start.17
  34.6 0.1 collective-permute-start.7
  34.7 0.4 collective-permute-done.6.piece
  35.1 3.2 %collective-permute-start.8 = (bf16[512,384]{1,0:T(8,128)(2,1)S(1)}, bf16[512,384]{1,0:T(8,128)(2,1)S(1)}, u32[]{:S(2)}, u32[]{:S(2)}) collective-permute-start(bf16[512,384]{1,0:T(8,128)(2,1)S(1)} %shard_map.69.refs_7_), channel_id=1, source_target_pairs={{0,1},{1,2},{2,3},{3,4},{4,5},{5,6},{6,7},{7,0},{8,15},{9,8},{10,9... | collective-permute-start | bytes 1179656 | tf_op jit(solution)/shard_map/ppermute | solution.py:262
  38.4 3.2 %collective-permute-done.7.piece = bf16[512,384]{1,0:T(8,128)(2,1)S(1)} collective-permute-done((bf16[512,384]{1,0:T(8,128)(2,1)S(1)}, bf16[512,384]{1,0:T(8,128)(2,1)S(1)}, u32[]{:S(2)}, u32[]{:S(2)}) %collective-permute-start.7) | collective-permute-done | bytes 393248 | tf_op jit(solution)/shard_map/ppermute | solution.py:262
  41.6 1.2 %collective-permute-start.9 = (bf16[512,384]{1,0:T(8,128)(2,1)S(1)}, bf16[512,384]{1,0:T(8,128)(2,1)S(1)}, u32[]{:S(2)}, u32[]{:S(2)}) collective-permute-start(bf16[512,384]{1,0:T(8,128)(2,1)S(1)} %shard_map.70.refs_8_), channel_id=1, source_target_pairs={{0,1},{1,2},{2,3},{3,4},{4,5},{5,6},{6,7},{7,0},{8,15},{9,8},{10,9... | collective-permute-start | bytes 1179656 | tf_op jit(solution)/shard_map/ppermute | solution.py:262
  42.8 3.0 %collective-permute-done.8.piece = bf16[512,384]{1,0:T(8,128)(2,1)S(1)} collective-permute-done((bf16[512,384]{1,0:T(8,128)(2,1)S(1)}, bf16[512,384]{1,0:T(8,128)(2,1)S(1)}, u32[]{:S(2)}, u32[]{:S(2)}) %collective-permute-start.8) | collective-permute-done | bytes 393248 | tf_op jit(solution)/shard_map/ppermute | solution.py:262
  45.8 1.2 %collective-permute-start.10 = (bf16[512,384]{1,0:T(8,128)(2,1)S(1)}, bf16[512,384]{1,0:T(8,128)(2,1)S(1)}, u32[]{:S(2)}, u32[]{:S(2)}) collective-permute-start(bf16[512,384]{1,0:T(8,128)(2,1)S(1)} %shard_map.71.refs_9_), channel_id=1, source_target_pairs={{0,1},{1,2},{2,3},{3,4},{4,5},{5,6},{6,7},{7,0},{8,15},{9,8},{10,9... | collective-permute-start | bytes 1179656 | tf_op jit(solution)/shard_map/ppermute | solution.py:262
  47.0 1.3 %collective-permute-done.21 = bf16[768,768]{1,0:T(8,128)(2,1)S(1)} collective-permute-done((bf16[768,768]{1,0:T(8,128)(2,1)S(1)}, bf16[768,768]{1,0:T(8,128)(2,1)S(1)}, u32[]{:S(2)}, u32[]{:S(2)}) %collective-permute-start.21) | collective-permute-done | bytes 1179680 | tf_op jit(solution)/shard_map/ppermute | solution.py:271
  48.3 0.1 pad_maximum_fusion.1.refs_16_
  48.4 0.1 collective-permute-start.22
  48.5 1.4 %collective-permute-done.17 = bf16[768,768]{1,0:T(8,128)(2,1)S(1)} collective-permute-done((bf16[768,768]{1,0:T(8,128)(2,1)S(1)}, bf16[768,768]{1,0:T(8,128)(2,1)S(1)}, u32[]{:S(2)}, u32[]{:S(2)}) %collective-permute-start.17) | collective-permute-done | bytes 1179680 | tf_op jit(solution)/shard_map/ppermute | solution.py:271
  50.0 0.1 pad_maximum_fusion.refs_16_
  50.1 2.6 %collective-permute-start.18 = (bf16[1536,512]{1,0:T(8,128)(2,1)S(1)}, bf16[1536,512]{1,0:T(8,128)(2,1)S(1)}, u32[]{:S(2)}, u32[]{:S(2)}) collective-permute-start(bf16[1536,512]{1,0:T(8,128)(2,1)S(1)} %pad_maximum_fusion.refs_16_), channel_id=1, source_target_pairs={{0,64},{8,56},{16,80},{24,40},{32,96},{40,24},{48,112},{56,8},{64,... | collective-permute-start | bytes 4718600 | tf_op jit(solution)/shard_map/ppermute | solution.py:280
  52.7 1.6 %collective-permute-done.10.piece = bf16[512,384]{1,0:T(8,128)(2,1)S(1)} collective-permute-done((bf16[512,384]{1,0:T(8,128)(2,1)S(1)}, bf16[512,384]{1,0:T(8,128)(2,1)S(1)}, u32[]{:S(2)}, u32[]{:S(2)}) %collective-permute-start.10) | collective-permute-done | bytes 393248 | tf_op jit(solution)/shard_map/ppermute | solution.py:262
  54.2 1.2 %collective-permute-start.12 = (bf16[512,384]{1,0:T(8,128)(2,1)S(1)}, bf16[512,384]{1,0:T(8,128)(2,1)S(1)}, u32[]{:S(2)}, u32[]{:S(2)}) collective-permute-start(bf16[512,384]{1,0:T(8,128)(2,1)S(1)} %shard_map.73.refs_11_), channel_id=1, source_target_pairs={{0,1},{1,2},{2,3},{3,4},{4,5},{5,6},{6,7},{7,0},{8,15},{9,8},{10,9... | collective-permute-start | bytes 1179656 | tf_op jit(solution)/shard_map/ppermute | solution.py:262
  55.4 4.1 %collective-permute-done.11.piece = bf16[512,384]{1,0:T(8,128)(2,1)S(1)} collective-permute-done((bf16[512,384]{1,0:T(8,128)(2,1)S(1)}, bf16[512,384]{1,0:T(8,128)(2,1)S(1)}, u32[]{:S(2)}, u32[]{:S(2)}) %collective-permute-start.11) | collective-permute-done | bytes 393248 | tf_op jit(solution)/shard_map/ppermute | solution.py:262
  59.6 1.2 %collective-permute-start.13 = (bf16[512,384]{1,0:T(8,128)(2,1)S(1)}, bf16[512,384]{1,0:T(8,128)(2,1)S(1)}, u32[]{:S(2)}, u32[]{:S(2)}) collective-permute-start(bf16[512,384]{1,0:T(8,128)(2,1)S(1)} %shard_map.74.refs_12_), channel_id=1, source_target_pairs={{0,1},{1,2},{2,3},{3,4},{4,5},{5,6},{6,7},{7,0},{8,15},{9,8},{10,9... | collective-permute-start | bytes 1179656 | tf_op jit(solution)/shard_map/ppermute | solution.py:262
  60.8 3.0 %collective-permute-done.12.piece = bf16[512,384]{1,0:T(8,128)(2,1)S(1)} collective-permute-done((bf16[512,384]{1,0:T(8,128)(2,1)S(1)}, bf16[512,384]{1,0:T(8,128)(2,1)S(1)}, u32[]{:S(2)}, u32[]{:S(2)}) %collective-permute-start.12) | collective-permute-done | bytes 393248 | tf_op jit(solution)/shard_map/ppermute | solution.py:262
  63.8 1.2 %collective-permute-start.14 = (bf16[512,384]{1,0:T(8,128)(2,1)S(1)}, bf16[512,384]{1,0:T(8,128)(2,1)S(1)}, u32[]{:S(2)}, u32[]{:S(2)}) collective-permute-start(bf16[512,384]{1,0:T(8,128)(2,1)S(1)} %shard_map.75.refs_13_), channel_id=1, source_target_pairs={{0,1},{1,2},{2,3},{3,4},{4,5},{5,6},{6,7},{7,0},{8,15},{9,8},{10,9... | collective-permute-start | bytes 1179656 | tf_op jit(solution)/shard_map/ppermute | solution.py:262
  65.0 0.7 dynamic-slice_bitcast_fusion.info
  65.7 2.3 %collective-permute-done.13.piece = bf16[512,384]{1,0:T(8,128)(2,1)S(1)} collective-permute-done((bf16[512,384]{1,0:T(8,128)(2,1)S(1)}, bf16[512,384]{1,0:T(8,128)(2,1)S(1)}, u32[]{:S(2)}, u32[]{:S(2)}) %collective-permute-start.13) | collective-permute-done | bytes 393248 | tf_op jit(solution)/shard_map/ppermute | solution.py:262
  68.0 4.2 %collective-permute-done.14.piece = bf16[512,384]{1,0:T(8,128)(2,1)S(1)} collective-permute-done((bf16[512,384]{1,0:T(8,128)(2,1)S(1)}, bf16[512,384]{1,0:T(8,128)(2,1)S(1)}, u32[]{:S(2)}, u32[]{:S(2)}) %collective-permute-start.14) | collective-permute-done | bytes 393248 | tf_op jit(solution)/shard_map/ppermute | solution.py:262
  72.2 4.0 %shard_map.79 = bf16[1024,512]{1,0:T(8,128)(2,1)S(1)} custom-call(s32[37]{0:T(128)S(1)} %dynamic-slice_bitcast_fusion.info, bf16[512,384]{1,0:T(8,128)(2,1)S(1)} %get-tuple-element.36.refs_0_, bf16[512,384]{1,0:T(8,128)(2,1)S(1)} %collective-permute-done.refs_1_, bf16[512,384]{1,0:T(8,128)(2,1)S(1)} %shard_map.64.refs_2_, ...), custom_call_target="tpu_custom_call" | custom-call | flops 3221225472 | bytes 1048576 | tf_op jit(solution)/shard_map/pallas_call | solution.py:121
  76.2 2.4 %collective-permute-start.23 = (bf16[1024,512]{1,0:T(8,128)(2,1)S(1)}, bf16[1024,512]{1,0:T(8,128)(2,1)S(1)}, u32[]{:S(2)}, u32[]{:S(2)}) collective-permute-start(bf16[1024,512]{1,0:T(8,128)(2,1)S(1)} %shard_map.79), channel_id=1, source_target_pairs={{0,8},{8,0},{16,24},{24,16},{32,40},{40,32},{48,56},{56,48},{64,72... | collective-permute-start | bytes 3145736 | tf_op jit(solution)/shard_map/ppermute | solution.py:299
  78.8 0.3 collective-permute-start.25
  79.3 2.2 %collective-permute-start.24 = (bf16[1536,256]{1,0:T(8,128)(2,1)S(1)}, bf16[1536,256]{1,0:T(8,128)(2,1)S(1)}, u32[]{:S(2)}, u32[]{:S(2)}) collective-permute-start(bf16[1536,256]{1,0:T(8,128)(2,1)S(1)} %pad_maximum_fusion.4.refs_16_), channel_id=1, source_target_pairs={{0,64},{8,56},{16,80},{24,40},{32,96},{40,24},{48,112},{56,8},{64,... | collective-permute-start | bytes 2359304 | tf_op jit(solution)/shard_map/ppermute | solution.py:280
  81.4 4.0 %shard_map.78.mine = f32[1024,512]{1,0:T(8,128)S(1)} custom-call(s32[37]{0:T(128)S(1)} %dynamic-slice_bitcast_fusion.info, bf16[512,384]{1,0:T(8,128)(2,1)S(1)} %get-tuple-element.36.refs_0_, bf16[512,384]{1,0:T(8,128)(2,1)S(1)} %collective-permute-done.refs_1_, bf16[512,384]{1,0:T(8,128)(2,1)S(1)} %shard_map.64.refs_2_, ...), custom_call_target="tpu_custom_call" | custom-call | flops 3221225472 | bytes 1048576 | tf_op jit(solution)/shard_map/pallas_call | solution.py:121
  85.4 0.8 shard_map.80
  86.3 0.6 collective-permute-start.27
  86.9 3.4 %collective-permute-done.25.refs_17_ = bf16[1536,256]{1,0:T(8,128)(2,1)S(1)} collective-permute-done((bf16[1536,256]{1,0:T(8,128)(2,1)S(1)}, bf16[1536,256]{1,0:T(8,128)(2,1)S(1)}, u32[]{:S(2)}, u32[]{:S(2)}) %collective-permute-start.25) | collective-permute-done | bytes 786464 | tf_op jit(solution)/shard_map/ppermute | solution.py:280
  90.3 2.4 %shard_map.82 = bf16[1024,256]{1,0:T(8,128)(2,1)S(1)} custom-call(s32[37]{0:T(128)S(1)} %dynamic-slice_bitcast_fusion.info, bf16[512,384]{1,0:T(8,128)(2,1)S(1)} %get-tuple-element.36.refs_0_, bf16[512,384]{1,0:T(8,128)(2,1)S(1)} %collective-permute-done.refs_1_, bf16[512,384]{1,0:T(8,128)(2,1)S(1)} %shard_map.64.refs_2_, ...), custom_call_target="tpu_custom_call" | custom-call | flops 1610612736 | bytes 1048576 | tf_op jit(solution)/shard_map/pallas_call | solution.py:121
  92.7 1.6 %collective-permute-start.28 = (bf16[2,128,128]{2,1,0:T(8,128)(2,1)S(1)}, bf16[2,128,128]{2,1,0:T(8,128)(2,1)S(1)}, u32[]{:S(2)}, u32[]{:S(2)}) collective-permute-start(bf16[2,128,128]{2,1,0:T(8,128)(2,1)S(1)} %add_convert_fusion.2), channel_id=1, source_target_pairs={{0,48},{8,56},{16,32},{24,40},{32,16},{40,24},{48,0},{56,8},{64,11... | collective-permute-start | bytes 196616 | tf_op jit(solution)/shard_map/ppermute | solution.py:314
  94.3 2.4 %collective-permute-start.26 = (bf16[1024,256]{1,0:T(8,128)(2,1)S(1)}, bf16[1024,256]{1,0:T(8,128)(2,1)S(1)}, u32[]{:S(2)}, u32[]{:S(2)}) collective-permute-start(bf16[1024,256]{1,0:T(8,128)(2,1)S(1)} %shard_map.82), channel_id=1, source_target_pairs={{0,8},{8,0},{16,24},{24,16},{32,40},{40,32},{48,56},{56,48},{64,72... | collective-permute-start | bytes 1572872 | tf_op jit(solution)/shard_map/ppermute | solution.py:304
  96.7 0.4 collective-permute-done.28.got_1
  97.1 0.5 collective-permute-start.29
  97.7 2.4 %shard_map.81.mine = f32[1024,256]{1,0:T(8,128)S(1)} custom-call(s32[37]{0:T(128)S(1)} %dynamic-slice_bitcast_fusion.info, bf16[512,384]{1,0:T(8,128)(2,1)S(1)} %get-tuple-element.36.refs_0_, bf16[512,384]{1,0:T(8,128)(2,1)S(1)} %collective-permute-done.refs_1_, bf16[512,384]{1,0:T(8,128)(2,1)S(1)} %shard_map.64.refs_2_, ...), custom_call_target="tpu_custom_call" | custom-call | flops 1610612736 | bytes 1048576 | tf_op jit(solution)/shard_map/pallas_call | solution.py:121
  100.1 0.2 collective-permute-done.29.got_2
  100.4 2.1 %collective-permute-start.30 = (bf16[2,128,128]{2,1,0:T(8,128)(2,1)S(1)}, bf16[2,128,128]{2,1,0:T(8,128)(2,1)S(1)}, u32[]{:S(2)}, u32[]{:S(2)}) collective-permute-start(bf16[2,128,128]{2,1,0:T(8,128)(2,1)S(1)} %add_convert_fusion), channel_id=1, source_target_pairs={{0,192},{8,200},{16,208},{24,216},{32,224},{40,232},{48,240},{56,2... | collective-permute-start | bytes 196616 | tf_op jit(solution)/shard_map/ppermute | solution.py:314
  102.5 0.9 shard_map.83
  103.4 1.3 %collective-permute-done.30.got_3 = bf16[2,128,128]{2,1,0:T(8,128)(2,1)S(1)} collective-permute-done((bf16[2,128,128]{2,1,0:T(8,128)(2,1)S(1)}, bf16[2,128,128]{2,1,0:T(8,128)(2,1)S(1)}, u32[]{:S(2)}, u32[]{:S(2)}) %collective-permute-start.30) | collective-permute-done | bytes 65568 | tf_op jit(solution)/shard_map/ppermute | solution.py:314
  104.8 0.9 shard_map.85
  105.7 5.3 %collective-permute-start.31 = (bf16[512,256]{1,0:T(8,128)(2,1)S(1)}, bf16[512,256]{1,0:T(8,128)(2,1)S(1)}, u32[]{:S(2)}, u32[]{:S(2)}) collective-permute-start(bf16[512,256]{1,0:T(8,128)(2,1)S(1)} %shard_map.85), channel_id=1, source_target_pairs={{0,8},{8,0},{16,24},{24,16},{32,40},{40,32},{48,56},{56,48},{64,72... | collective-permute-start | bytes 786440 | tf_op jit(solution)/shard_map/ppermute | solution.py:318
  111.1 0.9 shard_map.84
  112.0 0.2 collective-permute-done.31
  112.3 0.8 pad_maximum_fusion.8
  (57 shorter events, 0.9 us)
Async XLA Ops:
  0.0 9.1 %copy-start.2 = (bf16[192,512]{1,0:T(8,128)(2,1)S(1)}, bf16[192,512]{1,0:T(8,128)(2,1)}, u32[]{:S(2)}) copy-start(bf16[192,512]{1,0:T(8,128)(2,1)} %param.8) | copy-start | bytes 589828
  0.0 9.1 %copy-start.3 = (bf16[192,512]{1,0:T(8,128)(2,1)S(1)}, bf16[192,512]{1,0:T(8,128)(2,1)}, u32[]{:S(2)}) copy-start(bf16[192,512]{1,0:T(8,128)(2,1)} %param.9) | copy-start | bytes 589828
  1.5 8.9 %copy-start.1 = (bf16[192,512]{1,0:T(8,128)(2,1)S(1)}, bf16[192,512]{1,0:T(8,128)(2,1)}, u32[]{:S(2)}) copy-start(bf16[192,512]{1,0:T(8,128)(2,1)} %param.7) | copy-start | bytes 589828
  1.9 7.2 %collective-permute-start = (bf16[512,384]{1,0:T(8,128)(2,1)S(1)}, bf16[512,384]{1,0:T(8,128)(2,1)S(1)}, u32[]{:S(2)}, u32[]{:S(2)}) collective-permute-start(bf16[512,384]{1,0:T(8,128)(2,1)S(1)} %get-tuple-element.35), channel_id=1, source_target_pairs={{0,8},{8,0},{16,24},{24,16},{32,40},{40,32},{48,56},{56,48},{64,72... | collective-permute-start | bytes 1179656 | tf_op jit(solution)/shard_map/ppermute | solution.py:258
  5.2 8.6 %collective-permute-start.1 = (bf16[512,384]{1,0:T(8,128)(2,1)S(1)}, bf16[512,384]{1,0:T(8,128)(2,1)S(1)}, u32[]{:S(2)}, u32[]{:S(2)}) collective-permute-start(bf16[512,384]{1,0:T(8,128)(2,1)S(1)} %get-tuple-element.36.refs_0_), channel_id=1, source_target_pairs={{0,1},{1,2},{2,3},{3,4},{4,5},{5,6},{6,7},{7,0},{8,15},{9,8},{10,9... | collective-permute-start | bytes 1179656 | tf_op jit(solution)/shard_map/ppermute | solution.py:262
  9.1 8.9 %collective-permute-start.2 = (bf16[512,384]{1,0:T(8,128)(2,1)S(1)}, bf16[512,384]{1,0:T(8,128)(2,1)S(1)}, u32[]{:S(2)}, u32[]{:S(2)}) collective-permute-start(bf16[512,384]{1,0:T(8,128)(2,1)S(1)} %collective-permute-done.refs_1_), channel_id=1, source_target_pairs={{0,1},{1,2},{2,3},{3,4},{4,5},{5,6},{6,7},{7,0},{8,15},{9,8},{10,9... | collective-permute-start | bytes 1179656 | tf_op jit(solution)/shard_map/ppermute | solution.py:262
  10.5 10.6 %collective-permute-start.19 = (bf16[192,768]{1,0:T(8,128)(2,1)S(1)}, bf16[192,768]{1,0:T(8,128)(2,1)S(1)}, u32[]{:S(2)}, u32[]{:S(2)}) collective-permute-start(bf16[192,768]{1,0:T(8,128)(2,1)S(1)} %get-tuple-element.41), channel_id=1, source_target_pairs={{0,16},{8,72},{16,0},{24,88},{32,48},{40,104},{48,32},{56,120},{64... | collective-permute-start | bytes 884744 | tf_op jit(solution)/shard_map/ppermute | solution.py:271
  11.9 11.8 %collective-permute-start.15 = (bf16[192,768]{1,0:T(8,128)(2,1)S(1)}, bf16[192,768]{1,0:T(8,128)(2,1)S(1)}, u32[]{:S(2)}, u32[]{:S(2)}) collective-permute-start(bf16[192,768]{1,0:T(8,128)(2,1)S(1)} %get-tuple-element.42), channel_id=1, source_target_pairs={{0,48},{8,200},{16,32},{24,216},{32,16},{40,232},{48,0},{56,248},{... | collective-permute-start | bytes 884744 | tf_op jit(solution)/shard_map/ppermute | solution.py:271
  13.8 10.0 %collective-permute-start.3 = (bf16[512,384]{1,0:T(8,128)(2,1)S(1)}, bf16[512,384]{1,0:T(8,128)(2,1)S(1)}, u32[]{:S(2)}, u32[]{:S(2)}) collective-permute-start(bf16[512,384]{1,0:T(8,128)(2,1)S(1)} %shard_map.64.refs_2_), channel_id=1, source_target_pairs={{0,1},{1,2},{2,3},{3,4},{4,5},{5,6},{6,7},{7,0},{8,15},{9,8},{10,9... | collective-permute-start | bytes 1179656 | tf_op jit(solution)/shard_map/ppermute | solution.py:262
  18.0 8.4 %collective-permute-start.4 = (bf16[512,384]{1,0:T(8,128)(2,1)S(1)}, bf16[512,384]{1,0:T(8,128)(2,1)S(1)}, u32[]{:S(2)}, u32[]{:S(2)}) collective-permute-start(bf16[512,384]{1,0:T(8,128)(2,1)S(1)} %shard_map.65.refs_3_), channel_id=1, source_target_pairs={{0,1},{1,2},{2,3},{3,4},{4,5},{5,6},{6,7},{7,0},{8,15},{9,8},{10,9... | collective-permute-start | bytes 1179656 | tf_op jit(solution)/shard_map/ppermute | solution.py:262
  21.2 10.3 %collective-permute-start.20 = (bf16[384,768]{1,0:T(8,128)(2,1)S(1)}, bf16[384,768]{1,0:T(8,128)(2,1)S(1)}, u32[]{:S(2)}, u32[]{:S(2)}) collective-permute-start(bf16[384,768]{1,0:T(8,128)(2,1)S(1)} %pad_maximum_fusion.7), channel_id=1, source_target_pairs={{0,64},{8,56},{16,80},{24,40},{32,96},{40,24},{48,112},{56,8},{64,... | collective-permute-start | bytes 1769480 | tf_op jit(solution)/shard_map/ppermute | solution.py:271
  23.8 10.6 %collective-permute-start.16 = (bf16[384,768]{1,0:T(8,128)(2,1)S(1)}, bf16[384,768]{1,0:T(8,128)(2,1)S(1)}, u32[]{:S(2)}, u32[]{:S(2)}) collective-permute-start(bf16[384,768]{1,0:T(8,128)(2,1)S(1)} %pad_maximum_fusion.6), channel_id=1, source_target_pairs={{0,192},{8,24},{16,208},{24,8},{32,224},{40,56},{48,240},{56,40},{... | collective-permute-start | bytes 1769480 | tf_op jit(solution)/shard_map/ppermute | solution.py:271
  23.9 10.7 %collective-permute-start.5 = (bf16[512,384]{1,0:T(8,128)(2,1)S(1)}, bf16[512,384]{1,0:T(8,128)(2,1)S(1)}, u32[]{:S(2)}, u32[]{:S(2)}) collective-permute-start(bf16[512,384]{1,0:T(8,128)(2,1)S(1)} %shard_map.66.refs_4_), channel_id=1, source_target_pairs={{0,1},{1,2},{2,3},{3,4},{4,5},{5,6},{6,7},{7,0},{8,15},{9,8},{10,9... | collective-permute-start | bytes 1179656 | tf_op jit(solution)/shard_map/ppermute | solution.py:262
  26.4 8.7 %collective-permute-start.6 = (bf16[512,384]{1,0:T(8,128)(2,1)S(1)}, bf16[512,384]{1,0:T(8,128)(2,1)S(1)}, u32[]{:S(2)}, u32[]{:S(2)}) collective-permute-start(bf16[512,384]{1,0:T(8,128)(2,1)S(1)} %shard_map.67.refs_5_), channel_id=1, source_target_pairs={{0,1},{1,2},{2,3},{3,4},{4,5},{5,6},{6,7},{7,0},{8,15},{9,8},{10,9... | collective-permute-start | bytes 1179656 | tf_op jit(solution)/shard_map/ppermute | solution.py:262
  31.6 16.7 %collective-permute-start.21 = (bf16[768,768]{1,0:T(8,128)(2,1)S(1)}, bf16[768,768]{1,0:T(8,128)(2,1)S(1)}, u32[]{:S(2)}, u32[]{:S(2)}) collective-permute-start(bf16[768,768]{1,0:T(8,128)(2,1)S(1)} %pad_maximum_fusion.3), channel_id=1, source_target_pairs={{0,48},{8,200},{16,32},{24,216},{32,16},{40,232},{48,0},{56,248},{... | collective-permute-start | bytes 3538952 | tf_op jit(solution)/shard_map/ppermute | solution.py:271
  34.5 15.4 %collective-permute-start.17 = (bf16[768,768]{1,0:T(8,128)(2,1)S(1)}, bf16[768,768]{1,0:T(8,128)(2,1)S(1)}, u32[]{:S(2)}, u32[]{:S(2)}) collective-permute-start(bf16[768,768]{1,0:T(8,128)(2,1)S(1)} %pad_maximum_fusion.2), channel_id=1, source_target_pairs={{0,16},{8,72},{16,0},{24,88},{32,48},{40,104},{48,32},{56,120},{64... | collective-permute-start | bytes 3538952 | tf_op jit(solution)/shard_map/ppermute | solution.py:271
  34.6 7.0 %collective-permute-start.7 = (bf16[512,384]{1,0:T(8,128)(2,1)S(1)}, bf16[512,384]{1,0:T(8,128)(2,1)S(1)}, u32[]{:S(2)}, u32[]{:S(2)}) collective-permute-start(bf16[512,384]{1,0:T(8,128)(2,1)S(1)} %shard_map.68.refs_6_), channel_id=1, source_target_pairs={{0,1},{1,2},{2,3},{3,4},{4,5},{5,6},{6,7},{7,0},{8,15},{9,8},{10,9... | collective-permute-start | bytes 1179656 | tf_op jit(solution)/shard_map/ppermute | solution.py:262
  35.1 10.7 %collective-permute-start.8 = (bf16[512,384]{1,0:T(8,128)(2,1)S(1)}, bf16[512,384]{1,0:T(8,128)(2,1)S(1)}, u32[]{:S(2)}, u32[]{:S(2)}) collective-permute-start(bf16[512,384]{1,0:T(8,128)(2,1)S(1)} %shard_map.69.refs_7_), channel_id=1, source_target_pairs={{0,1},{1,2},{2,3},{3,4},{4,5},{5,6},{6,7},{7,0},{8,15},{9,8},{10,9... | collective-permute-start | bytes 1179656 | tf_op jit(solution)/shard_map/ppermute | solution.py:262
  41.6 11.1 %collective-permute-start.9 = (bf16[512,384]{1,0:T(8,128)(2,1)S(1)}, bf16[512,384]{1,0:T(8,128)(2,1)S(1)}, u32[]{:S(2)}, u32[]{:S(2)}) collective-permute-start(bf16[512,384]{1,0:T(8,128)(2,1)S(1)} %shard_map.70.refs_8_), channel_id=1, source_target_pairs={{0,1},{1,2},{2,3},{3,4},{4,5},{5,6},{6,7},{7,0},{8,15},{9,8},{10,9... | collective-permute-start | bytes 1179656 | tf_op jit(solution)/shard_map/ppermute | solution.py:262
  45.8 8.4 %collective-permute-start.10 = (bf16[512,384]{1,0:T(8,128)(2,1)S(1)}, bf16[512,384]{1,0:T(8,128)(2,1)S(1)}, u32[]{:S(2)}, u32[]{:S(2)}) collective-permute-start(bf16[512,384]{1,0:T(8,128)(2,1)S(1)} %shard_map.71.refs_9_), channel_id=1, source_target_pairs={{0,1},{1,2},{2,3},{3,4},{4,5},{5,6},{6,7},{7,0},{8,15},{9,8},{10,9... | collective-permute-start | bytes 1179656 | tf_op jit(solution)/shard_map/ppermute | solution.py:262
  48.4 23.8 %collective-permute-start.22 = (bf16[1536,512]{1,0:T(8,128)(2,1)S(1)}, bf16[1536,512]{1,0:T(8,128)(2,1)S(1)}, u32[]{:S(2)}, u32[]{:S(2)}) collective-permute-start(bf16[1536,512]{1,0:T(8,128)(2,1)S(1)} %pad_maximum_fusion.1.refs_16_), channel_id=1, source_target_pairs={{0,192},{8,24},{16,208},{24,8},{32,224},{40,56},{48,240},{56,40},{... | collective-permute-start | bytes 4718600 | tf_op jit(solution)/shard_map/ppermute | solution.py:280
  50.1 22.1 %collective-permute-start.18 = (bf16[1536,512]{1,0:T(8,128)(2,1)S(1)}, bf16[1536,512]{1,0:T(8,128)(2,1)S(1)}, u32[]{:S(2)}, u32[]{:S(2)}) collective-permute-start(bf16[1536,512]{1,0:T(8,128)(2,1)S(1)} %pad_maximum_fusion.refs_16_), channel_id=1, source_target_pairs={{0,64},{8,56},{16,80},{24,40},{32,96},{40,24},{48,112},{56,8},{64,... | collective-permute-start | bytes 4718600 | tf_op jit(solution)/shard_map/ppermute | solution.py:280
  52.6 6.9 %collective-permute-start.11 = (bf16[512,384]{1,0:T(8,128)(2,1)S(1)}, bf16[512,384]{1,0:T(8,128)(2,1)S(1)}, u32[]{:S(2)}, u32[]{:S(2)}) collective-permute-start(bf16[512,384]{1,0:T(8,128)(2,1)S(1)} %shard_map.72.refs_10_), channel_id=1, source_target_pairs={{0,1},{1,2},{2,3},{3,4},{4,5},{5,6},{6,7},{7,0},{8,15},{9,8},{10,9... | collective-permute-start | bytes 1179656 | tf_op jit(solution)/shard_map/ppermute | solution.py:262
  54.2 9.6 %collective-permute-start.12 = (bf16[512,384]{1,0:T(8,128)(2,1)S(1)}, bf16[512,384]{1,0:T(8,128)(2,1)S(1)}, u32[]{:S(2)}, u32[]{:S(2)}) collective-permute-start(bf16[512,384]{1,0:T(8,128)(2,1)S(1)} %shard_map.73.refs_11_), channel_id=1, source_target_pairs={{0,1},{1,2},{2,3},{3,4},{4,5},{5,6},{6,7},{7,0},{8,15},{9,8},{10,9... | collective-permute-start | bytes 1179656 | tf_op jit(solution)/shard_map/ppermute | solution.py:262
  59.6 8.4 %collective-permute-start.13 = (bf16[512,384]{1,0:T(8,128)(2,1)S(1)}, bf16[512,384]{1,0:T(8,128)(2,1)S(1)}, u32[]{:S(2)}, u32[]{:S(2)}) collective-permute-start(bf16[512,384]{1,0:T(8,128)(2,1)S(1)} %shard_map.74.refs_12_), channel_id=1, source_target_pairs={{0,1},{1,2},{2,3},{3,4},{4,5},{5,6},{6,7},{7,0},{8,15},{9,8},{10,9... | collective-permute-start | bytes 1179656 | tf_op jit(solution)/shard_map/ppermute | solution.py:262
  63.8 8.4 %collective-permute-start.14 = (bf16[512,384]{1,0:T(8,128)(2,1)S(1)}, bf16[512,384]{1,0:T(8,128)(2,1)S(1)}, u32[]{:S(2)}, u32[]{:S(2)}) collective-permute-start(bf16[512,384]{1,0:T(8,128)(2,1)S(1)} %shard_map.75.refs_13_), channel_id=1, source_target_pairs={{0,1},{1,2},{2,3},{3,4},{4,5},{5,6},{6,7},{7,0},{8,15},{9,8},{10,9... | collective-permute-start | bytes 1179656 | tf_op jit(solution)/shard_map/ppermute | solution.py:262
  76.2 9.2 %collective-permute-start.23 = (bf16[1024,512]{1,0:T(8,128)(2,1)S(1)}, bf16[1024,512]{1,0:T(8,128)(2,1)S(1)}, u32[]{:S(2)}, u32[]{:S(2)}) collective-permute-start(bf16[1024,512]{1,0:T(8,128)(2,1)S(1)} %shard_map.79), channel_id=1, source_target_pairs={{0,8},{8,0},{16,24},{24,16},{32,40},{40,32},{48,56},{56,48},{64,72... | collective-permute-start | bytes 3145736 | tf_op jit(solution)/shard_map/ppermute | solution.py:299
  78.8 11.5 %collective-permute-start.25 = (bf16[1536,256]{1,0:T(8,128)(2,1)S(1)}, bf16[1536,256]{1,0:T(8,128)(2,1)S(1)}, u32[]{:S(2)}, u32[]{:S(2)}) collective-permute-start(bf16[1536,256]{1,0:T(8,128)(2,1)S(1)} %pad_maximum_fusion.5.refs_16_), channel_id=1, source_target_pairs={{0,192},{8,24},{16,208},{24,8},{32,224},{40,56},{48,240},{56,40},{... | collective-permute-start | bytes 2359304 | tf_op jit(solution)/shard_map/ppermute | solution.py:280
  79.3 18.4 %collective-permute-start.24 = (bf16[1536,256]{1,0:T(8,128)(2,1)S(1)}, bf16[1536,256]{1,0:T(8,128)(2,1)S(1)}, u32[]{:S(2)}, u32[]{:S(2)}) collective-permute-start(bf16[1536,256]{1,0:T(8,128)(2,1)S(1)} %pad_maximum_fusion.4.refs_16_), channel_id=1, source_target_pairs={{0,64},{8,56},{16,80},{24,40},{32,96},{40,24},{48,112},{56,8},{64,... | collective-permute-start | bytes 2359304 | tf_op jit(solution)/shard_map/ppermute | solution.py:280
  86.3 6.4 %collective-permute-start.27 = (bf16[2,128,128]{2,1,0:T(8,128)(2,1)S(1)}, bf16[2,128,128]{2,1,0:T(8,128)(2,1)S(1)}, u32[]{:S(2)}, u32[]{:S(2)}) collective-permute-start(bf16[2,128,128]{2,1,0:T(8,128)(2,1)S(1)} %get-tuple-element.24), channel_id=1, source_target_pairs={{0,16},{8,24},{16,0},{24,8},{32,48},{40,56},{48,32},{56,40},{64,80... | collective-permute-start | bytes 196616 | tf_op jit(solution)/shard_map/ppermute | solution.py:314
  92.7 4.4 %collective-permute-start.28 = (bf16[2,128,128]{2,1,0:T(8,128)(2,1)S(1)}, bf16[2,128,128]{2,1,0:T(8,128)(2,1)S(1)}, u32[]{:S(2)}, u32[]{:S(2)}) collective-permute-start(bf16[2,128,128]{2,1,0:T(8,128)(2,1)S(1)} %add_convert_fusion.2), channel_id=1, source_target_pairs={{0,48},{8,56},{16,32},{24,40},{32,16},{40,24},{48,0},{56,8},{64,11... | collective-permute-start | bytes 196616 | tf_op jit(solution)/shard_map/ppermute | solution.py:314
  94.3 8.2 %collective-permute-start.26 = (bf16[1024,256]{1,0:T(8,128)(2,1)S(1)}, bf16[1024,256]{1,0:T(8,128)(2,1)S(1)}, u32[]{:S(2)}, u32[]{:S(2)}) collective-permute-start(bf16[1024,256]{1,0:T(8,128)(2,1)S(1)} %shard_map.82), channel_id=1, source_target_pairs={{0,8},{8,0},{16,24},{24,16},{32,40},{40,32},{48,56},{56,48},{64,72... | collective-permute-start | bytes 1572872 | tf_op jit(solution)/shard_map/ppermute | solution.py:304
  97.1 3.2 %collective-permute-start.29 = (bf16[2,128,128]{2,1,0:T(8,128)(2,1)S(1)}, bf16[2,128,128]{2,1,0:T(8,128)(2,1)S(1)}, u32[]{:S(2)}, u32[]{:S(2)}) collective-permute-start(bf16[2,128,128]{2,1,0:T(8,128)(2,1)S(1)} %add_convert_fusion.1), channel_id=1, source_target_pairs={{0,64},{8,72},{16,80},{24,88},{32,96},{40,104},{48,112},{56,120},{... | collective-permute-start | bytes 196616 | tf_op jit(solution)/shard_map/ppermute | solution.py:314
  100.1 4.7 %copy-start = (f32[512]{0:T(512)S(1)}, f32[512]{0:T(512)}, u32[]{:S(2)}) copy-start(f32[512]{0:T(512)} %param.10) | copy-start | bytes 6148
  100.4 4.4 %collective-permute-start.30 = (bf16[2,128,128]{2,1,0:T(8,128)(2,1)S(1)}, bf16[2,128,128]{2,1,0:T(8,128)(2,1)S(1)}, u32[]{:S(2)}, u32[]{:S(2)}) collective-permute-start(bf16[2,128,128]{2,1,0:T(8,128)(2,1)S(1)} %add_convert_fusion), channel_id=1, source_target_pairs={{0,192},{8,200},{16,208},{24,216},{32,224},{40,232},{48,240},{56,2... | collective-permute-start | bytes 196616 | tf_op jit(solution)/shard_map/ppermute | solution.py:314
  105.7 6.5 %collective-permute-start.31 = (bf16[512,256]{1,0:T(8,128)(2,1)S(1)}, bf16[512,256]{1,0:T(8,128)(2,1)S(1)}, u32[]{:S(2)}, u32[]{:S(2)}) collective-permute-start(bf16[512,256]{1,0:T(8,128)(2,1)S(1)} %shard_map.85), channel_id=1, source_target_pairs={{0,8},{8,0},{16,24},{24,16},{32,40},{40,32},{48,56},{56,48},{64,72... | collective-permute-start | bytes 786440 | tf_op jit(solution)/shard_map/ppermute | solution.py:318

commit v9 on v8

--- a/solution.py
+++ b/solution.py
@@ -276,7 +276,7 @@
     for low, high in ((0, 2 * HALF), (2 * HALF, 3 * HALF)):
         near = [jnp.concatenate([part[:, low:high] for part in pair], axis=0) for pair in pairs]
         if low:
-            near = [after(part, second[-1]) for part in near]
+            near = [after(part, first[-1]) for part in near]
         blocks.append([[near[j], lax.ppermute(near[j], "seq", cube_pairs(j, 3))] for j in range(2)])
     pieces = zip(first, second)
     return [p for pair in pieces for p in pair], blocks
@@ -307,7 +307,7 @@
     for step, dim in enumerate((0, 2, 1, 3)):
         if got:
             group = (group.astype(F32) + got[-1].astype(F32)).astype(BF16)
-        if step == 1:
+        if step == 2:
             group = after(group, q_theirs)
         if step == 3:
             group = after(group, q_mine)

time: 115 us -> 113 us (0.983)
  starting transfers between devices: 58.2 us -> 54.1 us
    ppermute x4, waiting for transfers between devices: 2.01 us -> 6.15 us  [local(): got.append(lax.ppermute(group, 'seq', exchange_pairs(dim)))]
    ppermute x4, waiting for transfers between devices: 3.38 us -> 0.01 us  [gather(): lax.ppermute(near[j], 'seq', cube_pairs(j, 3))]
    ppermute x1, starting transfers between devices: 5.35 us -> 2.99 us  [local(): out_got = lax.ppermute(finish(False, *last), 'seq', SWAP)]
    ppermute x1, starting transfers between devices: 2.36 us -> 0.76 us  [local(): q_got = lax.ppermute(q_theirs, 'seq', SWAP)]
  transfers between devices with their start and end apart: 32 -> 32, of which waited for: 18 -> 16; matrix products, arithmetic and copies ran while one was open for 2% -> 2% of each run, Pallas kernels for 10% -> 10%
where the time goes in v9:
time: 113 us; the launch traced here: 110 us
  starting transfers between devices  54.1 us (48%)
  waiting for transfers between devices  34.4 us (30%)
  Pallas kernels  16.4 us (15%)
  local copies, waits for them, and re-layouts  3.19 us (3%)
  other arithmetic  1.92 us (2%)
    ppermute x14, starting transfers between devices, pass_on(): return lax.ppermute(piece, ('seq', 'head'), ring)  25.8 us
    ppermute x14, waiting for transfers between devices, pass_on(): return lax.ppermute(piece, ('seq', 'head'), ring)  23.7 us
    pallas_call x4, Pallas kernels, product(): pl.pallas_call(functools.partial(product_kernel, mine), out_shape=jax.Sha...  12.7 us
    ppermute x6, starting transfers between devices, gather(): lax.ppermute(streams[j], 'seq', cube_pairs(j, step))  8.86 us
    ppermute x4, waiting for transfers between devices, local(): got.append(lax.ppermute(group, 'seq', exchange_pairs(dim)))  6.15 us
    ppermute x4, starting transfers between devices, local(): got.append(lax.ppermute(group, 'seq', exchange_pairs(dim)))  5.08 us
    ppermute x4, starting transfers between devices, gather(): lax.ppermute(near[j], 'seq', cube_pairs(j, 3))  4.91 us
    ppermute x6, waiting for transfers between devices, gather(): lax.ppermute(streams[j], 'seq', cube_pairs(j, step))  4.27 us
  transfers between devices with their start and end apart: 32, of which 16 were waited for; matrix products, arithmetic and copies ran while one was open for 2% of the time, Pallas kernels for 10%

profile of v9, /device:TPU:1, one launch (start us, length us, event | category | flops | bytes accessed | tf_op | source)
XLA Modules:
  0.0 110.4 jit_solution(9626797692069286351)
XLA Ops:
  0.0 1.6 %fusion = (bf16[512,192]{1,0:T(8,128)(2,1)S(1)}, bf16[512,192]{1,0:T(8,128)(2,1)S(1)}, bf16[512,192]{1,0:T(8,128)(2,1)S(1)}, bf16[512,192]{1,0:T(8,128)(2,1)S(1)}) fusion(bf16[512,768]{1,0:T(8,128)(2,1)} %param.6), kind=kLoop, calls=%fused_computation.23 | loop fusion | bytes 1572864 | tf_op jit(solution)/shard_map/slice | solution.py:255
  1.6 0.3 broadcast_select_fusion
  2.0 3.3 %collective-permute-start = (bf16[512,384]{1,0:T(8,128)(2,1)S(1)}, bf16[512,384]{1,0:T(8,128)(2,1)S(1)}, u32[]{:S(2)}, u32[]{:S(2)}) collective-permute-start(bf16[512,384]{1,0:T(8,128)(2,1)S(1)} %get-tuple-element.35), channel_id=1, source_target_pairs={{0,8},{8,0},{16,24},{24,16},{32,40},{40,32},{48,56},{56,48},{64,72... | collective-permute-start | bytes 1179656 | tf_op jit(solution)/shard_map/ppermute | solution.py:258
  5.3 3.8 %collective-permute-start.1 = (bf16[512,384]{1,0:T(8,128)(2,1)S(1)}, bf16[512,384]{1,0:T(8,128)(2,1)S(1)}, u32[]{:S(2)}, u32[]{:S(2)}) collective-permute-start(bf16[512,384]{1,0:T(8,128)(2,1)S(1)} %get-tuple-element.36.refs_0_), channel_id=1, source_target_pairs={{0,1},{1,2},{2,3},{3,4},{4,5},{5,6},{6,7},{7,0},{8,15},{9,8},{10,9... | collective-permute-start | bytes 1179656 | tf_op jit(solution)/shard_map/ppermute | solution.py:262
  9.2 1.3 %collective-permute-start.2 = (bf16[512,384]{1,0:T(8,128)(2,1)S(1)}, bf16[512,384]{1,0:T(8,128)(2,1)S(1)}, u32[]{:S(2)}, u32[]{:S(2)}) collective-permute-start(bf16[512,384]{1,0:T(8,128)(2,1)S(1)} %collective-permute-done.refs_1_), channel_id=1, source_target_pairs={{0,1},{1,2},{2,3},{3,4},{4,5},{5,6},{6,7},{7,0},{8,15},{9,8},{10,9... | collective-permute-start | bytes 1179656 | tf_op jit(solution)/shard_map/ppermute | solution.py:262
  10.5 0.1 broadcast_select_fusion.2
  10.6 1.4 %collective-permute-start.19 = (bf16[192,768]{1,0:T(8,128)(2,1)S(1)}, bf16[192,768]{1,0:T(8,128)(2,1)S(1)}, u32[]{:S(2)}, u32[]{:S(2)}) collective-permute-start(bf16[192,768]{1,0:T(8,128)(2,1)S(1)} %get-tuple-element.41), channel_id=1, source_target_pairs={{0,16},{8,72},{16,0},{24,88},{32,48},{40,104},{48,32},{56,120},{64... | collective-permute-start | bytes 884744 | tf_op jit(solution)/shard_map/ppermute | solution.py:271
  12.0 1.9 %collective-permute-start.15 = (bf16[192,768]{1,0:T(8,128)(2,1)S(1)}, bf16[192,768]{1,0:T(8,128)(2,1)S(1)}, u32[]{:S(2)}, u32[]{:S(2)}) collective-permute-start(bf16[192,768]{1,0:T(8,128)(2,1)S(1)} %get-tuple-element.42), channel_id=1, source_target_pairs={{0,48},{8,200},{16,32},{24,216},{32,16},{40,232},{48,0},{56,248},{... | collective-permute-start | bytes 884744 | tf_op jit(solution)/shard_map/ppermute | solution.py:271
  13.9 3.4 %collective-permute-start.3 = (bf16[512,384]{1,0:T(8,128)(2,1)S(1)}, bf16[512,384]{1,0:T(8,128)(2,1)S(1)}, u32[]{:S(2)}, u32[]{:S(2)}) collective-permute-start(bf16[512,384]{1,0:T(8,128)(2,1)S(1)} %shard_map.64.refs_2_), channel_id=1, source_target_pairs={{0,1},{1,2},{2,3},{3,4},{4,5},{5,6},{6,7},{7,0},{8,15},{9,8},{10,9... | collective-permute-start | bytes 1179656 | tf_op jit(solution)/shard_map/ppermute | solution.py:262
  17.3 0.8 collective-permute-done.2.piece
  18.1 3.1 %collective-permute-start.4 = (bf16[512,384]{1,0:T(8,128)(2,1)S(1)}, bf16[512,384]{1,0:T(8,128)(2,1)S(1)}, u32[]{:S(2)}, u32[]{:S(2)}) collective-permute-start(bf16[512,384]{1,0:T(8,128)(2,1)S(1)} %shard_map.65.refs_3_), channel_id=1, source_target_pairs={{0,1},{1,2},{2,3},{3,4},{4,5},{5,6},{6,7},{7,0},{8,15},{9,8},{10,9... | collective-permute-start | bytes 1179656 | tf_op jit(solution)/shard_map/ppermute | solution.py:262
  21.2 2.6 %collective-permute-start.20 = (bf16[384,768]{1,0:T(8,128)(2,1)S(1)}, bf16[384,768]{1,0:T(8,128)(2,1)S(1)}, u32[]{:S(2)}, u32[]{:S(2)}) collective-permute-start(bf16[384,768]{1,0:T(8,128)(2,1)S(1)} %pad_maximum_fusion.7), channel_id=1, source_target_pairs={{0,64},{8,56},{16,80},{24,40},{32,96},{40,24},{48,112},{56,8},{64,... | collective-permute-start | bytes 1769480 | tf_op jit(solution)/shard_map/ppermute | solution.py:271
  23.8 0.1 collective-permute-start.16
  24.0 1.4 %collective-permute-start.5 = (bf16[512,384]{1,0:T(8,128)(2,1)S(1)}, bf16[512,384]{1,0:T(8,128)(2,1)S(1)}, u32[]{:S(2)}, u32[]{:S(2)}) collective-permute-start(bf16[512,384]{1,0:T(8,128)(2,1)S(1)} %shard_map.66.refs_4_), channel_id=1, source_target_pairs={{0,1},{1,2},{2,3},{3,4},{4,5},{5,6},{6,7},{7,0},{8,15},{9,8},{10,9... | collective-permute-start | bytes 1179656 | tf_op jit(solution)/shard_map/ppermute | solution.py:262
  25.4 1.1 collective-permute-done.4.piece
  26.5 3.4 %collective-permute-start.6 = (bf16[512,384]{1,0:T(8,128)(2,1)S(1)}, bf16[512,384]{1,0:T(8,128)(2,1)S(1)}, u32[]{:S(2)}, u32[]{:S(2)}) collective-permute-start(bf16[512,384]{1,0:T(8,128)(2,1)S(1)} %shard_map.67.refs_5_), channel_id=1, source_target_pairs={{0,1},{1,2},{2,3},{3,4},{4,5},{5,6},{6,7},{7,0},{8,15},{9,8},{10,9... | collective-permute-start | bytes 1179656 | tf_op jit(solution)/shard_map/ppermute | solution.py:262
  29.9 1.7 %collective-permute-done.20 = bf16[384,768]{1,0:T(8,128)(2,1)S(1)} collective-permute-done((bf16[384,768]{1,0:T(8,128)(2,1)S(1)}, bf16[384,768]{1,0:T(8,128)(2,1)S(1)}, u32[]{:S(2)}, u32[]{:S(2)}) %collective-permute-start.20) | collective-permute-done | bytes 589856 | tf_op jit(solution)/shard_map/ppermute | solution.py:271
  31.5 0.1 pad_maximum_fusion.3
  31.6 2.8 %collective-permute-start.21 = (bf16[768,768]{1,0:T(8,128)(2,1)S(1)}, bf16[768,768]{1,0:T(8,128)(2,1)S(1)}, u32[]{:S(2)}, u32[]{:S(2)}) collective-permute-start(bf16[768,768]{1,0:T(8,128)(2,1)S(1)} %pad_maximum_fusion.3), channel_id=1, source_target_pairs={{0,48},{8,200},{16,32},{24,216},{32,16},{40,232},{48,0},{56,248},{... | collective-permute-start | bytes 3538952 | tf_op jit(solution)/shard_map/ppermute | solution.py:271
  34.5 0.1 collective-permute-start.17
  34.7 0.1 collective-permute-start.7
  34.7 0.4 collective-permute-done.6.piece
  35.2 3.2 %collective-permute-start.8 = (bf16[512,384]{1,0:T(8,128)(2,1)S(1)}, bf16[512,384]{1,0:T(8,128)(2,1)S(1)}, u32[]{:S(2)}, u32[]{:S(2)}) collective-permute-start(bf16[512,384]{1,0:T(8,128)(2,1)S(1)} %shard_map.69.refs_7_), channel_id=1, source_target_pairs={{0,1},{1,2},{2,3},{3,4},{4,5},{5,6},{6,7},{7,0},{8,15},{9,8},{10,9... | collective-permute-start | bytes 1179656 | tf_op jit(solution)/shard_map/ppermute | solution.py:262
  38.4 3.2 %collective-permute-done.7.piece = bf16[512,384]{1,0:T(8,128)(2,1)S(1)} collective-permute-done((bf16[512,384]{1,0:T(8,128)(2,1)S(1)}, bf16[512,384]{1,0:T(8,128)(2,1)S(1)}, u32[]{:S(2)}, u32[]{:S(2)}) %collective-permute-start.7) | collective-permute-done | bytes 393248 | tf_op jit(solution)/shard_map/ppermute | solution.py:262
  41.7 1.2 %collective-permute-start.9 = (bf16[512,384]{1,0:T(8,128)(2,1)S(1)}, bf16[512,384]{1,0:T(8,128)(2,1)S(1)}, u32[]{:S(2)}, u32[]{:S(2)}) collective-permute-start(bf16[512,384]{1,0:T(8,128)(2,1)S(1)} %shard_map.70.refs_8_), channel_id=1, source_target_pairs={{0,1},{1,2},{2,3},{3,4},{4,5},{5,6},{6,7},{7,0},{8,15},{9,8},{10,9... | collective-permute-start | bytes 1179656 | tf_op jit(solution)/shard_map/ppermute | solution.py:262
  42.9 3.0 %collective-permute-done.8.piece = bf16[512,384]{1,0:T(8,128)(2,1)S(1)} collective-permute-done((bf16[512,384]{1,0:T(8,128)(2,1)S(1)}, bf16[512,384]{1,0:T(8,128)(2,1)S(1)}, u32[]{:S(2)}, u32[]{:S(2)}) %collective-permute-start.8) | collective-permute-done | bytes 393248 | tf_op jit(solution)/shard_map/ppermute | solution.py:262
  45.9 1.2 %collective-permute-start.10 = (bf16[512,384]{1,0:T(8,128)(2,1)S(1)}, bf16[512,384]{1,0:T(8,128)(2,1)S(1)}, u32[]{:S(2)}, u32[]{:S(2)}) collective-permute-start(bf16[512,384]{1,0:T(8,128)(2,1)S(1)} %shard_map.71.refs_9_), channel_id=1, source_target_pairs={{0,1},{1,2},{2,3},{3,4},{4,5},{5,6},{6,7},{7,0},{8,15},{9,8},{10,9... | collective-permute-start | bytes 1179656 | tf_op jit(solution)/shard_map/ppermute | solution.py:262
  47.1 1.3 %collective-permute-done.21 = bf16[768,768]{1,0:T(8,128)(2,1)S(1)} collective-permute-done((bf16[768,768]{1,0:T(8,128)(2,1)S(1)}, bf16[768,768]{1,0:T(8,128)(2,1)S(1)}, u32[]{:S(2)}, u32[]{:S(2)}) %collective-permute-start.21) | collective-permute-done | bytes 1179680 | tf_op jit(solution)/shard_map/ppermute | solution.py:271
  48.4 0.1 pad_maximum_fusion.1.refs_16_
  48.5 0.1 collective-permute-start.22
  48.6 1.4 %collective-permute-done.17 = bf16[768,768]{1,0:T(8,128)(2,1)S(1)} collective-permute-done((bf16[768,768]{1,0:T(8,128)(2,1)S(1)}, bf16[768,768]{1,0:T(8,128)(2,1)S(1)}, u32[]{:S(2)}, u32[]{:S(2)}) %collective-permute-start.17) | collective-permute-done | bytes 1179680 | tf_op jit(solution)/shard_map/ppermute | solution.py:271
  50.0 0.1 pad_maximum_fusion.refs_16_
  50.1 2.6 %collective-permute-start.18 = (bf16[1536,512]{1,0:T(8,128)(2,1)S(1)}, bf16[1536,512]{1,0:T(8,128)(2,1)S(1)}, u32[]{:S(2)}, u32[]{:S(2)}) collective-permute-start(bf16[1536,512]{1,0:T(8,128)(2,1)S(1)} %pad_maximum_fusion.refs_16_), channel_id=1, source_target_pairs={{0,64},{8,56},{16,80},{24,40},{32,96},{40,24},{48,112},{56,8},{64,... | collective-permute-start | bytes 4718600 | tf_op jit(solution)/shard_map/ppermute | solution.py:280
  52.7 1.6 %collective-permute-done.10.piece = bf16[512,384]{1,0:T(8,128)(2,1)S(1)} collective-permute-done((bf16[512,384]{1,0:T(8,128)(2,1)S(1)}, bf16[512,384]{1,0:T(8,128)(2,1)S(1)}, u32[]{:S(2)}, u32[]{:S(2)}) %collective-permute-start.10) | collective-permute-done | bytes 393248 | tf_op jit(solution)/shard_map/ppermute | solution.py:262
  54.3 1.2 %collective-permute-start.12 = (bf16[512,384]{1,0:T(8,128)(2,1)S(1)}, bf16[512,384]{1,0:T(8,128)(2,1)S(1)}, u32[]{:S(2)}, u32[]{:S(2)}) collective-permute-start(bf16[512,384]{1,0:T(8,128)(2,1)S(1)} %shard_map.73.refs_11_), channel_id=1, source_target_pairs={{0,1},{1,2},{2,3},{3,4},{4,5},{5,6},{6,7},{7,0},{8,15},{9,8},{10,9... | collective-permute-start | bytes 1179656 | tf_op jit(solution)/shard_map/ppermute | solution.py:262
  55.5 4.1 %collective-permute-done.11.piece = bf16[512,384]{1,0:T(8,128)(2,1)S(1)} collective-permute-done((bf16[512,384]{1,0:T(8,128)(2,1)S(1)}, bf16[512,384]{1,0:T(8,128)(2,1)S(1)}, u32[]{:S(2)}, u32[]{:S(2)}) %collective-permute-start.11) | collective-permute-done | bytes 393248 | tf_op jit(solution)/shard_map/ppermute | solution.py:262
  59.6 1.2 %collective-permute-start.13 = (bf16[512,384]{1,0:T(8,128)(2,1)S(1)}, bf16[512,384]{1,0:T(8,128)(2,1)S(1)}, u32[]{:S(2)}, u32[]{:S(2)}) collective-permute-start(bf16[512,384]{1,0:T(8,128)(2,1)S(1)} %shard_map.74.refs_12_), channel_id=1, source_target_pairs={{0,1},{1,2},{2,3},{3,4},{4,5},{5,6},{6,7},{7,0},{8,15},{9,8},{10,9... | collective-permute-start | bytes 1179656 | tf_op jit(solution)/shard_map/ppermute | solution.py:262
  60.9 3.0 %collective-permute-done.12.piece = bf16[512,384]{1,0:T(8,128)(2,1)S(1)} collective-permute-done((bf16[512,384]{1,0:T(8,128)(2,1)S(1)}, bf16[512,384]{1,0:T(8,128)(2,1)S(1)}, u32[]{:S(2)}, u32[]{:S(2)}) %collective-permute-start.12) | collective-permute-done | bytes 393248 | tf_op jit(solution)/shard_map/ppermute | solution.py:262
  63.9 1.2 %collective-permute-start.14 = (bf16[512,384]{1,0:T(8,128)(2,1)S(1)}, bf16[512,384]{1,0:T(8,128)(2,1)S(1)}, u32[]{:S(2)}, u32[]{:S(2)}) collective-permute-start(bf16[512,384]{1,0:T(8,128)(2,1)S(1)} %shard_map.75.refs_13_), channel_id=1, source_target_pairs={{0,1},{1,2},{2,3},{3,4},{4,5},{5,6},{6,7},{7,0},{8,15},{9,8},{10,9... | collective-permute-start | bytes 1179656 | tf_op jit(solution)/shard_map/ppermute | solution.py:262
  65.1 0.7 dynamic-slice_bitcast_fusion.info
  65.8 2.3 %collective-permute-done.13.piece = bf16[512,384]{1,0:T(8,128)(2,1)S(1)} collective-permute-done((bf16[512,384]{1,0:T(8,128)(2,1)S(1)}, bf16[512,384]{1,0:T(8,128)(2,1)S(1)}, u32[]{:S(2)}, u32[]{:S(2)}) %collective-permute-start.13) | collective-permute-done | bytes 393248 | tf_op jit(solution)/shard_map/ppermute | solution.py:262
  68.1 4.2 %collective-permute-done.14.piece = bf16[512,384]{1,0:T(8,128)(2,1)S(1)} collective-permute-done((bf16[512,384]{1,0:T(8,128)(2,1)S(1)}, bf16[512,384]{1,0:T(8,128)(2,1)S(1)}, u32[]{:S(2)}, u32[]{:S(2)}) %collective-permute-start.14) | collective-permute-done | bytes 393248 | tf_op jit(solution)/shard_map/ppermute | solution.py:262
  72.3 4.0 %shard_map.79 = bf16[1024,512]{1,0:T(8,128)(2,1)S(1)} custom-call(s32[37]{0:T(128)S(1)} %dynamic-slice_bitcast_fusion.info, bf16[512,384]{1,0:T(8,128)(2,1)S(1)} %get-tuple-element.36.refs_0_, bf16[512,384]{1,0:T(8,128)(2,1)S(1)} %collective-permute-done.refs_1_, bf16[512,384]{1,0:T(8,128)(2,1)S(1)} %shard_map.64.refs_2_, ...), custom_call_target="tpu_custom_call" | custom-call | flops 3221225472 | bytes 1048576 | tf_op jit(solution)/shard_map/pallas_call | solution.py:121
  76.3 2.4 %collective-permute-start.23 = (bf16[1024,512]{1,0:T(8,128)(2,1)S(1)}, bf16[1024,512]{1,0:T(8,128)(2,1)S(1)}, u32[]{:S(2)}, u32[]{:S(2)}) collective-permute-start(bf16[1024,512]{1,0:T(8,128)(2,1)S(1)} %shard_map.79), channel_id=1, source_target_pairs={{0,8},{8,0},{16,24},{24,16},{32,40},{40,32},{48,56},{56,48},{64,72... | collective-permute-start | bytes 3145736 | tf_op jit(solution)/shard_map/ppermute | solution.py:299
  78.9 0.3 collective-permute-start.25
  79.3 0.5 slice-done
  79.9 1.9 %collective-permute-start.24 = (bf16[1536,256]{1,0:T(8,128)(2,1)S(1)}, bf16[1536,256]{1,0:T(8,128)(2,1)S(1)}, u32[]{:S(2)}, u32[]{:S(2)}) collective-permute-start(bf16[1536,256]{1,0:T(8,128)(2,1)S(1)} %pad_maximum_fusion.4.refs_16_), channel_id=1, source_target_pairs={{0,64},{8,56},{16,80},{24,40},{32,96},{40,24},{48,112},{56,8},{64,... | collective-permute-start | bytes 2359304 | tf_op jit(solution)/shard_map/ppermute | solution.py:280
  81.8 4.0 %shard_map.78.mine = f32[1024,512]{1,0:T(8,128)S(1)} custom-call(s32[37]{0:T(128)S(1)} %dynamic-slice_bitcast_fusion.info, bf16[512,384]{1,0:T(8,128)(2,1)S(1)} %get-tuple-element.36.refs_0_, bf16[512,384]{1,0:T(8,128)(2,1)S(1)} %collective-permute-done.refs_1_, bf16[512,384]{1,0:T(8,128)(2,1)S(1)} %shard_map.64.refs_2_, ...), custom_call_target="tpu_custom_call" | custom-call | flops 3221225472 | bytes 1048576 | tf_op jit(solution)/shard_map/pallas_call | solution.py:121
  85.8 0.8 shard_map.80
  86.6 0.4 collective-permute-start.27
  87.0 4.6 %collective-permute-done.27.got_0 = bf16[2,128,128]{2,1,0:T(8,128)(2,1)S(1)} collective-permute-done((bf16[2,128,128]{2,1,0:T(8,128)(2,1)S(1)}, bf16[2,128,128]{2,1,0:T(8,128)(2,1)S(1)}, u32[]{:S(2)}, u32[]{:S(2)}) %collective-permute-start.27) | collective-permute-done | bytes 65568 | tf_op jit(solution)/shard_map/ppermute | solution.py:314
  91.6 1.9 %collective-permute-start.28 = (bf16[2,128,128]{2,1,0:T(8,128)(2,1)S(1)}, bf16[2,128,128]{2,1,0:T(8,128)(2,1)S(1)}, u32[]{:S(2)}, u32[]{:S(2)}) collective-permute-start(bf16[2,128,128]{2,1,0:T(8,128)(2,1)S(1)} %add_convert_fusion.2), channel_id=1, source_target_pairs={{0,48},{8,56},{16,32},{24,40},{32,16},{40,24},{48,0},{56,8},{64,11... | collective-permute-start | bytes 196616 | tf_op jit(solution)/shard_map/ppermute | solution.py:314
  93.5 2.4 %shard_map.82 = bf16[1024,256]{1,0:T(8,128)(2,1)S(1)} custom-call(s32[37]{0:T(128)S(1)} %dynamic-slice_bitcast_fusion.info, bf16[512,384]{1,0:T(8,128)(2,1)S(1)} %get-tuple-element.36.refs_0_, bf16[512,384]{1,0:T(8,128)(2,1)S(1)} %collective-permute-done.refs_1_, bf16[512,384]{1,0:T(8,128)(2,1)S(1)} %shard_map.64.refs_2_, ...), custom_call_target="tpu_custom_call" | custom-call | flops 1610612736 | bytes 1048576 | tf_op jit(solution)/shard_map/pallas_call | solution.py:121
  95.9 0.8 collective-permute-start.26
  96.6 0.9 collective-permute-start.29
  97.6 2.4 %shard_map.81.mine = f32[1024,256]{1,0:T(8,128)S(1)} custom-call(s32[37]{0:T(128)S(1)} %dynamic-slice_bitcast_fusion.info, bf16[512,384]{1,0:T(8,128)(2,1)S(1)} %get-tuple-element.36.refs_0_, bf16[512,384]{1,0:T(8,128)(2,1)S(1)} %collective-permute-done.refs_1_, bf16[512,384]{1,0:T(8,128)(2,1)S(1)} %shard_map.64.refs_2_, ...), custom_call_target="tpu_custom_call" | custom-call | flops 1610612736 | bytes 1048576 | tf_op jit(solution)/shard_map/pallas_call | solution.py:121
  100.0 1.9 %collective-permute-start.30 = (bf16[2,128,128]{2,1,0:T(8,128)(2,1)S(1)}, bf16[2,128,128]{2,1,0:T(8,128)(2,1)S(1)}, u32[]{:S(2)}, u32[]{:S(2)}) collective-permute-start(bf16[2,128,128]{2,1,0:T(8,128)(2,1)S(1)} %add_convert_fusion), channel_id=1, source_target_pairs={{0,192},{8,200},{16,208},{24,216},{32,224},{40,232},{48,240},{56,2... | collective-permute-start | bytes 196616 | tf_op jit(solution)/shard_map/ppermute | solution.py:314
  101.9 0.9 shard_map.83
  102.8 1.6 %collective-permute-done.30.got_3 = bf16[2,128,128]{2,1,0:T(8,128)(2,1)S(1)} collective-permute-done((bf16[2,128,128]{2,1,0:T(8,128)(2,1)S(1)}, bf16[2,128,128]{2,1,0:T(8,128)(2,1)S(1)}, u32[]{:S(2)}, u32[]{:S(2)}) %collective-permute-start.30) | collective-permute-done | bytes 65568 | tf_op jit(solution)/shard_map/ppermute | solution.py:314
  104.4 0.9 shard_map.85
  105.4 3.0 %collective-permute-start.31 = (bf16[512,256]{1,0:T(8,128)(2,1)S(1)}, bf16[512,256]{1,0:T(8,128)(2,1)S(1)}, u32[]{:S(2)}, u32[]{:S(2)}) collective-permute-start(bf16[512,256]{1,0:T(8,128)(2,1)S(1)} %shard_map.85), channel_id=1, source_target_pairs={{0,8},{8,0},{16,24},{24,16},{32,40},{40,32},{48,56},{56,48},{64,72... | collective-permute-start | bytes 786440 | tf_op jit(solution)/shard_map/ppermute | solution.py:318
  108.4 0.9 shard_map.84
  109.3 0.2 collective-permute-done.31
  109.6 0.8 pad_maximum_fusion.8
  (60 shorter events, 0.8 us)
Async XLA Ops:
  0.0 9.1 %copy-start.3 = (bf16[192,512]{1,0:T(8,128)(2,1)S(1)}, bf16[192,512]{1,0:T(8,128)(2,1)}, u32[]{:S(2)}) copy-start(bf16[192,512]{1,0:T(8,128)(2,1)} %param.8) | copy-start | bytes 589828
  0.0 9.1 %copy-start.4 = (bf16[192,512]{1,0:T(8,128)(2,1)S(1)}, bf16[192,512]{1,0:T(8,128)(2,1)}, u32[]{:S(2)}) copy-start(bf16[192,512]{1,0:T(8,128)(2,1)} %param.9) | copy-start | bytes 589828
  1.6 8.9 %copy-start.2 = (bf16[192,512]{1,0:T(8,128)(2,1)S(1)}, bf16[192,512]{1,0:T(8,128)(2,1)}, u32[]{:S(2)}) copy-start(bf16[192,512]{1,0:T(8,128)(2,1)} %param.7) | copy-start | bytes 589828
  2.0 7.2 %collective-permute-start = (bf16[512,384]{1,0:T(8,128)(2,1)S(1)}, bf16[512,384]{1,0:T(8,128)(2,1)S(1)}, u32[]{:S(2)}, u32[]{:S(2)}) collective-permute-start(bf16[512,384]{1,0:T(8,128)(2,1)S(1)} %get-tuple-element.35), channel_id=1, source_target_pairs={{0,8},{8,0},{16,24},{24,16},{32,40},{40,32},{48,56},{56,48},{64,72... | collective-permute-start | bytes 1179656 | tf_op jit(solution)/shard_map/ppermute | solution.py:258
  5.3 8.6 %collective-permute-start.1 = (bf16[512,384]{1,0:T(8,128)(2,1)S(1)}, bf16[512,384]{1,0:T(8,128)(2,1)S(1)}, u32[]{:S(2)}, u32[]{:S(2)}) collective-permute-start(bf16[512,384]{1,0:T(8,128)(2,1)S(1)} %get-tuple-element.36.refs_0_), channel_id=1, source_target_pairs={{0,1},{1,2},{2,3},{3,4},{4,5},{5,6},{6,7},{7,0},{8,15},{9,8},{10,9... | collective-permute-start | bytes 1179656 | tf_op jit(solution)/shard_map/ppermute | solution.py:262
  9.2 8.9 %collective-permute-start.2 = (bf16[512,384]{1,0:T(8,128)(2,1)S(1)}, bf16[512,384]{1,0:T(8,128)(2,1)S(1)}, u32[]{:S(2)}, u32[]{:S(2)}) collective-permute-start(bf16[512,384]{1,0:T(8,128)(2,1)S(1)} %collective-permute-done.refs_1_), channel_id=1, source_target_pairs={{0,1},{1,2},{2,3},{3,4},{4,5},{5,6},{6,7},{7,0},{8,15},{9,8},{10,9... | collective-permute-start | bytes 1179656 | tf_op jit(solution)/shard_map/ppermute | solution.py:262
  10.6 10.6 %collective-permute-start.19 = (bf16[192,768]{1,0:T(8,128)(2,1)S(1)}, bf16[192,768]{1,0:T(8,128)(2,1)S(1)}, u32[]{:S(2)}, u32[]{:S(2)}) collective-permute-start(bf16[192,768]{1,0:T(8,128)(2,1)S(1)} %get-tuple-element.41), channel_id=1, source_target_pairs={{0,16},{8,72},{16,0},{24,88},{32,48},{40,104},{48,32},{56,120},{64... | collective-permute-start | bytes 884744 | tf_op jit(solution)/shard_map/ppermute | solution.py:271
  12.0 11.8 %collective-permute-start.15 = (bf16[192,768]{1,0:T(8,128)(2,1)S(1)}, bf16[192,768]{1,0:T(8,128)(2,1)S(1)}, u32[]{:S(2)}, u32[]{:S(2)}) collective-permute-start(bf16[192,768]{1,0:T(8,128)(2,1)S(1)} %get-tuple-element.42), channel_id=1, source_target_pairs={{0,48},{8,200},{16,32},{24,216},{32,16},{40,232},{48,0},{56,248},{... | collective-permute-start | bytes 884744 | tf_op jit(solution)/shard_map/ppermute | solution.py:271
  13.9 10.0 %collective-permute-start.3 = (bf16[512,384]{1,0:T(8,128)(2,1)S(1)}, bf16[512,384]{1,0:T(8,128)(2,1)S(1)}, u32[]{:S(2)}, u32[]{:S(2)}) collective-permute-start(bf16[512,384]{1,0:T(8,128)(2,1)S(1)} %shard_map.64.refs_2_), channel_id=1, source_target_pairs={{0,1},{1,2},{2,3},{3,4},{4,5},{5,6},{6,7},{7,0},{8,15},{9,8},{10,9... | collective-permute-start | bytes 1179656 | tf_op jit(solution)/shard_map/ppermute | solution.py:262
  18.1 8.4 %collective-permute-start.4 = (bf16[512,384]{1,0:T(8,128)(2,1)S(1)}, bf16[512,384]{1,0:T(8,128)(2,1)S(1)}, u32[]{:S(2)}, u32[]{:S(2)}) collective-permute-start(bf16[512,384]{1,0:T(8,128)(2,1)S(1)} %shard_map.65.refs_3_), channel_id=1, source_target_pairs={{0,1},{1,2},{2,3},{3,4},{4,5},{5,6},{6,7},{7,0},{8,15},{9,8},{10,9... | collective-permute-start | bytes 1179656 | tf_op jit(solution)/shard_map/ppermute | solution.py:262
  21.2 10.3 %collective-permute-start.20 = (bf16[384,768]{1,0:T(8,128)(2,1)S(1)}, bf16[384,768]{1,0:T(8,128)(2,1)S(1)}, u32[]{:S(2)}, u32[]{:S(2)}) collective-permute-start(bf16[384,768]{1,0:T(8,128)(2,1)S(1)} %pad_maximum_fusion.7), channel_id=1, source_target_pairs={{0,64},{8,56},{16,80},{24,40},{32,96},{40,24},{48,112},{56,8},{64,... | collective-permute-start | bytes 1769480 | tf_op jit(solution)/shard_map/ppermute | solution.py:271
  23.8 10.6 %collective-permute-start.16 = (bf16[384,768]{1,0:T(8,128)(2,1)S(1)}, bf16[384,768]{1,0:T(8,128)(2,1)S(1)}, u32[]{:S(2)}, u32[]{:S(2)}) collective-permute-start(bf16[384,768]{1,0:T(8,128)(2,1)S(1)} %pad_maximum_fusion.6), channel_id=1, source_target_pairs={{0,192},{8,24},{16,208},{24,8},{32,224},{40,56},{48,240},{56,40},{... | collective-permute-start | bytes 1769480 | tf_op jit(solution)/shard_map/ppermute | solution.py:271
  24.0 10.7 %collective-permute-start.5 = (bf16[512,384]{1,0:T(8,128)(2,1)S(1)}, bf16[512,384]{1,0:T(8,128)(2,1)S(1)}, u32[]{:S(2)}, u32[]{:S(2)}) collective-permute-start(bf16[512,384]{1,0:T(8,128)(2,1)S(1)} %shard_map.66.refs_4_), channel_id=1, source_target_pairs={{0,1},{1,2},{2,3},{3,4},{4,5},{5,6},{6,7},{7,0},{8,15},{9,8},{10,9... | collective-permute-start | bytes 1179656 | tf_op jit(solution)/shard_map/ppermute | solution.py:262
  26.5 8.7 %collective-permute-start.6 = (bf16[512,384]{1,0:T(8,128)(2,1)S(1)}, bf16[512,384]{1,0:T(8,128)(2,1)S(1)}, u32[]{:S(2)}, u32[]{:S(2)}) collective-permute-start(bf16[512,384]{1,0:T(8,128)(2,1)S(1)} %shard_map.67.refs_5_), channel_id=1, source_target_pairs={{0,1},{1,2},{2,3},{3,4},{4,5},{5,6},{6,7},{7,0},{8,15},{9,8},{10,9... | collective-permute-start | bytes 1179656 | tf_op jit(solution)/shard_map/ppermute | solution.py:262
  31.6 16.7 %collective-permute-start.21 = (bf16[768,768]{1,0:T(8,128)(2,1)S(1)}, bf16[768,768]{1,0:T(8,128)(2,1)S(1)}, u32[]{:S(2)}, u32[]{:S(2)}) collective-permute-start(bf16[768,768]{1,0:T(8,128)(2,1)S(1)} %pad_maximum_fusion.3), channel_id=1, source_target_pairs={{0,48},{8,200},{16,32},{24,216},{32,16},{40,232},{48,0},{56,248},{... | collective-permute-start | bytes 3538952 | tf_op jit(solution)/shard_map/ppermute | solution.py:271
  34.5 15.4 %collective-permute-start.17 = (bf16[768,768]{1,0:T(8,128)(2,1)S(1)}, bf16[768,768]{1,0:T(8,128)(2,1)S(1)}, u32[]{:S(2)}, u32[]{:S(2)}) collective-permute-start(bf16[768,768]{1,0:T(8,128)(2,1)S(1)} %pad_maximum_fusion.2), channel_id=1, source_target_pairs={{0,16},{8,72},{16,0},{24,88},{32,48},{40,104},{48,32},{56,120},{64... | collective-permute-start | bytes 3538952 | tf_op jit(solution)/shard_map/ppermute | solution.py:271
  34.7 7.0 %collective-permute-start.7 = (bf16[512,384]{1,0:T(8,128)(2,1)S(1)}, bf16[512,384]{1,0:T(8,128)(2,1)S(1)}, u32[]{:S(2)}, u32[]{:S(2)}) collective-permute-start(bf16[512,384]{1,0:T(8,128)(2,1)S(1)} %shard_map.68.refs_6_), channel_id=1, source_target_pairs={{0,1},{1,2},{2,3},{3,4},{4,5},{5,6},{6,7},{7,0},{8,15},{9,8},{10,9... | collective-permute-start | bytes 1179656 | tf_op jit(solution)/shard_map/ppermute | solution.py:262
  35.2 10.7 %collective-permute-start.8 = (bf16[512,384]{1,0:T(8,128)(2,1)S(1)}, bf16[512,384]{1,0:T(8,128)(2,1)S(1)}, u32[]{:S(2)}, u32[]{:S(2)}) collective-permute-start(bf16[512,384]{1,0:T(8,128)(2,1)S(1)} %shard_map.69.refs_7_), channel_id=1, source_target_pairs={{0,1},{1,2},{2,3},{3,4},{4,5},{5,6},{6,7},{7,0},{8,15},{9,8},{10,9... | collective-permute-start | bytes 1179656 | tf_op jit(solution)/shard_map/ppermute | solution.py:262
  41.7 11.1 %collective-permute-start.9 = (bf16[512,384]{1,0:T(8,128)(2,1)S(1)}, bf16[512,384]{1,0:T(8,128)(2,1)S(1)}, u32[]{:S(2)}, u32[]{:S(2)}) collective-permute-start(bf16[512,384]{1,0:T(8,128)(2,1)S(1)} %shard_map.70.refs_8_), channel_id=1, source_target_pairs={{0,1},{1,2},{2,3},{3,4},{4,5},{5,6},{6,7},{7,0},{8,15},{9,8},{10,9... | collective-permute-start | bytes 1179656 | tf_op jit(solution)/shard_map/ppermute | solution.py:262
  45.9 8.4 %collective-permute-start.10 = (bf16[512,384]{1,0:T(8,128)(2,1)S(1)}, bf16[512,384]{1,0:T(8,128)(2,1)S(1)}, u32[]{:S(2)}, u32[]{:S(2)}) collective-permute-start(bf16[512,384]{1,0:T(8,128)(2,1)S(1)} %shard_map.71.refs_9_), channel_id=1, source_target_pairs={{0,1},{1,2},{2,3},{3,4},{4,5},{5,6},{6,7},{7,0},{8,15},{9,8},{10,9... | collective-permute-start | bytes 1179656 | tf_op jit(solution)/shard_map/ppermute | solution.py:262
  48.5 23.8 %collective-permute-start.22 = (bf16[1536,512]{1,0:T(8,128)(2,1)S(1)}, bf16[1536,512]{1,0:T(8,128)(2,1)S(1)}, u32[]{:S(2)}, u32[]{:S(2)}) collective-permute-start(bf16[1536,512]{1,0:T(8,128)(2,1)S(1)} %pad_maximum_fusion.1.refs_16_), channel_id=1, source_target_pairs={{0,192},{8,24},{16,208},{24,8},{32,224},{40,56},{48,240},{56,40},{... | collective-permute-start | bytes 4718600 | tf_op jit(solution)/shard_map/ppermute | solution.py:280
  50.0 28.8 %copy-start.1 = (bf16[768,768]{1,0:T(8,128)(2,1)}, bf16[768,768]{1,0:T(8,128)(2,1)S(1)}, u32[]{:S(2)}) copy-start(bf16[768,768]{1,0:T(8,128)(2,1)S(1)} %collective-permute-done.17) | copy-start | bytes 3538948
  50.1 22.1 %collective-permute-start.18 = (bf16[1536,512]{1,0:T(8,128)(2,1)S(1)}, bf16[1536,512]{1,0:T(8,128)(2,1)S(1)}, u32[]{:S(2)}, u32[]{:S(2)}) collective-permute-start(bf16[1536,512]{1,0:T(8,128)(2,1)S(1)} %pad_maximum_fusion.refs_16_), channel_id=1, source_target_pairs={{0,64},{8,56},{16,80},{24,40},{32,96},{40,24},{48,112},{56,8},{64,... | collective-permute-start | bytes 4718600 | tf_op jit(solution)/shard_map/ppermute | solution.py:280
  52.7 6.9 %collective-permute-start.11 = (bf16[512,384]{1,0:T(8,128)(2,1)S(1)}, bf16[512,384]{1,0:T(8,128)(2,1)S(1)}, u32[]{:S(2)}, u32[]{:S(2)}) collective-permute-start(bf16[512,384]{1,0:T(8,128)(2,1)S(1)} %shard_map.72.refs_10_), channel_id=1, source_target_pairs={{0,1},{1,2},{2,3},{3,4},{4,5},{5,6},{6,7},{7,0},{8,15},{9,8},{10,9... | collective-permute-start | bytes 1179656 | tf_op jit(solution)/shard_map/ppermute | solution.py:262
  54.3 9.6 %collective-permute-start.12 = (bf16[512,384]{1,0:T(8,128)(2,1)S(1)}, bf16[512,384]{1,0:T(8,128)(2,1)S(1)}, u32[]{:S(2)}, u32[]{:S(2)}) collective-permute-start(bf16[512,384]{1,0:T(8,128)(2,1)S(1)} %shard_map.73.refs_11_), channel_id=1, source_target_pairs={{0,1},{1,2},{2,3},{3,4},{4,5},{5,6},{6,7},{7,0},{8,15},{9,8},{10,9... | collective-permute-start | bytes 1179656 | tf_op jit(solution)/shard_map/ppermute | solution.py:262
  59.6 8.4 %collective-permute-start.13 = (bf16[512,384]{1,0:T(8,128)(2,1)S(1)}, bf16[512,384]{1,0:T(8,128)(2,1)S(1)}, u32[]{:S(2)}, u32[]{:S(2)}) collective-permute-start(bf16[512,384]{1,0:T(8,128)(2,1)S(1)} %shard_map.74.refs_12_), channel_id=1, source_target_pairs={{0,1},{1,2},{2,3},{3,4},{4,5},{5,6},{6,7},{7,0},{8,15},{9,8},{10,9... | collective-permute-start | bytes 1179656 | tf_op jit(solution)/shard_map/ppermute | solution.py:262
  63.9 8.4 %collective-permute-start.14 = (bf16[512,384]{1,0:T(8,128)(2,1)S(1)}, bf16[512,384]{1,0:T(8,128)(2,1)S(1)}, u32[]{:S(2)}, u32[]{:S(2)}) collective-permute-start(bf16[512,384]{1,0:T(8,128)(2,1)S(1)} %shard_map.75.refs_13_), channel_id=1, source_target_pairs={{0,1},{1,2},{2,3},{3,4},{4,5},{5,6},{6,7},{7,0},{8,15},{9,8},{10,9... | collective-permute-start | bytes 1179656 | tf_op jit(solution)/shard_map/ppermute | solution.py:262
  76.3 9.5 %collective-permute-start.23 = (bf16[1024,512]{1,0:T(8,128)(2,1)S(1)}, bf16[1024,512]{1,0:T(8,128)(2,1)S(1)}, u32[]{:S(2)}, u32[]{:S(2)}) collective-permute-start(bf16[1024,512]{1,0:T(8,128)(2,1)S(1)} %shard_map.79), channel_id=1, source_target_pairs={{0,8},{8,0},{16,24},{24,16},{32,40},{40,32},{48,56},{56,48},{64,72... | collective-permute-start | bytes 3145736 | tf_op jit(solution)/shard_map/ppermute | solution.py:299
  78.8 1.0 slice-start
  78.9 14.6 %collective-permute-start.25 = (bf16[1536,256]{1,0:T(8,128)(2,1)S(1)}, bf16[1536,256]{1,0:T(8,128)(2,1)S(1)}, u32[]{:S(2)}, u32[]{:S(2)}) collective-permute-start(bf16[1536,256]{1,0:T(8,128)(2,1)S(1)} %pad_maximum_fusion.5.refs_16_), channel_id=1, source_target_pairs={{0,192},{8,24},{16,208},{24,8},{32,224},{40,56},{48,240},{56,40},{... | collective-permute-start | bytes 2359304 | tf_op jit(solution)/shard_map/ppermute | solution.py:280
  79.9 17.7 %collective-permute-start.24 = (bf16[1536,256]{1,0:T(8,128)(2,1)S(1)}, bf16[1536,256]{1,0:T(8,128)(2,1)S(1)}, u32[]{:S(2)}, u32[]{:S(2)}) collective-permute-start(bf16[1536,256]{1,0:T(8,128)(2,1)S(1)} %pad_maximum_fusion.4.refs_16_), channel_id=1, source_target_pairs={{0,64},{8,56},{16,80},{24,40},{32,96},{40,24},{48,112},{56,8},{64,... | collective-permute-start | bytes 2359304 | tf_op jit(solution)/shard_map/ppermute | solution.py:280
  86.6 4.9 %collective-permute-start.27 = (bf16[2,128,128]{2,1,0:T(8,128)(2,1)S(1)}, bf16[2,128,128]{2,1,0:T(8,128)(2,1)S(1)}, u32[]{:S(2)}, u32[]{:S(2)}) collective-permute-start(bf16[2,128,128]{2,1,0:T(8,128)(2,1)S(1)} %get-tuple-element.24), channel_id=1, source_target_pairs={{0,16},{8,24},{16,0},{24,8},{32,48},{40,56},{48,32},{56,40},{64,80... | collective-permute-start | bytes 196616 | tf_op jit(solution)/shard_map/ppermute | solution.py:314
  91.6 5.1 %collective-permute-start.28 = (bf16[2,128,128]{2,1,0:T(8,128)(2,1)S(1)}, bf16[2,128,128]{2,1,0:T(8,128)(2,1)S(1)}, u32[]{:S(2)}, u32[]{:S(2)}) collective-permute-start(bf16[2,128,128]{2,1,0:T(8,128)(2,1)S(1)} %add_convert_fusion.2), channel_id=1, source_target_pairs={{0,48},{8,56},{16,32},{24,40},{32,16},{40,24},{48,0},{56,8},{64,11... | collective-permute-start | bytes 196616 | tf_op jit(solution)/shard_map/ppermute | solution.py:314
  95.9 6.1 %collective-permute-start.26 = (bf16[1024,256]{1,0:T(8,128)(2,1)S(1)}, bf16[1024,256]{1,0:T(8,128)(2,1)S(1)}, u32[]{:S(2)}, u32[]{:S(2)}) collective-permute-start(bf16[1024,256]{1,0:T(8,128)(2,1)S(1)} %shard_map.82), channel_id=1, source_target_pairs={{0,8},{8,0},{16,24},{24,16},{32,40},{40,32},{48,56},{56,48},{64,72... | collective-permute-start | bytes 1572872 | tf_op jit(solution)/shard_map/ppermute | solution.py:304
  96.6 3.3 %collective-permute-start.29 = (bf16[2,128,128]{2,1,0:T(8,128)(2,1)S(1)}, bf16[2,128,128]{2,1,0:T(8,128)(2,1)S(1)}, u32[]{:S(2)}, u32[]{:S(2)}) collective-permute-start(bf16[2,128,128]{2,1,0:T(8,128)(2,1)S(1)} %add_convert_fusion.1), channel_id=1, source_target_pairs={{0,64},{8,72},{16,80},{24,88},{32,96},{40,104},{48,112},{56,120},{... | collective-permute-start | bytes 196616 | tf_op jit(solution)/shard_map/ppermute | solution.py:314
  100.0 4.5 %copy-start = (f32[512]{0:T(512)S(1)}, f32[512]{0:T(512)}, u32[]{:S(2)}) copy-start(f32[512]{0:T(512)} %param.10) | copy-start | bytes 6148
  100.0 4.4 %collective-permute-start.30 = (bf16[2,128,128]{2,1,0:T(8,128)(2,1)S(1)}, bf16[2,128,128]{2,1,0:T(8,128)(2,1)S(1)}, u32[]{:S(2)}, u32[]{:S(2)}) collective-permute-start(bf16[2,128,128]{2,1,0:T(8,128)(2,1)S(1)} %add_convert_fusion), channel_id=1, source_target_pairs={{0,192},{8,200},{16,208},{24,216},{32,224},{40,232},{48,240},{56,2... | collective-permute-start | bytes 196616 | tf_op jit(solution)/shard_map/ppermute | solution.py:314
  105.4 4.2 %collective-permute-start.31 = (bf16[512,256]{1,0:T(8,128)(2,1)S(1)}, bf16[512,256]{1,0:T(8,128)(2,1)S(1)}, u32[]{:S(2)}, u32[]{:S(2)}) collective-permute-start(bf16[512,256]{1,0:T(8,128)(2,1)S(1)} %shard_map.85), channel_id=1, source_target_pairs={{0,8},{8,0},{16,24},{24,16},{32,40},{40,32},{48,56},{56,48},{64,72... | collective-permute-start | bytes 786440 | tf_op jit(solution)/shard_map/ppermute | solution.py:318

commit v10 on v9

--- a/solution.py
+++ b/solution.py
@@ -50,9 +50,9 @@
     ]
 
 
-def ring_pairs():
+def ring_pairs(stream):
     return [
-        (s * Z + z, s * Z + (z + (1 if s % C == 0 else -1)) % Z)
+        (s * Z + z, s * Z + (z + (1 if (s + stream) % 2 == 0 else -1)) % Z)
         for s in range(Y * X * C)
         for z in range(Z)
     ]
@@ -256,16 +256,11 @@
     odd = jnp.concatenate([tokens[:, ROWS : 2 * ROWS], tokens[:, 3 * ROWS :]], axis=1)
     own = jnp.where(core == 0, even, odd)
     theirs = lax.ppermute(jnp.where(core == 0, odd, even), "seq", SWAP)
-    ring = ring_pairs()
-
-    def pass_on(piece):
-        return lax.ppermute(piece, ("seq", "head"), ring)
-
-    first, second = [own], [theirs]
-    for k in range(1, Z):
-        for stream in (first, second):
-            piece = stream[-1]
-            stream.append(pace(pass_on(piece)))
+    rings = [[own], [theirs]]
+    for _ in range(1, Z):
+        for j, ring in enumerate(rings):
+            ring.append(pace(lax.ppermute(ring[-1], ("seq", "head"), ring_pairs(j))))
+    first, second = rings
     streams = list(weights)
     for step in range(3):
         got = [lax.ppermute(streams[j], "seq", cube_pairs(j, step)) for j in range(2)]
@@ -278,7 +273,7 @@
         if low:
             near = [after(part, first[-1]) for part in near]
         blocks.append([[near[j], lax.ppermute(near[j], "seq", cube_pairs(j, 3))] for j in range(2)])
-    pieces = zip(first, second)
+    pieces = zip(first, second[:1] + second[:0:-1])
     return [p for pair in pieces for p in pair], blocks
 
 

time: 113 us -> 125 us (1.11); the launches traced: 110 us -> 125 us
  waiting for transfers between devices: 34.4 us -> 49.5 us
    ppermute x14, waiting for transfers between devices: 23.7 us -> 43.3 us  [gather(): ring.append(pace(lax.ppermute(ring[-1], ('seq', 'head'), ring_pairs(j))))]
    ppermute x6, waiting for transfers between devices: 4.27 us -> 0.02 us  [gather(): lax.ppermute(streams[j], 'seq', cube_pairs(j, step))]
    ppermute x14, starting transfers between devices: 25.8 us -> 22.6 us  [gather(): ring.append(pace(lax.ppermute(ring[-1], ('seq', 'head'), ring_pairs(j))))]
    ppermute x4, starting transfers between devices: 4.91 us -> 6.53 us  [gather(): lax.ppermute(near[j], 'seq', cube_pairs(j, 3))]
    ppermute x1, starting transfers between devices: 2.45 us -> 3.8 us  [local(): kv_got = lax.ppermute(kv_theirs, 'seq', SWAP)]
  transfers between devices with their start and end apart: 32 -> 32, of which waited for: 16 -> 13; matrix products, arithmetic and copies ran while one was open for 2% -> 1% of each run, Pallas kernels for 10% -> 9%
where the time goes in v10:
time: 125 us
  starting transfers between devices  53.8 us (43%)
  waiting for transfers between devices  49.5 us (40%)
  Pallas kernels  16.4 us (13%)
  local copies, waits for them, and re-layouts  2.65 us (2%)
  other arithmetic  1.92 us (2%)
    ppermute x14, waiting for transfers between devices, gather(): ring.append(pace(lax.ppermute(ring[-1], ('seq', 'head'), ring_pairs(j))))  43.3 us
    ppermute x14, starting transfers between devices, gather(): ring.append(pace(lax.ppermute(ring[-1], ('seq', 'head'), ring_pairs(j))))  22.6 us
    pallas_call x4, Pallas kernels, product(): pl.pallas_call(functools.partial(product_kernel, mine), out_shape=jax.Sha...  12.7 us
    ppermute x6, starting transfers between devices, gather(): lax.ppermute(streams[j], 'seq', cube_pairs(j, step))  8.86 us
    ppermute x4, starting transfers between devices, gather(): lax.ppermute(near[j], 'seq', cube_pairs(j, 3))  6.53 us
    ppermute x4, waiting for transfers between devices, local(): got.append(lax.ppermute(group, 'seq', exchange_pairs(dim)))  5.89 us
    ppermute x4, starting transfers between devices, local(): got.append(lax.ppermute(group, 'seq', exchange_pairs(dim)))  5.14 us
    ppermute x1, starting transfers between devices, local(): kv_got = lax.ppermute(kv_theirs, 'seq', SWAP)  3.8 us
  transfers between devices with their start and end apart: 32, of which 13 were waited for; matrix products, arithmetic and copies ran while one was open for 1% of the time, Pallas kernels for 9%

profile of v10, /device:TPU:1, one launch (start us, length us, event | category | flops | bytes accessed | tf_op | source)
XLA Modules:
  0.0 124.6 jit_solution(12752999541040889859)
XLA Ops:
  0.0 1.6 %fusion = (bf16[512,192]{1,0:T(8,128)(2,1)S(1)}, bf16[512,192]{1,0:T(8,128)(2,1)S(1)}, bf16[512,192]{1,0:T(8,128)(2,1)S(1)}, bf16[512,192]{1,0:T(8,128)(2,1)S(1)}) fusion(bf16[512,768]{1,0:T(8,128)(2,1)} %param.6), kind=kLoop, calls=%fused_computation.23 | loop fusion | bytes 1572864 | tf_op jit(solution)/shard_map/slice | solution.py:255
  1.6 0.0 copy-start.2
  1.6 0.3 broadcast_select_fusion
  2.0 3.3 %collective-permute-start = (bf16[512,384]{1,0:T(8,128)(2,1)S(1)}, bf16[512,384]{1,0:T(8,128)(2,1)S(1)}, u32[]{:S(2)}, u32[]{:S(2)}) collective-permute-start(bf16[512,384]{1,0:T(8,128)(2,1)S(1)} %get-tuple-element.35), channel_id=1, source_target_pairs={{0,8},{8,0},{16,24},{24,16},{32,40},{40,32},{48,56},{56,48},{64,72... | collective-permute-start | bytes 1179656 | tf_op jit(solution)/shard_map/ppermute | solution.py:258
  5.3 3.8 %collective-permute-start.1 = (bf16[512,384]{1,0:T(8,128)(2,1)S(1)}, bf16[512,384]{1,0:T(8,128)(2,1)S(1)}, u32[]{:S(2)}, u32[]{:S(2)}) collective-permute-start(bf16[512,384]{1,0:T(8,128)(2,1)S(1)} %get-tuple-element.36.refs_0_), channel_id=1, source_target_pairs={{0,1},{1,2},{2,3},{3,4},{4,5},{5,6},{6,7},{7,0},{8,15},{9,8},{10,9... | collective-permute-start | bytes 1179656 | tf_op jit(solution)/shard_map/ppermute | solution.py:262
  9.2 0.1 collective-permute-start.2
  9.3 0.1 broadcast_select_fusion.2
  9.4 1.4 %collective-permute-start.19 = (bf16[192,768]{1,0:T(8,128)(2,1)S(1)}, bf16[192,768]{1,0:T(8,128)(2,1)S(1)}, u32[]{:S(2)}, u32[]{:S(2)}) collective-permute-start(bf16[192,768]{1,0:T(8,128)(2,1)S(1)} %get-tuple-element.41), channel_id=1, source_target_pairs={{0,16},{8,72},{16,0},{24,88},{32,48},{40,104},{48,32},{56,120},{64... | collective-permute-start | bytes 884744 | tf_op jit(solution)/shard_map/ppermute | solution.py:266
  10.8 1.9 %collective-permute-start.15 = (bf16[192,768]{1,0:T(8,128)(2,1)S(1)}, bf16[192,768]{1,0:T(8,128)(2,1)S(1)}, u32[]{:S(2)}, u32[]{:S(2)}) collective-permute-start(bf16[192,768]{1,0:T(8,128)(2,1)S(1)} %get-tuple-element.42), channel_id=1, source_target_pairs={{0,48},{8,200},{16,32},{24,216},{32,16},{40,232},{48,0},{56,248},{... | collective-permute-start | bytes 884744 | tf_op jit(solution)/shard_map/ppermute | solution.py:266
  12.7 3.1 %collective-permute-done.1.piece = bf16[512,384]{1,0:T(8,128)(2,1)S(1)} collective-permute-done((bf16[512,384]{1,0:T(8,128)(2,1)S(1)}, bf16[512,384]{1,0:T(8,128)(2,1)S(1)}, u32[]{:S(2)}, u32[]{:S(2)}) %collective-permute-start.1) | collective-permute-done | bytes 393248 | tf_op jit(solution)/shard_map/ppermute | solution.py:262
  15.8 3.4 %collective-permute-start.9 = (bf16[512,384]{1,0:T(8,128)(2,1)S(1)}, bf16[512,384]{1,0:T(8,128)(2,1)S(1)}, u32[]{:S(2)}, u32[]{:S(2)}) collective-permute-start(bf16[512,384]{1,0:T(8,128)(2,1)S(1)} %shard_map.64.refs_2_), channel_id=1, source_target_pairs={{0,1},{1,2},{2,3},{3,4},{4,5},{5,6},{6,7},{7,0},{8,15},{9,8},{10,9... | collective-permute-start | bytes 1179656 | tf_op jit(solution)/shard_map/ppermute | solution.py:262
  19.3 2.6 %collective-permute-start.20 = (bf16[384,768]{1,0:T(8,128)(2,1)S(1)}, bf16[384,768]{1,0:T(8,128)(2,1)S(1)}, u32[]{:S(2)}, u32[]{:S(2)}) collective-permute-start(bf16[384,768]{1,0:T(8,128)(2,1)S(1)} %pad_maximum_fusion.7), channel_id=1, source_target_pairs={{0,64},{8,56},{16,80},{24,40},{32,96},{40,24},{48,112},{56,8},{64,... | collective-permute-start | bytes 1769480 | tf_op jit(solution)/shard_map/ppermute | solution.py:266
  21.9 0.1 collective-permute-start.16
  22.0 3.0 %collective-permute-done.9.piece = bf16[512,384]{1,0:T(8,128)(2,1)S(1)} collective-permute-done((bf16[512,384]{1,0:T(8,128)(2,1)S(1)}, bf16[512,384]{1,0:T(8,128)(2,1)S(1)}, u32[]{:S(2)}, u32[]{:S(2)}) %collective-permute-start.9) | collective-permute-done | bytes 393248 | tf_op jit(solution)/shard_map/ppermute | solution.py:262
  25.0 3.4 %collective-permute-start.10 = (bf16[512,384]{1,0:T(8,128)(2,1)S(1)}, bf16[512,384]{1,0:T(8,128)(2,1)S(1)}, u32[]{:S(2)}, u32[]{:S(2)}) collective-permute-start(bf16[512,384]{1,0:T(8,128)(2,1)S(1)} %shard_map.72.refs_4_), channel_id=1, source_target_pairs={{0,1},{1,2},{2,3},{3,4},{4,5},{5,6},{6,7},{7,0},{8,15},{9,8},{10,9... | collective-permute-start | bytes 1179656 | tf_op jit(solution)/shard_map/ppermute | solution.py:262
  28.4 1.9 %collective-permute-done.3.piece = bf16[512,384]{1,0:T(8,128)(2,1)S(1)} collective-permute-done((bf16[512,384]{1,0:T(8,128)(2,1)S(1)}, bf16[512,384]{1,0:T(8,128)(2,1)S(1)}, u32[]{:S(2)}, u32[]{:S(2)}) %collective-permute-start.3) | collective-permute-done | bytes 393248 | tf_op jit(solution)/shard_map/ppermute | solution.py:262
  30.3 0.1 pad_maximum_fusion.3
  30.4 2.8 %collective-permute-start.21 = (bf16[768,768]{1,0:T(8,128)(2,1)S(1)}, bf16[768,768]{1,0:T(8,128)(2,1)S(1)}, u32[]{:S(2)}, u32[]{:S(2)}) collective-permute-start(bf16[768,768]{1,0:T(8,128)(2,1)S(1)} %pad_maximum_fusion.3), channel_id=1, source_target_pairs={{0,48},{8,200},{16,32},{24,216},{32,16},{40,232},{48,0},{56,248},{... | collective-permute-start | bytes 3538952 | tf_op jit(solution)/shard_map/ppermute | solution.py:266
  33.2 0.1 pad_maximum_fusion.2
  33.3 0.1 collective-permute-start.17
  33.4 2.8 %collective-permute-start.11 = (bf16[512,384]{1,0:T(8,128)(2,1)S(1)}, bf16[512,384]{1,0:T(8,128)(2,1)S(1)}, u32[]{:S(2)}, u32[]{:S(2)}) collective-permute-start(bf16[512,384]{1,0:T(8,128)(2,1)S(1)} %shard_map.73.refs_6_), channel_id=1, source_target_pairs={{0,1},{1,2},{2,3},{3,4},{4,5},{5,6},{6,7},{7,0},{8,15},{9,8},{10,9... | collective-permute-start | bytes 1179656 | tf_op jit(solution)/shard_map/ppermute | solution.py:262
  36.2 6.0 %collective-permute-done.4.piece = bf16[512,384]{1,0:T(8,128)(2,1)S(1)} collective-permute-done((bf16[512,384]{1,0:T(8,128)(2,1)S(1)}, bf16[512,384]{1,0:T(8,128)(2,1)S(1)}, u32[]{:S(2)}, u32[]{:S(2)}) %collective-permute-start.4) | collective-permute-done | bytes 393248 | tf_op jit(solution)/shard_map/ppermute | solution.py:262
  42.2 0.1 slice.72
  42.3 0.1 slice.74
  42.3 2.9 %collective-permute-start.12 = (bf16[512,384]{1,0:T(8,128)(2,1)S(1)}, bf16[512,384]{1,0:T(8,128)(2,1)S(1)}, u32[]{:S(2)}, u32[]{:S(2)}) collective-permute-start(bf16[512,384]{1,0:T(8,128)(2,1)S(1)} %shard_map.74.refs_8_), channel_id=1, source_target_pairs={{0,1},{1,2},{2,3},{3,4},{4,5},{5,6},{6,7},{7,0},{8,15},{9,8},{10,9... | collective-permute-start | bytes 1179656 | tf_op jit(solution)/shard_map/ppermute | solution.py:262
  45.2 8.9 %collective-permute-done.5.piece = bf16[512,384]{1,0:T(8,128)(2,1)S(1)} collective-permute-done((bf16[512,384]{1,0:T(8,128)(2,1)S(1)}, bf16[512,384]{1,0:T(8,128)(2,1)S(1)}, u32[]{:S(2)}, u32[]{:S(2)}) %collective-permute-start.5) | collective-permute-done | bytes 393248 | tf_op jit(solution)/shard_map/ppermute | solution.py:262
  54.1 0.1 slice.75
  54.2 0.1 pad_maximum_fusion.1.refs_16_
  54.3 0.7 collective-permute-start.22
  55.0 0.1 slice.73
  55.0 0.1 pad_maximum_fusion.refs_16_
  55.1 2.0 %collective-permute-start.18 = (bf16[1536,512]{1,0:T(8,128)(2,1)S(1)}, bf16[1536,512]{1,0:T(8,128)(2,1)S(1)}, u32[]{:S(2)}, u32[]{:S(2)}) collective-permute-start(bf16[1536,512]{1,0:T(8,128)(2,1)S(1)} %pad_maximum_fusion.refs_16_), channel_id=1, source_target_pairs={{0,64},{8,56},{16,80},{24,40},{32,96},{40,24},{48,112},{56,8},{64,... | collective-permute-start | bytes 4718600 | tf_op jit(solution)/shard_map/ppermute | solution.py:275
  57.2 2.7 %collective-permute-start.13 = (bf16[512,384]{1,0:T(8,128)(2,1)S(1)}, bf16[512,384]{1,0:T(8,128)(2,1)S(1)}, u32[]{:S(2)}, u32[]{:S(2)}) collective-permute-start(bf16[512,384]{1,0:T(8,128)(2,1)S(1)} %shard_map.75.refs_10_), channel_id=1, source_target_pairs={{0,1},{1,2},{2,3},{3,4},{4,5},{5,6},{6,7},{7,0},{8,15},{9,8},{10,9... | collective-permute-start | bytes 1179656 | tf_op jit(solution)/shard_map/ppermute | solution.py:262
  59.8 5.3 %collective-permute-done.6.piece = bf16[512,384]{1,0:T(8,128)(2,1)S(1)} collective-permute-done((bf16[512,384]{1,0:T(8,128)(2,1)S(1)}, bf16[512,384]{1,0:T(8,128)(2,1)S(1)}, u32[]{:S(2)}, u32[]{:S(2)}) %collective-permute-start.6) | collective-permute-done | bytes 393248 | tf_op jit(solution)/shard_map/ppermute | solution.py:262
  65.2 2.2 %collective-permute-done.13.piece = bf16[512,384]{1,0:T(8,128)(2,1)S(1)} collective-permute-done((bf16[512,384]{1,0:T(8,128)(2,1)S(1)}, bf16[512,384]{1,0:T(8,128)(2,1)S(1)}, u32[]{:S(2)}, u32[]{:S(2)}) %collective-permute-start.13) | collective-permute-done | bytes 393248 | tf_op jit(solution)/shard_map/ppermute | solution.py:262
  67.4 3.4 %collective-permute-start.14 = (bf16[512,384]{1,0:T(8,128)(2,1)S(1)}, bf16[512,384]{1,0:T(8,128)(2,1)S(1)}, u32[]{:S(2)}, u32[]{:S(2)}) collective-permute-start(bf16[512,384]{1,0:T(8,128)(2,1)S(1)} %shard_map.76.refs_12_), channel_id=1, source_target_pairs={{0,1},{1,2},{2,3},{3,4},{4,5},{5,6},{6,7},{7,0},{8,15},{9,8},{10,9... | collective-permute-start | bytes 1179656 | tf_op jit(solution)/shard_map/ppermute | solution.py:262
  70.8 4.5 %collective-permute-done.7.piece = bf16[512,384]{1,0:T(8,128)(2,1)S(1)} collective-permute-done((bf16[512,384]{1,0:T(8,128)(2,1)S(1)}, bf16[512,384]{1,0:T(8,128)(2,1)S(1)}, u32[]{:S(2)}, u32[]{:S(2)}) %collective-permute-start.7) | collective-permute-done | bytes 393248 | tf_op jit(solution)/shard_map/ppermute | solution.py:262
  75.3 0.7 dynamic-slice_bitcast_fusion.info
  76.0 3.3 %collective-permute-done.14.piece = bf16[512,384]{1,0:T(8,128)(2,1)S(1)} collective-permute-done((bf16[512,384]{1,0:T(8,128)(2,1)S(1)}, bf16[512,384]{1,0:T(8,128)(2,1)S(1)}, u32[]{:S(2)}, u32[]{:S(2)}) %collective-permute-start.14) | collective-permute-done | bytes 393248 | tf_op jit(solution)/shard_map/ppermute | solution.py:262
  79.2 5.2 %collective-permute-done.8.piece = bf16[512,384]{1,0:T(8,128)(2,1)S(1)} collective-permute-done((bf16[512,384]{1,0:T(8,128)(2,1)S(1)}, bf16[512,384]{1,0:T(8,128)(2,1)S(1)}, u32[]{:S(2)}, u32[]{:S(2)}) %collective-permute-start.8) | collective-permute-done | bytes 393248 | tf_op jit(solution)/shard_map/ppermute | solution.py:262
  84.4 4.0 %shard_map.79 = bf16[1024,512]{1,0:T(8,128)(2,1)S(1)} custom-call(s32[37]{0:T(128)S(1)} %dynamic-slice_bitcast_fusion.info, bf16[512,384]{1,0:T(8,128)(2,1)S(1)} %get-tuple-element.36.refs_0_, bf16[512,384]{1,0:T(8,128)(2,1)S(1)} %collective-permute-done.refs_1_, bf16[512,384]{1,0:T(8,128)(2,1)S(1)} %shard_map.64.refs_2_, ...), custom_call_target="tpu_custom_call" | custom-call | flops 3221225472 | bytes 1048576 | tf_op jit(solution)/shard_map/pallas_call | solution.py:121
  88.5 3.8 %collective-permute-start.23 = (bf16[1024,512]{1,0:T(8,128)(2,1)S(1)}, bf16[1024,512]{1,0:T(8,128)(2,1)S(1)}, u32[]{:S(2)}, u32[]{:S(2)}) collective-permute-start(bf16[1024,512]{1,0:T(8,128)(2,1)S(1)} %shard_map.79), channel_id=1, source_target_pairs={{0,8},{8,0},{16,24},{24,16},{32,40},{40,32},{48,56},{56,48},{64,72... | collective-permute-start | bytes 3145736 | tf_op jit(solution)/shard_map/ppermute | solution.py:294
  92.4 0.1 pad_maximum_fusion.5.refs_16_
  92.4 1.0 collective-permute-start.25
  93.4 0.1 pad_maximum_fusion.4.refs_16_
  93.5 2.9 %collective-permute-start.24 = (bf16[1536,256]{1,0:T(8,128)(2,1)S(1)}, bf16[1536,256]{1,0:T(8,128)(2,1)S(1)}, u32[]{:S(2)}, u32[]{:S(2)}) collective-permute-start(bf16[1536,256]{1,0:T(8,128)(2,1)S(1)} %pad_maximum_fusion.4.refs_16_), channel_id=1, source_target_pairs={{0,64},{8,56},{16,80},{24,40},{32,96},{40,24},{48,112},{56,8},{64,... | collective-permute-start | bytes 2359304 | tf_op jit(solution)/shard_map/ppermute | solution.py:275
  96.3 4.0 %shard_map.78.mine = f32[1024,512]{1,0:T(8,128)S(1)} custom-call(s32[37]{0:T(128)S(1)} %dynamic-slice_bitcast_fusion.info, bf16[512,384]{1,0:T(8,128)(2,1)S(1)} %get-tuple-element.36.refs_0_, bf16[512,384]{1,0:T(8,128)(2,1)S(1)} %collective-permute-done.refs_1_, bf16[512,384]{1,0:T(8,128)(2,1)S(1)} %shard_map.64.refs_2_, ...), custom_call_target="tpu_custom_call" | custom-call | flops 3221225472 | bytes 1048576 | tf_op jit(solution)/shard_map/pallas_call | solution.py:121
  100.3 0.8 shard_map.80
  101.2 0.5 collective-permute-start.27
  101.7 3.8 %collective-permute-done.27.got_0 = bf16[2,128,128]{2,1,0:T(8,128)(2,1)S(1)} collective-permute-done((bf16[2,128,128]{2,1,0:T(8,128)(2,1)S(1)}, bf16[2,128,128]{2,1,0:T(8,128)(2,1)S(1)}, u32[]{:S(2)}, u32[]{:S(2)}) %collective-permute-start.27) | collective-permute-done | bytes 65568 | tf_op jit(solution)/shard_map/ppermute | solution.py:309
  105.5 1.7 %collective-permute-start.28 = (bf16[2,128,128]{2,1,0:T(8,128)(2,1)S(1)}, bf16[2,128,128]{2,1,0:T(8,128)(2,1)S(1)}, u32[]{:S(2)}, u32[]{:S(2)}) collective-permute-start(bf16[2,128,128]{2,1,0:T(8,128)(2,1)S(1)} %add_convert_fusion.2), channel_id=1, source_target_pairs={{0,48},{8,56},{16,32},{24,40},{32,16},{40,24},{48,0},{56,8},{64,11... | collective-permute-start | bytes 196616 | tf_op jit(solution)/shard_map/ppermute | solution.py:309
  107.2 2.4 %shard_map.82 = bf16[1024,256]{1,0:T(8,128)(2,1)S(1)} custom-call(s32[37]{0:T(128)S(1)} %dynamic-slice_bitcast_fusion.info, bf16[512,384]{1,0:T(8,128)(2,1)S(1)} %get-tuple-element.36.refs_0_, bf16[512,384]{1,0:T(8,128)(2,1)S(1)} %collective-permute-done.refs_1_, bf16[512,384]{1,0:T(8,128)(2,1)S(1)} %shard_map.64.refs_2_, ...), custom_call_target="tpu_custom_call" | custom-call | flops 1610612736 | bytes 1048576 | tf_op jit(solution)/shard_map/pallas_call | solution.py:121
  109.6 1.5 %collective-permute-start.26 = (bf16[1024,256]{1,0:T(8,128)(2,1)S(1)}, bf16[1024,256]{1,0:T(8,128)(2,1)S(1)}, u32[]{:S(2)}, u32[]{:S(2)}) collective-permute-start(bf16[1024,256]{1,0:T(8,128)(2,1)S(1)} %shard_map.82), channel_id=1, source_target_pairs={{0,8},{8,0},{16,24},{24,16},{32,40},{40,32},{48,56},{56,48},{64,72... | collective-permute-start | bytes 1572872 | tf_op jit(solution)/shard_map/ppermute | solution.py:299
  111.1 1.5 %collective-permute-start.29 = (bf16[2,128,128]{2,1,0:T(8,128)(2,1)S(1)}, bf16[2,128,128]{2,1,0:T(8,128)(2,1)S(1)}, u32[]{:S(2)}, u32[]{:S(2)}) collective-permute-start(bf16[2,128,128]{2,1,0:T(8,128)(2,1)S(1)} %add_convert_fusion.1), channel_id=1, source_target_pairs={{0,64},{8,72},{16,80},{24,88},{32,96},{40,104},{48,112},{56,120},{... | collective-permute-start | bytes 196616 | tf_op jit(solution)/shard_map/ppermute | solution.py:309
  112.6 2.4 %shard_map.81.mine = f32[1024,256]{1,0:T(8,128)S(1)} custom-call(s32[37]{0:T(128)S(1)} %dynamic-slice_bitcast_fusion.info, bf16[512,384]{1,0:T(8,128)(2,1)S(1)} %get-tuple-element.36.refs_0_, bf16[512,384]{1,0:T(8,128)(2,1)S(1)} %collective-permute-done.refs_1_, bf16[512,384]{1,0:T(8,128)(2,1)S(1)} %shard_map.64.refs_2_, ...), custom_call_target="tpu_custom_call" | custom-call | flops 1610612736 | bytes 1048576 | tf_op jit(solution)/shard_map/pallas_call | solution.py:121
  115.0 0.0 copy-start
  115.1 1.4 %collective-permute-start.30 = (bf16[2,128,128]{2,1,0:T(8,128)(2,1)S(1)}, bf16[2,128,128]{2,1,0:T(8,128)(2,1)S(1)}, u32[]{:S(2)}, u32[]{:S(2)}) collective-permute-start(bf16[2,128,128]{2,1,0:T(8,128)(2,1)S(1)} %add_convert_fusion), channel_id=1, source_target_pairs={{0,192},{8,200},{16,208},{24,216},{32,224},{40,232},{48,240},{56,2... | collective-permute-start | bytes 196616 | tf_op jit(solution)/shard_map/ppermute | solution.py:309
  116.5 0.9 shard_map.83
  117.4 2.1 %collective-permute-done.30.got_3 = bf16[2,128,128]{2,1,0:T(8,128)(2,1)S(1)} collective-permute-done((bf16[2,128,128]{2,1,0:T(8,128)(2,1)S(1)}, bf16[2,128,128]{2,1,0:T(8,128)(2,1)S(1)}, u32[]{:S(2)}, u32[]{:S(2)}) %collective-permute-start.30) | collective-permute-done | bytes 65568 | tf_op jit(solution)/shard_map/ppermute | solution.py:309
  119.5 0.9 shard_map.85
  120.5 2.1 %collective-permute-start.31 = (bf16[512,256]{1,0:T(8,128)(2,1)S(1)}, bf16[512,256]{1,0:T(8,128)(2,1)S(1)}, u32[]{:S(2)}, u32[]{:S(2)}) collective-permute-start(bf16[512,256]{1,0:T(8,128)(2,1)S(1)} %shard_map.85), channel_id=1, source_target_pairs={{0,8},{8,0},{16,24},{24,16},{32,40},{40,32},{48,56},{56,48},{64,72... | collective-permute-start | bytes 786440 | tf_op jit(solution)/shard_map/ppermute | solution.py:313
  122.6 0.9 shard_map.84
  123.5 0.2 collective-permute-done.31
  123.8 0.8 pad_maximum_fusion.8
  (60 shorter events, 0.4 us)
Async XLA Ops:
  0.0 9.1 %copy-start.3 = (bf16[192,512]{1,0:T(8,128)(2,1)S(1)}, bf16[192,512]{1,0:T(8,128)(2,1)}, u32[]{:S(2)}) copy-start(bf16[192,512]{1,0:T(8,128)(2,1)} %param.8) | copy-start | bytes 589828
  0.0 9.1 %copy-start.4 = (bf16[192,512]{1,0:T(8,128)(2,1)S(1)}, bf16[192,512]{1,0:T(8,128)(2,1)}, u32[]{:S(2)}) copy-start(bf16[192,512]{1,0:T(8,128)(2,1)} %param.9) | copy-start | bytes 589828
  1.6 7.7 %copy-start.2 = (bf16[192,512]{1,0:T(8,128)(2,1)S(1)}, bf16[192,512]{1,0:T(8,128)(2,1)}, u32[]{:S(2)}) copy-start(bf16[192,512]{1,0:T(8,128)(2,1)} %param.7) | copy-start | bytes 589828
  2.0 7.2 %collective-permute-start = (bf16[512,384]{1,0:T(8,128)(2,1)S(1)}, bf16[512,384]{1,0:T(8,128)(2,1)S(1)}, u32[]{:S(2)}, u32[]{:S(2)}) collective-permute-start(bf16[512,384]{1,0:T(8,128)(2,1)S(1)} %get-tuple-element.35), channel_id=1, source_target_pairs={{0,8},{8,0},{16,24},{24,16},{32,40},{40,32},{48,56},{56,48},{64,72... | collective-permute-start | bytes 1179656 | tf_op jit(solution)/shard_map/ppermute | solution.py:258
  5.3 10.5 %collective-permute-start.1 = (bf16[512,384]{1,0:T(8,128)(2,1)S(1)}, bf16[512,384]{1,0:T(8,128)(2,1)S(1)}, u32[]{:S(2)}, u32[]{:S(2)}) collective-permute-start(bf16[512,384]{1,0:T(8,128)(2,1)S(1)} %get-tuple-element.36.refs_0_), channel_id=1, source_target_pairs={{0,1},{1,2},{2,3},{3,4},{4,5},{5,6},{6,7},{7,0},{8,15},{9,8},{10,9... | collective-permute-start | bytes 1179656 | tf_op jit(solution)/shard_map/ppermute | solution.py:262
  9.2 10.1 %collective-permute-start.2 = (bf16[512,384]{1,0:T(8,128)(2,1)S(1)}, bf16[512,384]{1,0:T(8,128)(2,1)S(1)}, u32[]{:S(2)}, u32[]{:S(2)}) collective-permute-start(bf16[512,384]{1,0:T(8,128)(2,1)S(1)} %collective-permute-done.refs_1_), channel_id=1, source_target_pairs={{0,7},{1,0},{2,1},{3,2},{4,3},{5,4},{6,5},{7,6},{8,9},{9,10},{10,1... | collective-permute-start | bytes 1179656 | tf_op jit(solution)/shard_map/ppermute | solution.py:262
  9.4 9.8 %collective-permute-start.19 = (bf16[192,768]{1,0:T(8,128)(2,1)S(1)}, bf16[192,768]{1,0:T(8,128)(2,1)S(1)}, u32[]{:S(2)}, u32[]{:S(2)}) collective-permute-start(bf16[192,768]{1,0:T(8,128)(2,1)S(1)} %get-tuple-element.41), channel_id=1, source_target_pairs={{0,16},{8,72},{16,0},{24,88},{32,48},{40,104},{48,32},{56,120},{64... | collective-permute-start | bytes 884744 | tf_op jit(solution)/shard_map/ppermute | solution.py:266
  10.8 11.1 %collective-permute-start.15 = (bf16[192,768]{1,0:T(8,128)(2,1)S(1)}, bf16[192,768]{1,0:T(8,128)(2,1)S(1)}, u32[]{:S(2)}, u32[]{:S(2)}) collective-permute-start(bf16[192,768]{1,0:T(8,128)(2,1)S(1)} %get-tuple-element.42), channel_id=1, source_target_pairs={{0,48},{8,200},{16,32},{24,216},{32,16},{40,232},{48,0},{56,248},{... | collective-permute-start | bytes 884744 | tf_op jit(solution)/shard_map/ppermute | solution.py:266
  15.8 9.2 %collective-permute-start.9 = (bf16[512,384]{1,0:T(8,128)(2,1)S(1)}, bf16[512,384]{1,0:T(8,128)(2,1)S(1)}, u32[]{:S(2)}, u32[]{:S(2)}) collective-permute-start(bf16[512,384]{1,0:T(8,128)(2,1)S(1)} %shard_map.64.refs_2_), channel_id=1, source_target_pairs={{0,1},{1,2},{2,3},{3,4},{4,5},{5,6},{6,7},{7,0},{8,15},{9,8},{10,9... | collective-permute-start | bytes 1179656 | tf_op jit(solution)/shard_map/ppermute | solution.py:262
  19.2 11.1 %collective-permute-start.3 = (bf16[512,384]{1,0:T(8,128)(2,1)S(1)}, bf16[512,384]{1,0:T(8,128)(2,1)S(1)}, u32[]{:S(2)}, u32[]{:S(2)}) collective-permute-start(bf16[512,384]{1,0:T(8,128)(2,1)S(1)} %shard_map.65.refs_15_), channel_id=1, source_target_pairs={{0,7},{1,0},{2,1},{3,2},{4,3},{5,4},{6,5},{7,6},{8,9},{9,10},{10,1... | collective-permute-start | bytes 1179656 | tf_op jit(solution)/shard_map/ppermute | solution.py:262
  19.3 11.0 %collective-permute-start.20 = (bf16[384,768]{1,0:T(8,128)(2,1)S(1)}, bf16[384,768]{1,0:T(8,128)(2,1)S(1)}, u32[]{:S(2)}, u32[]{:S(2)}) collective-permute-start(bf16[384,768]{1,0:T(8,128)(2,1)S(1)} %pad_maximum_fusion.7), channel_id=1, source_target_pairs={{0,64},{8,56},{16,80},{24,40},{32,96},{40,24},{48,112},{56,8},{64,... | collective-permute-start | bytes 1769480 | tf_op jit(solution)/shard_map/ppermute | solution.py:266
  21.9 11.3 %collective-permute-start.16 = (bf16[384,768]{1,0:T(8,128)(2,1)S(1)}, bf16[384,768]{1,0:T(8,128)(2,1)S(1)}, u32[]{:S(2)}, u32[]{:S(2)}) collective-permute-start(bf16[384,768]{1,0:T(8,128)(2,1)S(1)} %pad_maximum_fusion.6), channel_id=1, source_target_pairs={{0,192},{8,24},{16,208},{24,8},{32,224},{40,56},{48,240},{56,40},{... | collective-permute-start | bytes 1769480 | tf_op jit(solution)/shard_map/ppermute | solution.py:266
  25.0 8.4 %collective-permute-start.10 = (bf16[512,384]{1,0:T(8,128)(2,1)S(1)}, bf16[512,384]{1,0:T(8,128)(2,1)S(1)}, u32[]{:S(2)}, u32[]{:S(2)}) collective-permute-start(bf16[512,384]{1,0:T(8,128)(2,1)S(1)} %shard_map.72.refs_4_), channel_id=1, source_target_pairs={{0,1},{1,2},{2,3},{3,4},{4,5},{5,6},{6,7},{7,0},{8,15},{9,8},{10,9... | collective-permute-start | bytes 1179656 | tf_op jit(solution)/shard_map/ppermute | solution.py:262
  30.3 11.9 %collective-permute-start.4 = (bf16[512,384]{1,0:T(8,128)(2,1)S(1)}, bf16[512,384]{1,0:T(8,128)(2,1)S(1)}, u32[]{:S(2)}, u32[]{:S(2)}) collective-permute-start(bf16[512,384]{1,0:T(8,128)(2,1)S(1)} %shard_map.66.refs_13_), channel_id=1, source_target_pairs={{0,7},{1,0},{2,1},{3,2},{4,3},{5,4},{6,5},{7,6},{8,9},{9,10},{10,1... | collective-permute-start | bytes 1179656 | tf_op jit(solution)/shard_map/ppermute | solution.py:262
  30.4 23.7 %collective-permute-start.21 = (bf16[768,768]{1,0:T(8,128)(2,1)S(1)}, bf16[768,768]{1,0:T(8,128)(2,1)S(1)}, u32[]{:S(2)}, u32[]{:S(2)}) collective-permute-start(bf16[768,768]{1,0:T(8,128)(2,1)S(1)} %pad_maximum_fusion.3), channel_id=1, source_target_pairs={{0,48},{8,200},{16,32},{24,216},{32,16},{40,232},{48,0},{56,248},{... | collective-permute-start | bytes 3538952 | tf_op jit(solution)/shard_map/ppermute | solution.py:266
  33.3 21.7 %collective-permute-start.17 = (bf16[768,768]{1,0:T(8,128)(2,1)S(1)}, bf16[768,768]{1,0:T(8,128)(2,1)S(1)}, u32[]{:S(2)}, u32[]{:S(2)}) collective-permute-start(bf16[768,768]{1,0:T(8,128)(2,1)S(1)} %pad_maximum_fusion.2), channel_id=1, source_target_pairs={{0,16},{8,72},{16,0},{24,88},{32,48},{40,104},{48,32},{56,120},{64... | collective-permute-start | bytes 3538952 | tf_op jit(solution)/shard_map/ppermute | solution.py:266
  33.4 8.9 %collective-permute-start.11 = (bf16[512,384]{1,0:T(8,128)(2,1)S(1)}, bf16[512,384]{1,0:T(8,128)(2,1)S(1)}, u32[]{:S(2)}, u32[]{:S(2)}) collective-permute-start(bf16[512,384]{1,0:T(8,128)(2,1)S(1)} %shard_map.73.refs_6_), channel_id=1, source_target_pairs={{0,1},{1,2},{2,3},{3,4},{4,5},{5,6},{6,7},{7,0},{8,15},{9,8},{10,9... | collective-permute-start | bytes 1179656 | tf_op jit(solution)/shard_map/ppermute | solution.py:262
  42.2 11.9 %collective-permute-start.5 = (bf16[512,384]{1,0:T(8,128)(2,1)S(1)}, bf16[512,384]{1,0:T(8,128)(2,1)S(1)}, u32[]{:S(2)}, u32[]{:S(2)}) collective-permute-start(bf16[512,384]{1,0:T(8,128)(2,1)S(1)} %shard_map.67.refs_11_), channel_id=1, source_target_pairs={{0,7},{1,0},{2,1},{3,2},{4,3},{5,4},{6,5},{7,6},{8,9},{9,10},{10,1... | collective-permute-start | bytes 1179656 | tf_op jit(solution)/shard_map/ppermute | solution.py:262
  42.3 14.8 %collective-permute-start.12 = (bf16[512,384]{1,0:T(8,128)(2,1)S(1)}, bf16[512,384]{1,0:T(8,128)(2,1)S(1)}, u32[]{:S(2)}, u32[]{:S(2)}) collective-permute-start(bf16[512,384]{1,0:T(8,128)(2,1)S(1)} %shard_map.74.refs_8_), channel_id=1, source_target_pairs={{0,1},{1,2},{2,3},{3,4},{4,5},{5,6},{6,7},{7,0},{8,15},{9,8},{10,9... | collective-permute-start | bytes 1179656 | tf_op jit(solution)/shard_map/ppermute | solution.py:262
  54.1 11.0 %collective-permute-start.6 = (bf16[512,384]{1,0:T(8,128)(2,1)S(1)}, bf16[512,384]{1,0:T(8,128)(2,1)S(1)}, u32[]{:S(2)}, u32[]{:S(2)}) collective-permute-start(bf16[512,384]{1,0:T(8,128)(2,1)S(1)} %shard_map.68.refs_9_), channel_id=1, source_target_pairs={{0,7},{1,0},{2,1},{3,2},{4,3},{5,4},{6,5},{7,6},{8,9},{9,10},{10,1... | collective-permute-start | bytes 1179656 | tf_op jit(solution)/shard_map/ppermute | solution.py:262
  54.3 30.1 %collective-permute-start.22 = (bf16[1536,512]{1,0:T(8,128)(2,1)S(1)}, bf16[1536,512]{1,0:T(8,128)(2,1)S(1)}, u32[]{:S(2)}, u32[]{:S(2)}) collective-permute-start(bf16[1536,512]{1,0:T(8,128)(2,1)S(1)} %pad_maximum_fusion.1.refs_16_), channel_id=1, source_target_pairs={{0,192},{8,24},{16,208},{24,8},{32,224},{40,56},{48,240},{56,40},{... | collective-permute-start | bytes 4718600 | tf_op jit(solution)/shard_map/ppermute | solution.py:275
  55.0 37.3 %copy-start.1 = (bf16[768,768]{1,0:T(8,128)(2,1)}, bf16[768,768]{1,0:T(8,128)(2,1)S(1)}, u32[]{:S(2)}) copy-start(bf16[768,768]{1,0:T(8,128)(2,1)S(1)} %collective-permute-done.17) | copy-start | bytes 3538948
  55.1 29.3 %collective-permute-start.18 = (bf16[1536,512]{1,0:T(8,128)(2,1)S(1)}, bf16[1536,512]{1,0:T(8,128)(2,1)S(1)}, u32[]{:S(2)}, u32[]{:S(2)}) collective-permute-start(bf16[1536,512]{1,0:T(8,128)(2,1)S(1)} %pad_maximum_fusion.refs_16_), channel_id=1, source_target_pairs={{0,64},{8,56},{16,80},{24,40},{32,96},{40,24},{48,112},{56,8},{64,... | collective-permute-start | bytes 4718600 | tf_op jit(solution)/shard_map/ppermute | solution.py:275
  57.2 10.2 %collective-permute-start.13 = (bf16[512,384]{1,0:T(8,128)(2,1)S(1)}, bf16[512,384]{1,0:T(8,128)(2,1)S(1)}, u32[]{:S(2)}, u32[]{:S(2)}) collective-permute-start(bf16[512,384]{1,0:T(8,128)(2,1)S(1)} %shard_map.75.refs_10_), channel_id=1, source_target_pairs={{0,1},{1,2},{2,3},{3,4},{4,5},{5,6},{6,7},{7,0},{8,15},{9,8},{10,9... | collective-permute-start | bytes 1179656 | tf_op jit(solution)/shard_map/ppermute | solution.py:262
  65.1 10.1 %collective-permute-start.7 = (bf16[512,384]{1,0:T(8,128)(2,1)S(1)}, bf16[512,384]{1,0:T(8,128)(2,1)S(1)}, u32[]{:S(2)}, u32[]{:S(2)}) collective-permute-start(bf16[512,384]{1,0:T(8,128)(2,1)S(1)} %shard_map.69.refs_7_), channel_id=1, source_target_pairs={{0,7},{1,0},{2,1},{3,2},{4,3},{5,4},{6,5},{7,6},{8,9},{9,10},{10,1... | collective-permute-start | bytes 1179656 | tf_op jit(solution)/shard_map/ppermute | solution.py:262
  67.4 11.8 %collective-permute-start.14 = (bf16[512,384]{1,0:T(8,128)(2,1)S(1)}, bf16[512,384]{1,0:T(8,128)(2,1)S(1)}, u32[]{:S(2)}, u32[]{:S(2)}) collective-permute-start(bf16[512,384]{1,0:T(8,128)(2,1)S(1)} %shard_map.76.refs_12_), channel_id=1, source_target_pairs={{0,1},{1,2},{2,3},{3,4},{4,5},{5,6},{6,7},{7,0},{8,15},{9,8},{10,9... | collective-permute-start | bytes 1179656 | tf_op jit(solution)/shard_map/ppermute | solution.py:262
  75.3 9.2 %collective-permute-start.8 = (bf16[512,384]{1,0:T(8,128)(2,1)S(1)}, bf16[512,384]{1,0:T(8,128)(2,1)S(1)}, u32[]{:S(2)}, u32[]{:S(2)}) collective-permute-start(bf16[512,384]{1,0:T(8,128)(2,1)S(1)} %shard_map.70.refs_5_), channel_id=1, source_target_pairs={{0,7},{1,0},{2,1},{3,2},{4,3},{5,4},{6,5},{7,6},{8,9},{9,10},{10,1... | collective-permute-start | bytes 1179656 | tf_op jit(solution)/shard_map/ppermute | solution.py:262
  88.5 11.9 %collective-permute-start.23 = (bf16[1024,512]{1,0:T(8,128)(2,1)S(1)}, bf16[1024,512]{1,0:T(8,128)(2,1)S(1)}, u32[]{:S(2)}, u32[]{:S(2)}) collective-permute-start(bf16[1024,512]{1,0:T(8,128)(2,1)S(1)} %shard_map.79), channel_id=1, source_target_pairs={{0,8},{8,0},{16,24},{24,16},{32,40},{40,32},{48,56},{56,48},{64,72... | collective-permute-start | bytes 3145736 | tf_op jit(solution)/shard_map/ppermute | solution.py:294
  92.3 1.1 slice-start
  92.4 14.8 %collective-permute-start.25 = (bf16[1536,256]{1,0:T(8,128)(2,1)S(1)}, bf16[1536,256]{1,0:T(8,128)(2,1)S(1)}, u32[]{:S(2)}, u32[]{:S(2)}) collective-permute-start(bf16[1536,256]{1,0:T(8,128)(2,1)S(1)} %pad_maximum_fusion.5.refs_16_), channel_id=1, source_target_pairs={{0,192},{8,24},{16,208},{24,8},{32,224},{40,56},{48,240},{56,40},{... | collective-permute-start | bytes 2359304 | tf_op jit(solution)/shard_map/ppermute | solution.py:275
  93.5 19.2 %collective-permute-start.24 = (bf16[1536,256]{1,0:T(8,128)(2,1)S(1)}, bf16[1536,256]{1,0:T(8,128)(2,1)S(1)}, u32[]{:S(2)}, u32[]{:S(2)}) collective-permute-start(bf16[1536,256]{1,0:T(8,128)(2,1)S(1)} %pad_maximum_fusion.4.refs_16_), channel_id=1, source_target_pairs={{0,64},{8,56},{16,80},{24,40},{32,96},{40,24},{48,112},{56,8},{64,... | collective-permute-start | bytes 2359304 | tf_op jit(solution)/shard_map/ppermute | solution.py:275
  101.2 4.3 %collective-permute-start.27 = (bf16[2,128,128]{2,1,0:T(8,128)(2,1)S(1)}, bf16[2,128,128]{2,1,0:T(8,128)(2,1)S(1)}, u32[]{:S(2)}, u32[]{:S(2)}) collective-permute-start(bf16[2,128,128]{2,1,0:T(8,128)(2,1)S(1)} %get-tuple-element.24), channel_id=1, source_target_pairs={{0,16},{8,24},{16,0},{24,8},{32,48},{40,56},{48,32},{56,40},{64,80... | collective-permute-start | bytes 196616 | tf_op jit(solution)/shard_map/ppermute | solution.py:309
  105.5 5.5 %collective-permute-start.28 = (bf16[2,128,128]{2,1,0:T(8,128)(2,1)S(1)}, bf16[2,128,128]{2,1,0:T(8,128)(2,1)S(1)}, u32[]{:S(2)}, u32[]{:S(2)}) collective-permute-start(bf16[2,128,128]{2,1,0:T(8,128)(2,1)S(1)} %add_convert_fusion.2), channel_id=1, source_target_pairs={{0,48},{8,56},{16,32},{24,40},{32,16},{40,24},{48,0},{56,8},{64,11... | collective-permute-start | bytes 196616 | tf_op jit(solution)/shard_map/ppermute | solution.py:309
  109.6 6.9 %collective-permute-start.26 = (bf16[1024,256]{1,0:T(8,128)(2,1)S(1)}, bf16[1024,256]{1,0:T(8,128)(2,1)S(1)}, u32[]{:S(2)}, u32[]{:S(2)}) collective-permute-start(bf16[1024,256]{1,0:T(8,128)(2,1)S(1)} %shard_map.82), channel_id=1, source_target_pairs={{0,8},{8,0},{16,24},{24,16},{32,40},{40,32},{48,56},{56,48},{64,72... | collective-permute-start | bytes 1572872 | tf_op jit(solution)/shard_map/ppermute | solution.py:299
  111.1 3.9 %collective-permute-start.29 = (bf16[2,128,128]{2,1,0:T(8,128)(2,1)S(1)}, bf16[2,128,128]{2,1,0:T(8,128)(2,1)S(1)}, u32[]{:S(2)}, u32[]{:S(2)}) collective-permute-start(bf16[2,128,128]{2,1,0:T(8,128)(2,1)S(1)} %add_convert_fusion.1), channel_id=1, source_target_pairs={{0,64},{8,72},{16,80},{24,88},{32,96},{40,104},{48,112},{56,120},{... | collective-permute-start | bytes 196616 | tf_op jit(solution)/shard_map/ppermute | solution.py:309
  115.0 4.5 %copy-start = (f32[512]{0:T(512)S(1)}, f32[512]{0:T(512)}, u32[]{:S(2)}) copy-start(f32[512]{0:T(512)} %param.10) | copy-start | bytes 6148
  115.1 4.4 %collective-permute-start.30 = (bf16[2,128,128]{2,1,0:T(8,128)(2,1)S(1)}, bf16[2,128,128]{2,1,0:T(8,128)(2,1)S(1)}, u32[]{:S(2)}, u32[]{:S(2)}) collective-permute-start(bf16[2,128,128]{2,1,0:T(8,128)(2,1)S(1)} %add_convert_fusion), channel_id=1, source_target_pairs={{0,192},{8,200},{16,208},{24,216},{32,224},{40,232},{48,240},{56,2... | collective-permute-start | bytes 196616 | tf_op jit(solution)/shard_map/ppermute | solution.py:309
  120.5 3.3 %collective-permute-start.31 = (bf16[512,256]{1,0:T(8,128)(2,1)S(1)}, bf16[512,256]{1,0:T(8,128)(2,1)S(1)}, u32[]{:S(2)}, u32[]{:S(2)}) collective-permute-start(bf16[512,256]{1,0:T(8,128)(2,1)S(1)} %shard_map.85), channel_id=1, source_target_pairs={{0,8},{8,0},{16,24},{24,16},{32,40},{40,32},{48,56},{56,48},{64,72... | collective-permute-start | bytes 786440 | tf_op jit(solution)/shard_map/ppermute | solution.py:313

commit v11 on v9

--- a/solution.py
+++ b/solution.py
@@ -251,11 +251,31 @@
     )(piece)
 
 
-def gather(tokens, weights, core):
+def part_kernel(core, tokens, own, other):
     even = jnp.concatenate([tokens[:, :ROWS], tokens[:, 2 * ROWS : 3 * ROWS]], axis=1)
     odd = jnp.concatenate([tokens[:, ROWS : 2 * ROWS], tokens[:, 3 * ROWS :]], axis=1)
-    own = jnp.where(core == 0, even, odd)
-    theirs = lax.ppermute(jnp.where(core == 0, odd, even), "seq", SWAP)
+    own[...] = jnp.where(core[0] == 0, even, odd)
+    other[...] = jnp.where(core[0] == 0, odd, even)
+
+
+def part_columns(core, tokens):
+    return pl.pallas_call(
+        part_kernel,
+        out_shape=[jax.ShapeDtypeStruct((SLAB, PIECE), BF16)] * 2,
+        in_specs=[SMEM, VMEM],
+        out_specs=[VMEM] * 2,
+        compiler_params=pltpu.CompilerParams(vmem_limit_bytes=8 * 2**20),
+        cost_estimate=pl.CostEstimate(flops=2**20, bytes_accessed=2**21, transcendentals=0),
+    )(core, tokens)
+
+
+def last_step(near):
+    return [[part, lax.ppermute(part, "seq", cube_pairs(j, 3))] for j, part in enumerate(near)]
+
+
+def gather(tokens, weights, core):
+    own, other = part_columns(core.astype(jnp.int32).reshape(1), tokens)
+    theirs = lax.ppermute(other, "seq", SWAP)
     ring = ring_pairs()
 
     def pass_on(piece):
@@ -272,14 +292,13 @@
         pairs = list(zip(streams, got))
         if step < 2:
             streams = [jnp.concatenate(pair, axis=0) for pair in pairs]
-    blocks = []
-    for low, high in ((0, 2 * HALF), (2 * HALF, 3 * HALF)):
-        near = [jnp.concatenate([part[:, low:high] for part in pair], axis=0) for pair in pairs]
-        if low:
-            near = [after(part, first[-1]) for part in near]
-        blocks.append([[near[j], lax.ppermute(near[j], "seq", cube_pairs(j, 3))] for j in range(2)])
+    near_kv, near_q = (
+        [jnp.concatenate([part[:, cut] for part in pair], axis=0) for pair in pairs]
+        for cut in (slice(0, 2 * HALF), slice(2 * HALF, 3 * HALF))
+    )
+    blocks = last_step(near_kv)
     pieces = zip(first, second)
-    return [p for pair in pieces for p in pair], blocks
+    return [p for pair in pieces for p in pair], blocks, near_q
 
 
 def local(tokens, w_query, w_key, w_value, gain):
@@ -293,25 +312,23 @@
         for j in range(2)
     )
     halves = [jnp.where(core == 0, high, low), jnp.where(core == 0, low, high)]
-    pieces, (kv_blocks, q_blocks) = gather(tokens, halves, core)
+    pieces, kv_blocks, near_q = gather(tokens, halves, core)
 
     kv_theirs = product(after(info, kv_blocks[1][1]), pieces, kv_blocks, 0)
     kv_got = lax.ppermute(kv_theirs, "seq", SWAP)
     kv_mine = product(info, pieces, kv_blocks, 1)
     key, value, within, total = pair_states(kv_mine, kv_got)
 
-    q_theirs = product(after(info, total), pieces, q_blocks, 0)
-    q_got = lax.ppermute(q_theirs, "seq", SWAP)
-    q_mine = product(after(info, total), pieces, q_blocks, 1)
+    q_blocks = last_step([after(part, total) for part in near_q])
     got, group = [], total
     for step, dim in enumerate((0, 2, 1, 3)):
         if got:
             group = (group.astype(F32) + got[-1].astype(F32)).astype(BF16)
-        if step == 2:
-            group = after(group, q_theirs)
         if step == 3:
-            group = after(group, q_mine)
+            q_theirs = product(after(info, got[2]), pieces, q_blocks, 0)
         got.append(lax.ppermute(group, "seq", exchange_pairs(dim)))
+    q_got = lax.ppermute(q_theirs, "seq", SWAP)
+    q_mine = product(after(info, got[2]), pieces, q_blocks, 1)
     query, inside = local_part(q_mine, q_got, key, value)
 
     last = (info, query, inside, within, *got, gain.reshape(1, 2 * HALF))

time: 113 us -> 117 us (1.035); the launches traced: 110 us -> 116 us
  starting transfers between devices: 54.1 us -> 58 us
  waiting for transfers between devices: 34.4 us -> 35.8 us
    ppermute x1, starting transfers between devices: 0.76 us -> 8.1 us  [local(): q_got = lax.ppermute(q_theirs, 'seq', SWAP)]
    ppermute x1, starting transfers between devices: 2.99 us -> 0.39 us  [local(): out_got = lax.ppermute(finish(False, *last), 'seq', SWAP)]
    slice x10 -> x9, local copies, waits for them, and re-layouts: 2.44 us -> 0.3 us  [gather(): part[:, cut]]
    ppermute x4, waiting for transfers between devices: 6.15 us -> 7.46 us  [local(): got.append(lax.ppermute(group, 'seq', exchange_pairs(dim)))]
  transfers between devices with their start and end apart: 32 -> 32, of which waited for: 16 -> 17; matrix products, arithmetic and copies ran while one was open for 2% -> 2% of each run, Pallas kernels for 10% -> 9%
where the time goes in v11:
time: 117 us; the launch traced here: 116 us
  starting transfers between devices  58 us (50%)
  waiting for transfers between devices  35.8 us (31%)
  Pallas kernels  16.6 us (14%)
  local copies, waits for them, and re-layouts  3.21 us (3%)
  other arithmetic  1.58 us (1%)
    ppermute x14, starting transfers between devices, pass_on(): return lax.ppermute(piece, ('seq', 'head'), ring)  24.8 us
    ppermute x14, waiting for transfers between devices, pass_on(): return lax.ppermute(piece, ('seq', 'head'), ring)  23.7 us
    pallas_call x4, Pallas kernels, product(): pl.pallas_call(functools.partial(product_kernel, mine), out_shape=jax.Sha...  12.8 us
    ppermute x6, starting transfers between devices, gather(): lax.ppermute(streams[j], 'seq', cube_pairs(j, step))  8.86 us
    ppermute x1, starting transfers between devices, local(): q_got = lax.ppermute(q_theirs, 'seq', SWAP)  8.1 us
    ppermute x4, waiting for transfers between devices, local(): got.append(lax.ppermute(group, 'seq', exchange_pairs(dim)))  7.46 us
    ppermute x4, starting transfers between devices, local(): got.append(lax.ppermute(group, 'seq', exchange_pairs(dim)))  5.24 us
    ppermute x4, starting transfers between devices, last_step(): lax.ppermute(part, 'seq', cube_pairs(j, 3))  4.9 us
  transfers between devices with their start and end apart: 32, of which 17 were waited for; matrix products, arithmetic and copies ran while one was open for 2% of the time, Pallas kernels for 9%

profile of v11, /device:TPU:1, one launch (start us, length us, event | category | flops | bytes accessed | tf_op | source)
XLA Modules:
  0.0 115.6 jit_solution(3751197515116488995)
XLA Ops:
  0.0 1.1 copy-done
  1.1 0.2 shard_map.64
  1.3 3.3 %collective-permute-start = (bf16[512,384]{1,0:T(8,128)(2,1)S(1)}, bf16[512,384]{1,0:T(8,128)(2,1)S(1)}, u32[]{:S(2)}, u32[]{:S(2)}) collective-permute-start(bf16[512,384]{1,0:T(8,128)(2,1)S(1)} %get-tuple-element.24), channel_id=1, source_target_pairs={{0,8},{8,0},{16,24},{24,16},{32,40},{40,32},{48,56},{56,48},{64,72... | collective-permute-start | bytes 1179656 | tf_op jit(solution)/shard_map/ppermute | solution.py:278
  4.7 3.8 %collective-permute-start.1 = (bf16[512,384]{1,0:T(8,128)(2,1)S(1)}, bf16[512,384]{1,0:T(8,128)(2,1)S(1)}, u32[]{:S(2)}, u32[]{:S(2)}) collective-permute-start(bf16[512,384]{1,0:T(8,128)(2,1)S(1)} %get-tuple-element.23.refs_0_), channel_id=1, source_target_pairs={{0,1},{1,2},{2,3},{3,4},{4,5},{5,6},{6,7},{7,0},{8,15},{9,8},{10,9... | collective-permute-start | bytes 1179656 | tf_op jit(solution)/shard_map/ppermute | solution.py:282
  8.5 1.1 fusion
  9.6 0.8 collective-permute-start.2
  10.4 0.1 broadcast_select_fusion
  10.5 1.4 %collective-permute-start.19 = (bf16[192,768]{1,0:T(8,128)(2,1)S(1)}, bf16[192,768]{1,0:T(8,128)(2,1)S(1)}, u32[]{:S(2)}, u32[]{:S(2)}) collective-permute-start(bf16[192,768]{1,0:T(8,128)(2,1)S(1)} %get-tuple-element.35), channel_id=1, source_target_pairs={{0,16},{8,72},{16,0},{24,88},{32,48},{40,104},{48,32},{56,120},{64... | collective-permute-start | bytes 884744 | tf_op jit(solution)/shard_map/ppermute | solution.py:291
  11.9 1.9 %collective-permute-start.15 = (bf16[192,768]{1,0:T(8,128)(2,1)S(1)}, bf16[192,768]{1,0:T(8,128)(2,1)S(1)}, u32[]{:S(2)}, u32[]{:S(2)}) collective-permute-start(bf16[192,768]{1,0:T(8,128)(2,1)S(1)} %get-tuple-element.36), channel_id=1, source_target_pairs={{0,48},{8,200},{16,32},{24,216},{32,16},{40,232},{48,0},{56,248},{... | collective-permute-start | bytes 884744 | tf_op jit(solution)/shard_map/ppermute | solution.py:291
  13.8 2.8 %collective-permute-start.3 = (bf16[512,384]{1,0:T(8,128)(2,1)S(1)}, bf16[512,384]{1,0:T(8,128)(2,1)S(1)}, u32[]{:S(2)}, u32[]{:S(2)}) collective-permute-start(bf16[512,384]{1,0:T(8,128)(2,1)S(1)} %shard_map.65.refs_2_), channel_id=1, source_target_pairs={{0,1},{1,2},{2,3},{3,4},{4,5},{5,6},{6,7},{7,0},{8,15},{9,8},{10,9... | collective-permute-start | bytes 1179656 | tf_op jit(solution)/shard_map/ppermute | solution.py:282
  16.6 0.8 collective-permute-done.2.piece
  17.4 3.1 %collective-permute-start.4 = (bf16[512,384]{1,0:T(8,128)(2,1)S(1)}, bf16[512,384]{1,0:T(8,128)(2,1)S(1)}, u32[]{:S(2)}, u32[]{:S(2)}) collective-permute-start(bf16[512,384]{1,0:T(8,128)(2,1)S(1)} %shard_map.66.refs_3_), channel_id=1, source_target_pairs={{0,1},{1,2},{2,3},{3,4},{4,5},{5,6},{6,7},{7,0},{8,15},{9,8},{10,9... | collective-permute-start | bytes 1179656 | tf_op jit(solution)/shard_map/ppermute | solution.py:282
  20.6 2.6 %collective-permute-start.20 = (bf16[384,768]{1,0:T(8,128)(2,1)S(1)}, bf16[384,768]{1,0:T(8,128)(2,1)S(1)}, u32[]{:S(2)}, u32[]{:S(2)}) collective-permute-start(bf16[384,768]{1,0:T(8,128)(2,1)S(1)} %pad_maximum_fusion.7), channel_id=1, source_target_pairs={{0,64},{8,56},{16,80},{24,40},{32,96},{40,24},{48,112},{56,8},{64,... | collective-permute-start | bytes 1769480 | tf_op jit(solution)/shard_map/ppermute | solution.py:291
  23.2 0.1 collective-permute-start.16
  23.3 1.4 %collective-permute-start.5 = (bf16[512,384]{1,0:T(8,128)(2,1)S(1)}, bf16[512,384]{1,0:T(8,128)(2,1)S(1)}, u32[]{:S(2)}, u32[]{:S(2)}) collective-permute-start(bf16[512,384]{1,0:T(8,128)(2,1)S(1)} %shard_map.67.refs_4_), channel_id=1, source_target_pairs={{0,1},{1,2},{2,3},{3,4},{4,5},{5,6},{6,7},{7,0},{8,15},{9,8},{10,9... | collective-permute-start | bytes 1179656 | tf_op jit(solution)/shard_map/ppermute | solution.py:282
  24.8 1.1 collective-permute-done.4.piece
  25.9 3.4 %collective-permute-start.6 = (bf16[512,384]{1,0:T(8,128)(2,1)S(1)}, bf16[512,384]{1,0:T(8,128)(2,1)S(1)}, u32[]{:S(2)}, u32[]{:S(2)}) collective-permute-start(bf16[512,384]{1,0:T(8,128)(2,1)S(1)} %shard_map.68.refs_5_), channel_id=1, source_target_pairs={{0,1},{1,2},{2,3},{3,4},{4,5},{5,6},{6,7},{7,0},{8,15},{9,8},{10,9... | collective-permute-start | bytes 1179656 | tf_op jit(solution)/shard_map/ppermute | solution.py:282
  29.3 1.7 %collective-permute-done.20 = bf16[384,768]{1,0:T(8,128)(2,1)S(1)} collective-permute-done((bf16[384,768]{1,0:T(8,128)(2,1)S(1)}, bf16[384,768]{1,0:T(8,128)(2,1)S(1)}, u32[]{:S(2)}, u32[]{:S(2)}) %collective-permute-start.20) | collective-permute-done | bytes 589856 | tf_op jit(solution)/shard_map/ppermute | solution.py:291
  31.0 2.8 %collective-permute-start.21 = (bf16[768,768]{1,0:T(8,128)(2,1)S(1)}, bf16[768,768]{1,0:T(8,128)(2,1)S(1)}, u32[]{:S(2)}, u32[]{:S(2)}) collective-permute-start(bf16[768,768]{1,0:T(8,128)(2,1)S(1)} %pad_maximum_fusion.3), channel_id=1, source_target_pairs={{0,48},{8,200},{16,32},{24,216},{32,16},{40,232},{48,0},{56,248},{... | collective-permute-start | bytes 3538952 | tf_op jit(solution)/shard_map/ppermute | solution.py:291
  33.9 0.1 collective-permute-start.17
  34.0 0.1 collective-permute-start.7
  34.1 0.4 collective-permute-done.6.piece
  34.6 3.2 %collective-permute-start.8 = (bf16[512,384]{1,0:T(8,128)(2,1)S(1)}, bf16[512,384]{1,0:T(8,128)(2,1)S(1)}, u32[]{:S(2)}, u32[]{:S(2)}) collective-permute-start(bf16[512,384]{1,0:T(8,128)(2,1)S(1)} %shard_map.70.refs_7_), channel_id=1, source_target_pairs={{0,1},{1,2},{2,3},{3,4},{4,5},{5,6},{6,7},{7,0},{8,15},{9,8},{10,9... | collective-permute-start | bytes 1179656 | tf_op jit(solution)/shard_map/ppermute | solution.py:282
  37.8 3.2 %collective-permute-done.7.piece = bf16[512,384]{1,0:T(8,128)(2,1)S(1)} collective-permute-done((bf16[512,384]{1,0:T(8,128)(2,1)S(1)}, bf16[512,384]{1,0:T(8,128)(2,1)S(1)}, u32[]{:S(2)}, u32[]{:S(2)}) %collective-permute-start.7) | collective-permute-done | bytes 393248 | tf_op jit(solution)/shard_map/ppermute | solution.py:282
  41.0 1.2 %collective-permute-start.9 = (bf16[512,384]{1,0:T(8,128)(2,1)S(1)}, bf16[512,384]{1,0:T(8,128)(2,1)S(1)}, u32[]{:S(2)}, u32[]{:S(2)}) collective-permute-start(bf16[512,384]{1,0:T(8,128)(2,1)S(1)} %shard_map.71.refs_8_), channel_id=1, source_target_pairs={{0,1},{1,2},{2,3},{3,4},{4,5},{5,6},{6,7},{7,0},{8,15},{9,8},{10,9... | collective-permute-start | bytes 1179656 | tf_op jit(solution)/shard_map/ppermute | solution.py:282
  42.3 3.0 %collective-permute-done.8.piece = bf16[512,384]{1,0:T(8,128)(2,1)S(1)} collective-permute-done((bf16[512,384]{1,0:T(8,128)(2,1)S(1)}, bf16[512,384]{1,0:T(8,128)(2,1)S(1)}, u32[]{:S(2)}, u32[]{:S(2)}) %collective-permute-start.8) | collective-permute-done | bytes 393248 | tf_op jit(solution)/shard_map/ppermute | solution.py:282
  45.3 1.2 %collective-permute-start.10 = (bf16[512,384]{1,0:T(8,128)(2,1)S(1)}, bf16[512,384]{1,0:T(8,128)(2,1)S(1)}, u32[]{:S(2)}, u32[]{:S(2)}) collective-permute-start(bf16[512,384]{1,0:T(8,128)(2,1)S(1)} %shard_map.72.refs_9_), channel_id=1, source_target_pairs={{0,1},{1,2},{2,3},{3,4},{4,5},{5,6},{6,7},{7,0},{8,15},{9,8},{10,9... | collective-permute-start | bytes 1179656 | tf_op jit(solution)/shard_map/ppermute | solution.py:282
  46.5 1.2 %collective-permute-done.21 = bf16[768,768]{1,0:T(8,128)(2,1)S(1)} collective-permute-done((bf16[768,768]{1,0:T(8,128)(2,1)S(1)}, bf16[768,768]{1,0:T(8,128)(2,1)S(1)}, u32[]{:S(2)}, u32[]{:S(2)}) %collective-permute-start.21) | collective-permute-done | bytes 1179680 | tf_op jit(solution)/shard_map/ppermute | solution.py:291
  47.8 0.1 pad_maximum_fusion.1.refs_16_
  47.9 0.1 collective-permute-start.22
  48.0 1.4 %collective-permute-done.17 = bf16[768,768]{1,0:T(8,128)(2,1)S(1)} collective-permute-done((bf16[768,768]{1,0:T(8,128)(2,1)S(1)}, bf16[768,768]{1,0:T(8,128)(2,1)S(1)}, u32[]{:S(2)}, u32[]{:S(2)}) %collective-permute-start.17) | collective-permute-done | bytes 1179680 | tf_op jit(solution)/shard_map/ppermute | solution.py:291
  49.4 0.1 pad_maximum_fusion.refs_16_
  49.5 2.6 %collective-permute-start.18 = (bf16[1536,512]{1,0:T(8,128)(2,1)S(1)}, bf16[1536,512]{1,0:T(8,128)(2,1)S(1)}, u32[]{:S(2)}, u32[]{:S(2)}) collective-permute-start(bf16[1536,512]{1,0:T(8,128)(2,1)S(1)} %pad_maximum_fusion.refs_16_), channel_id=1, source_target_pairs={{0,64},{8,56},{16,80},{24,40},{32,96},{40,24},{48,112},{56,8},{64,... | collective-permute-start | bytes 4718600 | tf_op jit(solution)/shard_map/ppermute | solution.py:273
  52.1 1.6 %collective-permute-done.10.piece = bf16[512,384]{1,0:T(8,128)(2,1)S(1)} collective-permute-done((bf16[512,384]{1,0:T(8,128)(2,1)S(1)}, bf16[512,384]{1,0:T(8,128)(2,1)S(1)}, u32[]{:S(2)}, u32[]{:S(2)}) %collective-permute-start.10) | collective-permute-done | bytes 393248 | tf_op jit(solution)/shard_map/ppermute | solution.py:282
  53.7 1.2 %collective-permute-start.12 = (bf16[512,384]{1,0:T(8,128)(2,1)S(1)}, bf16[512,384]{1,0:T(8,128)(2,1)S(1)}, u32[]{:S(2)}, u32[]{:S(2)}) collective-permute-start(bf16[512,384]{1,0:T(8,128)(2,1)S(1)} %shard_map.74.refs_11_), channel_id=1, source_target_pairs={{0,1},{1,2},{2,3},{3,4},{4,5},{5,6},{6,7},{7,0},{8,15},{9,8},{10,9... | collective-permute-start | bytes 1179656 | tf_op jit(solution)/shard_map/ppermute | solution.py:282
  54.9 4.1 %collective-permute-done.11.piece = bf16[512,384]{1,0:T(8,128)(2,1)S(1)} collective-permute-done((bf16[512,384]{1,0:T(8,128)(2,1)S(1)}, bf16[512,384]{1,0:T(8,128)(2,1)S(1)}, u32[]{:S(2)}, u32[]{:S(2)}) %collective-permute-start.11) | collective-permute-done | bytes 393248 | tf_op jit(solution)/shard_map/ppermute | solution.py:282
  59.0 1.2 %collective-permute-start.13 = (bf16[512,384]{1,0:T(8,128)(2,1)S(1)}, bf16[512,384]{1,0:T(8,128)(2,1)S(1)}, u32[]{:S(2)}, u32[]{:S(2)}) collective-permute-start(bf16[512,384]{1,0:T(8,128)(2,1)S(1)} %shard_map.75.refs_12_), channel_id=1, source_target_pairs={{0,1},{1,2},{2,3},{3,4},{4,5},{5,6},{6,7},{7,0},{8,15},{9,8},{10,9... | collective-permute-start | bytes 1179656 | tf_op jit(solution)/shard_map/ppermute | solution.py:282
  60.2 3.0 %collective-permute-done.12.piece = bf16[512,384]{1,0:T(8,128)(2,1)S(1)} collective-permute-done((bf16[512,384]{1,0:T(8,128)(2,1)S(1)}, bf16[512,384]{1,0:T(8,128)(2,1)S(1)}, u32[]{:S(2)}, u32[]{:S(2)}) %collective-permute-start.12) | collective-permute-done | bytes 393248 | tf_op jit(solution)/shard_map/ppermute | solution.py:282
  63.2 1.2 %collective-permute-start.14 = (bf16[512,384]{1,0:T(8,128)(2,1)S(1)}, bf16[512,384]{1,0:T(8,128)(2,1)S(1)}, u32[]{:S(2)}, u32[]{:S(2)}) collective-permute-start(bf16[512,384]{1,0:T(8,128)(2,1)S(1)} %shard_map.76.refs_13_), channel_id=1, source_target_pairs={{0,1},{1,2},{2,3},{3,4},{4,5},{5,6},{6,7},{7,0},{8,15},{9,8},{10,9... | collective-permute-start | bytes 1179656 | tf_op jit(solution)/shard_map/ppermute | solution.py:282
  64.5 0.7 dynamic-slice_bitcast_fusion.info
  65.1 2.3 %collective-permute-done.13.piece = bf16[512,384]{1,0:T(8,128)(2,1)S(1)} collective-permute-done((bf16[512,384]{1,0:T(8,128)(2,1)S(1)}, bf16[512,384]{1,0:T(8,128)(2,1)S(1)}, u32[]{:S(2)}, u32[]{:S(2)}) %collective-permute-start.13) | collective-permute-done | bytes 393248 | tf_op jit(solution)/shard_map/ppermute | solution.py:282
  67.5 4.2 %collective-permute-done.14.piece = bf16[512,384]{1,0:T(8,128)(2,1)S(1)} collective-permute-done((bf16[512,384]{1,0:T(8,128)(2,1)S(1)}, bf16[512,384]{1,0:T(8,128)(2,1)S(1)}, u32[]{:S(2)}, u32[]{:S(2)}) %collective-permute-start.14) | collective-permute-done | bytes 393248 | tf_op jit(solution)/shard_map/ppermute | solution.py:282
  71.7 4.0 %shard_map.80 = bf16[1024,512]{1,0:T(8,128)(2,1)S(1)} custom-call(s32[37]{0:T(128)S(1)} %dynamic-slice_bitcast_fusion.info, bf16[512,384]{1,0:T(8,128)(2,1)S(1)} %get-tuple-element.23.refs_0_, bf16[512,384]{1,0:T(8,128)(2,1)S(1)} %collective-permute-done.refs_1_, bf16[512,384]{1,0:T(8,128)(2,1)S(1)} %shard_map.65.refs_2_, ...), custom_call_target="tpu_custom_call" | custom-call | flops 3221225472 | bytes 1048576 | tf_op jit(solution)/shard_map/pallas_call | solution.py:121
  75.7 2.4 %collective-permute-start.23 = (bf16[1024,512]{1,0:T(8,128)(2,1)S(1)}, bf16[1024,512]{1,0:T(8,128)(2,1)S(1)}, u32[]{:S(2)}, u32[]{:S(2)}) collective-permute-start(bf16[1024,512]{1,0:T(8,128)(2,1)S(1)} %shard_map.80), channel_id=1, source_target_pairs={{0,8},{8,0},{16,24},{24,16},{32,40},{40,32},{48,56},{56,48},{64,72... | collective-permute-start | bytes 3145736 | tf_op jit(solution)/shard_map/ppermute | solution.py:318
  78.2 4.0 %shard_map.79.mine = f32[1024,512]{1,0:T(8,128)S(1)} custom-call(s32[37]{0:T(128)S(1)} %dynamic-slice_bitcast_fusion.info, bf16[512,384]{1,0:T(8,128)(2,1)S(1)} %get-tuple-element.23.refs_0_, bf16[512,384]{1,0:T(8,128)(2,1)S(1)} %collective-permute-done.refs_1_, bf16[512,384]{1,0:T(8,128)(2,1)S(1)} %shard_map.65.refs_2_, ...), custom_call_target="tpu_custom_call" | custom-call | flops 3221225472 | bytes 1048576 | tf_op jit(solution)/shard_map/pallas_call | solution.py:121
  82.2 0.8 shard_map.81
  83.0 0.3 collective-permute-start.24
  83.4 1.3 %collective-permute-start.28 = (bf16[1536,256]{1,0:T(8,128)(2,1)S(1)}, bf16[1536,256]{1,0:T(8,128)(2,1)S(1)}, u32[]{:S(2)}, u32[]{:S(2)}) collective-permute-start(bf16[1536,256]{1,0:T(8,128)(2,1)S(1)} %pad_maximum_fusion.5.refs_16_), channel_id=1, source_target_pairs={{0,192},{8,24},{16,208},{24,8},{32,224},{40,56},{48,240},{56,40},{... | collective-permute-start | bytes 2359304 | tf_op jit(solution)/shard_map/ppermute | solution.py:273
  84.8 2.0 %collective-permute-done.24.got_0 = bf16[2,128,128]{2,1,0:T(8,128)(2,1)S(1)} collective-permute-done((bf16[2,128,128]{2,1,0:T(8,128)(2,1)S(1)}, bf16[2,128,128]{2,1,0:T(8,128)(2,1)S(1)}, u32[]{:S(2)}, u32[]{:S(2)}) %collective-permute-start.24) | collective-permute-done | bytes 65568 | tf_op jit(solution)/shard_map/ppermute | solution.py:329
  86.9 2.1 %collective-permute-start.25 = (bf16[2,128,128]{2,1,0:T(8,128)(2,1)S(1)}, bf16[2,128,128]{2,1,0:T(8,128)(2,1)S(1)}, u32[]{:S(2)}, u32[]{:S(2)}) collective-permute-start(bf16[2,128,128]{2,1,0:T(8,128)(2,1)S(1)} %add_convert_fusion.2), channel_id=1, source_target_pairs={{0,48},{8,56},{16,32},{24,40},{32,16},{40,24},{48,0},{56,8},{64,11... | collective-permute-start | bytes 196616 | tf_op jit(solution)/shard_map/ppermute | solution.py:329
  89.0 0.9 collective-permute-start.27
  90.0 1.8 %collective-permute-done.25.got_1 = bf16[2,128,128]{2,1,0:T(8,128)(2,1)S(1)} collective-permute-done((bf16[2,128,128]{2,1,0:T(8,128)(2,1)S(1)}, bf16[2,128,128]{2,1,0:T(8,128)(2,1)S(1)}, u32[]{:S(2)}, u32[]{:S(2)}) %collective-permute-start.25) | collective-permute-done | bytes 65568 | tf_op jit(solution)/shard_map/ppermute | solution.py:329
  91.8 0.5 collective-permute-start.26
  92.3 3.6 %collective-permute-done.26.got_2 = bf16[2,128,128]{2,1,0:T(8,128)(2,1)S(1)} collective-permute-done((bf16[2,128,128]{2,1,0:T(8,128)(2,1)S(1)}, bf16[2,128,128]{2,1,0:T(8,128)(2,1)S(1)}, u32[]{:S(2)}, u32[]{:S(2)}) %collective-permute-start.26) | collective-permute-done | bytes 65568 | tf_op jit(solution)/shard_map/ppermute | solution.py:329
  96.0 2.4 %shard_map.83 = bf16[1024,256]{1,0:T(8,128)(2,1)S(1)} custom-call(s32[37]{0:T(128)S(1)} %dynamic-slice_bitcast_fusion.info, bf16[512,384]{1,0:T(8,128)(2,1)S(1)} %get-tuple-element.23.refs_0_, bf16[512,384]{1,0:T(8,128)(2,1)S(1)} %collective-permute-done.refs_1_, bf16[512,384]{1,0:T(8,128)(2,1)S(1)} %shard_map.65.refs_2_, ...), custom_call_target="tpu_custom_call" | custom-call | flops 1610612736 | bytes 1048576 | tf_op jit(solution)/shard_map/pallas_call | solution.py:121
  98.4 8.1 %collective-permute-start.29 = (bf16[1024,256]{1,0:T(8,128)(2,1)S(1)}, bf16[1024,256]{1,0:T(8,128)(2,1)S(1)}, u32[]{:S(2)}, u32[]{:S(2)}) collective-permute-start(bf16[1024,256]{1,0:T(8,128)(2,1)S(1)} %shard_map.83), channel_id=1, source_target_pairs={{0,8},{8,0},{16,24},{24,16},{32,40},{40,32},{48,56},{56,48},{64,72... | collective-permute-start | bytes 1572872 | tf_op jit(solution)/shard_map/ppermute | solution.py:330
  106.5 2.2 %collective-permute-start.30 = (bf16[2,128,128]{2,1,0:T(8,128)(2,1)S(1)}, bf16[2,128,128]{2,1,0:T(8,128)(2,1)S(1)}, u32[]{:S(2)}, u32[]{:S(2)}) collective-permute-start(bf16[2,128,128]{2,1,0:T(8,128)(2,1)S(1)} %add_convert_fusion), channel_id=1, source_target_pairs={{0,192},{8,200},{16,208},{24,216},{32,224},{40,232},{48,240},{56,2... | collective-permute-start | bytes 196616 | tf_op jit(solution)/shard_map/ppermute | solution.py:329
  108.7 2.4 %shard_map.82.mine = f32[1024,256]{1,0:T(8,128)S(1)} custom-call(s32[37]{0:T(128)S(1)} %dynamic-slice_bitcast_fusion.info, bf16[512,384]{1,0:T(8,128)(2,1)S(1)} %get-tuple-element.23.refs_0_, bf16[512,384]{1,0:T(8,128)(2,1)S(1)} %collective-permute-done.refs_1_, bf16[512,384]{1,0:T(8,128)(2,1)S(1)} %shard_map.65.refs_2_, ...), custom_call_target="tpu_custom_call" | custom-call | flops 1610612736 | bytes 1048576 | tf_op jit(solution)/shard_map/pallas_call | solution.py:121
  111.2 0.9 shard_map.84
  112.1 0.9 shard_map.86
  113.1 0.4 collective-permute-start.31
  113.5 0.9 shard_map.85
  114.4 0.3 collective-permute-done.31
  114.7 0.8 pad_maximum_fusion.8
  (57 shorter events, 0.8 us)
Async XLA Ops:
  0.0 1.1 copy-start
  1.1 9.3 %copy-start.3 = (bf16[192,512]{1,0:T(8,128)(2,1)S(1)}, bf16[192,512]{1,0:T(8,128)(2,1)}, u32[]{:S(2)}) copy-start(bf16[192,512]{1,0:T(8,128)(2,1)} %param.7) | copy-start | bytes 589828
  1.3 8.2 %collective-permute-start = (bf16[512,384]{1,0:T(8,128)(2,1)S(1)}, bf16[512,384]{1,0:T(8,128)(2,1)S(1)}, u32[]{:S(2)}, u32[]{:S(2)}) collective-permute-start(bf16[512,384]{1,0:T(8,128)(2,1)S(1)} %get-tuple-element.24), channel_id=1, source_target_pairs={{0,8},{8,0},{16,24},{24,16},{32,40},{40,32},{48,56},{56,48},{64,72... | collective-permute-start | bytes 1179656 | tf_op jit(solution)/shard_map/ppermute | solution.py:278
  4.7 9.1 %collective-permute-start.1 = (bf16[512,384]{1,0:T(8,128)(2,1)S(1)}, bf16[512,384]{1,0:T(8,128)(2,1)S(1)}, u32[]{:S(2)}, u32[]{:S(2)}) collective-permute-start(bf16[512,384]{1,0:T(8,128)(2,1)S(1)} %get-tuple-element.23.refs_0_), channel_id=1, source_target_pairs={{0,1},{1,2},{2,3},{3,4},{4,5},{5,6},{6,7},{7,0},{8,15},{9,8},{10,9... | collective-permute-start | bytes 1179656 | tf_op jit(solution)/shard_map/ppermute | solution.py:282
  9.6 7.9 %collective-permute-start.2 = (bf16[512,384]{1,0:T(8,128)(2,1)S(1)}, bf16[512,384]{1,0:T(8,128)(2,1)S(1)}, u32[]{:S(2)}, u32[]{:S(2)}) collective-permute-start(bf16[512,384]{1,0:T(8,128)(2,1)S(1)} %collective-permute-done.refs_1_), channel_id=1, source_target_pairs={{0,1},{1,2},{2,3},{3,4},{4,5},{5,6},{6,7},{7,0},{8,15},{9,8},{10,9... | collective-permute-start | bytes 1179656 | tf_op jit(solution)/shard_map/ppermute | solution.py:282
  10.5 10.0 %collective-permute-start.19 = (bf16[192,768]{1,0:T(8,128)(2,1)S(1)}, bf16[192,768]{1,0:T(8,128)(2,1)S(1)}, u32[]{:S(2)}, u32[]{:S(2)}) collective-permute-start(bf16[192,768]{1,0:T(8,128)(2,1)S(1)} %get-tuple-element.35), channel_id=1, source_target_pairs={{0,16},{8,72},{16,0},{24,88},{32,48},{40,104},{48,32},{56,120},{64... | collective-permute-start | bytes 884744 | tf_op jit(solution)/shard_map/ppermute | solution.py:291
  11.9 11.3 %collective-permute-start.15 = (bf16[192,768]{1,0:T(8,128)(2,1)S(1)}, bf16[192,768]{1,0:T(8,128)(2,1)S(1)}, u32[]{:S(2)}, u32[]{:S(2)}) collective-permute-start(bf16[192,768]{1,0:T(8,128)(2,1)S(1)} %get-tuple-element.36), channel_id=1, source_target_pairs={{0,48},{8,200},{16,32},{24,216},{32,16},{40,232},{48,0},{56,248},{... | collective-permute-start | bytes 884744 | tf_op jit(solution)/shard_map/ppermute | solution.py:291
  13.8 9.5 %collective-permute-start.3 = (bf16[512,384]{1,0:T(8,128)(2,1)S(1)}, bf16[512,384]{1,0:T(8,128)(2,1)S(1)}, u32[]{:S(2)}, u32[]{:S(2)}) collective-permute-start(bf16[512,384]{1,0:T(8,128)(2,1)S(1)} %shard_map.65.refs_2_), channel_id=1, source_target_pairs={{0,1},{1,2},{2,3},{3,4},{4,5},{5,6},{6,7},{7,0},{8,15},{9,8},{10,9... | collective-permute-start | bytes 1179656 | tf_op jit(solution)/shard_map/ppermute | solution.py:282
  17.4 8.4 %collective-permute-start.4 = (bf16[512,384]{1,0:T(8,128)(2,1)S(1)}, bf16[512,384]{1,0:T(8,128)(2,1)S(1)}, u32[]{:S(2)}, u32[]{:S(2)}) collective-permute-start(bf16[512,384]{1,0:T(8,128)(2,1)S(1)} %shard_map.66.refs_3_), channel_id=1, source_target_pairs={{0,1},{1,2},{2,3},{3,4},{4,5},{5,6},{6,7},{7,0},{8,15},{9,8},{10,9... | collective-permute-start | bytes 1179656 | tf_op jit(solution)/shard_map/ppermute | solution.py:282
  20.6 10.3 %collective-permute-start.20 = (bf16[384,768]{1,0:T(8,128)(2,1)S(1)}, bf16[384,768]{1,0:T(8,128)(2,1)S(1)}, u32[]{:S(2)}, u32[]{:S(2)}) collective-permute-start(bf16[384,768]{1,0:T(8,128)(2,1)S(1)} %pad_maximum_fusion.7), channel_id=1, source_target_pairs={{0,64},{8,56},{16,80},{24,40},{32,96},{40,24},{48,112},{56,8},{64,... | collective-permute-start | bytes 1769480 | tf_op jit(solution)/shard_map/ppermute | solution.py:291
  23.2 10.6 %collective-permute-start.16 = (bf16[384,768]{1,0:T(8,128)(2,1)S(1)}, bf16[384,768]{1,0:T(8,128)(2,1)S(1)}, u32[]{:S(2)}, u32[]{:S(2)}) collective-permute-start(bf16[384,768]{1,0:T(8,128)(2,1)S(1)} %pad_maximum_fusion.6), channel_id=1, source_target_pairs={{0,192},{8,24},{16,208},{24,8},{32,224},{40,56},{48,240},{56,40},{... | collective-permute-start | bytes 1769480 | tf_op jit(solution)/shard_map/ppermute | solution.py:291
  23.3 10.7 %collective-permute-start.5 = (bf16[512,384]{1,0:T(8,128)(2,1)S(1)}, bf16[512,384]{1,0:T(8,128)(2,1)S(1)}, u32[]{:S(2)}, u32[]{:S(2)}) collective-permute-start(bf16[512,384]{1,0:T(8,128)(2,1)S(1)} %shard_map.67.refs_4_), channel_id=1, source_target_pairs={{0,1},{1,2},{2,3},{3,4},{4,5},{5,6},{6,7},{7,0},{8,15},{9,8},{10,9... | collective-permute-start | bytes 1179656 | tf_op jit(solution)/shard_map/ppermute | solution.py:282
  25.9 8.7 %collective-permute-start.6 = (bf16[512,384]{1,0:T(8,128)(2,1)S(1)}, bf16[512,384]{1,0:T(8,128)(2,1)S(1)}, u32[]{:S(2)}, u32[]{:S(2)}) collective-permute-start(bf16[512,384]{1,0:T(8,128)(2,1)S(1)} %shard_map.68.refs_5_), channel_id=1, source_target_pairs={{0,1},{1,2},{2,3},{3,4},{4,5},{5,6},{6,7},{7,0},{8,15},{9,8},{10,9... | collective-permute-start | bytes 1179656 | tf_op jit(solution)/shard_map/ppermute | solution.py:282
  31.0 16.7 %collective-permute-start.21 = (bf16[768,768]{1,0:T(8,128)(2,1)S(1)}, bf16[768,768]{1,0:T(8,128)(2,1)S(1)}, u32[]{:S(2)}, u32[]{:S(2)}) collective-permute-start(bf16[768,768]{1,0:T(8,128)(2,1)S(1)} %pad_maximum_fusion.3), channel_id=1, source_target_pairs={{0,48},{8,200},{16,32},{24,216},{32,16},{40,232},{48,0},{56,248},{... | collective-permute-start | bytes 3538952 | tf_op jit(solution)/shard_map/ppermute | solution.py:291
  33.9 15.4 %collective-permute-start.17 = (bf16[768,768]{1,0:T(8,128)(2,1)S(1)}, bf16[768,768]{1,0:T(8,128)(2,1)S(1)}, u32[]{:S(2)}, u32[]{:S(2)}) collective-permute-start(bf16[768,768]{1,0:T(8,128)(2,1)S(1)} %pad_maximum_fusion.2), channel_id=1, source_target_pairs={{0,16},{8,72},{16,0},{24,88},{32,48},{40,104},{48,32},{56,120},{64... | collective-permute-start | bytes 3538952 | tf_op jit(solution)/shard_map/ppermute | solution.py:291
  34.0 7.0 %collective-permute-start.7 = (bf16[512,384]{1,0:T(8,128)(2,1)S(1)}, bf16[512,384]{1,0:T(8,128)(2,1)S(1)}, u32[]{:S(2)}, u32[]{:S(2)}) collective-permute-start(bf16[512,384]{1,0:T(8,128)(2,1)S(1)} %shard_map.69.refs_6_), channel_id=1, source_target_pairs={{0,1},{1,2},{2,3},{3,4},{4,5},{5,6},{6,7},{7,0},{8,15},{9,8},{10,9... | collective-permute-start | bytes 1179656 | tf_op jit(solution)/shard_map/ppermute | solution.py:282
  34.6 10.7 %collective-permute-start.8 = (bf16[512,384]{1,0:T(8,128)(2,1)S(1)}, bf16[512,384]{1,0:T(8,128)(2,1)S(1)}, u32[]{:S(2)}, u32[]{:S(2)}) collective-permute-start(bf16[512,384]{1,0:T(8,128)(2,1)S(1)} %shard_map.70.refs_7_), channel_id=1, source_target_pairs={{0,1},{1,2},{2,3},{3,4},{4,5},{5,6},{6,7},{7,0},{8,15},{9,8},{10,9... | collective-permute-start | bytes 1179656 | tf_op jit(solution)/shard_map/ppermute | solution.py:282
  41.0 11.1 %collective-permute-start.9 = (bf16[512,384]{1,0:T(8,128)(2,1)S(1)}, bf16[512,384]{1,0:T(8,128)(2,1)S(1)}, u32[]{:S(2)}, u32[]{:S(2)}) collective-permute-start(bf16[512,384]{1,0:T(8,128)(2,1)S(1)} %shard_map.71.refs_8_), channel_id=1, source_target_pairs={{0,1},{1,2},{2,3},{3,4},{4,5},{5,6},{6,7},{7,0},{8,15},{9,8},{10,9... | collective-permute-start | bytes 1179656 | tf_op jit(solution)/shard_map/ppermute | solution.py:282
  45.3 8.4 %collective-permute-start.10 = (bf16[512,384]{1,0:T(8,128)(2,1)S(1)}, bf16[512,384]{1,0:T(8,128)(2,1)S(1)}, u32[]{:S(2)}, u32[]{:S(2)}) collective-permute-start(bf16[512,384]{1,0:T(8,128)(2,1)S(1)} %shard_map.72.refs_9_), channel_id=1, source_target_pairs={{0,1},{1,2},{2,3},{3,4},{4,5},{5,6},{6,7},{7,0},{8,15},{9,8},{10,9... | collective-permute-start | bytes 1179656 | tf_op jit(solution)/shard_map/ppermute | solution.py:282
  47.7 30.4 %copy-start.2 = (bf16[768,768]{1,0:T(8,128)(2,1)}, bf16[768,768]{1,0:T(8,128)(2,1)S(1)}, u32[]{:S(2)}) copy-start(bf16[768,768]{1,0:T(8,128)(2,1)S(1)} %collective-permute-done.21) | copy-start | bytes 3538948
  47.9 23.8 %collective-permute-start.22 = (bf16[1536,512]{1,0:T(8,128)(2,1)S(1)}, bf16[1536,512]{1,0:T(8,128)(2,1)S(1)}, u32[]{:S(2)}, u32[]{:S(2)}) collective-permute-start(bf16[1536,512]{1,0:T(8,128)(2,1)S(1)} %pad_maximum_fusion.1.refs_16_), channel_id=1, source_target_pairs={{0,192},{8,24},{16,208},{24,8},{32,224},{40,56},{48,240},{56,40},{... | collective-permute-start | bytes 4718600 | tf_op jit(solution)/shard_map/ppermute | solution.py:273
  49.5 22.1 %collective-permute-start.18 = (bf16[1536,512]{1,0:T(8,128)(2,1)S(1)}, bf16[1536,512]{1,0:T(8,128)(2,1)S(1)}, u32[]{:S(2)}, u32[]{:S(2)}) collective-permute-start(bf16[1536,512]{1,0:T(8,128)(2,1)S(1)} %pad_maximum_fusion.refs_16_), channel_id=1, source_target_pairs={{0,64},{8,56},{16,80},{24,40},{32,96},{40,24},{48,112},{56,8},{64,... | collective-permute-start | bytes 4718600 | tf_op jit(solution)/shard_map/ppermute | solution.py:273
  52.1 6.9 %collective-permute-start.11 = (bf16[512,384]{1,0:T(8,128)(2,1)S(1)}, bf16[512,384]{1,0:T(8,128)(2,1)S(1)}, u32[]{:S(2)}, u32[]{:S(2)}) collective-permute-start(bf16[512,384]{1,0:T(8,128)(2,1)S(1)} %shard_map.73.refs_10_), channel_id=1, source_target_pairs={{0,1},{1,2},{2,3},{3,4},{4,5},{5,6},{6,7},{7,0},{8,15},{9,8},{10,9... | collective-permute-start | bytes 1179656 | tf_op jit(solution)/shard_map/ppermute | solution.py:282
  53.7 9.6 %collective-permute-start.12 = (bf16[512,384]{1,0:T(8,128)(2,1)S(1)}, bf16[512,384]{1,0:T(8,128)(2,1)S(1)}, u32[]{:S(2)}, u32[]{:S(2)}) collective-permute-start(bf16[512,384]{1,0:T(8,128)(2,1)S(1)} %shard_map.74.refs_11_), channel_id=1, source_target_pairs={{0,1},{1,2},{2,3},{3,4},{4,5},{5,6},{6,7},{7,0},{8,15},{9,8},{10,9... | collective-permute-start | bytes 1179656 | tf_op jit(solution)/shard_map/ppermute | solution.py:282
  59.0 8.4 %collective-permute-start.13 = (bf16[512,384]{1,0:T(8,128)(2,1)S(1)}, bf16[512,384]{1,0:T(8,128)(2,1)S(1)}, u32[]{:S(2)}, u32[]{:S(2)}) collective-permute-start(bf16[512,384]{1,0:T(8,128)(2,1)S(1)} %shard_map.75.refs_12_), channel_id=1, source_target_pairs={{0,1},{1,2},{2,3},{3,4},{4,5},{5,6},{6,7},{7,0},{8,15},{9,8},{10,9... | collective-permute-start | bytes 1179656 | tf_op jit(solution)/shard_map/ppermute | solution.py:282
  63.2 8.4 %collective-permute-start.14 = (bf16[512,384]{1,0:T(8,128)(2,1)S(1)}, bf16[512,384]{1,0:T(8,128)(2,1)S(1)}, u32[]{:S(2)}, u32[]{:S(2)}) collective-permute-start(bf16[512,384]{1,0:T(8,128)(2,1)S(1)} %shard_map.76.refs_13_), channel_id=1, source_target_pairs={{0,1},{1,2},{2,3},{3,4},{4,5},{5,6},{6,7},{7,0},{8,15},{9,8},{10,9... | collective-permute-start | bytes 1179656 | tf_op jit(solution)/shard_map/ppermute | solution.py:282
  75.7 6.5 %collective-permute-start.23 = (bf16[1024,512]{1,0:T(8,128)(2,1)S(1)}, bf16[1024,512]{1,0:T(8,128)(2,1)S(1)}, u32[]{:S(2)}, u32[]{:S(2)}) collective-permute-start(bf16[1024,512]{1,0:T(8,128)(2,1)S(1)} %shard_map.80), channel_id=1, source_target_pairs={{0,8},{8,0},{16,24},{24,16},{32,40},{40,32},{48,56},{56,48},{64,72... | collective-permute-start | bytes 3145736 | tf_op jit(solution)/shard_map/ppermute | solution.py:318
  82.2 1.2 %slice-start = ((bf16[768,768]{1,0:T(8,128)(2,1)}), bf16[768,256]{1,0:T(8,128)(2,1)S(1)}, s32[]{:S(2)}) async-start(bf16[768,768]{1,0:T(8,128)(2,1)} %copy-done.2), calls=%async_computation | async-start | bytes 786432 | tf_op jit(solution)/shard_map/slice | solution.py:296
  83.0 3.8 %collective-permute-start.24 = (bf16[2,128,128]{2,1,0:T(8,128)(2,1)S(1)}, bf16[2,128,128]{2,1,0:T(8,128)(2,1)S(1)}, u32[]{:S(2)}, u32[]{:S(2)}) collective-permute-start(bf16[2,128,128]{2,1,0:T(8,128)(2,1)S(1)} %get-tuple-element.26), channel_id=1, source_target_pairs={{0,16},{8,24},{16,0},{24,8},{32,48},{40,56},{48,32},{56,40},{64,80... | collective-permute-start | bytes 196616 | tf_op jit(solution)/shard_map/ppermute | solution.py:329
  83.4 12.5 %collective-permute-start.28 = (bf16[1536,256]{1,0:T(8,128)(2,1)S(1)}, bf16[1536,256]{1,0:T(8,128)(2,1)S(1)}, u32[]{:S(2)}, u32[]{:S(2)}) collective-permute-start(bf16[1536,256]{1,0:T(8,128)(2,1)S(1)} %pad_maximum_fusion.5.refs_16_), channel_id=1, source_target_pairs={{0,192},{8,24},{16,208},{24,8},{32,224},{40,56},{48,240},{56,40},{... | collective-permute-start | bytes 2359304 | tf_op jit(solution)/shard_map/ppermute | solution.py:273
  86.9 4.9 %collective-permute-start.25 = (bf16[2,128,128]{2,1,0:T(8,128)(2,1)S(1)}, bf16[2,128,128]{2,1,0:T(8,128)(2,1)S(1)}, u32[]{:S(2)}, u32[]{:S(2)}) collective-permute-start(bf16[2,128,128]{2,1,0:T(8,128)(2,1)S(1)} %add_convert_fusion.2), channel_id=1, source_target_pairs={{0,48},{8,56},{16,32},{24,40},{32,16},{40,24},{48,0},{56,8},{64,11... | collective-permute-start | bytes 196616 | tf_op jit(solution)/shard_map/ppermute | solution.py:329
  89.0 19.7 %collective-permute-start.27 = (bf16[1536,256]{1,0:T(8,128)(2,1)S(1)}, bf16[1536,256]{1,0:T(8,128)(2,1)S(1)}, u32[]{:S(2)}, u32[]{:S(2)}) collective-permute-start(bf16[1536,256]{1,0:T(8,128)(2,1)S(1)} %pad_maximum_fusion.4.refs_16_), channel_id=1, source_target_pairs={{0,64},{8,56},{16,80},{24,40},{32,96},{40,24},{48,112},{56,8},{64,... | collective-permute-start | bytes 2359304 | tf_op jit(solution)/shard_map/ppermute | solution.py:273
  91.8 4.2 %collective-permute-start.26 = (bf16[2,128,128]{2,1,0:T(8,128)(2,1)S(1)}, bf16[2,128,128]{2,1,0:T(8,128)(2,1)S(1)}, u32[]{:S(2)}, u32[]{:S(2)}) collective-permute-start(bf16[2,128,128]{2,1,0:T(8,128)(2,1)S(1)} %add_convert_fusion.1), channel_id=1, source_target_pairs={{0,64},{8,72},{16,80},{24,88},{32,96},{40,104},{48,112},{56,120},{... | collective-permute-start | bytes 196616 | tf_op jit(solution)/shard_map/ppermute | solution.py:329
  98.4 12.8 %collective-permute-start.29 = (bf16[1024,256]{1,0:T(8,128)(2,1)S(1)}, bf16[1024,256]{1,0:T(8,128)(2,1)S(1)}, u32[]{:S(2)}, u32[]{:S(2)}) collective-permute-start(bf16[1024,256]{1,0:T(8,128)(2,1)S(1)} %shard_map.83), channel_id=1, source_target_pairs={{0,8},{8,0},{16,24},{24,16},{32,40},{40,32},{48,56},{56,48},{64,72... | collective-permute-start | bytes 1572872 | tf_op jit(solution)/shard_map/ppermute | solution.py:330
  106.5 5.6 %collective-permute-start.30 = (bf16[2,128,128]{2,1,0:T(8,128)(2,1)S(1)}, bf16[2,128,128]{2,1,0:T(8,128)(2,1)S(1)}, u32[]{:S(2)}, u32[]{:S(2)}) collective-permute-start(bf16[2,128,128]{2,1,0:T(8,128)(2,1)S(1)} %add_convert_fusion), channel_id=1, source_target_pairs={{0,192},{8,200},{16,208},{24,216},{32,224},{40,232},{48,240},{56,2... | collective-permute-start | bytes 196616 | tf_op jit(solution)/shard_map/ppermute | solution.py:329
  111.2 1.0 copy-start.1
  113.1 1.6 %collective-permute-start.31 = (bf16[512,256]{1,0:T(8,128)(2,1)S(1)}, bf16[512,256]{1,0:T(8,128)(2,1)S(1)}, u32[]{:S(2)}, u32[]{:S(2)}) collective-permute-start(bf16[512,256]{1,0:T(8,128)(2,1)S(1)} %shard_map.86), channel_id=1, source_target_pairs={{0,8},{8,0},{16,24},{24,16},{32,40},{40,32},{48,56},{56,48},{64,72... | collective-permute-start | bytes 786440 | tf_op jit(solution)/shard_map/ppermute | solution.py:335
